TPU v7x, 32 devices: a whole 2x2x4 slice. The times are simulated.
32 devices in a mesh: groups: 2 (over x), row: 16 (over z, y, core).
Axes of the slice: x: 2, y: 2, z: 4, core: 2. Of those that a mesh axis runs over, the one named last changes fastest.
Arguments:
- pairwise_state: bfloat16 [384, 192, 128], P(('groups', 'row')), parts along dimension 0, may hold values from -6 to 6
- homolog_embedding: bfloat16 [64, 384, 64], P(None, ('groups', 'row')), parts along dimension 1, may hold values from -6 to 6
- alignment_depth: int32 [384], P('groups'), parts along dimension 0, may hold values from 0 to 64
- chain_labels: int32 [384], P('groups'), parts along dimension 0, may hold values from 0 to 7, never falling along the last dimension, each value on 1 to 48 neighbouring positions
- homolog_layer_scale: float32 [64], replicated, may hold values from 0.1 to 1.9
- homolog_layer_shift: float32 [64], replicated, may hold values from -3 to 3
- outer_source_matrix: bfloat16 [64, 32], replicated, may hold values from -0.75 to 0.75
- outer_target_matrix: bfloat16 [64, 32], replicated, may hold values from -0.75 to 0.75
- output_weight: bfloat16 [1024, 128], replicated, may hold values from -0.5 to 0.5
- output_bias: float32 [128], replicated, may hold values from -3 to 3
- chain_match: float32 [128], replicated, may hold values from -3 to 3
- pairwise_norm_gain: float32 [128], replicated, may hold values from 0.1 to 1.9
- pairwise_norm_bias: float32 [128], replicated, may hold values from -3 to 3
- input_projection_weight: bfloat16 [128, 256], replicated, may hold values from -0.5 to 0.5
- input_gate_weight: bfloat16 [128, 256], replicated, may hold values from -0.5 to 0.5
Outputs:
- pair_next: bfloat16 [384, 192, 128], P(('groups', 'row')), parts along dimension 0
- column_inputs: bfloat16 [384, 192, 256], P('groups', 'row'), parts along dimension 0
There are 2 independent parts, one for each index of `groups`. A program takes and returns all parts, laid end to end along the dimension named above; an argument that names none is the same for every part. Nothing has to cross between parts.
Inputs may be any that keep to these rules, and one draw needn't show every extreme that they name: Sequence s is aligned for token n exactly when s < alignment_depth[n]. `chain_labels`: chain ids never fall along the tokens.
All inputs are finite; a program needn't handle non-finite values.
Results may differ from a plain program's by a relative error of at most 0.0074.
Values may be sent and summed in bfloat16 or wider, within the bound.
No kernel may reach another device: no remote copies, remote signals or barrier semaphores. Data moves between devices by JAX's collectives and lax.ppermute only.
A program may use at most 64 MiB of HBM per device.

v0:
```python
import math

import jax
import jax.numpy as jnp
from jax import lax
from jax.sharding import PartitionSpec as P


def normalized_rows(values, gain, shift):
    centre = values - jnp.mean(values, axis=-1, keepdims=True)
    spread = jnp.mean(centre * centre, axis=-1, keepdims=True)
    return centre * lax.rsqrt(spread + 1e-05) * gain + shift


def triangle_inputs(
    tiles, pairwise_norm_gain, pairwise_norm_bias, input_projection_weight, input_gate_weight
):
    tri_normed = normalized_rows(
        tiles.astype(jnp.float32), pairwise_norm_gain, pairwise_norm_bias
    ).astype(jnp.bfloat16)
    projected = jnp.dot(tri_normed, input_projection_weight, preferred_element_type=jnp.float32)
    gating = jnp.dot(tri_normed, input_gate_weight, preferred_element_type=jnp.float32)
    return (projected * jax.nn.sigmoid(gating)).astype(jnp.bfloat16)


def body(
    pairwise_state,
    homolog_embedding,
    alignment_depth,
    chain_labels,
    homolog_layer_scale,
    homolog_layer_shift,
    outer_source_matrix,
    outer_target_matrix,
    output_weight,
    output_bias,
    chain_match,
    pairwise_norm_gain,
    pairwise_norm_bias,
    input_projection_weight,
    input_gate_weight,
):
    token_rows = pairwise_state.shape[0]
    sequence_total = homolog_embedding.shape[0]
    proj_width = outer_source_matrix.shape[1]
    first_row = lax.axis_index("row") * token_rows
    depth_per_row = lax.dynamic_slice_in_dim(alignment_depth, first_row, token_rows)
    chain_rows = lax.dynamic_slice_in_dim(chain_labels, first_row, token_rows)
    normalized_input = normalized_rows(
        homolog_embedding.astype(jnp.float32), homolog_layer_scale, homolog_layer_shift
    ).astype(jnp.bfloat16)
    sequence_index = lax.broadcasted_iota(jnp.int32, (token_rows, sequence_total), 1)
    sequence_mask = (sequence_index < depth_per_row[:, None]).astype(jnp.float32)[:, :, None]
    left_projected = (
        jnp.einsum(
            "snc,cd->nsd", normalized_input, outer_source_matrix, preferred_element_type=jnp.float32
        )
        * sequence_mask
    ).astype(jnp.bfloat16)
    right_proj = (
        jnp.einsum(
            "snc,cd->nsd", normalized_input, outer_target_matrix, preferred_element_type=jnp.float32
        )
        * sequence_mask
    ).astype(jnp.bfloat16)
    right_proj = right_proj.reshape(token_rows, sequence_total * proj_width)
    col_piece = lax.all_gather(right_proj, "row", axis=0, tiled=True)
    col_count = col_piece.shape[0]
    column_block = math.gcd(col_count, 128)
    initial = jnp.zeros((token_rows, col_count, output_weight.shape[1]), jnp.float32)

    def add_block(loop_index, buffer):
        start_offset = loop_index * column_block
        block_cols = lax.dynamic_slice_in_dim(col_piece, start_offset, column_block).reshape(
            column_block, sequence_total, proj_width
        )
        depth_in_block = lax.dynamic_slice_in_dim(alignment_depth, start_offset, column_block)
        shared_terms = jnp.maximum(
            jnp.minimum(depth_per_row[:, None], depth_in_block[None, :]), 1
        ).astype(jnp.float32)
        outer_sum = jnp.einsum(
            "isc,jsd->ijcd", left_projected, block_cols, preferred_element_type=jnp.float32
        )
        outer_sum = (outer_sum / shared_terms[:, :, None, None]).astype(jnp.bfloat16)
        outer_sum = outer_sum.reshape(token_rows, column_block, proj_width * proj_width)
        mixed_out = jnp.einsum(
            "ijh,he->ije", outer_sum, output_weight, preferred_element_type=jnp.float32
        )
        return lax.dynamic_update_slice_in_dim(buffer, mixed_out, start_offset, 1)

    outer_proj = lax.fori_loop(0, col_count // column_block, add_block, initial)
    same = (chain_rows[:, None] == chain_labels[None, :]).astype(jnp.float32)
    pair_next = (
        pairwise_state.astype(jnp.float32)
        + same[:, :, None] * chain_match
        + outer_proj
        + output_bias
    )
    pair_next = pair_next.astype(jnp.bfloat16)
    gated_rows = triangle_inputs(
        pair_next,
        pairwise_norm_gain,
        pairwise_norm_bias,
        input_projection_weight,
        input_gate_weight,
    )
    column_inputs = lax.all_to_all(gated_rows, "row", split_axis=1, concat_axis=0, tiled=True)
    return (pair_next, column_inputs)


def solution(mesh):
    return jax.shard_map(
        body,
        mesh=mesh,
        in_specs=(
            P(("groups", "row"), None, None),
            P(None, ("groups", "row"), None),
            P("groups"),
            P("groups"),
            P(),
            P(),
            P(),
            P(),
            P(),
            P(),
            P(),
            P(),
            P(),
            P(),
            P(),
        ),
        out_specs=(P(("groups", "row"), None, None), P("groups", "row", None)),
        check_vma=False,
    )
```

profile of v0, /device:TPU:0, one launch (start us, length us, event | category | flops | bytes accessed | tf_op | source)
XLA Modules:
  0.0 93.0 jit_solution(12395183364962869699)
XLA Ops:
  0.6 0.0 copy-start
  0.6 0.8 dynamic_slice.21
  1.4 0.1 fusion.29
  1.5 1.1 %convert_reduce_fusion.1 = f32[64,12]{0,1:T(8,128)S(1)} fusion(bf16[64,12,64]{2,0,1:T(8,128)(2,1)} %param.18), kind=kLoop, calls=%fused_computation.25 | loop fusion | flops 97536 | bytes 101376 | tf_op jit(solution)/shard_map/reduce_sum | solution.py:10
  2.6 1.3 %fusion.16 = f32[64,12]{0,1:T(8,128)S(1)} fusion(bf16[64,12,64]{2,0,1:T(8,128)(2,1)} %param.18, f32[64,12]{0,1:T(8,128)S(1)} %broadcast_multiply_fusion.1), kind=kLoop, calls=%fused_computation.28 | loop fusion | flops 195840 | bytes 104448 | tf_op jit(solution)/shard_map/reduce_sum | solution.py:11
  3.9 1.4 %fusion.12 = bf16[12,64,32]{1,2,0:T(8,128)(2,1)S(1)} fusion(f32[12,64]{1,0:T(8,128)S(1)} %fusion.29, bf16[64,12,64]{2,0,1:T(8,128)(2,1)} %param.18, f32[64]{0:T(128)} %param.22, f32[64]{0:T(128)} %param.21, f32[64,12]{0,1:T(8,128)S(1)} %add_rsqrt_fusion.1, f32[64,12]{0,1:T(8,128)S(1)} %broadcast_multiply_fusion.1, bf16[64,32]{0,1:T(8,128)(2,1)} %param.24), kind=kOutput, calls=%fused_computation.22 | convolution fusion | flops 3489792 | bytes 161280 | tf_op jit(solution)/shard_map/snc,cd->nsd/dot_general | solution.py:61
  5.3 0.1 copy.27
  5.4 0.2 reshape.129
  5.7 26.2 %all-gather = bf16[16,12,2048]{2,1,0:T(8,128)(2,1)S(1)} all-gather(bf16[1,12,2048]{2,1,0:T(8,128)(2,1)S(1)} %reshape.129), channel_id=1, replica_groups=mesh['groups'=2,'row'=16] {'row'}, dimensions={0}, use_global_device_ids=true | all-gather | bytes 835584 | tf_op jit(solution)/shard_map/all_gather | solution.py:67
  31.9 0.0 copy-start.3
  31.9 0.0 copy-start.10
  31.9 0.0 copy-start.12
  31.9 0.2 reshape.130
  32.1 0.7 copy-done.3
  32.8 0.0 copy-done.10
  32.8 0.0 copy-done.12
  32.8 0.0 copy-done.13
  32.8 0.0 copy-start.1
  32.8 0.0 copy-start.11
  32.9 0.4 fusion.13
  33.3 0.1 broadcast_in_dim.8
  33.4 0.4 copy-done.1
  33.8 0.0 copy-done.11
  33.8 0.0 copy-start.4
  33.8 13.6 %while.13 = (s32[]{:T(128)}, f32[12,192,128]{2,1,0:T(8,128)S(1)}, bf16[192,2048]{1,0:T(8,128)(2,1)S(1)}, bf16[12,64,32]{1,2,0:T(8,128)(2,1)S(1)}, s32[12]{0:T(12...) while((s32[]{:T(128)}, f32[12,192,128]{2,1,0:T(8,128)S(1)}, ...), condition=%wide.region_3.0_spmd, body=%wide.region_2.0_spmd.sunk | while | flops 303565056 | bytes 9886679 | solution.py:91
  33.8 0.1 dynamic_slice.26
  33.9 0.1 maximum_convert_fusion.2
  34.0 0.3 copy.45
  34.3 1.0 %fusion.40 = bf16[12,64,32,32]{1,2,0,3:T(8,128)(2,1)S(1)} fusion(f32[12,64]{1,0:T(8,128)S(1)} %maximum_convert_fusion.2, bf16[64,64,32,1]{0,2,1,3:T(8,128)(2,1)S(1)} %bitcast.58, bf16[12,64,32]{1,2,0:T(8,128)(2,1)S(1)} %get-tuple-element.225), kind=kOutput, calls=%fused_computation.1.clone.1 | convolution fusion | flops 102236160 | bytes 1887232 | tf_op jit(solution)/shard_map/while/body/eval_jaxpr/isc,jsd->ijcd/dot_general | solution.py:81
  35.3 2.0 %copy.46 = bf16[12,64,32,32]{1,3,2,0:T(8,128)(2,1)S(1)} copy(bf16[12,64,32,32]{1,2,0,3:T(8,128)(2,1)S(1)} %fusion.40) | data formatting | bytes 3145728 | tf_op jit(solution)/shard_map/while/body/eval_jaxpr/convert_element_type | solution.py:84
  37.3 1.0 %convolution_dynamic-update-slice_fusion.2 = f32[12,192,128]{2,1,0:T(8,128)S(1)} fusion(f32[12,192,128]{2,1,0:T(8,128)S(1)} %get-tuple-element.212, s32[]{:T(128)S(6)} %select_n.15, bf16[12,64,1024]{1,2,0:T(8,128)(2,1)S(1)} %bitcast.57, bf16[1024,128]{1,0:T(8,128)(2,1)S(1)} %get-tuple-element.228), kind=kOutput, calls=%fused_computation.2.clone.1 | convolution fusion | flops 201326592 | bytes 3801092 | tf_op jit(solution)/shard_map/while/body/eval_jaxpr/ijh,he->ije/dot_general | solution.py:86
  38.3 0.1 dynamic_slice.26
  38.4 0.1 maximum_convert_fusion.2
  38.5 0.3 copy.45
  38.8 1.0 %fusion.40 = bf16[12,64,32,32]{1,2,0,3:T(8,128)(2,1)S(1)} fusion(f32[12,64]{1,0:T(8,128)S(1)} %maximum_convert_fusion.2, bf16[64,64,32,1]{0,2,1,3:T(8,128)(2,1)S(1)} %bitcast.58, bf16[12,64,32]{1,2,0:T(8,128)(2,1)S(1)} %get-tuple-element.225), kind=kOutput, calls=%fused_computation.1.clone.1 | convolution fusion | flops 102236160 | bytes 1887232 | tf_op jit(solution)/shard_map/while/body/eval_jaxpr/isc,jsd->ijcd/dot_general | solution.py:81
  39.8 2.0 %copy.46 = bf16[12,64,32,32]{1,3,2,0:T(8,128)(2,1)S(1)} copy(bf16[12,64,32,32]{1,2,0,3:T(8,128)(2,1)S(1)} %fusion.40) | data formatting | bytes 3145728 | tf_op jit(solution)/shard_map/while/body/eval_jaxpr/convert_element_type | solution.py:84
  41.8 1.0 %convolution_dynamic-update-slice_fusion.2 = f32[12,192,128]{2,1,0:T(8,128)S(1)} fusion(f32[12,192,128]{2,1,0:T(8,128)S(1)} %get-tuple-element.212, s32[]{:T(128)S(6)} %select_n.15, bf16[12,64,1024]{1,2,0:T(8,128)(2,1)S(1)} %bitcast.57, bf16[1024,128]{1,0:T(8,128)(2,1)S(1)} %get-tuple-element.228), kind=kOutput, calls=%fused_computation.2.clone.1 | convolution fusion | flops 201326592 | bytes 3801092 | tf_op jit(solution)/shard_map/while/body/eval_jaxpr/ijh,he->ije/dot_general | solution.py:86
  42.9 0.1 dynamic_slice.26
  42.9 0.1 maximum_convert_fusion.2
  43.0 0.3 copy.45
  43.3 1.0 %fusion.40 = bf16[12,64,32,32]{1,2,0,3:T(8,128)(2,1)S(1)} fusion(f32[12,64]{1,0:T(8,128)S(1)} %maximum_convert_fusion.2, bf16[64,64,32,1]{0,2,1,3:T(8,128)(2,1)S(1)} %bitcast.58, bf16[12,64,32]{1,2,0:T(8,128)(2,1)S(1)} %get-tuple-element.225), kind=kOutput, calls=%fused_computation.1.clone.1 | convolution fusion | flops 102236160 | bytes 1887232 | tf_op jit(solution)/shard_map/while/body/eval_jaxpr/isc,jsd->ijcd/dot_general | solution.py:81
  44.3 2.0 %copy.46 = bf16[12,64,32,32]{1,3,2,0:T(8,128)(2,1)S(1)} copy(bf16[12,64,32,32]{1,2,0,3:T(8,128)(2,1)S(1)} %fusion.40) | data formatting | bytes 3145728 | tf_op jit(solution)/shard_map/while/body/eval_jaxpr/convert_element_type | solution.py:84
  46.3 1.0 %convolution_dynamic-update-slice_fusion.2 = f32[12,192,128]{2,1,0:T(8,128)S(1)} fusion(f32[12,192,128]{2,1,0:T(8,128)S(1)} %get-tuple-element.212, s32[]{:T(128)S(6)} %select_n.15, bf16[12,64,1024]{1,2,0:T(8,128)(2,1)S(1)} %bitcast.57, bf16[1024,128]{1,0:T(8,128)(2,1)S(1)} %get-tuple-element.228), kind=kOutput, calls=%fused_computation.2.clone.1 | convolution fusion | flops 201326592 | bytes 3801092 | tf_op jit(solution)/shard_map/while/body/eval_jaxpr/ijh,he->ije/dot_general | solution.py:86
  47.4 0.0 copy-done.4
  47.4 0.1 dynamic_slice.20
  47.5 0.1 compare_convert_fusion
  47.5 0.0 copy-done.5
  47.5 0.0 copy-done.6
  47.6 0.0 copy-start.8
  47.6 1.9 %convert_reduce_fusion = (f32[12,192]{1,0:T(8,128)S(1)}, bf16[12,192,128]{2,1,0:T(8,128)(2,1)S(1)}) fusion(f32[128]{0:T(128)S(1)} %copy-done.5, f32[12,192,128]{2,1,0:T(8,128)S(1)} %get-tuple-element.126, f32[128]{0:T(128)S(1)} %copy-done.6, f32[12,192]{1,0:T(8,128)S(1)} %compare_convert_fusion, bf16[12,192,128]{2,1,0:T(8,128)(2,1)} %param.17), kind=kLoop, calls=%fused_computation.10 | loop fusion | flops 2356992 | bytes 2378752 | tf_op jit(solution)/shard_map/reduce_sum | solution.py:10
  49.5 0.0 copy-start.2
  49.5 0.8 fusion.6
  50.3 0.0 copy-done
  50.4 0.0 copy-done.7
  50.4 0.0 copy-done.8
  50.4 0.0 copy-start.9
  50.4 0.8 fusion.20
  51.2 0.0 copy-done.2
  51.2 0.0 copy-done.9
  51.2 1.1 %multiply_convert_fusion = bf16[12,192,256]{2,1,0:T(8,128)(2,1)S(1)} fusion(f32[12,192,256]{2,1,0:T(8,128)S(1)} %fusion.20, bf16[12,192,128]{2,1,0:T(8,128)(2,1)S(1)} %get-tuple-element.156, f32[128]{0:T(128)S(1)} %copy-done.7, f32[128]{0:T(128)S(1)} %copy-done.8, f32[12,192]{1,0:T(8,128)S(1)} %add_rsqrt_fusion, f32[12,192]{1,0:T(8,128)S(1)} %broadcast_multiply_fusion, ...), kind=kOutput, calls=%fused_computation.8 | convolution fusion | flops 155713536 | bytes 4213760 | tf_op jit(solution)/shard_map/dot_general | solution.py:21
  52.3 0.7 copy.29
  53.0 38.7 %all_to_all.18 = bf16[12,192,256]{2,0,1:T(8,128)(2,1)S(1)} all-to-all(bf16[12,192,256]{2,0,1:T(8,128)(2,1)S(1)} %copy.29), channel_id=1, replica_groups=mesh['groups'=2,'row'=16] {'row'}, dimensions={1} | all-to-all | bytes 2359296 | tf_op jit(solution)/shard_map/all_to_all | solution.py:107
  91.7 0.1 copy.31
  91.8 1.2 %all_to_all.16 = bf16[192,12,256]{2,0,1:T(8,128)(2,1)} reshape(bf16[16,12,12,256]{3,1,0,2:T(8,128)(2,1)S(1)} %copy.31) | data formatting | bytes 2359296 | tf_op jit(solution)/shard_map/all_to_all | solution.py:107
  (11 shorter events, 0.1 us)
Async XLA Ops:
  0.6 49.7 %copy-start = (bf16[128,256]{1,0:T(8,128)(2,1)S(1)}, bf16[128,256]{1,0:T(8,128)(2,1)}, u32[]{:S(2)}) copy-start(bf16[128,256]{1,0:T(8,128)(2,1)} %param.31) | copy-start | bytes 196612
  31.9 0.9 copy-start.3
  31.9 0.9 copy-start.10
  31.9 0.9 copy-start.12
  31.9 0.9 copy-start.13
  32.8 1.0 %copy-start.1 = (bf16[1024,128]{1,0:T(8,128)(2,1)S(1)}, bf16[1024,128]{1,0:T(8,128)(2,1)}, u32[]{:S(2)}) copy-start(bf16[1024,128]{1,0:T(8,128)(2,1)} %param.25) | copy-start | bytes 786436
  32.8 0.9 %copy-start.11 = (s32[192]{0:T(256)S(1)}, s32[192]{0:T(256)}, u32[]{:S(2)}) copy-start(s32[192]{0:T(256)} %param.19) | copy-start | bytes 2308
  33.8 13.6 %copy-start.4 = (s32[192]{0:T(256)S(1)}, s32[192]{0:T(256)}, u32[]{:S(2)}) copy-start(s32[192]{0:T(256)} %param.20) | copy-start | bytes 2308
  33.8 13.8 %copy-start.5 = (f32[128]{0:T(128)S(1)}, f32[128]{0:T(128)}, u32[]{:S(2)}) copy-start(f32[128]{0:T(128)} %param.26) | copy-start | bytes 1540
  33.8 13.8 %copy-start.6 = (f32[128]{0:T(128)S(1)}, f32[128]{0:T(128)}, u32[]{:S(2)}) copy-start(f32[128]{0:T(128)} %param.27) | copy-start | bytes 1540
  47.5 2.8 %copy-start.7 = (f32[128]{0:T(128)S(1)}, f32[128]{0:T(128)}, u32[]{:S(2)}) copy-start(f32[128]{0:T(128)} %param.29) | copy-start | bytes 1540
  47.6 2.8 %copy-start.8 = (f32[128]{0:T(128)S(1)}, f32[128]{0:T(128)}, u32[]{:S(2)}) copy-start(f32[128]{0:T(128)} %param.28) | copy-start | bytes 1540
  49.5 1.7 %copy-start.2 = (bf16[12,192,128]{2,1,0:T(8,128)(2,1)}, bf16[12,192,128]{2,1,0:T(8,128)(2,1)S(1)}, u32[]{:S(2)}) copy-start(bf16[12,192,128]{2,1,0:T(8,128)(2,1)S(1)} %get-tuple-element.156) | copy-start | bytes 1769476
  50.4 0.8 copy-start.9
where the time goes:
time: 93.7 us; the launch traced here: 93 us
  blocking collectives  64.9 us (69%)
  local copies, waits for them, and re-layouts  11.9 us (13%)
  matrix products  9.66 us (10%)
  other arithmetic  5.49 us (6%)
    all_to_all x1, blocking collectives, body(): lax.all_to_all(gated_rows, 'row', split_axis=1, concat_axis=0, tiled=True)  38.7 us
    all_gather x1, blocking collectives, body(): col_piece = lax.all_gather(right_proj, 'row', axis=0, tiled=True)  26.2 us
    convert_element_type x3, local copies, waits for them, and re-layouts, add_block(): (outer_sum / shared_terms[:, :, None, None]).astype(jnp.bfloat16)  6.08 us
    dot_general x3, matrix products, add_block(): jnp.einsum('ijh,he->ije', outer_sum, output_weight, preferred_element_typ...  3.05 us
    reduce_sum x2, other arithmetic, normalized_rows(): centre = values - jnp.mean(values, axis=-1, keepdims=True)  3.01 us
    dot_general x3, matrix products, add_block(): jnp.einsum('isc,jsd->ijcd', left_projected, block_cols, preferred_element...  2.94 us
    reduce_sum x2, other arithmetic, normalized_rows(): spread = jnp.mean(centre * centre, axis=-1, keepdims=True)  2.08 us

commit v1 on v0

v1 whole, which is shorter than its diff:
```python
import functools

import jax
import jax.numpy as jnp
from jax import lax
from jax.experimental import pallas as pl
from jax.experimental.pallas import tpu as pltpu
from jax.sharding import PartitionSpec as P

F32 = jnp.float32
BF16 = jnp.bfloat16
NT = (((1,), (1,)), ((), ()))
VMEM = pltpu.VMEM
SMEM = pltpu.SMEM
LIMIT = 48 * 1024 * 1024


def whole(space):
    return pl.BlockSpec(memory_space=space)


def params(**kw):
    return pltpu.CompilerParams(vmem_limit_bytes=LIMIT, **kw)


def project_kernel(
    row_ref, depth_ref, hom_ref, scale_ref, shift_ref, src_ref, tgt_ref, left_ref, right_ref, packed_ref, tmp_ref
):
    tokens, seqs, feats = hom_ref.shape
    width = src_ref.shape[0]
    half = width // 2
    values = hom_ref[...].astype(F32).reshape(tokens * seqs, feats)
    centre = values - jnp.mean(values, axis=-1, keepdims=True)
    spread = jnp.mean(centre * centre, axis=-1, keepdims=True)
    normed = (centre * lax.rsqrt(spread + 1e-05) * scale_ref[...] + shift_ref[...]).astype(BF16)
    left = lax.dot_general(normed, src_ref[...], NT, preferred_element_type=F32)
    right = lax.dot_general(normed, tgt_ref[...], NT, preferred_element_type=F32)
    both = jnp.concatenate([src_ref[...], tgt_ref[...]], axis=0)
    first = row_ref[0] * tokens
    row_pos = lax.broadcasted_iota(jnp.int32, (seqs, width), 0)
    lane_pos = lax.broadcasted_iota(jnp.int32, (2 * width, seqs), 1)
    tmp_ref[...] = jnp.zeros_like(tmp_ref)
    for n in range(tokens):
        depth = depth_ref[first + n]
        rows = slice(n * seqs, (n + 1) * seqs)
        left_ref[rows] = jnp.where(row_pos < depth, left[rows], 0.0).astype(BF16)
        right_ref[rows] = jnp.where(row_pos < depth, right[rows], 0.0).astype(BF16)
        turned = lax.dot_general(both, normed[rows], NT, preferred_element_type=F32)
        turned = jnp.where(lane_pos < depth, turned, 0.0)
        tmp_ref[n, 0:half] = jnp.concatenate([turned[0:half], turned[half:width]], axis=1)
        tmp_ref[n, half:width] = jnp.concatenate(
            [turned[width : width + half], turned[width + half :]], axis=1
        )
    for q in range(width):
        packed_ref[:, q * 2 * seqs : (q + 1) * 2 * seqs] = tmp_ref[:, q, :].astype(BF16)


def tiles_kernel(row_ref, state_ref, *rest):
    count = (len(rest) - 4) // 1
    outs, (wide_ref, msg_ref, narrow_ref, sems) = rest[:count], rest[count:]
    tokens = state_ref.shape[0]
    wide_ref[...] = state_ref[...].astype(F32)
    for d in range(count):
        for i in range(tokens):
            msg_ref[i * tokens : (i + 1) * tokens] = wide_ref[i, d * tokens : (d + 1) * tokens, :]
        narrow_ref[d] = msg_ref[...].astype(BF16)
    row = row_ref[0]
    copies = [
        pltpu.make_async_copy(narrow_ref.at[row ^ k], outs[k], sems.at[k]) for k in range(count)
    ]
    for copy in copies:
        copy.start()
    for copy in copies:
        copy.wait()


def mix_kernel(left_ref, right_ref, turned_ref, weight_ref, y_ref, z_ref):
    q = pl.program_id(0)
    half = pl.num_programs(0)
    seqs = y_ref.shape[0] // 2
    width = weight_ref.shape[2]
    tokens = left_ref.shape[0] // seqs
    for lhs, w_ref, out_ref in ((left_ref, turned_ref, y_ref), (right_ref, weight_ref, z_ref)):
        pair = jnp.concatenate([w_ref[q], w_ref[q + half]], axis=1)
        mixed = jnp.dot(lhs[...], pair, preferred_element_type=F32).astype(BF16)
        for n in range(tokens):
            rows = slice(n * seqs, (n + 1) * seqs)
            cols = slice(n * width, (n + 1) * width)
            out_ref[0:seqs, cols] = mixed[rows, 0:width]
            out_ref[seqs : 2 * seqs, cols] = mixed[rows, width : 2 * width]


def pair_kernel(row_ref, depth_ref, chain_ref, depth_col, chain_col, match_ref, bias_ref, state_ref, y_ref, z_ref, *rest):
    items, (next_ref, col_ref, all_ref, inv_ref, close_ref, sems) = rest[:-6], rest[-6:]
    step = pl.program_id(0)
    row = row_ref[0]
    count = len(items)
    pad = items[0].shape[0]
    inner = y_ref.shape[0]
    block, total, width = state_ref.shape
    tokens = total // count

    @pl.when(step == 0)
    def _():
        copies = [
            pltpu.make_async_copy(
                items[k], all_ref.at[pl.ds(pl.multiple_of((row ^ k) * pad, pad), pad)], sems.at[k]
            )
            for k in range(count)
        ]
        for copy in copies:
            copy.start()
        inv_ref[...] = 1.0 / jnp.maximum(
            jnp.broadcast_to(depth_col[...], inv_ref.shape).astype(F32), 1.0
        )
        for copy in copies:
            copy.wait()

    for cols, w_ref, out_ref, is_row in (
        (slice(inner, 2 * inner), y_ref, next_ref, True),
        (slice(0, inner), z_ref, col_ref, False),
    ):
        prod = jnp.dot(all_ref[:, cols], w_ref[...], preferred_element_type=F32)
        for t in range(block):
            own = row * tokens + step * block + t
            inv_own = 1.0 / jnp.maximum(jnp.full((1, width), depth_ref[own], jnp.int32).astype(F32), 1.0)
            lanes = slice(t * width, (t + 1) * width)
            for s in range(count):
                close_ref[s * tokens : (s + 1) * tokens] = prod[s * pad : s * pad + tokens, lanes]
            extra = jnp.where(chain_col[...] == chain_ref[own], match_ref[...], 0.0) + bias_ref[...]
            value = close_ref[...] * jnp.maximum(inv_ref[...], inv_own) + extra
            if is_row:
                out_ref[t] = (state_ref[t].astype(F32) + value).astype(BF16)
            else:
                out_ref[t] = value


def gate_kernel(row_ref, col_ref, gain_ref, shift_ref, proj_ref, gate_ref, *rest):
    tiles, (out_ref, msg_ref, wide_ref, sems) = rest[:-4], rest[-4:]
    step = pl.program_id(0)
    row = row_ref[0]
    count = len(tiles)
    rows = tiles[0].shape[0]
    total, width = col_ref.shape[1:]
    tokens = total // count

    @pl.when(step == 0)
    def _():
        copies = [
            pltpu.make_async_copy(tiles[k], msg_ref.at[row ^ k], sems.at[k]) for k in range(count)
        ]
        for copy in copies:
            copy.start()
        for copy in copies:
            copy.wait()
        for s in range(count):
            wide_ref[s * rows : (s + 1) * rows] = msg_ref[s].astype(F32)

    state = wide_ref[pl.ds(step, total, stride=tokens), :]
    pair = (state + col_ref[0]).astype(BF16)
    ones = jnp.full((width, width), 1.0 / width, BF16)
    centre = pair.astype(F32) - jnp.dot(pair, ones, preferred_element_type=F32)
    square = centre * centre
    high = square.astype(BF16)
    low = (square - high.astype(F32)).astype(BF16)
    spread = jnp.dot(
        jnp.concatenate([high, low], axis=1),
        jnp.concatenate([ones, ones], axis=0),
        preferred_element_type=F32,
    )
    normed = (centre * lax.rsqrt(spread + 1e-05) * gain_ref[...] + shift_ref[...]).astype(BF16)
    projected = jnp.dot(normed, proj_ref[...], preferred_element_type=F32)
    gating = jnp.dot(normed, gate_ref[...], preferred_element_type=F32)
    out_ref[0] = (projected * (0.5 + 0.5 * jnp.tanh(0.5 * gating))).astype(BF16)


def body(
    pairwise_state,
    homolog_embedding,
    alignment_depth,
    chain_labels,
    homolog_layer_scale,
    homolog_layer_shift,
    outer_source_matrix,
    outer_target_matrix,
    output_weight,
    output_bias,
    chain_match,
    pairwise_norm_gain,
    pairwise_norm_bias,
    input_projection_weight,
    input_gate_weight,
    *,
    count,
):
    tokens, total, width = pairwise_state.shape
    seqs, _, feats = homolog_embedding.shape
    factor = outer_source_matrix.shape[1]
    half = factor // 2
    pad = -(-tokens // 16) * 16
    inner = factor * seqs
    gated = input_projection_weight.shape[1]
    row = lax.axis_index("row").astype(jnp.int32).reshape(1)

    def swap(array, bit):
        return lax.ppermute(array, "row", [(r, r ^ bit) for r in range(count)])

    left, right, packed = pl.pallas_call(
        project_kernel,
        out_shape=(
            jax.ShapeDtypeStruct((tokens * seqs, factor), BF16),
            jax.ShapeDtypeStruct((tokens * seqs, factor), BF16),
            jax.ShapeDtypeStruct((pad, 2 * inner), BF16),
        ),
        in_specs=[whole(SMEM), whole(SMEM)] + [whole(VMEM)] * 5,
        out_specs=(whole(VMEM),) * 3,
        scratch_shapes=[VMEM((pad, factor, 2 * seqs), F32)],
        compiler_params=params(),
        name="project",
    )(
        row,
        alignment_depth,
        homolog_embedding.transpose(1, 0, 2),
        homolog_layer_scale.reshape(1, feats),
        homolog_layer_shift.reshape(1, feats),
        outer_source_matrix.T,
        outer_target_matrix.T,
    )
    items = {0: packed}
    bit = count // 2
    while bit:
        for k in sorted(items):
            items[k | bit] = swap(items[k], bit)
        bit //= 2

    tiles = pl.pallas_call(
        tiles_kernel,
        out_shape=tuple(jax.ShapeDtypeStruct((tokens * tokens, width), BF16) for _ in range(count)),
        in_specs=[whole(SMEM), whole(VMEM)],
        out_specs=(whole(pl.ANY),) * count,
        scratch_shapes=[
            VMEM((tokens, total, width), F32),
            VMEM((tokens * tokens, width), F32),
            VMEM((count, tokens * tokens, width), BF16),
            pltpu.SemaphoreType.DMA((count,)),
        ],
        compiler_params=params(),
        name="tiles",
    )(row, pairwise_state)
    tiles = [tiles[0]] + [swap(tiles[k], k) for k in range(1, count)]

    weight = output_weight.reshape(factor, factor, width)
    y, z = pl.pallas_call(
        mix_kernel,
        grid=(half,),
        out_shape=(jax.ShapeDtypeStruct((inner, tokens * width), BF16),) * 2,
        in_specs=[whole(VMEM)] * 4,
        out_specs=(pl.BlockSpec((2 * seqs, tokens * width), lambda q: (q, 0)),) * 2,
        compiler_params=params(),
        cost_estimate=pl.CostEstimate(
            flops=4 * tokens * seqs * factor * factor * width,
            bytes_accessed=4 * inner * tokens * width,
            transcendentals=0,
        ),
        name="mix",
    )(left, right, weight.transpose(1, 0, 2), weight)

    block = 2
    steps = tokens // block
    pair_next, columns = pl.pallas_call(
        pair_kernel,
        grid=(steps,),
        out_shape=(
            jax.ShapeDtypeStruct((tokens, total, width), BF16),
            jax.ShapeDtypeStruct((tokens, total, width), F32),
        ),
        in_specs=[whole(SMEM)] * 3
        + [whole(VMEM)] * 4
        + [
            pl.BlockSpec((block, total, width), lambda g: (g, 0, 0)),
            pl.BlockSpec((inner, block * width), lambda g: (0, g)),
            pl.BlockSpec((inner, block * width), lambda g: (0, g)),
        ]
        + [whole(pl.ANY)] * count,
        out_specs=(pl.BlockSpec((block, total, width), lambda g: (g, 0, 0)),) * 2,
        scratch_shapes=[
            VMEM((count * pad, 2 * inner), BF16),
            VMEM((total, width), F32),
            VMEM((total, width), F32),
            pltpu.SemaphoreType.DMA((count,)),
        ],
        compiler_params=params(),
        cost_estimate=pl.CostEstimate(
            flops=4 * count * pad * inner * tokens * width,
            bytes_accessed=4 * inner * tokens * width + 8 * tokens * total * width,
            transcendentals=0,
        ),
        name="pair",
    )(
        row,
        alignment_depth,
        chain_labels,
        alignment_depth.reshape(total, 1),
        chain_labels.reshape(total, 1),
        chain_match.reshape(1, width),
        output_bias.reshape(1, width),
        pairwise_state,
        y,
        z,
        *[items[k] for k in range(count)],
    )

    out = pl.pallas_call(
        gate_kernel,
        grid=(tokens,),
        out_shape=jax.ShapeDtypeStruct((tokens, total, gated), BF16),
        in_specs=[whole(SMEM), pl.BlockSpec((1, total, width), lambda j: (j, 0, 0))]
        + [whole(VMEM)] * 4
        + [whole(pl.ANY)] * count,
        out_specs=pl.BlockSpec((1, total, gated), lambda j: (j, 0, 0)),
        scratch_shapes=[
            VMEM((count, tokens * tokens, width), BF16),
            VMEM((count * tokens * tokens, width), F32),
            pltpu.SemaphoreType.DMA((count,)),
        ],
        compiler_params=params(),
        cost_estimate=pl.CostEstimate(
            flops=4 * tokens * total * width * gated,
            bytes_accessed=tokens * total * (2 * gated + 6 * width),
            transcendentals=tokens * total * gated,
        ),
        name="gate",
    )(
        row,
        columns,
        pairwise_norm_gain.reshape(1, width),
        pairwise_norm_bias.reshape(1, width),
        input_projection_weight,
        input_gate_weight,
        *tiles,
    )
    return pair_next, out.transpose(1, 0, 2)


def solution(mesh):
    return jax.shard_map(
        functools.partial(body, count=mesh.shape["row"]),
        mesh=mesh,
        in_specs=(
            P(("groups", "row"), None, None),
            P(None, ("groups", "row"), None),
            P("groups"),
            P("groups"),
        )
        + (P(),) * 11,
        out_specs=(P(("groups", "row"), None, None), P("groups", "row", None)),
        check_vma=False,
    )
```

time: 93.7 us -> 100 us (1.067)
  blocking collectives: 64.9 us -> 0 us
  Pallas kernels: 0 us -> 33.7 us
  starting transfers between devices: 0 us -> 33 us
  waiting for transfers between devices: 0 us -> 19.3 us
  matrix products: 9.66 us -> 0 us
  other arithmetic: 5.49 us -> 0 us
    all_to_all x1 -> x0, blocking collectives: 38.7 us -> none  [body(): lax.all_to_all(gated_rows, 'row', split_axis=1, concat_axis=0, tiled=True)]
    pallas_call x0 -> x5, Pallas kernels: none -> 33.7 us  [the longest x1 12.4 us: body(): pl.pallas_call(pair_kernel, grid=(steps,), out_shape=(jax.ShapeDtypeStruc...]
    ppermute x0 -> x30, starting transfers between devices: none -> 33 us  [swap(): return lax.ppermute(array, 'row', [(r, r ^ bit) for r in range(count)])]
    all_gather x1 -> x0, blocking collectives: 26.2 us -> none  [body(): col_piece = lax.all_gather(right_proj, 'row', axis=0, tiled=True)]
    ppermute x0 -> x30, waiting for transfers between devices: none -> 19.3 us  [swap(): return lax.ppermute(array, 'row', [(r, r ^ bit) for r in range(count)])]
    dot_general x10 -> x0, matrix products: 9.66 us -> none  [the longest x3 3.05 us: add_block(): jnp.einsum('ijh,he->ije', outer_sum, output_weight, preferred_element_typ...]
    unnamed x29 -> x34, local copies, waits for them, and re-layouts: 1.45 us -> 10.1 us
    convert_element_type x5 -> x0, local copies, waits for them, and re-layouts: 6.93 us -> none  [the longest x3 6.08 us: add_block(): (outer_sum / shared_terms[:, :, None, None]).astype(jnp.bfloat16)]
  transfers between devices with their start and end apart: 0 -> 30, of which waited for: 0 -> 8; matrix products, arithmetic and copies ran while one was open for 0% -> 3% of each run, Pallas kernels for 0% -> 24%
where the time goes in v1:
time: 100 us; the launch traced here: 99.5 us
  Pallas kernels  33.7 us (34%)
  starting transfers between devices  33 us (33%)
  waiting for transfers between devices  19.3 us (19%)
  local copies, waits for them, and re-layouts  12.7 us (13%)
    ppermute x30, starting transfers between devices, swap(): return lax.ppermute(array, 'row', [(r, r ^ bit) for r in range(count)])  33 us
    ppermute x30, waiting for transfers between devices, swap(): return lax.ppermute(array, 'row', [(r, r ^ bit) for r in range(count)])  19.3 us
    pallas_call x1, Pallas kernels, body(): pl.pallas_call(pair_kernel, grid=(steps,), out_shape=(jax.ShapeDtypeStruc...  12.4 us
    pallas_call x1, Pallas kernels, body(): pl.pallas_call(mix_kernel, grid=(half,), out_shape=(jax.ShapeDtypeStruct(...  10.4 us
    unnamed x34, local copies, waits for them, and re-layouts  10.1 us
    pallas_call x1, Pallas kernels, body(): pl.pallas_call(gate_kernel, grid=(tokens,), out_shape=jax.ShapeDtypeStruc...  8.3 us
  transfers between devices with their start and end apart: 30, of which 8 were waited for; matrix products, arithmetic and copies ran while one was open for 3% of the time, Pallas kernels for 24%

profile of v1, /device:TPU:0, one launch (start us, length us, event | category | flops | bytes accessed | tf_op | source)
XLA Modules:
  0.0 99.5 jit_solution(13590974431973652223)
XLA Ops:
  0.6 0.9 copy-done.3
  1.6 0.7 copy-done.6
  2.2 0.7 copy-done.8
  2.9 0.7 copy-done.9
  3.6 0.7 copy-done.13
  4.3 0.7 copy-done.14
  4.9 1.4 %project.1 = (bf16[768,32]{1,0:T(8,128)(2,1)S(1)}, bf16[768,32]{1,0:T(8,128)(2,1)S(1)}, bf16[16,4096]{1,0:T(8,128)(2,1)S(1)}) custom-call(s32[1]{0:T(128)} %bitcast.row_ref, s32[192]{0:T(256)S(1)} %copy-done.6, bf16[12,64,64]{2,1,0:T(8,128)(2,1)S(1)} %bitcast.18, f32[1,64]{1,0:T(1,128)S(1)} %bitcast.25, f32[1,64]{1,0:T(1,128)S(1)} %bitcast.26, ...), custom_call_target="tpu_custom_call" | custom-call | tf_op jit(solution)/shard_map/project/pallas_call | solution.py:208
  6.4 4.1 %collective-permute-start.7 = (bf16[16,4096]{1,0:T(8,128)(2,1)S(1)}, bf16[16,4096]{1,0:T(8,128)(2,1)S(1)}, u32[]{:S(2)}, u32[]{:S(2)}) collective-permute-start(bf16[16,4096]{1,0:T(8,128)(2,1)S(1)} %get-tuple-element.29.rest_0_), channel_id=1, source_target_pairs={{0,8},{1,9},{2,10},{3,11},{4,12},{5,13},{6,14},{7,15},{8,0},{9,1},... | collective-permute-start | bytes 393224 | tf_op jit(solution)/shard_map/ppermute | solution.py:206
  10.5 1.1 %copy-done = bf16[12,192,128]{2,1,0:T(8,128)(2,1)S(1)} copy-done((bf16[12,192,128]{2,1,0:T(8,128)(2,1)S(1)}, bf16[12,192,128]{2,1,0:T(8,128)(2,1)}, u32[]{:S(2)}) %copy-start) | copy-done | bytes 589848
  11.5 1.2 %tiles.1 = (bf16[144,128]{1,0:T(8,128)(2,1)S(1)}, bf16[144,128]{1,0:T(8,128)(2,1)S(1)}, bf16[144,128]{1,0:T(8,128)(2,1)S(1)}, bf16[144,128]{1,0:T(8,128)(2,1)S(1...) custom-call(s32[1]{0:T(128)} %bitcast.row_ref, ...), custom_call_target="tpu_custom_call" | custom-call | tf_op jit(solution)/shard_map/tiles/pallas_call | solution.py:236
  12.7 0.1 collective-permute-start.15
  12.8 1.6 %collective-permute-start.16 = (bf16[144,128]{1,0:T(8,128)(2,1)S(1)}, bf16[144,128]{1,0:T(8,128)(2,1)S(1)}, u32[]{:S(2)}, u32[]{:S(2)}) collective-permute-start(bf16[144,128]{1,0:T(8,128)(2,1)S(1)} %get-tuple-element.34), channel_id=1, source_target_pairs={{0,2},{1,3},{2,0},{3,1},{4,6},{5,7},{6,4},{7,5},{8,10},{9,11},{10,... | collective-permute-start | bytes 110600 | tf_op jit(solution)/shard_map/ppermute | solution.py:206
  14.4 0.3 collective-permute-start.17
  14.7 1.6 %collective-permute-start.18 = (bf16[144,128]{1,0:T(8,128)(2,1)S(1)}, bf16[144,128]{1,0:T(8,128)(2,1)S(1)}, u32[]{:S(2)}, u32[]{:S(2)}) collective-permute-start(bf16[144,128]{1,0:T(8,128)(2,1)S(1)} %get-tuple-element.36), channel_id=1, source_target_pairs={{0,4},{1,5},{2,6},{3,7},{4,0},{5,1},{6,2},{7,3},{8,12},{9,13},{10,... | collective-permute-start | bytes 110600 | tf_op jit(solution)/shard_map/ppermute | solution.py:206
  16.3 0.1 collective-permute-start.19
  16.4 0.5 collective-permute-done.16.rest_2_
  16.8 2.9 %collective-permute-start.20 = (bf16[144,128]{1,0:T(8,128)(2,1)S(1)}, bf16[144,128]{1,0:T(8,128)(2,1)S(1)}, u32[]{:S(2)}, u32[]{:S(2)}) collective-permute-start(bf16[144,128]{1,0:T(8,128)(2,1)S(1)} %get-tuple-element.38), channel_id=1, source_target_pairs={{0,6},{1,7},{2,4},{3,5},{4,2},{5,3},{6,0},{7,1},{8,14},{9,15},{10,... | collective-permute-start | bytes 110600 | tf_op jit(solution)/shard_map/ppermute | solution.py:206
  19.7 0.0 collective-permute-done.17.rest_3_
  19.7 0.0 collective-permute-start.21
  19.7 0.0 collective-permute-done.18.rest_4_
  19.7 1.0 collective-permute-start.3
  20.7 0.0 collective-permute-done.19.rest_5_
  20.7 1.5 %collective-permute-start.1 = (bf16[16,4096]{1,0:T(8,128)(2,1)S(1)}, bf16[16,4096]{1,0:T(8,128)(2,1)S(1)}, u32[]{:S(2)}, u32[]{:S(2)}) collective-permute-start(bf16[16,4096]{1,0:T(8,128)(2,1)S(1)} %get-tuple-element.29.rest_0_), channel_id=1, source_target_pairs={{0,2},{1,3},{2,0},{3,1},{4,6},{5,7},{6,4},{7,5},{8,10},{9,11},{10,... | collective-permute-start | bytes 393224 | tf_op jit(solution)/shard_map/ppermute | solution.py:206
  22.2 0.6 collective-permute-start
  22.8 0.5 collective-permute-start.11
  23.3 0.8 collective-permute-done.21.rest_7_
  24.1 0.3 collective-permute-start.22
  24.5 5.1 %collective-permute-done.22.rest_8_ = bf16[144,128]{1,0:T(8,128)(2,1)S(1)} collective-permute-done((bf16[144,128]{1,0:T(8,128)(2,1)S(1)}, bf16[144,128]{1,0:T(8,128)(2,1)S(1)}, u32[]{:S(2)}, u32[]{:S(2)}) %collective-permute-start.22) | collective-permute-done | bytes 36896 | tf_op jit(solution)/shard_map/ppermute | solution.py:206
  29.5 1.4 %collective-permute-start.23 = (bf16[144,128]{1,0:T(8,128)(2,1)S(1)}, bf16[144,128]{1,0:T(8,128)(2,1)S(1)}, u32[]{:S(2)}, u32[]{:S(2)}) collective-permute-start(bf16[144,128]{1,0:T(8,128)(2,1)S(1)} %get-tuple-element.41), channel_id=1, source_target_pairs={{0,9},{1,8},{2,11},{3,10},{4,13},{5,12},{6,15},{7,14},{8,1},{9,0},... | collective-permute-start | bytes 110600 | tf_op jit(solution)/shard_map/ppermute | solution.py:206
  30.9 3.5 %collective-permute-done.23.rest_9_ = bf16[144,128]{1,0:T(8,128)(2,1)S(1)} collective-permute-done((bf16[144,128]{1,0:T(8,128)(2,1)S(1)}, bf16[144,128]{1,0:T(8,128)(2,1)S(1)}, u32[]{:S(2)}, u32[]{:S(2)}) %collective-permute-start.23) | collective-permute-done | bytes 36896 | tf_op jit(solution)/shard_map/ppermute | solution.py:206
  34.4 2.7 %collective-permute-start.24 = (bf16[144,128]{1,0:T(8,128)(2,1)S(1)}, bf16[144,128]{1,0:T(8,128)(2,1)S(1)}, u32[]{:S(2)}, u32[]{:S(2)}) collective-permute-start(bf16[144,128]{1,0:T(8,128)(2,1)S(1)} %get-tuple-element.42), channel_id=1, source_target_pairs={{0,10},{1,11},{2,8},{3,9},{4,14},{5,15},{6,12},{7,13},{8,2},{9,3},... | collective-permute-start | bytes 110600 | tf_op jit(solution)/shard_map/ppermute | solution.py:206
  37.1 3.1 %collective-permute-done.24.rest_10_ = bf16[144,128]{1,0:T(8,128)(2,1)S(1)} collective-permute-done((bf16[144,128]{1,0:T(8,128)(2,1)S(1)}, bf16[144,128]{1,0:T(8,128)(2,1)S(1)}, u32[]{:S(2)}, u32[]{:S(2)}) %collective-permute-start.24) | collective-permute-done | bytes 36896 | tf_op jit(solution)/shard_map/ppermute | solution.py:206
  40.1 1.0 %collective-permute-start.9 = (bf16[16,4096]{1,0:T(8,128)(2,1)S(1)}, bf16[16,4096]{1,0:T(8,128)(2,1)S(1)}, u32[]{:S(2)}, u32[]{:S(2)}) collective-permute-start(bf16[16,4096]{1,0:T(8,128)(2,1)S(1)} %collective-permute-done.7.rest_8_), channel_id=1, source_target_pairs={{0,2},{1,3},{2,0},{3,1},{4,6},{5,7},{6,4},{7,5},{8,10},{9,11},{10,... | collective-permute-start | bytes 393224 | tf_op jit(solution)/shard_map/ppermute | solution.py:206
  41.2 1.0 collective-permute-start.5
  42.2 0.0 collective-permute-done.rest_1_
  42.2 0.5 collective-permute-start.4
  42.7 1.0 %collective-permute-start.13 = (bf16[16,4096]{1,0:T(8,128)(2,1)S(1)}, bf16[16,4096]{1,0:T(8,128)(2,1)S(1)}, u32[]{:S(2)}, u32[]{:S(2)}) collective-permute-start(bf16[16,4096]{1,0:T(8,128)(2,1)S(1)} %collective-permute-done.11.rest_12_), channel_id=1, source_target_pairs={{0,2},{1,3},{2,0},{3,1},{4,6},{5,7},{6,4},{7,5},{8,10},{9,11},{10,... | collective-permute-start | bytes 393224 | tf_op jit(solution)/shard_map/ppermute | solution.py:206
  43.7 2.8 %collective-permute-done.9.rest_10_ = bf16[16,4096]{1,0:T(8,128)(2,1)S(1)} collective-permute-done((bf16[16,4096]{1,0:T(8,128)(2,1)S(1)}, bf16[16,4096]{1,0:T(8,128)(2,1)S(1)}, u32[]{:S(2)}, u32[]{:S(2)}) %collective-permute-start.9) | collective-permute-done | bytes 131104 | tf_op jit(solution)/shard_map/ppermute | solution.py:206
  46.5 2.7 %collective-permute-done.5.rest_6_ = bf16[16,4096]{1,0:T(8,128)(2,1)S(1)} collective-permute-done((bf16[16,4096]{1,0:T(8,128)(2,1)S(1)}, bf16[16,4096]{1,0:T(8,128)(2,1)S(1)}, u32[]{:S(2)}, u32[]{:S(2)}) %collective-permute-start.5) | collective-permute-done | bytes 131104 | tf_op jit(solution)/shard_map/ppermute | solution.py:206
  49.2 0.0 collective-permute-start.12
  49.2 0.0 collective-permute-done.8.rest_9_
  49.2 0.5 collective-permute-start.10
  49.8 0.1 collective-permute-start.6
  49.8 0.8 collective-permute-done.13.rest_14_
  50.6 1.1 %copy.18.turned_ref = bf16[32,32,128]{2,1,0:T(8,128)(2,1)S(1)} copy(bf16[32,32,128]{2,0,1:T(8,128)(2,1)} %bitcast.16) | data formatting | bytes 524288 | tf_op jit(solution)/shard_map/transpose | solution.py:266
  51.7 0.8 copy.19.depth_col
  52.5 0.8 copy.20.chain_col
  53.3 0.0 copy-start.2
  53.3 0.9 copy-done.2
  54.3 10.4 %mix.1 = (bf16[2048,1536]{1,0:T(8,128)(2,1)}, bf16[2048,1536]{1,0:T(8,128)(2,1)}) custom-call(bf16[768,32]{1,0:T(8,128)(2,1)S(1)} %get-tuple-element.25.left_ref, bf16[768,32]{1,0:T(8,128)(2,1)S(1)} %get-tuple-element.26.right_ref, bf16[32,32,128]{2,1,0:T(8,128)(2,1)S(1)} %copy.18.turned_ref, bf16[32,32,128]{2,1,0:T(8,128)(2,1)S(1)} %bitcast.17), custom_call_target="tpu_custom_call" | custom-call | flops 402653184 | bytes 12582912 | tf_op jit(solution)/shard_map/mix/pallas_call | solution.py:253
  64.7 0.0 collective-permute-done.2.rest_3_
  64.7 2.3 %collective-permute-start.25 = (bf16[144,128]{1,0:T(8,128)(2,1)S(1)}, bf16[144,128]{1,0:T(8,128)(2,1)S(1)}, u32[]{:S(2)}, u32[]{:S(2)}) collective-permute-start(bf16[144,128]{1,0:T(8,128)(2,1)S(1)} %get-tuple-element.43), channel_id=1, source_target_pairs={{0,11},{1,10},{2,9},{3,8},{4,15},{5,14},{6,13},{7,12},{8,3},{9,2},... | collective-permute-start | bytes 110600 | tf_op jit(solution)/shard_map/ppermute | solution.py:206
  67.0 0.4 collective-permute-start.26
  67.4 2.7 %collective-permute-start.27 = (bf16[144,128]{1,0:T(8,128)(2,1)S(1)}, bf16[144,128]{1,0:T(8,128)(2,1)S(1)}, u32[]{:S(2)}, u32[]{:S(2)}) collective-permute-start(bf16[144,128]{1,0:T(8,128)(2,1)S(1)} %get-tuple-element.45), channel_id=1, source_target_pairs={{0,13},{1,12},{2,15},{3,14},{4,9},{5,8},{6,11},{7,10},{8,5},{9,4},... | collective-permute-start | bytes 110600 | tf_op jit(solution)/shard_map/ppermute | solution.py:206
  70.1 0.0 collective-permute-done.6.rest_7_
  70.1 0.5 collective-permute-start.28
  70.7 4.3 %collective-permute-start.29 = (bf16[144,128]{1,0:T(8,128)(2,1)S(1)}, bf16[144,128]{1,0:T(8,128)(2,1)S(1)}, u32[]{:S(2)}, u32[]{:S(2)}) collective-permute-start(bf16[144,128]{1,0:T(8,128)(2,1)S(1)} %get-tuple-element.47), channel_id=1, source_target_pairs={{0,15},{1,14},{2,13},{3,12},{4,11},{5,10},{6,9},{7,8},{8,7},{9,6},... | collective-permute-start | bytes 110600 | tf_op jit(solution)/shard_map/ppermute | solution.py:206
  75.0 1.1 %copy-done.1 = bf16[12,192,128]{2,1,0:T(8,128)(2,1)S(1)} copy-done((bf16[12,192,128]{2,1,0:T(8,128)(2,1)S(1)}, bf16[12,192,128]{2,1,0:T(8,128)(2,1)}, u32[]{:S(2)}) %copy-start.1) | copy-done | bytes 589848
  76.0 0.7 copy-done.7
  76.7 0.7 copy-done.10
  77.4 0.7 copy-done.11
  78.0 0.7 copy-done.12
  78.7 12.4 %pair.1 = (bf16[12,192,128]{2,1,0:T(8,128)(2,1)}, f32[12,192,128]{2,1,0:T(8,128)S(1)}) custom-call(s32[1]{0:T(128)} %bitcast.row_ref, s32[192]{0:T(256)S(1)} %copy-done.7, s32[192]{0:T(256)S(1)} %copy-done.10, s32[192,1]{1,0:T(8,128)S(1)} %copy.19.depth_col, s32[192,1]{1,0:T(8,128)S(1)} %copy.20.chain_col, f32[1,128]{1,0:T(1,128)S(1)} %bitcast.23, ...), custom_call_target="tpu_custom_call" | custom-call | flops 3221225472 | bytes 14942208 | tf_op jit(solution)/shard_map/pair/pallas_call | solution.py:270
  91.2 8.3 %gate.1 = bf16[12,192,256]{2,1,0:T(8,128)(2,1)} custom-call(s32[1]{0:T(128)} %bitcast.row_ref, f32[12,192,128]{2,1,0:T(8,128)S(1)} %get-tuple-element.31.col_ref, f32[1,128]{1,0:T(1,128)S(1)} %bitcast.27, f32[1,128]{1,0:T(1,128)S(1)} %bitcast.28, bf16[128,256]{1,0:T(8,128)(2,1)S(1)} %copy-done.4, bf16[128,256]{1,0:T(8,128)(2,1)S(1)} %copy-done.5, ...), custom_call_target="tpu_custom_call" | custom-call | flops 301989888 | bytes 2949120 | tf_op jit(solution)/shard_map/gate/pallas_call | solution.py:313
  (38 shorter events, 0.1 us)
Async XLA Ops:
  0.6 0.9 copy-start.3
  1.6 0.7 copy-start.6
  2.2 0.7 copy-start.8
  2.9 0.7 copy-start.9
  3.6 0.7 copy-start.13
  4.3 0.7 copy-start.14
  6.4 16.4 %collective-permute-start.7 = (bf16[16,4096]{1,0:T(8,128)(2,1)S(1)}, bf16[16,4096]{1,0:T(8,128)(2,1)S(1)}, u32[]{:S(2)}, u32[]{:S(2)}) collective-permute-start(bf16[16,4096]{1,0:T(8,128)(2,1)S(1)} %get-tuple-element.29.rest_0_), channel_id=1, source_target_pairs={{0,8},{1,9},{2,10},{3,11},{4,12},{5,13},{6,14},{7,15},{8,0},{9,1},... | collective-permute-start | bytes 393224 | tf_op jit(solution)/shard_map/ppermute | solution.py:206
  10.5 1.1 %copy-start = (bf16[12,192,128]{2,1,0:T(8,128)(2,1)S(1)}, bf16[12,192,128]{2,1,0:T(8,128)(2,1)}, u32[]{:S(2)}) copy-start(bf16[12,192,128]{2,1,0:T(8,128)(2,1)} %state_ref.3) | copy-start | bytes 1769476
  12.7 3.5 %collective-permute-start.15 = (bf16[144,128]{1,0:T(8,128)(2,1)S(1)}, bf16[144,128]{1,0:T(8,128)(2,1)S(1)}, u32[]{:S(2)}, u32[]{:S(2)}) collective-permute-start(bf16[144,128]{1,0:T(8,128)(2,1)S(1)} %get-tuple-element.33), channel_id=1, source_target_pairs={{0,1},{1,0},{2,3},{3,2},{4,5},{5,4},{6,7},{7,6},{8,9},{9,8},{10,11... | collective-permute-start | bytes 110600 | tf_op jit(solution)/shard_map/ppermute | solution.py:206
  12.8 4.0 %collective-permute-start.16 = (bf16[144,128]{1,0:T(8,128)(2,1)S(1)}, bf16[144,128]{1,0:T(8,128)(2,1)S(1)}, u32[]{:S(2)}, u32[]{:S(2)}) collective-permute-start(bf16[144,128]{1,0:T(8,128)(2,1)S(1)} %get-tuple-element.34), channel_id=1, source_target_pairs={{0,2},{1,3},{2,0},{3,1},{4,6},{5,7},{6,4},{7,5},{8,10},{9,11},{10,... | collective-permute-start | bytes 110600 | tf_op jit(solution)/shard_map/ppermute | solution.py:206
  14.4 5.3 %collective-permute-start.17 = (bf16[144,128]{1,0:T(8,128)(2,1)S(1)}, bf16[144,128]{1,0:T(8,128)(2,1)S(1)}, u32[]{:S(2)}, u32[]{:S(2)}) collective-permute-start(bf16[144,128]{1,0:T(8,128)(2,1)S(1)} %get-tuple-element.35), channel_id=1, source_target_pairs={{0,3},{1,2},{2,1},{3,0},{4,7},{5,6},{6,5},{7,4},{8,11},{9,10},{10,... | collective-permute-start | bytes 110600 | tf_op jit(solution)/shard_map/ppermute | solution.py:206
  14.7 5.0 %collective-permute-start.18 = (bf16[144,128]{1,0:T(8,128)(2,1)S(1)}, bf16[144,128]{1,0:T(8,128)(2,1)S(1)}, u32[]{:S(2)}, u32[]{:S(2)}) collective-permute-start(bf16[144,128]{1,0:T(8,128)(2,1)S(1)} %get-tuple-element.36), channel_id=1, source_target_pairs={{0,4},{1,5},{2,6},{3,7},{4,0},{5,1},{6,2},{7,3},{8,12},{9,13},{10,... | collective-permute-start | bytes 110600 | tf_op jit(solution)/shard_map/ppermute | solution.py:206
  16.3 4.4 %collective-permute-start.19 = (bf16[144,128]{1,0:T(8,128)(2,1)S(1)}, bf16[144,128]{1,0:T(8,128)(2,1)S(1)}, u32[]{:S(2)}, u32[]{:S(2)}) collective-permute-start(bf16[144,128]{1,0:T(8,128)(2,1)S(1)} %get-tuple-element.37), channel_id=1, source_target_pairs={{0,5},{1,4},{2,7},{3,6},{4,1},{5,0},{6,3},{7,2},{8,13},{9,12},{10,... | collective-permute-start | bytes 110600 | tf_op jit(solution)/shard_map/ppermute | solution.py:206
  16.8 5.3 %collective-permute-start.20 = (bf16[144,128]{1,0:T(8,128)(2,1)S(1)}, bf16[144,128]{1,0:T(8,128)(2,1)S(1)}, u32[]{:S(2)}, u32[]{:S(2)}) collective-permute-start(bf16[144,128]{1,0:T(8,128)(2,1)S(1)} %get-tuple-element.38), channel_id=1, source_target_pairs={{0,6},{1,7},{2,4},{3,5},{4,2},{5,3},{6,0},{7,1},{8,14},{9,15},{10,... | collective-permute-start | bytes 110600 | tf_op jit(solution)/shard_map/ppermute | solution.py:206
  19.7 4.4 %collective-permute-start.21 = (bf16[144,128]{1,0:T(8,128)(2,1)S(1)}, bf16[144,128]{1,0:T(8,128)(2,1)S(1)}, u32[]{:S(2)}, u32[]{:S(2)}) collective-permute-start(bf16[144,128]{1,0:T(8,128)(2,1)S(1)} %get-tuple-element.39), channel_id=1, source_target_pairs={{0,7},{1,6},{2,5},{3,4},{4,3},{5,2},{6,1},{7,0},{8,15},{9,14},{10,... | collective-permute-start | bytes 110600 | tf_op jit(solution)/shard_map/ppermute | solution.py:206
  19.7 21.5 %collective-permute-start.3 = (bf16[16,4096]{1,0:T(8,128)(2,1)S(1)}, bf16[16,4096]{1,0:T(8,128)(2,1)S(1)}, u32[]{:S(2)}, u32[]{:S(2)}) collective-permute-start(bf16[16,4096]{1,0:T(8,128)(2,1)S(1)} %get-tuple-element.29.rest_0_), channel_id=1, source_target_pairs={{0,4},{1,5},{2,6},{3,7},{4,0},{5,1},{6,2},{7,3},{8,12},{9,13},{10,... | collective-permute-start | bytes 393224 | tf_op jit(solution)/shard_map/ppermute | solution.py:206
  20.7 21.5 %collective-permute-start.1 = (bf16[16,4096]{1,0:T(8,128)(2,1)S(1)}, bf16[16,4096]{1,0:T(8,128)(2,1)S(1)}, u32[]{:S(2)}, u32[]{:S(2)}) collective-permute-start(bf16[16,4096]{1,0:T(8,128)(2,1)S(1)} %get-tuple-element.29.rest_0_), channel_id=1, source_target_pairs={{0,2},{1,3},{2,0},{3,1},{4,6},{5,7},{6,4},{7,5},{8,10},{9,11},{10,... | collective-permute-start | bytes 393224 | tf_op jit(solution)/shard_map/ppermute | solution.py:206
  22.2 20.0 %collective-permute-start = (bf16[16,4096]{1,0:T(8,128)(2,1)S(1)}, bf16[16,4096]{1,0:T(8,128)(2,1)S(1)}, u32[]{:S(2)}, u32[]{:S(2)}) collective-permute-start(bf16[16,4096]{1,0:T(8,128)(2,1)S(1)} %get-tuple-element.29.rest_0_), channel_id=1, source_target_pairs={{0,1},{1,0},{2,3},{3,2},{4,5},{5,4},{6,7},{7,6},{8,9},{9,8},{10,11... | collective-permute-start | bytes 393224 | tf_op jit(solution)/shard_map/ppermute | solution.py:206
  22.8 19.9 %collective-permute-start.11 = (bf16[16,4096]{1,0:T(8,128)(2,1)S(1)}, bf16[16,4096]{1,0:T(8,128)(2,1)S(1)}, u32[]{:S(2)}, u32[]{:S(2)}) collective-permute-start(bf16[16,4096]{1,0:T(8,128)(2,1)S(1)} %collective-permute-done.7.rest_8_), channel_id=1, source_target_pairs={{0,4},{1,5},{2,6},{3,7},{4,0},{5,1},{6,2},{7,3},{8,12},{9,13},{10,... | collective-permute-start | bytes 393224 | tf_op jit(solution)/shard_map/ppermute | solution.py:206
  24.1 5.4 %collective-permute-start.22 = (bf16[144,128]{1,0:T(8,128)(2,1)S(1)}, bf16[144,128]{1,0:T(8,128)(2,1)S(1)}, u32[]{:S(2)}, u32[]{:S(2)}) collective-permute-start(bf16[144,128]{1,0:T(8,128)(2,1)S(1)} %get-tuple-element.40), channel_id=1, source_target_pairs={{0,8},{1,9},{2,10},{3,11},{4,12},{5,13},{6,14},{7,15},{8,0},{9,1},... | collective-permute-start | bytes 110600 | tf_op jit(solution)/shard_map/ppermute | solution.py:206
  29.5 4.8 %collective-permute-start.23 = (bf16[144,128]{1,0:T(8,128)(2,1)S(1)}, bf16[144,128]{1,0:T(8,128)(2,1)S(1)}, u32[]{:S(2)}, u32[]{:S(2)}) collective-permute-start(bf16[144,128]{1,0:T(8,128)(2,1)S(1)} %get-tuple-element.41), channel_id=1, source_target_pairs={{0,9},{1,8},{2,11},{3,10},{4,13},{5,12},{6,15},{7,14},{8,1},{9,0},... | collective-permute-start | bytes 110600 | tf_op jit(solution)/shard_map/ppermute | solution.py:206
  34.4 5.8 %collective-permute-start.24 = (bf16[144,128]{1,0:T(8,128)(2,1)S(1)}, bf16[144,128]{1,0:T(8,128)(2,1)S(1)}, u32[]{:S(2)}, u32[]{:S(2)}) collective-permute-start(bf16[144,128]{1,0:T(8,128)(2,1)S(1)} %get-tuple-element.42), channel_id=1, source_target_pairs={{0,10},{1,11},{2,8},{3,9},{4,14},{5,15},{6,12},{7,13},{8,2},{9,3},... | collective-permute-start | bytes 110600 | tf_op jit(solution)/shard_map/ppermute | solution.py:206
  40.1 6.4 %collective-permute-start.9 = (bf16[16,4096]{1,0:T(8,128)(2,1)S(1)}, bf16[16,4096]{1,0:T(8,128)(2,1)S(1)}, u32[]{:S(2)}, u32[]{:S(2)}) collective-permute-start(bf16[16,4096]{1,0:T(8,128)(2,1)S(1)} %collective-permute-done.7.rest_8_), channel_id=1, source_target_pairs={{0,2},{1,3},{2,0},{3,1},{4,6},{5,7},{6,4},{7,5},{8,10},{9,11},{10,... | collective-permute-start | bytes 393224 | tf_op jit(solution)/shard_map/ppermute | solution.py:206
  41.2 8.0 %collective-permute-start.5 = (bf16[16,4096]{1,0:T(8,128)(2,1)S(1)}, bf16[16,4096]{1,0:T(8,128)(2,1)S(1)}, u32[]{:S(2)}, u32[]{:S(2)}) collective-permute-start(bf16[16,4096]{1,0:T(8,128)(2,1)S(1)} %collective-permute-done.3.rest_4_), channel_id=1, source_target_pairs={{0,2},{1,3},{2,0},{3,1},{4,6},{5,7},{6,4},{7,5},{8,10},{9,11},{10,... | collective-permute-start | bytes 393224 | tf_op jit(solution)/shard_map/ppermute | solution.py:206
  42.2 7.1 %collective-permute-start.8 = (bf16[16,4096]{1,0:T(8,128)(2,1)S(1)}, bf16[16,4096]{1,0:T(8,128)(2,1)S(1)}, u32[]{:S(2)}, u32[]{:S(2)}) collective-permute-start(bf16[16,4096]{1,0:T(8,128)(2,1)S(1)} %collective-permute-done.7.rest_8_), channel_id=1, source_target_pairs={{0,1},{1,0},{2,3},{3,2},{4,5},{5,4},{6,7},{7,6},{8,9},{9,8},{10,11... | collective-permute-start | bytes 393224 | tf_op jit(solution)/shard_map/ppermute | solution.py:206
  42.2 7.6 %collective-permute-start.4 = (bf16[16,4096]{1,0:T(8,128)(2,1)S(1)}, bf16[16,4096]{1,0:T(8,128)(2,1)S(1)}, u32[]{:S(2)}, u32[]{:S(2)}) collective-permute-start(bf16[16,4096]{1,0:T(8,128)(2,1)S(1)} %collective-permute-done.3.rest_4_), channel_id=1, source_target_pairs={{0,1},{1,0},{2,3},{3,2},{4,5},{5,4},{6,7},{7,6},{8,9},{9,8},{10,11... | collective-permute-start | bytes 393224 | tf_op jit(solution)/shard_map/ppermute | solution.py:206
  42.7 8.0 %collective-permute-start.13 = (bf16[16,4096]{1,0:T(8,128)(2,1)S(1)}, bf16[16,4096]{1,0:T(8,128)(2,1)S(1)}, u32[]{:S(2)}, u32[]{:S(2)}) collective-permute-start(bf16[16,4096]{1,0:T(8,128)(2,1)S(1)} %collective-permute-done.11.rest_12_), channel_id=1, source_target_pairs={{0,2},{1,3},{2,0},{3,1},{4,6},{5,7},{6,4},{7,5},{8,10},{9,11},{10,... | collective-permute-start | bytes 393224 | tf_op jit(solution)/shard_map/ppermute | solution.py:206
  46.5 18.2 %collective-permute-start.2 = (bf16[16,4096]{1,0:T(8,128)(2,1)S(1)}, bf16[16,4096]{1,0:T(8,128)(2,1)S(1)}, u32[]{:S(2)}, u32[]{:S(2)}) collective-permute-start(bf16[16,4096]{1,0:T(8,128)(2,1)S(1)} %collective-permute-done.1.rest_2_), channel_id=1, source_target_pairs={{0,1},{1,0},{2,3},{3,2},{4,5},{5,4},{6,7},{7,6},{8,9},{9,8},{10,11... | collective-permute-start | bytes 393224 | tf_op jit(solution)/shard_map/ppermute | solution.py:206
  49.2 17.7 %collective-permute-start.12 = (bf16[16,4096]{1,0:T(8,128)(2,1)S(1)}, bf16[16,4096]{1,0:T(8,128)(2,1)S(1)}, u32[]{:S(2)}, u32[]{:S(2)}) collective-permute-start(bf16[16,4096]{1,0:T(8,128)(2,1)S(1)} %collective-permute-done.11.rest_12_), channel_id=1, source_target_pairs={{0,1},{1,0},{2,3},{3,2},{4,5},{5,4},{6,7},{7,6},{8,9},{9,8},{10,11... | collective-permute-start | bytes 393224 | tf_op jit(solution)/shard_map/ppermute | solution.py:206
  49.2 18.1 %collective-permute-start.10 = (bf16[16,4096]{1,0:T(8,128)(2,1)S(1)}, bf16[16,4096]{1,0:T(8,128)(2,1)S(1)}, u32[]{:S(2)}, u32[]{:S(2)}) collective-permute-start(bf16[16,4096]{1,0:T(8,128)(2,1)S(1)} %collective-permute-done.9.rest_10_), channel_id=1, source_target_pairs={{0,1},{1,0},{2,3},{3,2},{4,5},{5,4},{6,7},{7,6},{8,9},{9,8},{10,11... | collective-permute-start | bytes 393224 | tf_op jit(solution)/shard_map/ppermute | solution.py:206
  49.8 20.4 %collective-permute-start.6 = (bf16[16,4096]{1,0:T(8,128)(2,1)S(1)}, bf16[16,4096]{1,0:T(8,128)(2,1)S(1)}, u32[]{:S(2)}, u32[]{:S(2)}) collective-permute-start(bf16[16,4096]{1,0:T(8,128)(2,1)S(1)} %collective-permute-done.5.rest_6_), channel_id=1, source_target_pairs={{0,1},{1,0},{2,3},{3,2},{4,5},{5,4},{6,7},{7,6},{8,9},{9,8},{10,11... | collective-permute-start | bytes 393224 | tf_op jit(solution)/shard_map/ppermute | solution.py:206
  50.6 20.0 %collective-permute-start.14 = (bf16[16,4096]{1,0:T(8,128)(2,1)S(1)}, bf16[16,4096]{1,0:T(8,128)(2,1)S(1)}, u32[]{:S(2)}, u32[]{:S(2)}) collective-permute-start(bf16[16,4096]{1,0:T(8,128)(2,1)S(1)} %collective-permute-done.13.rest_14_), channel_id=1, source_target_pairs={{0,1},{1,0},{2,3},{3,2},{4,5},{5,4},{6,7},{7,6},{8,9},{9,8},{10,11... | collective-permute-start | bytes 393224 | tf_op jit(solution)/shard_map/ppermute | solution.py:206
  53.3 1.0 copy-start.2
  64.7 26.5 %collective-permute-start.25 = (bf16[144,128]{1,0:T(8,128)(2,1)S(1)}, bf16[144,128]{1,0:T(8,128)(2,1)S(1)}, u32[]{:S(2)}, u32[]{:S(2)}) collective-permute-start(bf16[144,128]{1,0:T(8,128)(2,1)S(1)} %get-tuple-element.43), channel_id=1, source_target_pairs={{0,11},{1,10},{2,9},{3,8},{4,15},{5,14},{6,13},{7,12},{8,3},{9,2},... | collective-permute-start | bytes 110600 | tf_op jit(solution)/shard_map/ppermute | solution.py:206
  67.0 24.2 %collective-permute-start.26 = (bf16[144,128]{1,0:T(8,128)(2,1)S(1)}, bf16[144,128]{1,0:T(8,128)(2,1)S(1)}, u32[]{:S(2)}, u32[]{:S(2)}) collective-permute-start(bf16[144,128]{1,0:T(8,128)(2,1)S(1)} %get-tuple-element.44), channel_id=1, source_target_pairs={{0,12},{1,13},{2,14},{3,15},{4,8},{5,9},{6,10},{7,11},{8,4},{9,5},... | collective-permute-start | bytes 110600 | tf_op jit(solution)/shard_map/ppermute | solution.py:206
  67.4 23.8 %collective-permute-start.27 = (bf16[144,128]{1,0:T(8,128)(2,1)S(1)}, bf16[144,128]{1,0:T(8,128)(2,1)S(1)}, u32[]{:S(2)}, u32[]{:S(2)}) collective-permute-start(bf16[144,128]{1,0:T(8,128)(2,1)S(1)} %get-tuple-element.45), channel_id=1, source_target_pairs={{0,13},{1,12},{2,15},{3,14},{4,9},{5,8},{6,11},{7,10},{8,5},{9,4},... | collective-permute-start | bytes 110600 | tf_op jit(solution)/shard_map/ppermute | solution.py:206
  70.1 21.1 %collective-permute-start.28 = (bf16[144,128]{1,0:T(8,128)(2,1)S(1)}, bf16[144,128]{1,0:T(8,128)(2,1)S(1)}, u32[]{:S(2)}, u32[]{:S(2)}) collective-permute-start(bf16[144,128]{1,0:T(8,128)(2,1)S(1)} %get-tuple-element.46), channel_id=1, source_target_pairs={{0,14},{1,15},{2,12},{3,13},{4,10},{5,11},{6,8},{7,9},{8,6},{9,7},... | collective-permute-start | bytes 110600 | tf_op jit(solution)/shard_map/ppermute | solution.py:206
  70.7 20.5 %collective-permute-start.29 = (bf16[144,128]{1,0:T(8,128)(2,1)S(1)}, bf16[144,128]{1,0:T(8,128)(2,1)S(1)}, u32[]{:S(2)}, u32[]{:S(2)}) collective-permute-start(bf16[144,128]{1,0:T(8,128)(2,1)S(1)} %get-tuple-element.47), channel_id=1, source_target_pairs={{0,15},{1,14},{2,13},{3,12},{4,11},{5,10},{6,9},{7,8},{8,7},{9,6},... | collective-permute-start | bytes 110600 | tf_op jit(solution)/shard_map/ppermute | solution.py:206
  75.0 1.1 %copy-start.1 = (bf16[12,192,128]{2,1,0:T(8,128)(2,1)S(1)}, bf16[12,192,128]{2,1,0:T(8,128)(2,1)}, u32[]{:S(2)}) copy-start(bf16[12,192,128]{2,1,0:T(8,128)(2,1)} %state_ref.3) | copy-start | bytes 1769476
  76.0 0.7 copy-start.7
  76.7 0.7 copy-start.10
  77.4 0.7 copy-start.11
  78.0 0.7 copy-start.12
  78.7 12.5 %copy-start.4 = (bf16[128,256]{1,0:T(8,128)(2,1)S(1)}, bf16[128,256]{1,0:T(8,128)(2,1)}, u32[]{:S(2)}) copy-start(bf16[128,256]{1,0:T(8,128)(2,1)} %proj_ref.1) | copy-start | bytes 196612
  78.7 12.5 %copy-start.5 = (bf16[128,256]{1,0:T(8,128)(2,1)S(1)}, bf16[128,256]{1,0:T(8,128)(2,1)}, u32[]{:S(2)}) copy-start(bf16[128,256]{1,0:T(8,128)(2,1)} %gate_ref.1) | copy-start | bytes 196612
  78.7 12.5 %copy-start.15 = (f32[128]{0:T(128)S(1)}, f32[128]{0:T(128)}, u32[]{:S(2)}) copy-start(f32[128]{0:T(128)} %param.26) | copy-start | bytes 1540
  78.7 12.5 %copy-start.16 = (f32[128]{0:T(128)S(1)}, f32[128]{0:T(128)}, u32[]{:S(2)}) copy-start(f32[128]{0:T(128)} %param.27) | copy-start | bytes 1540

commit v2 on v1

v2 whole, which is shorter than its diff:
```python
import functools

import jax
import jax.numpy as jnp
from jax import lax
from jax.experimental import pallas as pl
from jax.experimental.pallas import tpu as pltpu
from jax.sharding import PartitionSpec as P

F32 = jnp.float32
BF16 = jnp.bfloat16
NT = (((1,), (1,)), ((), ()))
VMEM = pltpu.VMEM
SMEM = pltpu.SMEM
LIMIT = 48 * 1024 * 1024


def whole(space):
    return pl.BlockSpec(memory_space=space)


def params(**kw):
    return pltpu.CompilerParams(vmem_limit_bytes=LIMIT, **kw)


def project_kernel(
    row_ref, depth_ref, hom_ref, scale_ref, shift_ref, src_ref, tgt_ref, left_ref, right_ref, packed_ref, tmp_ref
):
    tokens, seqs, feats = hom_ref.shape
    width = src_ref.shape[0]
    half = width // 2
    values = hom_ref[...].astype(F32).reshape(tokens * seqs, feats)
    centre = values - jnp.mean(values, axis=-1, keepdims=True)
    spread = jnp.mean(centre * centre, axis=-1, keepdims=True)
    normed = (centre * lax.rsqrt(spread + 1e-05) * scale_ref[...] + shift_ref[...]).astype(BF16)
    left = lax.dot_general(normed, src_ref[...], NT, preferred_element_type=F32)
    right = lax.dot_general(normed, tgt_ref[...], NT, preferred_element_type=F32)
    both = jnp.concatenate([src_ref[...], tgt_ref[...]], axis=0)
    first = row_ref[0] * tokens
    row_pos = lax.broadcasted_iota(jnp.int32, (seqs, width), 0)
    lane_pos = lax.broadcasted_iota(jnp.int32, (2 * width, seqs), 1)
    for n in range(tokens):
        depth = depth_ref[first + n]
        rows = slice(n * seqs, (n + 1) * seqs)
        left_ref[rows] = jnp.where(row_pos < depth, left[rows], 0.0).astype(BF16)
        right_ref[rows] = jnp.where(row_pos < depth, right[rows], 0.0).astype(BF16)
        turned = lax.dot_general(both, normed[rows], NT, preferred_element_type=F32)
        turned = jnp.where(lane_pos < depth, turned, 0.0)
        tmp_ref[0, n] = jnp.concatenate([turned[0:half], turned[half:width]], axis=1)
        tmp_ref[1, n] = jnp.concatenate(
            [turned[width : width + half], turned[width + half :]], axis=1
        )
    for q in range(half):
        packed_ref[:, q * 2 * seqs : (q + 1) * 2 * seqs] = jnp.concatenate(
            [tmp_ref[0, :, q, :], tmp_ref[1, :, q, :]], axis=0
        ).astype(BF16)


def tiles_kernel(state_ref, out_ref, wide_ref, msg_ref):
    count = out_ref.shape[0]
    tokens = state_ref.shape[0]
    wide_ref[...] = state_ref[...].astype(F32)
    for d in range(count):
        for i in range(tokens):
            msg_ref[d, i * tokens : (i + 1) * tokens] = wide_ref[i, d * tokens : (d + 1) * tokens, :]
        out_ref[d] = msg_ref[d].astype(BF16)


def mix_kernel(left_ref, right_ref, weight_ref, y_ref, z_ref, wide_ref):
    step = pl.program_id(0)
    factor = left_ref.shape[1]
    half = factor // 2
    seqs = y_ref.shape[0] * pl.num_programs(0) // factor
    width = weight_ref.shape[1]
    per = y_ref.shape[0] // (2 * seqs)
    tokens = left_ref.shape[0] // seqs
    wide_ref[...] = weight_ref[...].astype(F32)
    for p in range(per):
        q = step * per + p
        pairs = (
            [wide_ref[pl.ds(q + t * half, factor, stride=factor), :] for t in (0, 1)],
            [wide_ref[pl.ds(pl.multiple_of((q + t * half) * factor, factor), factor), :] for t in (0, 1)],
        )
        for lhs, pair, out_ref in ((left_ref, pairs[0], y_ref), (right_ref, pairs[1], z_ref)):
            rhs = jnp.concatenate(pair, axis=1).astype(BF16)
            mixed = jnp.dot(lhs[...], rhs, preferred_element_type=F32).astype(BF16)
            for n in range(tokens):
                rows = slice(n * seqs, (n + 1) * seqs)
                cols = slice(n * width, (n + 1) * width)
                low = 2 * p * seqs
                out_ref[low : low + seqs, cols] = mixed[rows, 0:width]
                out_ref[low + seqs : low + 2 * seqs, cols] = mixed[rows, width : 2 * width]


def pair_kernel(
    row_ref, depth_ref, chain_ref, depth_row, chain_row, match_ref, bias_ref, state_ref, lhs_left, lhs_right, y_ref, z_ref,
    next_ref, col_ref, inv_ref, chain_col,
):
    step = pl.program_id(0)
    block, total, width = state_ref.shape
    own_first = row_ref[0] * (block * pl.num_programs(0)) + step * block

    @pl.when(step == 0)
    def _():
        same = lax.broadcasted_iota(jnp.int32, (total, total), 0) == lax.broadcasted_iota(
            jnp.int32, (total, total), 1
        )
        ones = jnp.ones((total, width), BF16)

        def column(ref):
            spread = jnp.where(same, ref[...].astype(F32), 0.0).astype(BF16)
            return jnp.dot(spread, ones, preferred_element_type=F32)

        inv_ref[...] = 1.0 / jnp.maximum(column(depth_row), 1.0)
        chain_col[...] = column(chain_row)

    for lhs, w_ref, out_ref, is_row in (
        (lhs_right, y_ref, next_ref, True),
        (lhs_left, z_ref, col_ref, False),
    ):
        for t in range(block):
            if t % 2 == 0:
                prod = jnp.dot(
                    lhs[...], w_ref[:, t * width : (t + 2) * width], preferred_element_type=F32
                )
            own = own_first + t
            inv_own = 1.0 / jnp.maximum(jnp.full((1, width), depth_ref[own], jnp.int32).astype(F32), 1.0)
            label = jnp.full((1, width), chain_ref[own], jnp.int32).astype(F32)
            extra = jnp.where(chain_col[...] == label, match_ref[...], 0.0) + bias_ref[...]
            value = prod[:, t % 2 * width : (t % 2 + 1) * width] * jnp.maximum(inv_ref[...], inv_own) + extra
            if is_row:
                out_ref[t] = (state_ref[t].astype(F32) + value).astype(BF16)
            else:
                out_ref[t] = value


def gate_kernel(col_ref, gain_ref, shift_ref, proj_ref, gate_ref, tiles_ref, out_ref, wide_ref):
    step = pl.program_id(0)
    count, rows, width = tiles_ref.shape
    block, total = col_ref.shape[:2]
    tokens = total // count

    @pl.when(step == 0)
    def _():
        wide_ref[...] = tiles_ref[...].astype(F32).reshape(count * rows, width)

    ones = jnp.full((width, width), 1.0 / width, BF16)
    none = jnp.zeros((width, width), BF16)
    means = jnp.concatenate(
        [jnp.concatenate([ones, none], axis=1), jnp.concatenate([none, ones], axis=1)], axis=0
    )
    for t in range(0, block, 2):
        halves = []
        for u in (0, 1):
            state = wide_ref[pl.ds(step * block + t + u, total, stride=tokens), :]
            halves.append(state + col_ref[t + u])
        pair = jnp.concatenate(halves, axis=1).astype(BF16)
        centre = pair.astype(F32) - jnp.dot(pair, means, preferred_element_type=F32)
        square = (centre * centre).astype(BF16)
        spread = jnp.dot(square, means, preferred_element_type=F32)
        scaled = centre * lax.rsqrt(spread + 1e-05)
        for u in (0, 1):
            normed = scaled[:, u * width : (u + 1) * width] * gain_ref[...] + shift_ref[...]
            normed = normed.astype(BF16)
            projected = jnp.dot(normed, proj_ref[...], preferred_element_type=F32)
            gating = jnp.dot(normed, gate_ref[...], preferred_element_type=F32)
            out_ref[t + u] = (projected * (0.5 + 0.5 * jnp.tanh(0.5 * gating))).astype(BF16)


def fixed(*shape):
    return pl.BlockSpec(shape, lambda g: (0,) * len(shape))


def body(
    pairwise_state,
    homolog_embedding,
    alignment_depth,
    chain_labels,
    homolog_layer_scale,
    homolog_layer_shift,
    outer_source_matrix,
    outer_target_matrix,
    output_weight,
    output_bias,
    chain_match,
    pairwise_norm_gain,
    pairwise_norm_bias,
    input_projection_weight,
    input_gate_weight,
    *,
    count,
):
    tokens, total, width = pairwise_state.shape
    seqs, _, feats = homolog_embedding.shape
    factor = outer_source_matrix.shape[1]
    half = factor // 2
    inner = factor * seqs
    gated = input_projection_weight.shape[1]
    row = lax.axis_index("row").astype(jnp.int32).reshape(1)

    left, right, packed = pl.pallas_call(
        project_kernel,
        grid=(1,),
        out_shape=(
            jax.ShapeDtypeStruct((tokens * seqs, factor), BF16),
            jax.ShapeDtypeStruct((tokens * seqs, factor), BF16),
            jax.ShapeDtypeStruct((2 * tokens, inner), BF16),
        ),
        in_specs=[
            whole(SMEM),
            whole(SMEM),
            fixed(tokens, seqs, feats),
            fixed(1, feats),
            fixed(1, feats),
            fixed(factor, feats),
            fixed(factor, feats),
        ],
        out_specs=(fixed(tokens * seqs, factor), fixed(tokens * seqs, factor), fixed(2 * tokens, inner)),
        scratch_shapes=[VMEM((2, tokens, half, 2 * seqs), F32)],
        compiler_params=params(),
        name="project",
    )(
        row,
        alignment_depth,
        homolog_embedding.transpose(1, 0, 2),
        homolog_layer_scale.reshape(1, feats),
        homolog_layer_shift.reshape(1, feats),
        outer_source_matrix.T,
        outer_target_matrix.T,
    )
    gathered = lax.all_gather(packed, "row", axis=0, tiled=False)
    all_left = gathered[:, :tokens].reshape(total, inner)
    all_right = gathered[:, tokens:].reshape(total, inner)

    tiles = pl.pallas_call(
        tiles_kernel,
        grid=(1,),
        out_shape=jax.ShapeDtypeStruct((count, tokens * tokens, width), BF16),
        in_specs=[fixed(tokens, total, width)],
        out_specs=fixed(count, tokens * tokens, width),
        scratch_shapes=[
            VMEM((tokens, total, width), F32),
            VMEM((count, tokens * tokens, width), F32),
        ],
        compiler_params=params(),
        name="tiles",
    )(pairwise_state)
    tiles = lax.all_to_all(tiles, "row", split_axis=0, concat_axis=0, tiled=True)

    parts = 4
    y, z = pl.pallas_call(
        mix_kernel,
        grid=(parts,),
        out_shape=(jax.ShapeDtypeStruct((inner, tokens * width), BF16),) * 2,
        in_specs=[
            fixed(tokens * seqs, factor),
            fixed(tokens * seqs, factor),
            fixed(factor * factor, width),
        ],
        out_specs=(pl.BlockSpec((inner // parts, tokens * width), lambda q: (q, 0)),) * 2,
        scratch_shapes=[VMEM((factor * factor, width), F32)],
        compiler_params=params(),
        cost_estimate=pl.CostEstimate(
            flops=4 * tokens * seqs * factor * factor * width,
            bytes_accessed=4 * inner * tokens * width,
            transcendentals=0,
        ),
        name="mix",
    )(left, right, output_weight)

    block = 4
    pair_next, columns = pl.pallas_call(
        pair_kernel,
        grid=(tokens // block,),
        out_shape=(
            jax.ShapeDtypeStruct((tokens, total, width), BF16),
            jax.ShapeDtypeStruct((tokens, total, width), F32),
        ),
        in_specs=[whole(SMEM)] * 3
        + [
            fixed(1, total),
            fixed(1, total),
            fixed(1, width),
            fixed(1, width),
            pl.BlockSpec((block, total, width), lambda g: (g, 0, 0)),
            fixed(total, inner),
            fixed(total, inner),
            pl.BlockSpec((inner, block * width), lambda g: (0, g)),
            pl.BlockSpec((inner, block * width), lambda g: (0, g)),
        ],
        out_specs=(pl.BlockSpec((block, total, width), lambda g: (g, 0, 0)),) * 2,
        scratch_shapes=[VMEM((total, width), F32), VMEM((total, width), F32)],
        compiler_params=params(),
        cost_estimate=pl.CostEstimate(
            flops=4 * total * inner * tokens * width,
            bytes_accessed=4 * inner * tokens * width + 8 * tokens * total * width,
            transcendentals=0,
        ),
        name="pair",
    )(
        row,
        alignment_depth,
        chain_labels,
        alignment_depth.reshape(1, total),
        chain_labels.reshape(1, total),
        chain_match.reshape(1, width),
        output_bias.reshape(1, width),
        pairwise_state,
        all_left,
        all_right,
        y,
        z,
    )

    out = pl.pallas_call(
        gate_kernel,
        grid=(tokens // block,),
        out_shape=jax.ShapeDtypeStruct((tokens, total, gated), BF16),
        in_specs=[
            pl.BlockSpec((block, total, width), lambda j: (j, 0, 0)),
            fixed(1, width),
            fixed(1, width),
            fixed(width, gated),
            fixed(width, gated),
            fixed(count, tokens * tokens, width),
        ],
        out_specs=pl.BlockSpec((block, total, gated), lambda j: (j, 0, 0)),
        scratch_shapes=[VMEM((count * tokens * tokens, width), F32)],
        compiler_params=params(),
        cost_estimate=pl.CostEstimate(
            flops=4 * tokens * total * width * gated,
            bytes_accessed=tokens * total * (2 * gated + 6 * width),
            transcendentals=tokens * total * gated,
        ),
        name="gate",
    )(
        columns,
        pairwise_norm_gain.reshape(1, width),
        pairwise_norm_bias.reshape(1, width),
        input_projection_weight,
        input_gate_weight,
        tiles,
    )
    return pair_next, out.transpose(1, 0, 2)


def solution(mesh):
    return jax.shard_map(
        functools.partial(body, count=mesh.shape["row"]),
        mesh=mesh,
        in_specs=(
            P(("groups", "row"), None, None),
            P(None, ("groups", "row"), None),
            P("groups"),
            P("groups"),
        )
        + (P(),) * 11,
        out_specs=(P(("groups", "row"), None, None), P("groups", "row", None)),
        check_vma=False,
    )
```

time: 100 us -> 84.8 us (0.85)
  starting transfers between devices: 33 us -> 7.42 us
  between operations: 0.82 us -> 14.2 us
  Pallas kernels: 33.7 us -> 20.4 us
  waiting for transfers between devices: 19.3 us -> 30.1 us
    ppermute x30 -> x0, starting transfers between devices: 33 us -> none  [swap(): return lax.ppermute(array, 'row', [(r, r ^ bit) for r in range(count)])]
    all_gather x0 -> x1, waiting for transfers between devices: none -> 30.1 us  [body(): gathered = lax.all_gather(packed, 'row', axis=0, tiled=False)]
    ppermute x30 -> x0, waiting for transfers between devices: 19.3 us -> none  [swap(): return lax.ppermute(array, 'row', [(r, r ^ bit) for r in range(count)])]
    pallas_call x5, Pallas kernels: 33.7 us -> 20.4 us  [the longest x1 7.36 us: body(): pl.pallas_call(pair_kernel, grid=(tokens // block,), out_shape=(jax.Shape...]
    all_to_all x0 -> x1, starting transfers between devices: none -> 7.39 us  [body(): lax.all_to_all(tiles, 'row', split_axis=0, concat_axis=0, tiled=True)]
    slice x0 -> x1, local copies, waits for them, and re-layouts: none -> 2.97 us  [body(): all_right = gathered[:, tokens:].reshape(total, inner)]
    unnamed x34 -> x38, local copies, waits for them, and re-layouts: 10.1 us -> 7.69 us
    transpose x1 -> x0, local copies, waits for them, and re-layouts: 1.05 us -> none  [body(): weight.transpose(1, 0, 2)]
  transfers between devices with their start and end apart: 30 -> 2, of which waited for: 8 -> 1; matrix products, arithmetic and copies ran while one was open for 3% -> 5% of each run, Pallas kernels for 24% -> 18%
where the time goes in v2:
time: 84.8 us; the launch traced here: 84.3 us
  waiting for transfers between devices  30.1 us (35%)
  Pallas kernels  20.4 us (24%)
  between operations  14.2 us (17%)
  local copies, waits for them, and re-layouts  12.2 us (14%)
  starting transfers between devices  7.42 us (9%)
    all_gather x1, waiting for transfers between devices, body(): gathered = lax.all_gather(packed, 'row', axis=0, tiled=False)  30.1 us
    unnamed x38, local copies, waits for them, and re-layouts  7.69 us
    all_to_all x1, starting transfers between devices, body(): lax.all_to_all(tiles, 'row', split_axis=0, concat_axis=0, tiled=True)  7.39 us
    pallas_call x1, Pallas kernels, body(): pl.pallas_call(pair_kernel, grid=(tokens // block,), out_shape=(jax.Shape...  7.36 us
    pallas_call x1, Pallas kernels, body(): pl.pallas_call(mix_kernel, grid=(parts,), out_shape=(jax.ShapeDtypeStruct...  6.46 us
    pallas_call x1, Pallas kernels, body(): pl.pallas_call(gate_kernel, grid=(tokens // block,), out_shape=jax.ShapeD...  3.56 us
    slice x1, local copies, waits for them, and re-layouts, body(): all_right = gathered[:, tokens:].reshape(total, inner)  2.97 us
    pallas_call x1, Pallas kernels, body(): pl.pallas_call(project_kernel, grid=(1,), out_shape=(jax.ShapeDtypeStruct...  1.89 us
  transfers between devices with their start and end apart: 2, of which 1 were waited for; matrix products, arithmetic and copies ran while one was open for 5% of the time, Pallas kernels for 18%

profile of v2, /device:TPU:0, one launch (start us, length us, event | category | flops | bytes accessed | tf_op | source)
XLA Modules:
  0.0 84.3 jit_solution(9503975097469247837)
XLA Ops:
  7.2 0.0 all-gather.3.cloned.1.call-start
  7.2 0.0 copy-start.4
  7.2 0.9 %copy-done.4 = bf16[64,12,64]{2,0,1:T(8,128)(2,1)S(1)} copy-done((bf16[64,12,64]{2,0,1:T(8,128)(2,1)S(1)}, bf16[64,12,64]{2,0,1:T(8,128)(2,1)}, u32[]{:S(2)}) %copy-start.4) | copy-done | bytes 98328
  8.1 0.0 copy-start.7
  8.1 0.7 copy-done.7
  8.8 0.0 copy-start.9
  8.8 0.7 copy-done.9
  9.5 0.0 copy-start.10
  9.5 0.7 copy-done.10
  10.2 0.0 copy-start.14
  10.2 0.7 copy-done.14
  10.9 0.0 copy-start.15
  10.9 0.7 copy-done.15
  11.5 0.0 copy-start.18
  11.5 1.9 %project.1 = (bf16[768,32]{1,0:T(8,128)(2,1)S(1)}, bf16[768,32]{1,0:T(8,128)(2,1)S(1)}, bf16[24,2048]{1,0:T(8,128)(2,1)}) custom-call(s32[1]{0:T(128)} %bitcast.row_ref, s32[192]{0:T(256)S(1)} %copy-done.7, bf16[12,64,64]{2,1,0:T(8,128)(2,1)S(1)} %bitcast.14, f32[1,64]{1,0:T(1,128)S(1)} %bitcast.21, f32[1,64]{1,0:T(1,128)S(1)} %bitcast.22, ...), custom_call_target="tpu_custom_call" | custom-call | tf_op jit(solution)/shard_map/project/pallas_call | solution.py:201
  13.4 0.0 all-gather.3.cloned.1.call-update
  13.5 0.0 copy-start
  13.5 1.1 %copy-done = bf16[12,192,128]{2,1,0:T(8,128)(2,1)S(1)} copy-done((bf16[12,192,128]{2,1,0:T(8,128)(2,1)S(1)}, bf16[12,192,128]{2,1,0:T(8,128)(2,1)}, u32[]{:S(2)}) %copy-start) | copy-done | bytes 589848
  14.5 1.1 %tiles.1 = bf16[16,144,128]{2,1,0:T(8,128)(2,1)} custom-call(bf16[12,192,128]{2,1,0:T(8,128)(2,1)S(1)} %copy-done), custom_call_target="tpu_custom_call" | custom-call | tf_op jit(solution)/shard_map/tiles/pallas_call | solution.py:235
  15.6 7.4 %all-to-all-start = ((bf16[16,144,128]{2,1,0:T(8,128)(2,1)}), bf16[16,144,128]{2,1,0:T(8,128)(2,1)S(1)}, u32[]{:S(2)}, u32[]{:S(2)}) async-start(bf16[16,144,128]{2,1,0:T(8,128)(2,1)} %tiles.1), calls=%async_computation | async-start | bytes 1179648 | tf_op jit(solution)/shard_map/all_to_all | solution.py:248
  23.0 0.0 copy-done.18
  23.0 6.5 %mix.1 = (bf16[2048,1536]{1,0:T(8,128)(2,1)}, bf16[2048,1536]{1,0:T(8,128)(2,1)}) custom-call(bf16[768,32]{1,0:T(8,128)(2,1)S(1)} %get-tuple-element.10.left_ref, bf16[768,32]{1,0:T(8,128)(2,1)S(1)} %get-tuple-element.11.right_ref, bf16[1024,128]{1,0:T(8,128)(2,1)S(1)} %copy-done.18), custom_call_target="tpu_custom_call" | custom-call | flops 402653184 | bytes 12582912 | tf_op jit(solution)/shard_map/mix/pallas_call | solution.py:251
  29.5 30.1 %all-gather.3.cloned.1.call-done = bf16[384,2048]{1,0:T(8,128)(2,1)} async-done(((bf16[24,2048]{1,0:T(8,128)(2,1)}), bf16[384,2048]{1,0:T(8,128)(2,1)}) %all-gather.3.cloned.1.call-update) | async-done | bytes 1572880 | tf_op jit(solution)/shard_map/all_gather | solution.py:231
  59.5 3.0 %fusion = (bf16[16,12,2048]{2,1,0:T(8,128)(2,1)}, bf16[16,12,2048]{2,1,0:T(8,128)(2,1)S(1)}) fusion(bf16[16,24,2048]{2,1,0:T(8,128)(2,1)} %bitcast.25), kind=kLoop, calls=%fused_computation | loop fusion | bytes 3145728 | tf_op jit(solution)/shard_map/slice | solution.py:233
  62.5 0.0 copy-start.1
  62.5 0.0 copy-start.8
  62.5 0.0 copy-start.11
  62.5 0.0 copy-start.12
  62.5 0.0 copy-start.13
  62.5 0.2 reshape.44.lhs_left
  62.7 1.3 %reshape.45.lhs_right = bf16[192,2048]{1,0:T(8,128)(2,1)S(1)} reshape(bf16[16,12,2048]{2,1,0:T(8,128)(2,1)} %get-tuple-element.16) | data formatting | bytes 1572864 | tf_op jit(solution)/shard_map/reshape | solution.py:233
  64.1 0.0 copy-done.1
  64.1 0.0 copy-done.8
  64.1 0.0 copy-done.11
  64.1 0.0 copy-done.12
  64.1 0.0 copy-done.13
  64.1 0.0 copy-start.5
  64.1 0.0 copy-start.6
  64.1 0.0 copy-start.16
  64.2 0.0 copy-start.17
  64.2 7.4 %pair.1 = (bf16[12,192,128]{2,1,0:T(8,128)(2,1)}, f32[12,192,128]{2,1,0:T(8,128)S(1)}) custom-call(s32[1]{0:T(128)} %bitcast.row_ref, s32[192]{0:T(256)S(1)} %copy-done.8, s32[192]{0:T(256)S(1)} %copy-done.11, s32[1,192]{1,0:T(1,128)S(1)} %bitcast.15, s32[1,192]{1,0:T(1,128)S(1)} %bitcast.18, f32[1,128]{1,0:T(1,128)S(1)} %bitcast.19, f32[1,128]{1,0:T(1,128)S(1)} %bitcast.20, ...), custom_call_target="tpu_custom_call" | custom-call | flops 2415919104 | bytes 14942208 | tf_op jit(solution)/shard_map/pair/pallas_call | solution.py:272
  71.5 0.0 copy-start.2
  71.5 1.0 %copy-done.2 = f32[12,192,128]{2,1,0:T(8,128)} copy-done((f32[12,192,128]{2,1,0:T(8,128)}, f32[12,192,128]{2,1,0:T(8,128)S(1)}, u32[]{:S(2)}) %copy-start.2) | copy-done | bytes 1179672
  72.5 0.0 all-to-all-done.tiles_ref
  72.5 0.0 copy-done.5
  72.5 0.0 copy-done.6
  72.6 0.0 copy-done.16
  72.6 0.0 copy-done.17
  72.6 0.0 copy-start.3
  72.6 1.3 %copy-done.3 = f32[12,192,128]{2,1,0:T(8,128)S(1)} copy-done((f32[12,192,128]{2,1,0:T(8,128)S(1)}, f32[12,192,128]{2,1,0:T(8,128)}, u32[]{:S(2)}) %copy-start.3) | copy-done | bytes 1179672
  73.8 3.6 %gate.1 = bf16[12,192,256]{2,1,0:T(8,128)(2,1)} custom-call(f32[12,192,128]{2,1,0:T(8,128)S(1)} %copy-done.3, f32[1,128]{1,0:T(1,128)S(1)} %bitcast.23, f32[1,128]{1,0:T(1,128)S(1)} %bitcast.24, bf16[128,256]{1,0:T(8,128)(2,1)S(1)} %copy-done.5, bf16[128,256]{1,0:T(8,128)(2,1)S(1)} %copy-done.6, bf16[16,144,128]{2,1,0:T(8,128)(2,1)S(1)} %all-to-all-done.tiles_ref), custom_call_target="tpu_custom_call" | custom-call | flops 301989888 | bytes 2949120 | tf_op jit(solution)/shard_map/gate/pallas_call | solution.py:315
Async XLA Ops:
  7.2 52.4 %all-gather.3.cloned.1.call-start = ((), (), s32[]{:S(2)}) async-start(), calls=%async_computation.1 | async-start | bytes 1671168 | tf_op jit(solution)/shard_map/all_gather | solution.py:231
  7.2 0.9 %copy-start.4 = (bf16[64,12,64]{2,0,1:T(8,128)(2,1)S(1)}, bf16[64,12,64]{2,0,1:T(8,128)(2,1)}, u32[]{:S(2)}) copy-start(bf16[64,12,64]{2,0,1:T(8,128)(2,1)} %param.16) | copy-start | bytes 294916
  8.1 0.7 copy-start.7
  8.8 0.7 copy-start.9
  9.5 0.7 copy-start.10
  10.2 0.7 copy-start.14
  10.9 0.7 copy-start.15
  11.5 11.5 %copy-start.18 = (bf16[1024,128]{1,0:T(8,128)(2,1)S(1)}, bf16[1024,128]{1,0:T(8,128)(2,1)}, u32[]{:S(2)}) copy-start(bf16[1024,128]{1,0:T(8,128)(2,1)} %weight_ref.1) | copy-start | bytes 786436
  13.5 1.1 %copy-start = (bf16[12,192,128]{2,1,0:T(8,128)(2,1)S(1)}, bf16[12,192,128]{2,1,0:T(8,128)(2,1)}, u32[]{:S(2)}) copy-start(bf16[12,192,128]{2,1,0:T(8,128)(2,1)} %state_ref.3) | copy-start | bytes 1769476
  15.6 56.9 %all-to-all-start = ((bf16[16,144,128]{2,1,0:T(8,128)(2,1)}), bf16[16,144,128]{2,1,0:T(8,128)(2,1)S(1)}, u32[]{:S(2)}, u32[]{:S(2)}) async-start(bf16[16,144,128]{2,1,0:T(8,128)(2,1)} %tiles.1), calls=%async_computation | async-start | bytes 1179648 | tf_op jit(solution)/shard_map/all_to_all | solution.py:248
  62.5 1.6 %copy-start.1 = (bf16[12,192,128]{2,1,0:T(8,128)(2,1)S(1)}, bf16[12,192,128]{2,1,0:T(8,128)(2,1)}, u32[]{:S(2)}) copy-start(bf16[12,192,128]{2,1,0:T(8,128)(2,1)} %state_ref.3) | copy-start | bytes 1769476
  62.5 1.6 %copy-start.8 = (s32[192]{0:T(256)S(1)}, s32[192]{0:T(256)}, u32[]{:S(2)}) copy-start(s32[192]{0:T(256)} %depth_ref.3) | copy-start | bytes 2308
  62.5 1.6 %copy-start.11 = (s32[192]{0:T(256)S(1)}, s32[192]{0:T(256)}, u32[]{:S(2)}) copy-start(s32[192]{0:T(256)} %chain_ref.1) | copy-start | bytes 2308
  62.5 1.6 %copy-start.12 = (f32[128]{0:T(128)S(1)}, f32[128]{0:T(128)}, u32[]{:S(2)}) copy-start(f32[128]{0:T(128)} %param.25) | copy-start | bytes 1540
  62.5 1.6 %copy-start.13 = (f32[128]{0:T(128)S(1)}, f32[128]{0:T(128)}, u32[]{:S(2)}) copy-start(f32[128]{0:T(128)} %param.24) | copy-start | bytes 1540
  64.1 8.4 %copy-start.5 = (bf16[128,256]{1,0:T(8,128)(2,1)S(1)}, bf16[128,256]{1,0:T(8,128)(2,1)}, u32[]{:S(2)}) copy-start(bf16[128,256]{1,0:T(8,128)(2,1)} %proj_ref.1) | copy-start | bytes 196612
  64.1 8.4 %copy-start.6 = (bf16[128,256]{1,0:T(8,128)(2,1)S(1)}, bf16[128,256]{1,0:T(8,128)(2,1)}, u32[]{:S(2)}) copy-start(bf16[128,256]{1,0:T(8,128)(2,1)} %gate_ref.1) | copy-start | bytes 196612
  64.1 8.4 %copy-start.16 = (f32[128]{0:T(128)S(1)}, f32[128]{0:T(128)}, u32[]{:S(2)}) copy-start(f32[128]{0:T(128)} %param.26) | copy-start | bytes 1540
  64.2 8.4 %copy-start.17 = (f32[128]{0:T(128)S(1)}, f32[128]{0:T(128)}, u32[]{:S(2)}) copy-start(f32[128]{0:T(128)} %param.27) | copy-start | bytes 1540
  71.5 1.0 %copy-start.2 = (f32[12,192,128]{2,1,0:T(8,128)}, f32[12,192,128]{2,1,0:T(8,128)S(1)}, u32[]{:S(2)}) copy-start(f32[12,192,128]{2,1,0:T(8,128)S(1)} %get-tuple-element.15.col_ref) | copy-start | bytes 3538948
  72.6 1.3 %copy-start.3 = (f32[12,192,128]{2,1,0:T(8,128)S(1)}, f32[12,192,128]{2,1,0:T(8,128)}, u32[]{:S(2)}) copy-start(f32[12,192,128]{2,1,0:T(8,128)} %copy-done.2) | copy-start | bytes 3538948
Sparse Core Ops, SparseCore 0:
  13.6 45.9 all-gather.2

commit v3 on v2

v3 whole, which is shorter than its diff:
```python
import functools

import jax
import jax.numpy as jnp
from jax import lax
from jax.experimental import pallas as pl
from jax.experimental.pallas import tpu as pltpu
from jax.sharding import PartitionSpec as P

F32 = jnp.float32
BF16 = jnp.bfloat16
NT = (((1,), (1,)), ((), ()))
VMEM = pltpu.VMEM
SMEM = pltpu.SMEM
HBM = pltpu.HBM
LANES = 128


def whole(space):
    return pl.BlockSpec(memory_space=space)


def params(mib):
    return pltpu.CompilerParams(vmem_limit_bytes=mib * 1024 * 1024)


def fetch(sems, *pairs):
    copies = [pltpu.make_async_copy(a, b, sems.at[n]) for n, (a, b) in enumerate(pairs)]
    for copy in copies:
        copy.start()
    return copies


def finish(copies):
    for copy in copies:
        copy.wait()


def project_kernel(
    row_ref, depth_hbm, hom_hbm, scale_hbm, shift_hbm, src_hbm, tgt_hbm,
    left_ref, right_ref, item_ref,
    depth_ref, hom_ref, scale_ref, shift_ref, both_ref, sems,
):
    tokens, seqs, feats = hom_ref.shape
    width = src_hbm.shape[0]
    half = width // 2
    finish(
        fetch(
            sems,
            (hom_hbm, hom_ref),
            (depth_hbm, depth_ref),
            (scale_hbm, scale_ref),
            (shift_hbm, shift_ref),
            (src_hbm, both_ref.at[0:width]),
            (tgt_hbm, both_ref.at[width : 2 * width]),
        )
    )
    values = hom_ref[...].reshape(tokens * seqs, feats)
    ones = jnp.full((feats, feats), 1.0 / feats, BF16)
    centre = values.astype(F32) - jnp.dot(values, ones, preferred_element_type=F32)
    square = centre * centre
    high = square.astype(BF16)
    low = (square - high.astype(F32)).astype(BF16)
    spread = jnp.dot(high, ones, preferred_element_type=F32) + jnp.dot(
        low, ones, preferred_element_type=F32
    )
    normed = (centre * lax.rsqrt(spread + 1e-05) * scale_ref[...] + shift_ref[...]).astype(BF16)
    both = both_ref[...]
    turned = lax.dot_general(both, normed, NT, preferred_element_type=F32)
    plain = lax.dot_general(normed, both, NT, preferred_element_type=F32)
    first = row_ref[0] * tokens
    row_pos = lax.broadcasted_iota(jnp.int32, (seqs, width), 0)
    lane = lax.broadcasted_iota(jnp.int32, (half, 2 * seqs), 1)
    front = lane < seqs
    seq_pos = jnp.where(front, lane, lane - seqs)
    for n in range(tokens):
        depth = depth_ref[first + n]
        rows = slice(n * seqs, (n + 1) * seqs)
        left_ref[rows] = jnp.where(row_pos < depth, plain[rows, 0:width], 0.0).astype(BF16)
        right_ref[rows] = jnp.where(row_pos < depth, plain[rows, width : 2 * width], 0.0).astype(BF16)
        keep = seq_pos < depth
        for side in (0, 1):
            upper = turned[side * width : side * width + half, rows]
            lower = turned[side * width + half : (side + 1) * width, rows]
            item_ref[side, n] = jnp.where(keep, jnp.concatenate([upper, lower], axis=1), 0.0).astype(BF16)


def tiles_kernel(state_hbm, out_ref, state_ref, wide_ref, msg_ref, sems):
    count = out_ref.shape[0]
    tokens = state_ref.shape[0]
    finish(fetch(sems, (state_hbm, state_ref)))
    wide_ref[...] = state_ref[...].astype(F32)
    for d in range(count):
        for i in range(tokens):
            msg_ref[d, i * tokens : (i + 1) * tokens] = wide_ref[i, d * tokens : (d + 1) * tokens, :]
        out_ref[d] = msg_ref[d].astype(BF16)


def mix_kernel(left_ref, right_ref, weight_hbm, y_ref, z_ref, weight_ref, wide_ref, sems):
    factor = left_ref.shape[1]
    half = factor // 2
    seqs = y_ref.shape[1] // factor
    width = weight_ref.shape[1]
    tokens = left_ref.shape[0] // seqs
    finish(fetch(sems, (weight_hbm, weight_ref)))
    wide_ref[...] = weight_ref[...].astype(F32)

    def one(q, carry):
        pairs = (
            [wide_ref[pl.ds(q + t * half, factor, stride=factor), :] for t in (0, 1)],
            [wide_ref[pl.ds(pl.multiple_of((q + t * half) * factor, factor), factor), :] for t in (0, 1)],
        )
        for lhs, pair, out_ref in ((left_ref, pairs[0], y_ref), (right_ref, pairs[1], z_ref)):
            rhs = jnp.concatenate(pair, axis=1).astype(BF16)
            mixed = jnp.dot(lhs[...], rhs, preferred_element_type=F32).astype(BF16)
            for n in range(tokens):
                rows = slice(n * seqs, (n + 1) * seqs)
                cols = slice(n % 2 * width, (n % 2 + 1) * width)
                for t in (0, 1):
                    spot = pl.ds(pl.multiple_of((2 * q + t) * seqs, seqs), seqs)
                    out_ref[n // 2, spot, cols] = mixed[rows, t * width : (t + 1) * width]
        return carry

    lax.fori_loop(0, half, one, 0)


def pair_kernel(
    order, row_ref, depth_ref, chain_ref, depth_row, chain_row, match_ref, bias_ref, state_ref, y_ref, z_ref, *rest
):
    pieces, (next_ref, col_ref, wide_ref, lhs_ref, inv_ref, chain_col) = rest[:-6], rest[-6:]
    step = pl.program_id(0)
    block, total, width = state_ref.shape
    row = row_ref[0]
    own_first = row * (block * pl.num_programs(0)) + step * block
    _, _, tokens, groups, lanes = pieces[0].shape

    @pl.when(step == 0)
    def _():
        size = tokens * groups
        for side in (0, 1):
            for piece, ks in zip(pieces, order):
                for m, k in enumerate(ks):
                    spot = pl.ds(pl.multiple_of((row ^ k) * size, size), size)
                    wide_ref[spot, :] = piece[m, side].astype(F32).reshape(size, lanes)
            for q in range(groups):
                lhs_ref[side, :, q * lanes : (q + 1) * lanes] = wide_ref[
                    pl.ds(q, total, stride=groups), :
                ].astype(BF16)
        same = lax.broadcasted_iota(jnp.int32, (total, total), 0) == lax.broadcasted_iota(
            jnp.int32, (total, total), 1
        )
        ones = jnp.ones((total, width), BF16)

        def column(ref):
            spread = jnp.where(same, ref[...].astype(F32), 0.0).astype(BF16)
            return jnp.dot(spread, ones, preferred_element_type=F32)

        inv_ref[...] = 1.0 / jnp.maximum(column(depth_row), 1.0)
        chain_col[...] = column(chain_row)

    for side, w_ref, out_ref in ((1, y_ref, next_ref), (0, z_ref, col_ref)):
        prod = jnp.dot(lhs_ref[side], w_ref[step], preferred_element_type=F32)
        for t in range(block):
            own = own_first + t
            inv_own = 1.0 / jnp.maximum(jnp.full((1, width), depth_ref[own], jnp.int32).astype(F32), 1.0)
            label = jnp.full((1, width), chain_ref[own], jnp.int32).astype(F32)
            extra = jnp.where(chain_col[...] == label, match_ref[...], 0.0) + bias_ref[...]
            value = prod[:, t * width : (t + 1) * width] * jnp.maximum(inv_ref[...], inv_own) + extra
            if side:
                out_ref[t] = (state_ref[t].astype(F32) + value).astype(BF16)
            else:
                out_ref[t] = value


def gate_kernel(
    col_ref, gain_ref, shift_ref, proj_hbm, gate_hbm, tiles_ref, out_ref, proj_ref, gate_ref, wide_ref, sems
):
    step = pl.program_id(0)
    count, rows, width = tiles_ref.shape
    block, total = col_ref.shape[:2]
    tokens = total // count

    @pl.when(step == 0)
    def _():
        copies = fetch(sems, (proj_hbm, proj_ref), (gate_hbm, gate_ref))
        wide_ref[...] = tiles_ref[...].astype(F32).reshape(count * rows, width)
        finish(copies)

    ones = jnp.full((width, width), 1.0 / width, BF16)
    none = jnp.zeros((width, width), BF16)
    means = jnp.concatenate(
        [jnp.concatenate([ones, none], axis=1), jnp.concatenate([none, ones], axis=1)], axis=0
    )
    for t in range(0, block, 2):
        halves = []
        for u in (0, 1):
            state = wide_ref[pl.ds(step * block + t + u, total, stride=tokens), :]
            halves.append(state + col_ref[t + u])
        pair = jnp.concatenate(halves, axis=1).astype(BF16)
        centre = pair.astype(F32) - jnp.dot(pair, means, preferred_element_type=F32)
        square = (centre * centre).astype(BF16)
        spread = jnp.dot(square, means, preferred_element_type=F32)
        scaled = centre * lax.rsqrt(spread + 1e-05)
        for u in (0, 1):
            normed = scaled[:, u * width : (u + 1) * width] * gain_ref[...] + shift_ref[...]
            normed = normed.astype(BF16)
            projected = jnp.dot(normed, proj_ref[...], preferred_element_type=F32)
            gating = jnp.dot(normed, gate_ref[...], preferred_element_type=F32)
            out_ref[t + u] = (projected * (0.5 + 0.5 * jnp.tanh(0.5 * gating))).astype(BF16)


def fixed(*shape):
    return pl.BlockSpec(shape, lambda g: (0,) * len(shape))


def body(
    pairwise_state,
    homolog_embedding,
    alignment_depth,
    chain_labels,
    homolog_layer_scale,
    homolog_layer_shift,
    outer_source_matrix,
    outer_target_matrix,
    output_weight,
    output_bias,
    chain_match,
    pairwise_norm_gain,
    pairwise_norm_bias,
    input_projection_weight,
    input_gate_weight,
    *,
    count,
):
    tokens, total, width = pairwise_state.shape
    seqs, _, feats = homolog_embedding.shape
    factor = outer_source_matrix.shape[1]
    half = factor // 2
    inner = factor * seqs
    gated = input_projection_weight.shape[1]
    row = lax.axis_index("row").astype(jnp.int32).reshape(1)

    def swap(array, bit):
        return lax.ppermute(array, "row", [(r, r ^ bit) for r in range(count)])

    left, right, item = pl.pallas_call(
        project_kernel,
        out_shape=(
            jax.ShapeDtypeStruct((tokens * seqs, factor), BF16),
            jax.ShapeDtypeStruct((tokens * seqs, factor), BF16),
            jax.ShapeDtypeStruct((2, tokens, half, 2 * seqs), BF16),
        ),
        in_specs=[whole(SMEM)] + [whole(HBM)] * 6,
        out_specs=(whole(VMEM),) * 3,
        scratch_shapes=[
            SMEM((total,), jnp.int32),
            VMEM((tokens, seqs, feats), BF16),
            VMEM((1, feats), F32),
            VMEM((1, feats), F32),
            VMEM((2 * factor, feats), BF16),
            pltpu.SemaphoreType.DMA((6,)),
        ],
        name="project",
    )(
        row,
        alignment_depth,
        homolog_embedding.transpose(1, 0, 2),
        homolog_layer_scale.reshape(1, feats),
        homolog_layer_shift.reshape(1, feats),
        outer_source_matrix.T,
        outer_target_matrix.T,
    )
    held, order = item[None], [0]
    bit = count // 2
    while bit > 1:
        came = swap(held, bit)
        new = [k ^ bit for k in order]
        if bit > 2:
            held, order = jnp.concatenate([held, came], axis=0), order + new
        bit //= 2
    pieces = [held, came, swap(held, 1), swap(came, 1)]
    orders = [order, new, [k ^ 1 for k in order], [k ^ 1 for k in new]]

    tiles = pl.pallas_call(
        tiles_kernel,
        out_shape=jax.ShapeDtypeStruct((count, tokens * tokens, width), BF16),
        in_specs=[whole(HBM)],
        out_specs=whole(VMEM),
        scratch_shapes=[
            VMEM((tokens, total, width), BF16),
            VMEM((tokens, total, width), F32),
            VMEM((count, tokens * tokens, width), F32),
            pltpu.SemaphoreType.DMA((1,)),
        ],
        name="tiles",
    )(pairwise_state)
    tiles = lax.all_to_all(tiles, "row", split_axis=0, concat_axis=0, tiled=True)

    y, z = pl.pallas_call(
        mix_kernel,
        out_shape=(jax.ShapeDtypeStruct((tokens // 2, inner, 2 * width), BF16),) * 2,
        in_specs=[whole(VMEM), whole(VMEM), whole(HBM)],
        out_specs=(whole(VMEM),) * 2,
        scratch_shapes=[
            VMEM((factor * factor, width), BF16),
            VMEM((factor * factor, width), F32),
            pltpu.SemaphoreType.DMA((1,)),
        ],
        compiler_params=params(16),
        cost_estimate=pl.CostEstimate(
            flops=4 * tokens * seqs * factor * factor * width,
            bytes_accessed=4 * inner * tokens * width,
            transcendentals=0,
        ),
        name="mix",
    )(left, right, output_weight)

    block = 2
    pair_next, columns = pl.pallas_call(
        functools.partial(pair_kernel, orders),
        grid=(tokens // block,),
        out_shape=(
            jax.ShapeDtypeStruct((tokens, total, width), BF16),
            jax.ShapeDtypeStruct((tokens, total, width), F32),
        ),
        in_specs=[whole(SMEM)] * 3
        + [
            fixed(1, total),
            fixed(1, total),
            fixed(1, width),
            fixed(1, width),
            pl.BlockSpec((block, total, width), lambda g: (g, 0, 0)),
        ]
        + [whole(VMEM)] * 6,
        out_specs=(pl.BlockSpec((block, total, width), lambda g: (g, 0, 0)),) * 2,
        scratch_shapes=[
            VMEM((total * half, 2 * seqs), F32),
            VMEM((2, total, inner), BF16),
            VMEM((total, width), F32),
            VMEM((total, width), F32),
        ],
        compiler_params=params(40),
        cost_estimate=pl.CostEstimate(
            flops=4 * total * inner * tokens * width,
            bytes_accessed=4 * inner * tokens * width + 8 * tokens * total * width,
            transcendentals=0,
        ),
        name="pair",
    )(
        row,
        alignment_depth,
        chain_labels,
        alignment_depth.reshape(1, total),
        chain_labels.reshape(1, total),
        chain_match.reshape(1, width),
        output_bias.reshape(1, width),
        pairwise_state,
        y,
        z,
        *pieces,
    )

    block = 4
    out = pl.pallas_call(
        gate_kernel,
        grid=(tokens // block,),
        out_shape=jax.ShapeDtypeStruct((tokens, total, gated), BF16),
        in_specs=[
            pl.BlockSpec((block, total, width), lambda j: (j, 0, 0)),
            fixed(1, width),
            fixed(1, width),
            whole(HBM),
            whole(HBM),
            fixed(count, tokens * tokens, width),
        ],
        out_specs=pl.BlockSpec((block, total, gated), lambda j: (j, 0, 0)),
        scratch_shapes=[
            VMEM((width, gated), BF16),
            VMEM((width, gated), BF16),
            VMEM((count * tokens * tokens, width), F32),
            pltpu.SemaphoreType.DMA((2,)),
        ],
        cost_estimate=pl.CostEstimate(
            flops=4 * tokens * total * width * gated,
            bytes_accessed=tokens * total * (2 * gated + 6 * width),
            transcendentals=tokens * total * gated,
        ),
        name="gate",
    )(
        columns,
        pairwise_norm_gain.reshape(1, width),
        pairwise_norm_bias.reshape(1, width),
        input_projection_weight,
        input_gate_weight,
        tiles,
    )
    return pair_next, out.transpose(1, 0, 2)


def solution(mesh):
    return jax.shard_map(
        functools.partial(body, count=mesh.shape["row"]),
        mesh=mesh,
        in_specs=(
            P(("groups", "row"), None, None),
            P(None, ("groups", "row"), None),
            P("groups"),
            P("groups"),
        )
        + (P(),) * 11,
        out_specs=(P(("groups", "row"), None, None), P("groups", "row", None)),
        check_vma=False,
    )
```

time: 84.8 us -> 72.1 us (0.85)
  between operations: 14.2 us -> 0.71 us
  waiting for transfers between devices: 30.1 us -> 20.1 us
  starting transfers between devices: 7.42 us -> 12.6 us
  Pallas kernels: 20.4 us -> 25.1 us
  other arithmetic: 0 us -> 1.85 us
  local copies, waits for them, and re-layouts: 12.2 us -> 11.1 us
    all_gather x1 -> x0, waiting for transfers between devices: 30.1 us -> none  [body(): gathered = lax.all_gather(packed, 'row', axis=0, tiled=False)]
    ppermute x0 -> x5, waiting for transfers between devices: none -> 20.1 us  [swap(): return lax.ppermute(array, 'row', [(r, r ^ bit) for r in range(count)])]
    ppermute x0 -> x5, starting transfers between devices: none -> 6.98 us  [swap(): return lax.ppermute(array, 'row', [(r, r ^ bit) for r in range(count)])]
    unnamed x38 -> x22, local copies, waits for them, and re-layouts: 7.69 us -> 11.1 us
    slice x1 -> x0, local copies, waits for them, and re-layouts: 2.97 us -> none  [body(): all_right = gathered[:, tokens:].reshape(total, inner)]
    pallas_call x4, Pallas kernels: 16.8 us -> 19.2 us  [the longest x1 8.86 us: body(): pl.pallas_call(functools.partial(pair_kernel, orders), grid=(tokens // bl...]
    pallas_call x1, Pallas kernels: 3.56 us -> 5.84 us  [body(): pl.pallas_call(gate_kernel, grid=(tokens // block,), out_shape=jax.ShapeD...]
    concatenate x0 -> x2, other arithmetic: none -> 1.85 us  [body(): held, order = (jnp.concatenate([held, came], axis=0), order + new)]
  transfers between devices with their start and end apart: 2 -> 6, of which waited for: 1 -> 2; matrix products, arithmetic and copies ran while one was open for 5% -> 1% of each run, Pallas kernels for 18% -> 23%
where the time goes in v3:
time: 72.1 us; the launch traced here: 71.4 us
  Pallas kernels  25.1 us (35%)
  waiting for transfers between devices  20.1 us (28%)
  starting transfers between devices  12.6 us (17%)
  local copies, waits for them, and re-layouts  11.1 us (15%)
  other arithmetic  1.85 us (3%)
    ppermute x5, waiting for transfers between devices, swap(): return lax.ppermute(array, 'row', [(r, r ^ bit) for r in range(count)])  20.1 us
    unnamed x22, local copies, waits for them, and re-layouts  11.1 us
    pallas_call x1, Pallas kernels, body(): pl.pallas_call(functools.partial(pair_kernel, orders), grid=(tokens // bl...  8.86 us
    ppermute x5, starting transfers between devices, swap(): return lax.ppermute(array, 'row', [(r, r ^ bit) for r in range(count)])  6.98 us
    pallas_call x1, Pallas kernels, body(): pl.pallas_call(gate_kernel, grid=(tokens // block,), out_shape=jax.ShapeD...  5.84 us
    pallas_call x1, Pallas kernels, body(): pl.pallas_call(mix_kernel, out_shape=(jax.ShapeDtypeStruct((tokens // 2,...  5.75 us
    all_to_all x1, starting transfers between devices, body(): lax.all_to_all(tiles, 'row', split_axis=0, concat_axis=0, tiled=True)  5.62 us
    pallas_call x1, Pallas kernels, body(): pl.pallas_call(project_kernel, out_shape=(jax.ShapeDtypeStruct((tokens *...  2.5 us
  transfers between devices with their start and end apart: 6, of which 2 were waited for; matrix products, arithmetic and copies ran while one was open for 1% of the time, Pallas kernels for 23%

profile of v3, /device:TPU:0, one launch (start us, length us, event | category | flops | bytes accessed | tf_op | source)
XLA Modules:
  0.0 71.4 jit_solution(1745700511733938155)
XLA Ops:
  0.6 2.5 %project.1 = (bf16[768,32]{1,0:T(8,128)(2,1)}, bf16[768,32]{1,0:T(8,128)(2,1)}, bf16[2,12,16,128]{3,2,1,0:T(8,128)(2,1)}) custom-call(s32[1]{0:T(128)} %bitcast.row_ref, s32[192]{0:T(256)} %depth_ref.1, bf16[12,64,64]{2,1,0:T(8,128)(2,1)} %bitcast.22, f32[1,64]{1,0:T(1,128)} %bitcast.25, f32[1,64]{1,0:T(1,128)} %bitcast.26, bf16[32,64]{1,0:T(8,128)(2,1)} %bitcast.23, ...), custom_call_target="tpu_custom_call" | custom-call | tf_op jit(solution)/shard_map/project/pallas_call | solution.py:246
  3.1 4.1 %collective-permute-start = (bf16[1,2,12,16,128]{4,3,2,1,0:T(8,128)(2,1)}, bf16[1,2,12,16,128]{4,3,2,1,0:T(8,128)(2,1)S(1)}, u32[]{:S(2)}, u32[]{:S(2)}) collective-permute-start(bf16[1,2,12,16,128]{4,3,2,1,0:T(8,128)(2,1)} %bitcast.19), channel_id=1, source_target_pairs={{0,8},{1,9},{2,10},{3,11},{4,12},{5,13},{6,14},{7,15},{8,0},{9,1},... | collective-permute-start | bytes 294920 | tf_op jit(solution)/shard_map/ppermute | solution.py:244
  7.2 5.1 %collective-permute-done = bf16[1,2,12,16,128]{4,3,2,1,0:T(8,128)(2,1)S(1)} collective-permute-done((bf16[1,2,12,16,128]{4,3,2,1,0:T(8,128)(2,1)}, bf16[1,2,12,16,128]{4,3,2,1,0:T(8,128)(2,1)S(1)}, u32[]{:S(2)}, u32[]{:S(2)}) %collective-permute-start) | collective-permute-done | bytes 98336 | tf_op jit(solution)/shard_map/ppermute | solution.py:244
  12.3 0.9 %pad_maximum_fusion.1 = bf16[2,2,12,16,128]{4,3,2,1,0:T(8,128)(2,1)S(1)} fusion(bf16[1,2,12,16,128]{4,3,2,1,0:T(8,128)(2,1)S(1)} %collective-permute-done, bf16[1,2,12,16,128]{4,3,2,1,0:T(8,128)(2,1)} %bitcast.20), kind=kLoop, calls=%fused_computation.1 | loop fusion | flops 98304 | bytes 393216 | tf_op jit(solution)/shard_map/concatenate | solution.py:279
  13.3 0.9 %collective-permute-start.1 = (bf16[2,2,12,16,128]{4,3,2,1,0:T(8,128)(2,1)S(1)}, bf16[2,2,12,16,128]{4,3,2,1,0:T(8,128)(2,1)S(1)}, u32[]{:S(2)}, u32[]{:S(2)}) collective-permute-start(bf16[2,2,12,16,128]{4,3,2,1,0:T(8,128)(2,1)S(1)} %pad_maximum_fusion.1), channel_id=1, source_target_pairs={{0,4},{1,5},{2,6},{3,7},{4,0},{5,1},{6,2},{7,3},{8,12},{9,13},{10,... | collective-permute-start | bytes 589832 | tf_op jit(solution)/shard_map/ppermute | solution.py:244
  14.2 2.1 %tiles.1 = bf16[16,144,128]{2,1,0:T(8,128)(2,1)} custom-call(bf16[12,192,128]{2,1,0:T(8,128)(2,1)} %state_hbm.1), custom_call_target="tpu_custom_call" | custom-call | tf_op jit(solution)/shard_map/tiles/pallas_call | solution.py:284
  16.3 5.6 %all-to-all-start = ((bf16[16,144,128]{2,1,0:T(8,128)(2,1)}), bf16[16,144,128]{2,1,0:T(8,128)(2,1)S(1)}, u32[]{:S(2)}, u32[]{:S(2)}) async-start(bf16[16,144,128]{2,1,0:T(8,128)(2,1)} %tiles.1), calls=%async_computation | async-start | bytes 1179648 | tf_op jit(solution)/shard_map/all_to_all | solution.py:297
  21.9 0.0 collective-permute-done.1
  21.9 0.9 %pad_maximum_fusion.rest_0_ = bf16[4,2,12,16,128]{4,3,2,1,0:T(8,128)(2,1)S(1)} fusion(bf16[2,2,12,16,128]{4,3,2,1,0:T(8,128)(2,1)S(1)} %collective-permute-done.1, bf16[1,2,12,16,128]{4,3,2,1,0:T(8,128)(2,1)S(1)} %collective-permute-done, bf16[1,2,12,16,128]{4,3,2,1,0:T(8,128)(2,1)} %bitcast.21), kind=kLoop, calls=%fused_computation | loop fusion | flops 393216 | bytes 786432 | tf_op jit(solution)/shard_map/concatenate | solution.py:279
  22.9 2.0 %collective-permute-start.2 = (bf16[4,2,12,16,128]{4,3,2,1,0:T(8,128)(2,1)S(1)}, bf16[4,2,12,16,128]{4,3,2,1,0:T(8,128)(2,1)S(1)}, u32[]{:S(2)}, u32[]{:S(2)}) collective-permute-start(bf16[4,2,12,16,128]{4,3,2,1,0:T(8,128)(2,1)S(1)} %pad_maximum_fusion.rest_0_), channel_id=1, source_target_pairs={{0,2},{1,3},{2,0},{3,1},{4,6},{5,7},{6,4},{7,5},{8,10},{9,11},{10,... | collective-permute-start | bytes 1179656 | tf_op jit(solution)/shard_map/ppermute | solution.py:244
  24.9 0.0 collective-permute-start.3
  24.9 14.9 %collective-permute-done.2.rest_1_ = bf16[4,2,12,16,128]{4,3,2,1,0:T(8,128)(2,1)S(1)} collective-permute-done((bf16[4,2,12,16,128]{4,3,2,1,0:T(8,128)(2,1)S(1)}, bf16[4,2,12,16,128]{4,3,2,1,0:T(8,128)(2,1)S(1)}, u32[]{:S(2)}, u32[]{:S(2)}) %collective-permute-start.2) | collective-permute-done | bytes 393248 | tf_op jit(solution)/shard_map/ppermute | solution.py:244
  39.8 0.0 collective-permute-start.4
  39.8 0.0 copy-start.7
  39.8 0.9 %copy-done.7 = bf16[1024,128]{1,0:T(8,128)(2,1)S(1)} copy-done((bf16[1024,128]{1,0:T(8,128)(2,1)S(1)}, bf16[1024,128]{1,0:T(8,128)(2,1)}, u32[]{:S(2)}) %copy-start.7) | copy-done | bytes 262168
  40.8 0.0 copy-start.8
  40.8 0.9 %copy-done.8 = bf16[768,32]{1,0:T(8,128)(2,1)S(1)} copy-done((bf16[768,32]{1,0:T(8,128)(2,1)S(1)}, bf16[768,32]{1,0:T(8,128)(2,1)}, u32[]{:S(2)}) %copy-start.8) | copy-done | bytes 49176
  41.7 0.0 copy-start.9
  41.7 0.9 %copy-done.9 = bf16[768,32]{1,0:T(8,128)(2,1)S(1)} copy-done((bf16[768,32]{1,0:T(8,128)(2,1)S(1)}, bf16[768,32]{1,0:T(8,128)(2,1)}, u32[]{:S(2)}) %copy-start.9) | copy-done | bytes 49176
  42.6 5.7 %mix.1 = (bf16[6,2048,256]{2,1,0:T(8,128)(2,1)S(1)}, bf16[6,2048,256]{2,1,0:T(8,128)(2,1)S(1)}) custom-call(bf16[768,32]{1,0:T(8,128)(2,1)S(1)} %copy-done.8, bf16[768,32]{1,0:T(8,128)(2,1)S(1)} %copy-done.9, bf16[1024,128]{1,0:T(8,128)(2,1)S(1)} %copy-done.7), custom_call_target="tpu_custom_call" | custom-call | flops 402653184 | bytes 12582912 | tf_op jit(solution)/shard_map/mix/pallas_call | solution.py:299
  48.4 0.0 copy-start
  48.4 2.7 %copy-done = bf16[6,2048,256]{2,1,0:T(8,128)(2,1)} copy-done((bf16[6,2048,256]{2,1,0:T(8,128)(2,1)}, bf16[6,2048,256]{2,1,0:T(8,128)(2,1)S(1)}, u32[]{:S(2)}) %copy-start) | copy-done | bytes 6291480
  51.0 0.0 collective-permute-done.3.rest_2_
  51.0 0.0 collective-permute-done.4.rest_3_
  51.0 0.0 copy-start.1
  51.0 1.1 %copy-done.1 = bf16[12,192,128]{2,1,0:T(8,128)(2,1)S(1)} copy-done((bf16[12,192,128]{2,1,0:T(8,128)(2,1)S(1)}, bf16[12,192,128]{2,1,0:T(8,128)(2,1)}, u32[]{:S(2)}) %copy-start.1) | copy-done | bytes 589848
  52.1 0.0 copy-start.3
  52.1 0.7 copy-done.3
  52.8 0.0 copy-start.4
  52.8 0.7 copy-done.4
  53.5 0.0 copy-start.5
  53.5 0.7 copy-done.5
  54.1 0.0 copy-start.6
  54.1 0.7 copy-done.6
  54.8 8.9 %pair.1 = (bf16[12,192,128]{2,1,0:T(8,128)(2,1)}, f32[12,192,128]{2,1,0:T(8,128)S(1)}) custom-call(s32[1]{0:T(128)} %bitcast.row_ref, s32[192]{0:T(256)S(1)} %copy-done.3, s32[192]{0:T(256)S(1)} %copy-done.4, s32[1,192]{1,0:T(1,128)S(1)} %bitcast.14, s32[1,192]{1,0:T(1,128)S(1)} %bitcast.15, f32[1,128]{1,0:T(1,128)S(1)} %bitcast.16, f32[1,128]{1,0:T(1,128)S(1)} %bitcast.17, ...), custom_call_target="tpu_custom_call" | custom-call | flops 2415919104 | bytes 14942208 | tf_op jit(solution)/shard_map/pair/pallas_call | solution.py:319
  63.6 0.0 copy-start.2
  63.6 1.0 %copy-done.2 = f32[12,192,128]{2,1,0:T(8,128)} copy-done((f32[12,192,128]{2,1,0:T(8,128)}, f32[12,192,128]{2,1,0:T(8,128)S(1)}, u32[]{:S(2)}) %copy-start.2) | copy-done | bytes 1179672
  64.7 0.0 all-to-all-done.tiles_ref
  64.7 0.0 copy-start.10
  64.7 0.8 %copy-done.10 = bf16[16,144,128]{2,1,0:T(8,128)(2,1)} copy-done((bf16[16,144,128]{2,1,0:T(8,128)(2,1)}, bf16[16,144,128]{2,1,0:T(8,128)(2,1)S(1)}, u32[]{:S(2)}) %copy-start.10) | copy-done | bytes 589848
  65.5 5.8 %gate.1 = bf16[12,192,256]{2,1,0:T(8,128)(2,1)} custom-call(f32[12,192,128]{2,1,0:T(8,128)} %copy-done.2, f32[1,128]{1,0:T(1,128)} %bitcast.27, f32[1,128]{1,0:T(1,128)} %bitcast.28, bf16[128,256]{1,0:T(8,128)(2,1)} %proj_hbm.1, bf16[128,256]{1,0:T(8,128)(2,1)} %gate_hbm.1, bf16[16,144,128]{2,1,0:T(8,128)(2,1)} %copy-done.10), custom_call_target="tpu_custom_call" | custom-call | flops 301989888 | bytes 2949120 | tf_op jit(solution)/shard_map/gate/pallas_call | solution.py:364
Async XLA Ops:
  3.1 9.2 %collective-permute-start = (bf16[1,2,12,16,128]{4,3,2,1,0:T(8,128)(2,1)}, bf16[1,2,12,16,128]{4,3,2,1,0:T(8,128)(2,1)S(1)}, u32[]{:S(2)}, u32[]{:S(2)}) collective-permute-start(bf16[1,2,12,16,128]{4,3,2,1,0:T(8,128)(2,1)} %bitcast.19), channel_id=1, source_target_pairs={{0,8},{1,9},{2,10},{3,11},{4,12},{5,13},{6,14},{7,15},{8,0},{9,1},... | collective-permute-start | bytes 294920 | tf_op jit(solution)/shard_map/ppermute | solution.py:244
  13.3 8.7 %collective-permute-start.1 = (bf16[2,2,12,16,128]{4,3,2,1,0:T(8,128)(2,1)S(1)}, bf16[2,2,12,16,128]{4,3,2,1,0:T(8,128)(2,1)S(1)}, u32[]{:S(2)}, u32[]{:S(2)}) collective-permute-start(bf16[2,2,12,16,128]{4,3,2,1,0:T(8,128)(2,1)S(1)} %pad_maximum_fusion.1), channel_id=1, source_target_pairs={{0,4},{1,5},{2,6},{3,7},{4,0},{5,1},{6,2},{7,3},{8,12},{9,13},{10,... | collective-permute-start | bytes 589832 | tf_op jit(solution)/shard_map/ppermute | solution.py:244
  16.3 48.4 %all-to-all-start = ((bf16[16,144,128]{2,1,0:T(8,128)(2,1)}), bf16[16,144,128]{2,1,0:T(8,128)(2,1)S(1)}, u32[]{:S(2)}, u32[]{:S(2)}) async-start(bf16[16,144,128]{2,1,0:T(8,128)(2,1)} %tiles.1), calls=%async_computation | async-start | bytes 1179648 | tf_op jit(solution)/shard_map/all_to_all | solution.py:297
  22.9 16.9 %collective-permute-start.2 = (bf16[4,2,12,16,128]{4,3,2,1,0:T(8,128)(2,1)S(1)}, bf16[4,2,12,16,128]{4,3,2,1,0:T(8,128)(2,1)S(1)}, u32[]{:S(2)}, u32[]{:S(2)}) collective-permute-start(bf16[4,2,12,16,128]{4,3,2,1,0:T(8,128)(2,1)S(1)} %pad_maximum_fusion.rest_0_), channel_id=1, source_target_pairs={{0,2},{1,3},{2,0},{3,1},{4,6},{5,7},{6,4},{7,5},{8,10},{9,11},{10,... | collective-permute-start | bytes 1179656 | tf_op jit(solution)/shard_map/ppermute | solution.py:244
  24.9 26.2 %collective-permute-start.3 = (bf16[4,2,12,16,128]{4,3,2,1,0:T(8,128)(2,1)S(1)}, bf16[4,2,12,16,128]{4,3,2,1,0:T(8,128)(2,1)S(1)}, u32[]{:S(2)}, u32[]{:S(2)}) collective-permute-start(bf16[4,2,12,16,128]{4,3,2,1,0:T(8,128)(2,1)S(1)} %pad_maximum_fusion.rest_0_), channel_id=1, source_target_pairs={{0,1},{1,0},{2,3},{3,2},{4,5},{5,4},{6,7},{7,6},{8,9},{9,8},{10,11... | collective-permute-start | bytes 1179656 | tf_op jit(solution)/shard_map/ppermute | solution.py:244
  39.8 11.2 %collective-permute-start.4 = (bf16[4,2,12,16,128]{4,3,2,1,0:T(8,128)(2,1)S(1)}, bf16[4,2,12,16,128]{4,3,2,1,0:T(8,128)(2,1)S(1)}, u32[]{:S(2)}, u32[]{:S(2)}) collective-permute-start(bf16[4,2,12,16,128]{4,3,2,1,0:T(8,128)(2,1)S(1)} %collective-permute-done.2.rest_1_), channel_id=1, source_target_pairs={{0,1},{1,0},{2,3},{3,2},{4,5},{5,4},{6,7},{7,6},{8,9},{9,8},{10,11... | collective-permute-start | bytes 1179656 | tf_op jit(solution)/shard_map/ppermute | solution.py:244
  39.8 1.0 %copy-start.7 = (bf16[1024,128]{1,0:T(8,128)(2,1)S(1)}, bf16[1024,128]{1,0:T(8,128)(2,1)}, u32[]{:S(2)}) copy-start(bf16[1024,128]{1,0:T(8,128)(2,1)} %weight_hbm.1) | copy-start | bytes 786436
  40.8 0.9 %copy-start.8 = (bf16[768,32]{1,0:T(8,128)(2,1)S(1)}, bf16[768,32]{1,0:T(8,128)(2,1)}, u32[]{:S(2)}) copy-start(bf16[768,32]{1,0:T(8,128)(2,1)} %get-tuple-element.9.left_ref) | copy-start | bytes 147460
  41.7 0.9 %copy-start.9 = (bf16[768,32]{1,0:T(8,128)(2,1)S(1)}, bf16[768,32]{1,0:T(8,128)(2,1)}, u32[]{:S(2)}) copy-start(bf16[768,32]{1,0:T(8,128)(2,1)} %get-tuple-element.10.right_ref) | copy-start | bytes 147460
  48.4 2.7 %copy-start = (bf16[6,2048,256]{2,1,0:T(8,128)(2,1)}, bf16[6,2048,256]{2,1,0:T(8,128)(2,1)S(1)}, u32[]{:S(2)}) copy-start(bf16[6,2048,256]{2,1,0:T(8,128)(2,1)S(1)} %get-tuple-element.12.z_ref) | copy-start | bytes 18874372
  51.0 1.1 %copy-start.1 = (bf16[12,192,128]{2,1,0:T(8,128)(2,1)S(1)}, bf16[12,192,128]{2,1,0:T(8,128)(2,1)}, u32[]{:S(2)}) copy-start(bf16[12,192,128]{2,1,0:T(8,128)(2,1)} %state_hbm.1) | copy-start | bytes 1769476
  52.1 0.7 copy-start.3
  52.8 0.7 copy-start.4
  53.5 0.7 copy-start.5
  54.1 0.7 copy-start.6
  63.6 1.0 %copy-start.2 = (f32[12,192,128]{2,1,0:T(8,128)}, f32[12,192,128]{2,1,0:T(8,128)S(1)}, u32[]{:S(2)}) copy-start(f32[12,192,128]{2,1,0:T(8,128)S(1)} %get-tuple-element.15.col_ref) | copy-start | bytes 3538948
  64.7 0.8 %copy-start.10 = (bf16[16,144,128]{2,1,0:T(8,128)(2,1)}, bf16[16,144,128]{2,1,0:T(8,128)(2,1)S(1)}, u32[]{:S(2)}) copy-start(bf16[16,144,128]{2,1,0:T(8,128)(2,1)S(1)} %all-to-all-done.tiles_ref) | copy-start | bytes 1769476

commit v4 on v3

--- a/solution.py
+++ b/solution.py
@@ -36,25 +36,39 @@
         copy.wait()
 
 
-def project_kernel(
-    row_ref, depth_hbm, hom_hbm, scale_hbm, shift_hbm, src_hbm, tgt_hbm,
-    left_ref, right_ref, item_ref,
-    depth_ref, hom_ref, scale_ref, shift_ref, both_ref, sems,
+def prepare_kernel(
+    row_ref, depth_hbm, hom_hbm, scale_hbm, shift_hbm, src_hbm, tgt_hbm, state_hbm, depth_row_hbm, chain_hbm, chain_row_hbm,
+    match_hbm, bias_hbm, gain_hbm, move_hbm, proj_hbm, gate_hbm,
+    left_ref, right_ref, item_ref, tiles_ref, aux_ref, gates_ref,
+    depth_ref, hom_ref, scale_ref, shift_ref, both_ref, state_ref, depth_row_ref, chain_ref, chain_row_ref, vec_ref,
+    wide_ref, msg_ref, sems,
 ):
     tokens, seqs, feats = hom_ref.shape
+    count, _, pair_width = tiles_ref.shape
+    total = depth_ref.shape[0]
     width = src_hbm.shape[0]
     half = width // 2
-    finish(
-        fetch(
-            sems,
-            (hom_hbm, hom_ref),
-            (depth_hbm, depth_ref),
-            (scale_hbm, scale_ref),
-            (shift_hbm, shift_ref),
-            (src_hbm, both_ref.at[0:width]),
-            (tgt_hbm, both_ref.at[width : 2 * width]),
-        )
-    )
+    gated = proj_hbm.shape[1]
+    first_copies = fetch(
+        sems,
+        (hom_hbm, hom_ref),
+        (depth_hbm, depth_ref),
+        (scale_hbm, scale_ref),
+        (shift_hbm, shift_ref),
+        (src_hbm, both_ref.at[0:width]),
+        (tgt_hbm, both_ref.at[width : 2 * width]),
+        (state_hbm, state_ref),
+        (chain_hbm, chain_ref),
+        (depth_row_hbm, depth_row_ref),
+        (chain_row_hbm, chain_row_ref),
+        (match_hbm, vec_ref.at[0]),
+        (bias_hbm, vec_ref.at[1]),
+        (gain_hbm, vec_ref.at[2]),
+        (move_hbm, vec_ref.at[3]),
+        (proj_hbm, gates_ref.at[0]),
+        (gate_hbm, gates_ref.at[1]),
+    )
+    finish(first_copies[:6])
     values = hom_ref[...].reshape(tokens * seqs, feats)
     ones = jnp.full((feats, feats), 1.0 / feats, BF16)
     centre = values.astype(F32) - jnp.dot(values, ones, preferred_element_type=F32)
@@ -84,16 +98,31 @@
             lower = turned[side * width + half : (side + 1) * width, rows]
             item_ref[side, n] = jnp.where(keep, jnp.concatenate([upper, lower], axis=1), 0.0).astype(BF16)
 
-
-def tiles_kernel(state_hbm, out_ref, state_ref, wide_ref, msg_ref, sems):
-    count = out_ref.shape[0]
-    tokens = state_ref.shape[0]
-    finish(fetch(sems, (state_hbm, state_ref)))
+    finish(first_copies[6:])
     wide_ref[...] = state_ref[...].astype(F32)
     for d in range(count):
         for i in range(tokens):
             msg_ref[d, i * tokens : (i + 1) * tokens] = wide_ref[i, d * tokens : (d + 1) * tokens, :]
-        out_ref[d] = msg_ref[d].astype(BF16)
+        tiles_ref[d] = msg_ref[d].astype(BF16)
+
+    same = lax.broadcasted_iota(jnp.int32, (total, total), 0) == lax.broadcasted_iota(
+        jnp.int32, (total, total), 1
+    )
+    fill = jnp.ones((total, pair_width), BF16)
+
+    def column(ref):
+        diagonal = jnp.where(same, ref[...].astype(F32), 0.0).astype(BF16)
+        return jnp.dot(diagonal, fill, preferred_element_type=F32)
+
+    aux_ref[0:total] = 1.0 / jnp.maximum(column(depth_row_ref), 1.0)
+    aux_ref[total : 2 * total] = column(chain_row_ref)
+    for n in range(tokens):
+        own = jnp.full((1, pair_width), depth_ref[first + n], jnp.int32).astype(F32)
+        aux_ref[2 * total + n : 2 * total + n + 1] = 1.0 / jnp.maximum(own, 1.0)
+        label = jnp.full((1, pair_width), chain_ref[first + n], jnp.int32).astype(F32)
+        aux_ref[2 * total + 16 + n : 2 * total + 17 + n] = label
+    for n in range(4):
+        aux_ref[2 * total + 32 + n : 2 * total + 33 + n] = vec_ref[n]
 
 
 def mix_kernel(left_ref, right_ref, weight_hbm, y_ref, z_ref, weight_ref, wide_ref, sems):
@@ -124,14 +153,11 @@
     lax.fori_loop(0, half, one, 0)
 
 
-def pair_kernel(
-    order, row_ref, depth_ref, chain_ref, depth_row, chain_row, match_ref, bias_ref, state_ref, y_ref, z_ref, *rest
-):
-    pieces, (next_ref, col_ref, wide_ref, lhs_ref, inv_ref, chain_col) = rest[:-6], rest[-6:]
+def pair_kernel(order, row_ref, aux_ref, state_ref, y_ref, z_ref, *rest):
+    pieces, (next_ref, col_ref, wide_ref, lhs_ref) = rest[:-4], rest[-4:]
     step = pl.program_id(0)
     block, total, width = state_ref.shape
     row = row_ref[0]
-    own_first = row * (block * pl.num_programs(0)) + step * block
     _, _, tokens, groups, lanes = pieces[0].shape
 
     @pl.when(step == 0)
@@ -146,35 +172,25 @@
                 lhs_ref[side, :, q * lanes : (q + 1) * lanes] = wide_ref[
                     pl.ds(q, total, stride=groups), :
                 ].astype(BF16)
-        same = lax.broadcasted_iota(jnp.int32, (total, total), 0) == lax.broadcasted_iota(
-            jnp.int32, (total, total), 1
-        )
-        ones = jnp.ones((total, width), BF16)
-
-        def column(ref):
-            spread = jnp.where(same, ref[...].astype(F32), 0.0).astype(BF16)
-            return jnp.dot(spread, ones, preferred_element_type=F32)
-
-        inv_ref[...] = 1.0 / jnp.maximum(column(depth_row), 1.0)
-        chain_col[...] = column(chain_row)
-
+
+    base = 2 * total
+    match = aux_ref[base + 32 : base + 33]
+    bias = aux_ref[base + 33 : base + 34]
     for side, w_ref, out_ref in ((1, y_ref, next_ref), (0, z_ref, col_ref)):
         prod = jnp.dot(lhs_ref[side], w_ref[step], preferred_element_type=F32)
         for t in range(block):
-            own = own_first + t
-            inv_own = 1.0 / jnp.maximum(jnp.full((1, width), depth_ref[own], jnp.int32).astype(F32), 1.0)
-            label = jnp.full((1, width), chain_ref[own], jnp.int32).astype(F32)
-            extra = jnp.where(chain_col[...] == label, match_ref[...], 0.0) + bias_ref[...]
-            value = prod[:, t * width : (t + 1) * width] * jnp.maximum(inv_ref[...], inv_own) + extra
+            own = step * block + t
+            inv_own = aux_ref[pl.ds(base + own, 1)]
+            label = aux_ref[pl.ds(base + 16 + own, 1)]
+            extra = jnp.where(aux_ref[total:base] == label, match, 0.0) + bias
+            value = prod[:, t * width : (t + 1) * width] * jnp.maximum(aux_ref[0:total], inv_own) + extra
             if side:
                 out_ref[t] = (state_ref[t].astype(F32) + value).astype(BF16)
             else:
                 out_ref[t] = value
 
 
-def gate_kernel(
-    col_ref, gain_ref, shift_ref, proj_hbm, gate_hbm, tiles_ref, out_ref, proj_ref, gate_ref, wide_ref, sems
-):
+def gate_kernel(aux_ref, col_ref, gates_ref, tiles_ref, out_ref, wide_ref):
     step = pl.program_id(0)
     count, rows, width = tiles_ref.shape
     block, total = col_ref.shape[:2]
@@ -182,10 +198,10 @@
 
     @pl.when(step == 0)
     def _():
-        copies = fetch(sems, (proj_hbm, proj_ref), (gate_hbm, gate_ref))
         wide_ref[...] = tiles_ref[...].astype(F32).reshape(count * rows, width)
-        finish(copies)
-
+
+    gain = aux_ref[2 * total + 34 : 2 * total + 35]
+    shift = aux_ref[2 * total + 35 : 2 * total + 36]
     ones = jnp.full((width, width), 1.0 / width, BF16)
     none = jnp.zeros((width, width), BF16)
     means = jnp.concatenate(
@@ -202,10 +218,10 @@
         spread = jnp.dot(square, means, preferred_element_type=F32)
         scaled = centre * lax.rsqrt(spread + 1e-05)
         for u in (0, 1):
-            normed = scaled[:, u * width : (u + 1) * width] * gain_ref[...] + shift_ref[...]
+            normed = scaled[:, u * width : (u + 1) * width] * gain + shift
             normed = normed.astype(BF16)
-            projected = jnp.dot(normed, proj_ref[...], preferred_element_type=F32)
-            gating = jnp.dot(normed, gate_ref[...], preferred_element_type=F32)
+            projected = jnp.dot(normed, gates_ref[0], preferred_element_type=F32)
+            gating = jnp.dot(normed, gates_ref[1], preferred_element_type=F32)
             out_ref[t + u] = (projected * (0.5 + 0.5 * jnp.tanh(0.5 * gating))).astype(BF16)
 
 
@@ -243,24 +259,35 @@
     def swap(array, bit):
         return lax.ppermute(array, "row", [(r, r ^ bit) for r in range(count)])
 
-    left, right, item = pl.pallas_call(
-        project_kernel,
+    aux_rows = 2 * total + 40
+    left, right, item, tiles, aux, gates = pl.pallas_call(
+        prepare_kernel,
         out_shape=(
             jax.ShapeDtypeStruct((tokens * seqs, factor), BF16),
             jax.ShapeDtypeStruct((tokens * seqs, factor), BF16),
             jax.ShapeDtypeStruct((2, tokens, half, 2 * seqs), BF16),
+            jax.ShapeDtypeStruct((count, tokens * tokens, width), BF16),
+            jax.ShapeDtypeStruct((aux_rows, width), F32),
+            jax.ShapeDtypeStruct((2, width, gated), BF16),
         ),
-        in_specs=[whole(SMEM)] + [whole(HBM)] * 6,
-        out_specs=(whole(VMEM),) * 3,
+        in_specs=[whole(SMEM)] + [whole(HBM)] * 16,
+        out_specs=(whole(VMEM),) * 6,
         scratch_shapes=[
             SMEM((total,), jnp.int32),
             VMEM((tokens, seqs, feats), BF16),
             VMEM((1, feats), F32),
             VMEM((1, feats), F32),
             VMEM((2 * factor, feats), BF16),
-            pltpu.SemaphoreType.DMA((6,)),
+            VMEM((tokens, total, width), BF16),
+            VMEM((1, total), jnp.int32),
+            SMEM((total,), jnp.int32),
+            VMEM((1, total), jnp.int32),
+            VMEM((4, 1, width), F32),
+            VMEM((tokens, total, width), F32),
+            VMEM((count, tokens * tokens, width), F32),
+            pltpu.SemaphoreType.DMA((16,)),
         ],
-        name="project",
+        name="prepare",
     )(
         row,
         alignment_depth,
@@ -269,32 +296,17 @@
         homolog_layer_shift.reshape(1, feats),
         outer_source_matrix.T,
         outer_target_matrix.T,
-    )
-    held, order = item[None], [0]
-    bit = count // 2
-    while bit > 1:
-        came = swap(held, bit)
-        new = [k ^ bit for k in order]
-        if bit > 2:
-            held, order = jnp.concatenate([held, came], axis=0), order + new
-        bit //= 2
-    pieces = [held, came, swap(held, 1), swap(came, 1)]
-    orders = [order, new, [k ^ 1 for k in order], [k ^ 1 for k in new]]
-
-    tiles = pl.pallas_call(
-        tiles_kernel,
-        out_shape=jax.ShapeDtypeStruct((count, tokens * tokens, width), BF16),
-        in_specs=[whole(HBM)],
-        out_specs=whole(VMEM),
-        scratch_shapes=[
-            VMEM((tokens, total, width), BF16),
-            VMEM((tokens, total, width), F32),
-            VMEM((count, tokens * tokens, width), F32),
-            pltpu.SemaphoreType.DMA((1,)),
-        ],
-        name="tiles",
-    )(pairwise_state)
-    tiles = lax.all_to_all(tiles, "row", split_axis=0, concat_axis=0, tiled=True)
+        pairwise_state,
+        alignment_depth.reshape(1, total),
+        chain_labels,
+        chain_labels.reshape(1, total),
+        chain_match.reshape(1, width),
+        output_bias.reshape(1, width),
+        pairwise_norm_gain.reshape(1, width),
+        pairwise_norm_bias.reshape(1, width),
+        input_projection_weight,
+        input_gate_weight,
+    )
 
     y, z = pl.pallas_call(
         mix_kernel,
@@ -315,6 +327,21 @@
         name="mix",
     )(left, right, output_weight)
 
+    held, order = item[None], [0]
+    bit = count // 2
+    while bit > 1:
+        came = swap(held, bit)
+        new = [k ^ bit for k in order]
+        if bit == 4:
+            came, y, z = lax.optimization_barrier((came, y, z))
+        if bit > 2:
+            held, order = jnp.concatenate([held, came], axis=0), order + new
+        bit //= 2
+    pieces = [held, came, swap(held, 1), swap(came, 1)]
+    orders = [order, new, [k ^ 1 for k in order], [k ^ 1 for k in new]]
+
+    tiles = lax.all_to_all(tiles, "row", split_axis=0, concat_axis=0, tiled=True)
+
     block = 2
     pair_next, columns = pl.pallas_call(
         functools.partial(pair_kernel, orders),
@@ -323,42 +350,21 @@
             jax.ShapeDtypeStruct((tokens, total, width), BF16),
             jax.ShapeDtypeStruct((tokens, total, width), F32),
         ),
-        in_specs=[whole(SMEM)] * 3
-        + [
-            fixed(1, total),
-            fixed(1, total),
-            fixed(1, width),
-            fixed(1, width),
-            pl.BlockSpec((block, total, width), lambda g: (g, 0, 0)),
-        ]
+        in_specs=[whole(SMEM), whole(VMEM), pl.BlockSpec((block, total, width), lambda g: (g, 0, 0))]
         + [whole(VMEM)] * 6,
         out_specs=(pl.BlockSpec((block, total, width), lambda g: (g, 0, 0)),) * 2,
         scratch_shapes=[
             VMEM((total * half, 2 * seqs), F32),
             VMEM((2, total, inner), BF16),
-            VMEM((total, width), F32),
-            VMEM((total, width), F32),
         ],
-        compiler_params=params(40),
+        compiler_params=params(24),
         cost_estimate=pl.CostEstimate(
             flops=4 * total * inner * tokens * width,
             bytes_accessed=4 * inner * tokens * width + 8 * tokens * total * width,
             transcendentals=0,
         ),
         name="pair",
-    )(
-        row,
-        alignment_depth,
-        chain_labels,
-        alignment_depth.reshape(1, total),
-        chain_labels.reshape(1, total),
-        chain_match.reshape(1, width),
-        output_bias.reshape(1, width),
-        pairwise_state,
-        y,
-        z,
-        *pieces,
-    )
+    )(row, aux, pairwise_state, y, z, *pieces)
 
     block = 4
     out = pl.pallas_call(
@@ -366,34 +372,21 @@
         grid=(tokens // block,),
         out_shape=jax.ShapeDtypeStruct((tokens, total, gated), BF16),
         in_specs=[
+            whole(VMEM),
             pl.BlockSpec((block, total, width), lambda j: (j, 0, 0)),
-            fixed(1, width),
-            fixed(1, width),
-            whole(HBM),
-            whole(HBM),
-            fixed(count, tokens * tokens, width),
+            whole(VMEM),
+            whole(VMEM),
         ],
         out_specs=pl.BlockSpec((block, total, gated), lambda j: (j, 0, 0)),
-        scratch_shapes=[
-            VMEM((width, gated), BF16),
-            VMEM((width, gated), BF16),
-            VMEM((count * tokens * tokens, width), F32),
-            pltpu.SemaphoreType.DMA((2,)),
-        ],
+        scratch_shapes=[VMEM((count * tokens * tokens, width), F32)],
+        compiler_params=params(24),
         cost_estimate=pl.CostEstimate(
             flops=4 * tokens * total * width * gated,
             bytes_accessed=tokens * total * (2 * gated + 6 * width),
             transcendentals=tokens * total * gated,
         ),
         name="gate",
-    )(
-        columns,
-        pairwise_norm_gain.reshape(1, width),
-        pairwise_norm_bias.reshape(1, width),
-        input_projection_weight,
-        input_gate_weight,
-        tiles,
-    )
+    )(aux, columns, gates, tiles)
     return pair_next, out.transpose(1, 0, 2)
 
 

time: 72.1 us -> 56.7 us (0.79)
  Pallas kernels: 25.1 us -> 18.4 us
  local copies, waits for them, and re-layouts: 11.1 us -> 4.8 us
  waiting for transfers between devices: 20.1 us -> 17.9 us
    unnamed x22 -> x14, local copies, waits for them, and re-layouts: 11.1 us -> 4.8 us
    pallas_call x1, Pallas kernels: 8.86 us -> 5.78 us  [body(): pl.pallas_call(functools.partial(pair_kernel, orders), grid=(tokens // bl...]
    pallas_call x1, Pallas kernels: 5.84 us -> 3.61 us  [body(): pl.pallas_call(gate_kernel, grid=(tokens // block,), out_shape=jax.ShapeD...]
    ppermute x5, waiting for transfers between devices: 20.1 us -> 17.9 us  [swap(): return lax.ppermute(array, 'row', [(r, r ^ bit) for r in range(count)])]
    pallas_call x2 -> x1, Pallas kernels: 4.63 us -> 3.21 us  [body(): pl.pallas_call(prepare_kernel, out_shape=(jax.ShapeDtypeStruct((tokens *...]
  transfers between devices with their start and end apart: 6 -> 6, of which waited for: 2 -> 3; matrix products, arithmetic and copies ran while one was open for 1% -> 2% of each run, Pallas kernels for 23% -> 21%
where the time goes in v4:
time: 56.7 us; the launch traced here: 56.2 us
  Pallas kernels  18.4 us (32%)
  waiting for transfers between devices  17.9 us (32%)
  starting transfers between devices  12.6 us (22%)
  local copies, waits for them, and re-layouts  4.8 us (8%)
  other arithmetic  1.85 us (3%)
  between operations  0.7 us (1%)
    ppermute x5, waiting for transfers between devices, swap(): return lax.ppermute(array, 'row', [(r, r ^ bit) for r in range(count)])  17.9 us
    ppermute x5, starting transfers between devices, swap(): return lax.ppermute(array, 'row', [(r, r ^ bit) for r in range(count)])  6.97 us
    pallas_call x1, Pallas kernels, body(): pl.pallas_call(functools.partial(pair_kernel, orders), grid=(tokens // bl...  5.78 us
    pallas_call x1, Pallas kernels, body(): pl.pallas_call(mix_kernel, out_shape=(jax.ShapeDtypeStruct((tokens // 2,...  5.76 us
    all_to_all x1, starting transfers between devices, body(): lax.all_to_all(tiles, 'row', split_axis=0, concat_axis=0, tiled=True)  5.61 us
    unnamed x14, local copies, waits for them, and re-layouts  4.8 us
    pallas_call x1, Pallas kernels, body(): pl.pallas_call(gate_kernel, grid=(tokens // block,), out_shape=jax.ShapeD...  3.61 us
    pallas_call x1, Pallas kernels, body(): pl.pallas_call(prepare_kernel, out_shape=(jax.ShapeDtypeStruct((tokens *...  3.21 us
  transfers between devices with their start and end apart: 6, of which 3 were waited for; matrix products, arithmetic and copies ran while one was open for 2% of the time, Pallas kernels for 21%

profile of v4, /device:TPU:0, one launch (start us, length us, event | category | flops | bytes accessed | tf_op | source)
XLA Modules:
  0.0 56.2 jit_solution(6359660691350217702)
XLA Ops:
  0.6 3.2 %prepare.1 = (bf16[768,32]{1,0:T(8,128)(2,1)}, bf16[768,32]{1,0:T(8,128)(2,1)}, bf16[2,12,16,128]{3,2,1,0:T(8,128)(2,1)}, bf16[16,144,128]{2,1,0:T(8,128)(2,1)},...) custom-call(s32[1]{0:T(128)} %bitcast.row_ref, s32[192]{0:T(256)} %depth_hbm.1, bf16[12,64,64]{2,1,0:T(8,128)(2,1)} %bitcast.18, ...), custom_call_target="tpu_custom_call" | custom-call | tf_op jit(solution)/shard_map/prepare/pallas_call | solution.py:263
  3.9 4.1 %collective-permute-start = (bf16[1,2,12,16,128]{4,3,2,1,0:T(8,128)(2,1)}, bf16[1,2,12,16,128]{4,3,2,1,0:T(8,128)(2,1)S(1)}, u32[]{:S(2)}, u32[]{:S(2)}) collective-permute-start(bf16[1,2,12,16,128]{4,3,2,1,0:T(8,128)(2,1)} %bitcast.15), channel_id=1, source_target_pairs={{0,8},{1,9},{2,10},{3,11},{4,12},{5,13},{6,14},{7,15},{8,0},{9,1},... | collective-permute-start | bytes 294920 | tf_op jit(solution)/shard_map/ppermute | solution.py:260
  8.0 5.1 %collective-permute-done = bf16[1,2,12,16,128]{4,3,2,1,0:T(8,128)(2,1)S(1)} collective-permute-done((bf16[1,2,12,16,128]{4,3,2,1,0:T(8,128)(2,1)}, bf16[1,2,12,16,128]{4,3,2,1,0:T(8,128)(2,1)S(1)}, u32[]{:S(2)}, u32[]{:S(2)}) %collective-permute-start) | collective-permute-done | bytes 98336 | tf_op jit(solution)/shard_map/ppermute | solution.py:260
  13.1 0.9 %pad_maximum_fusion.1 = bf16[2,2,12,16,128]{4,3,2,1,0:T(8,128)(2,1)S(1)} fusion(bf16[1,2,12,16,128]{4,3,2,1,0:T(8,128)(2,1)S(1)} %collective-permute-done, bf16[1,2,12,16,128]{4,3,2,1,0:T(8,128)(2,1)} %bitcast.16), kind=kLoop, calls=%fused_computation.1 | loop fusion | flops 98304 | bytes 393216 | tf_op jit(solution)/shard_map/concatenate | solution.py:338
  14.0 0.9 %collective-permute-start.1 = (bf16[2,2,12,16,128]{4,3,2,1,0:T(8,128)(2,1)S(1)}, bf16[2,2,12,16,128]{4,3,2,1,0:T(8,128)(2,1)S(1)}, u32[]{:S(2)}, u32[]{:S(2)}) collective-permute-start(bf16[2,2,12,16,128]{4,3,2,1,0:T(8,128)(2,1)S(1)} %pad_maximum_fusion.1), channel_id=1, source_target_pairs={{0,4},{1,5},{2,6},{3,7},{4,0},{5,1},{6,2},{7,3},{8,12},{9,13},{10,... | collective-permute-start | bytes 589832 | tf_op jit(solution)/shard_map/ppermute | solution.py:260
  14.9 5.6 %all-to-all-start = ((bf16[16,144,128]{2,1,0:T(8,128)(2,1)}), bf16[16,144,128]{2,1,0:T(8,128)(2,1)S(1)}, u32[]{:S(2)}, u32[]{:S(2)}) async-start(bf16[16,144,128]{2,1,0:T(8,128)(2,1)} %get-tuple-element.27), calls=%async_computation | async-start | bytes 1179648 | tf_op jit(solution)/shard_map/all_to_all | solution.py:343
  20.5 0.0 copy-start.4
  20.5 0.9 %copy-done.4 = bf16[1024,128]{1,0:T(8,128)(2,1)S(1)} copy-done((bf16[1024,128]{1,0:T(8,128)(2,1)S(1)}, bf16[1024,128]{1,0:T(8,128)(2,1)}, u32[]{:S(2)}) %copy-start.4) | copy-done | bytes 262168
  21.5 0.0 copy-start.5
  21.5 0.9 %copy-done.5 = bf16[768,32]{1,0:T(8,128)(2,1)S(1)} copy-done((bf16[768,32]{1,0:T(8,128)(2,1)S(1)}, bf16[768,32]{1,0:T(8,128)(2,1)}, u32[]{:S(2)}) %copy-start.5) | copy-done | bytes 49176
  22.4 0.0 copy-start.6
  22.4 0.9 %copy-done.6 = bf16[768,32]{1,0:T(8,128)(2,1)S(1)} copy-done((bf16[768,32]{1,0:T(8,128)(2,1)S(1)}, bf16[768,32]{1,0:T(8,128)(2,1)}, u32[]{:S(2)}) %copy-start.6) | copy-done | bytes 49176
  23.3 5.8 %mix.1 = (bf16[6,2048,256]{2,1,0:T(8,128)(2,1)S(1)}, bf16[6,2048,256]{2,1,0:T(8,128)(2,1)S(1)}) custom-call(bf16[768,32]{1,0:T(8,128)(2,1)S(1)} %copy-done.5, bf16[768,32]{1,0:T(8,128)(2,1)S(1)} %copy-done.6, bf16[1024,128]{1,0:T(8,128)(2,1)S(1)} %copy-done.4), custom_call_target="tpu_custom_call" | custom-call | flops 402653184 | bytes 12582912 | tf_op jit(solution)/shard_map/mix/pallas_call | solution.py:311
  29.1 0.0 collective-permute-done.1
  29.1 0.9 %pad_maximum_fusion.rest_0_ = bf16[4,2,12,16,128]{4,3,2,1,0:T(8,128)(2,1)S(1)} fusion(bf16[2,2,12,16,128]{4,3,2,1,0:T(8,128)(2,1)S(1)} %collective-permute-done.1, bf16[1,2,12,16,128]{4,3,2,1,0:T(8,128)(2,1)S(1)} %collective-permute-done, bf16[1,2,12,16,128]{4,3,2,1,0:T(8,128)(2,1)} %bitcast.17), kind=kLoop, calls=%fused_computation | loop fusion | flops 393216 | bytes 786432 | tf_op jit(solution)/shard_map/concatenate | solution.py:338
  30.0 2.0 %collective-permute-start.2 = (bf16[4,2,12,16,128]{4,3,2,1,0:T(8,128)(2,1)S(1)}, bf16[4,2,12,16,128]{4,3,2,1,0:T(8,128)(2,1)S(1)}, u32[]{:S(2)}, u32[]{:S(2)}) collective-permute-start(bf16[4,2,12,16,128]{4,3,2,1,0:T(8,128)(2,1)S(1)} %pad_maximum_fusion.rest_0_), channel_id=1, source_target_pairs={{0,2},{1,3},{2,0},{3,1},{4,6},{5,7},{6,4},{7,5},{8,10},{9,11},{10,... | collective-permute-start | bytes 1179656 | tf_op jit(solution)/shard_map/ppermute | solution.py:260
  32.0 0.0 collective-permute-start.3
  32.0 11.1 %collective-permute-done.2.rest_1_ = bf16[4,2,12,16,128]{4,3,2,1,0:T(8,128)(2,1)S(1)} collective-permute-done((bf16[4,2,12,16,128]{4,3,2,1,0:T(8,128)(2,1)S(1)}, bf16[4,2,12,16,128]{4,3,2,1,0:T(8,128)(2,1)S(1)}, u32[]{:S(2)}, u32[]{:S(2)}) %collective-permute-start.2) | collective-permute-done | bytes 393248 | tf_op jit(solution)/shard_map/ppermute | solution.py:260
  43.1 0.0 collective-permute-start.4
  43.1 0.0 collective-permute-done.3.rest_2_
  43.1 1.7 %collective-permute-done.4.rest_3_ = bf16[4,2,12,16,128]{4,3,2,1,0:T(8,128)(2,1)S(1)} collective-permute-done((bf16[4,2,12,16,128]{4,3,2,1,0:T(8,128)(2,1)S(1)}, bf16[4,2,12,16,128]{4,3,2,1,0:T(8,128)(2,1)S(1)}, u32[]{:S(2)}, u32[]{:S(2)}) %collective-permute-start.4) | collective-permute-done | bytes 393248 | tf_op jit(solution)/shard_map/ppermute | solution.py:260
  44.8 0.0 copy-start
  44.8 1.1 %copy-done = bf16[12,192,128]{2,1,0:T(8,128)(2,1)S(1)} copy-done((bf16[12,192,128]{2,1,0:T(8,128)(2,1)S(1)}, bf16[12,192,128]{2,1,0:T(8,128)(2,1)}, u32[]{:S(2)}) %copy-start) | copy-done | bytes 589848
  45.9 0.0 copy-start.1
  45.9 0.9 %copy-done.1 = f32[424,128]{1,0:T(8,128)S(1)} copy-done((f32[424,128]{1,0:T(8,128)S(1)}, f32[424,128]{1,0:T(8,128)}, u32[]{:S(2)}) %copy-start.1) | copy-done | bytes 217112
  46.8 0.0 copy-start.2
  46.8 0.0 copy-start.3
  46.8 5.8 %pair.1 = (bf16[12,192,128]{2,1,0:T(8,128)(2,1)}, f32[12,192,128]{2,1,0:T(8,128)S(1)}) custom-call(s32[1]{0:T(128)} %bitcast.row_ref, f32[424,128]{1,0:T(8,128)S(1)} %copy-done.1, bf16[12,192,128]{2,1,0:T(8,128)(2,1)S(1)} %copy-done, bf16[6,2048,256]{2,1,0:T(8,128)(2,1)S(1)} %get-tuple-element.21.y_ref, bf16[6,2048,256]{2,1,0:T(8,128)(2,1)S(1)} %get-tuple-element.22.z_ref, ...), custom_call_target="tpu_custom_call" | custom-call | flops 2415919104 | bytes 14942208 | tf_op jit(solution)/shard_map/pair/pallas_call | solution.py:346
  52.6 0.0 all-to-all-done.tiles_ref
  52.6 0.0 copy-done.2
  52.6 0.0 copy-done.3
  52.6 3.6 %gate.1 = bf16[12,192,256]{2,1,0:T(8,128)(2,1)} custom-call(f32[424,128]{1,0:T(8,128)S(1)} %copy-done.2, f32[12,192,128]{2,1,0:T(8,128)S(1)} %get-tuple-element.25.col_ref, bf16[2,128,256]{2,1,0:T(8,128)(2,1)S(1)} %copy-done.3, bf16[16,144,128]{2,1,0:T(8,128)(2,1)S(1)} %all-to-all-done.tiles_ref), custom_call_target="tpu_custom_call" | custom-call | flops 301989888 | bytes 2949120 | tf_op jit(solution)/shard_map/gate/pallas_call | solution.py:370
Async XLA Ops:
  3.9 9.2 %collective-permute-start = (bf16[1,2,12,16,128]{4,3,2,1,0:T(8,128)(2,1)}, bf16[1,2,12,16,128]{4,3,2,1,0:T(8,128)(2,1)S(1)}, u32[]{:S(2)}, u32[]{:S(2)}) collective-permute-start(bf16[1,2,12,16,128]{4,3,2,1,0:T(8,128)(2,1)} %bitcast.15), channel_id=1, source_target_pairs={{0,8},{1,9},{2,10},{3,11},{4,12},{5,13},{6,14},{7,15},{8,0},{9,1},... | collective-permute-start | bytes 294920 | tf_op jit(solution)/shard_map/ppermute | solution.py:260
  14.0 15.1 %collective-permute-start.1 = (bf16[2,2,12,16,128]{4,3,2,1,0:T(8,128)(2,1)S(1)}, bf16[2,2,12,16,128]{4,3,2,1,0:T(8,128)(2,1)S(1)}, u32[]{:S(2)}, u32[]{:S(2)}) collective-permute-start(bf16[2,2,12,16,128]{4,3,2,1,0:T(8,128)(2,1)S(1)} %pad_maximum_fusion.1), channel_id=1, source_target_pairs={{0,4},{1,5},{2,6},{3,7},{4,0},{5,1},{6,2},{7,3},{8,12},{9,13},{10,... | collective-permute-start | bytes 589832 | tf_op jit(solution)/shard_map/ppermute | solution.py:260
  14.9 37.7 %all-to-all-start = ((bf16[16,144,128]{2,1,0:T(8,128)(2,1)}), bf16[16,144,128]{2,1,0:T(8,128)(2,1)S(1)}, u32[]{:S(2)}, u32[]{:S(2)}) async-start(bf16[16,144,128]{2,1,0:T(8,128)(2,1)} %get-tuple-element.27), calls=%async_computation | async-start | bytes 1179648 | tf_op jit(solution)/shard_map/all_to_all | solution.py:343
  20.5 1.0 %copy-start.4 = (bf16[1024,128]{1,0:T(8,128)(2,1)S(1)}, bf16[1024,128]{1,0:T(8,128)(2,1)}, u32[]{:S(2)}) copy-start(bf16[1024,128]{1,0:T(8,128)(2,1)} %weight_hbm.1) | copy-start | bytes 786436
  21.5 0.9 %copy-start.5 = (bf16[768,32]{1,0:T(8,128)(2,1)S(1)}, bf16[768,32]{1,0:T(8,128)(2,1)}, u32[]{:S(2)}) copy-start(bf16[768,32]{1,0:T(8,128)(2,1)} %get-tuple-element.17.left_ref) | copy-start | bytes 147460
  22.4 0.9 %copy-start.6 = (bf16[768,32]{1,0:T(8,128)(2,1)S(1)}, bf16[768,32]{1,0:T(8,128)(2,1)}, u32[]{:S(2)}) copy-start(bf16[768,32]{1,0:T(8,128)(2,1)} %get-tuple-element.18.right_ref) | copy-start | bytes 147460
  30.0 13.1 %collective-permute-start.2 = (bf16[4,2,12,16,128]{4,3,2,1,0:T(8,128)(2,1)S(1)}, bf16[4,2,12,16,128]{4,3,2,1,0:T(8,128)(2,1)S(1)}, u32[]{:S(2)}, u32[]{:S(2)}) collective-permute-start(bf16[4,2,12,16,128]{4,3,2,1,0:T(8,128)(2,1)S(1)} %pad_maximum_fusion.rest_0_), channel_id=1, source_target_pairs={{0,2},{1,3},{2,0},{3,1},{4,6},{5,7},{6,4},{7,5},{8,10},{9,11},{10,... | collective-permute-start | bytes 1179656 | tf_op jit(solution)/shard_map/ppermute | solution.py:260
  32.0 11.1 %collective-permute-start.3 = (bf16[4,2,12,16,128]{4,3,2,1,0:T(8,128)(2,1)S(1)}, bf16[4,2,12,16,128]{4,3,2,1,0:T(8,128)(2,1)S(1)}, u32[]{:S(2)}, u32[]{:S(2)}) collective-permute-start(bf16[4,2,12,16,128]{4,3,2,1,0:T(8,128)(2,1)S(1)} %pad_maximum_fusion.rest_0_), channel_id=1, source_target_pairs={{0,1},{1,0},{2,3},{3,2},{4,5},{5,4},{6,7},{7,6},{8,9},{9,8},{10,11... | collective-permute-start | bytes 1179656 | tf_op jit(solution)/shard_map/ppermute | solution.py:260
  43.1 1.7 %collective-permute-start.4 = (bf16[4,2,12,16,128]{4,3,2,1,0:T(8,128)(2,1)S(1)}, bf16[4,2,12,16,128]{4,3,2,1,0:T(8,128)(2,1)S(1)}, u32[]{:S(2)}, u32[]{:S(2)}) collective-permute-start(bf16[4,2,12,16,128]{4,3,2,1,0:T(8,128)(2,1)S(1)} %collective-permute-done.2.rest_1_), channel_id=1, source_target_pairs={{0,1},{1,0},{2,3},{3,2},{4,5},{5,4},{6,7},{7,6},{8,9},{9,8},{10,11... | collective-permute-start | bytes 1179656 | tf_op jit(solution)/shard_map/ppermute | solution.py:260
  44.8 1.1 %copy-start = (bf16[12,192,128]{2,1,0:T(8,128)(2,1)S(1)}, bf16[12,192,128]{2,1,0:T(8,128)(2,1)}, u32[]{:S(2)}) copy-start(bf16[12,192,128]{2,1,0:T(8,128)(2,1)} %state_ref.1) | copy-start | bytes 1769476
  45.9 0.9 %copy-start.1 = (f32[424,128]{1,0:T(8,128)S(1)}, f32[424,128]{1,0:T(8,128)}, u32[]{:S(2)}) copy-start(f32[424,128]{1,0:T(8,128)} %get-tuple-element.15.aux_ref) | copy-start | bytes 651268
  46.8 5.8 %copy-start.2 = (f32[424,128]{1,0:T(8,128)S(1)}, f32[424,128]{1,0:T(8,128)}, u32[]{:S(2)}) copy-start(f32[424,128]{1,0:T(8,128)} %get-tuple-element.15.aux_ref) | copy-start | bytes 651268
  46.8 5.8 %copy-start.3 = (bf16[2,128,256]{2,1,0:T(8,128)(2,1)S(1)}, bf16[2,128,256]{2,1,0:T(8,128)(2,1)}, u32[]{:S(2)}) copy-start(bf16[2,128,256]{2,1,0:T(8,128)(2,1)} %get-tuple-element.26.gates_ref) | copy-start | bytes 393220

commit v5 on v4

--- a/solution.py
+++ b/solution.py
@@ -39,7 +39,7 @@
 def prepare_kernel(
     row_ref, depth_hbm, hom_hbm, scale_hbm, shift_hbm, src_hbm, tgt_hbm, state_hbm, depth_row_hbm, chain_hbm, chain_row_hbm,
     match_hbm, bias_hbm, gain_hbm, move_hbm, proj_hbm, gate_hbm,
-    left_ref, right_ref, item_ref, tiles_ref, aux_ref, gates_ref,
+    left_ref, right_ref, item_left, item_right, tiles_ref, aux_ref, gates_ref,
     depth_ref, hom_ref, scale_ref, shift_ref, both_ref, state_ref, depth_row_ref, chain_ref, chain_row_ref, vec_ref,
     wide_ref, msg_ref, sems,
 ):
@@ -93,10 +93,10 @@
         left_ref[rows] = jnp.where(row_pos < depth, plain[rows, 0:width], 0.0).astype(BF16)
         right_ref[rows] = jnp.where(row_pos < depth, plain[rows, width : 2 * width], 0.0).astype(BF16)
         keep = seq_pos < depth
-        for side in (0, 1):
+        for side, item_ref in ((0, item_left), (1, item_right)):
             upper = turned[side * width : side * width + half, rows]
             lower = turned[side * width + half : (side + 1) * width, rows]
-            item_ref[side, n] = jnp.where(keep, jnp.concatenate([upper, lower], axis=1), 0.0).astype(BF16)
+            item_ref[0, n] = jnp.where(keep, jnp.concatenate([upper, lower], axis=1), 0.0).astype(BF16)
 
     finish(first_copies[6:])
     wide_ref[...] = state_ref[...].astype(F32)
@@ -125,53 +125,83 @@
         aux_ref[2 * total + 32 + n : 2 * total + 33 + n] = vec_ref[n]
 
 
-def mix_kernel(left_ref, right_ref, weight_hbm, y_ref, z_ref, weight_ref, wide_ref, sems):
-    factor = left_ref.shape[1]
+def mix_kernel(strided, lhs_ref, weight_ref, out_ref, wide_ref):
+    factor = lhs_ref.shape[1]
     half = factor // 2
-    seqs = y_ref.shape[1] // factor
+    seqs = out_ref.shape[1] // factor
     width = weight_ref.shape[1]
-    tokens = left_ref.shape[0] // seqs
-    finish(fetch(sems, (weight_hbm, weight_ref)))
+    tokens = lhs_ref.shape[0] // seqs
     wide_ref[...] = weight_ref[...].astype(F32)
 
     def one(q, carry):
-        pairs = (
-            [wide_ref[pl.ds(q + t * half, factor, stride=factor), :] for t in (0, 1)],
-            [wide_ref[pl.ds(pl.multiple_of((q + t * half) * factor, factor), factor), :] for t in (0, 1)],
-        )
-        for lhs, pair, out_ref in ((left_ref, pairs[0], y_ref), (right_ref, pairs[1], z_ref)):
-            rhs = jnp.concatenate(pair, axis=1).astype(BF16)
-            mixed = jnp.dot(lhs[...], rhs, preferred_element_type=F32).astype(BF16)
-            for n in range(tokens):
-                rows = slice(n * seqs, (n + 1) * seqs)
-                cols = slice(n % 2 * width, (n % 2 + 1) * width)
-                for t in (0, 1):
-                    spot = pl.ds(pl.multiple_of((2 * q + t) * seqs, seqs), seqs)
-                    out_ref[n // 2, spot, cols] = mixed[rows, t * width : (t + 1) * width]
+        if strided:
+            pair = [wide_ref[pl.ds(q + t * half, factor, stride=factor), :] for t in (0, 1)]
+        else:
+            pair = [
+                wide_ref[pl.ds(pl.multiple_of((q + t * half) * factor, factor), factor), :] for t in (0, 1)
+            ]
+        rhs = jnp.concatenate(pair, axis=1).astype(BF16)
+        mixed = jnp.dot(lhs_ref[...], rhs, preferred_element_type=F32).astype(BF16)
+        for n in range(tokens):
+            rows = slice(n * seqs, (n + 1) * seqs)
+            cols = slice(n % 2 * width, (n % 2 + 1) * width)
+            for t in (0, 1):
+                spot = pl.ds(pl.multiple_of((2 * q + t) * seqs, seqs), seqs)
+                out_ref[n // 2, spot, cols] = mixed[rows, t * width : (t + 1) * width]
         return carry
 
     lax.fori_loop(0, half, one, 0)
 
 
-def pair_kernel(order, row_ref, aux_ref, state_ref, y_ref, z_ref, *rest):
+def join_kernel(*refs):
+    per = (len(refs) - 2) // 2
+    for side in (0, 1):
+        spot = 0
+        for piece in refs[side * per : (side + 1) * per]:
+            refs[2 * per + side][spot : spot + piece.shape[0]] = piece[...]
+            spot += piece.shape[0]
+
+
+def spread_items(row, wide_ref, sides):
+    for side, pieces in enumerate(sides):
+        for piece, ks in pieces:
+            _, tokens, groups, lanes = piece.shape
+            size = tokens * groups
+            for m, k in enumerate(ks):
+                spot = pl.ds(pl.multiple_of((row ^ k) * size, size), size)
+                wide_ref[side, spot, :] = piece[m].astype(F32).reshape(size, lanes)
+
+
+def first_half_kernel(orders, row_ref, state_ref, aux_ref, *rest):
+    pieces, (wide_ref, state_out, aux_out) = rest[:-3], rest[-3:]
+    per = len(pieces) // 2
+    state_out[...] = state_ref[...]
+    aux_out[...] = aux_ref[...]
+    spread_items(
+        row_ref[0], wide_ref, [list(zip(pieces[s * per : (s + 1) * per], orders[s])) for s in (0, 1)]
+    )
+
+
+def pair_kernel(orders, row_ref, aux_ref, state_ref, y_ref, z_ref, wide_in, *rest):
     pieces, (next_ref, col_ref, wide_ref, lhs_ref) = rest[:-4], rest[-4:]
     step = pl.program_id(0)
     block, total, width = state_ref.shape
-    row = row_ref[0]
-    _, _, tokens, groups, lanes = pieces[0].shape
+    _, tokens, groups, lanes = pieces[0].shape
+    per = len(pieces) // 2
 
     @pl.when(step == 0)
     def _():
-        size = tokens * groups
-        for side in (0, 1):
-            for piece, ks in zip(pieces, order):
-                for m, k in enumerate(ks):
-                    spot = pl.ds(pl.multiple_of((row ^ k) * size, size), size)
-                    wide_ref[spot, :] = piece[m, side].astype(F32).reshape(size, lanes)
-            for q in range(groups):
-                lhs_ref[side, :, q * lanes : (q + 1) * lanes] = wide_ref[
-                    pl.ds(q, total, stride=groups), :
-                ].astype(BF16)
+        spread_items(
+            row_ref[0], wide_ref, [list(zip(pieces[s * per : (s + 1) * per], orders[s])) for s in (0, 1)]
+        )
+
+        def one(q, carry):
+            cols = pl.ds(pl.multiple_of(q * lanes, lanes), lanes)
+            for side in (0, 1):
+                lhs_ref[side, :, cols] = wide_ref[side, pl.ds(q, total, stride=groups), :].astype(BF16)
+            return carry
+
+        lax.fori_loop(0, groups, one, 0, unroll=2)
 
     base = 2 * total
     match = aux_ref[base + 32 : base + 33]
@@ -260,18 +290,19 @@
         return lax.ppermute(array, "row", [(r, r ^ bit) for r in range(count)])
 
     aux_rows = 2 * total + 40
-    left, right, item, tiles, aux, gates = pl.pallas_call(
+    left, right, item_left, item_right, tiles, aux, gates = pl.pallas_call(
         prepare_kernel,
         out_shape=(
             jax.ShapeDtypeStruct((tokens * seqs, factor), BF16),
             jax.ShapeDtypeStruct((tokens * seqs, factor), BF16),
-            jax.ShapeDtypeStruct((2, tokens, half, 2 * seqs), BF16),
+            jax.ShapeDtypeStruct((1, tokens, half, 2 * seqs), BF16),
+            jax.ShapeDtypeStruct((1, tokens, half, 2 * seqs), BF16),
             jax.ShapeDtypeStruct((count, tokens * tokens, width), BF16),
             jax.ShapeDtypeStruct((aux_rows, width), F32),
             jax.ShapeDtypeStruct((2, width, gated), BF16),
         ),
         in_specs=[whole(SMEM)] + [whole(HBM)] * 16,
-        out_specs=(whole(VMEM),) * 6,
+        out_specs=(whole(VMEM),) * 7,
         scratch_shapes=[
             SMEM((total,), jnp.int32),
             VMEM((tokens, seqs, feats), BF16),
@@ -308,63 +339,90 @@
         input_gate_weight,
     )
 
-    y, z = pl.pallas_call(
-        mix_kernel,
-        out_shape=(jax.ShapeDtypeStruct((tokens // 2, inner, 2 * width), BF16),) * 2,
-        in_specs=[whole(VMEM), whole(VMEM), whole(HBM)],
-        out_specs=(whole(VMEM),) * 2,
-        scratch_shapes=[
-            VMEM((factor * factor, width), BF16),
-            VMEM((factor * factor, width), F32),
-            pltpu.SemaphoreType.DMA((1,)),
-        ],
+    def mixed(lhs, strided):
+        return pl.pallas_call(
+            functools.partial(mix_kernel, strided),
+            out_shape=jax.ShapeDtypeStruct((tokens // 2, inner, 2 * width), BF16),
+            in_specs=[whole(VMEM), whole(VMEM)],
+            out_specs=whole(VMEM),
+            scratch_shapes=[VMEM((factor * factor, width), F32)],
+            compiler_params=params(16),
+            cost_estimate=pl.CostEstimate(
+                flops=2 * tokens * seqs * factor * factor * width,
+                bytes_accessed=2 * inner * tokens * width,
+                transcendentals=0,
+            ),
+            name="mix",
+        )(lhs, output_weight)
+
+    def joined(lefts, rights):
+        shape = (sum(x.shape[0] for x in lefts), tokens, half, 2 * seqs)
+        return pl.pallas_call(
+            join_kernel,
+            out_shape=(jax.ShapeDtypeStruct(shape, BF16),) * 2,
+            in_specs=[whole(VMEM)] * (2 * len(lefts)),
+            out_specs=(whole(VMEM),) * 2,
+            compiler_params=params(16),
+            name="join",
+        )(*lefts, *rights)
+
+    bits = [1 << n for n in range(1, count.bit_length() - 1)][::-1]
+    turns = [bits, bits[-1:] + bits[:-1]]
+    own = [item_left, item_right]
+    far = [swap(x, t[0]) for x, t in zip(own, turns)]
+    near = [swap(x, t[1]) for x, t in zip(own, turns)]
+    both = [swap(x, t[1]) for x, t in zip(far, turns)]
+    y = mixed(left, True)
+    *both, y = lax.optimization_barrier((*both, y))
+    held = joined(*[[own[s], far[s], near[s], both[s]] for s in (0, 1)])
+    ranks = [[0, t[0], t[1], t[0] ^ t[1]] for t in turns]
+    for n in range(2, len(bits)):
+        came = [swap(x, t[n]) for x, t in zip(held, turns)]
+        new = [[k ^ t[n] for k in r] for r, t in zip(ranks, turns)]
+        if n + 1 < len(bits):
+            held = joined(*[[held[s], came[s]] for s in (0, 1)])
+            ranks = [r + m for r, m in zip(ranks, new)]
+    z = mixed(right, False)
+    early = [swap(x, 1) for x in held]
+    wide, state, aux = pl.pallas_call(
+        functools.partial(first_half_kernel, [[r, [k ^ 1 for k in r]] for r in ranks]),
+        out_shape=(
+            jax.ShapeDtypeStruct((2, total * half, 2 * seqs), F32),
+            jax.ShapeDtypeStruct((tokens, total, width), BF16),
+            jax.ShapeDtypeStruct((aux_rows, width), F32),
+        ),
+        in_specs=[whole(SMEM)] + [whole(VMEM)] * 6,
+        out_specs=(whole(VMEM),) * 3,
         compiler_params=params(16),
-        cost_estimate=pl.CostEstimate(
-            flops=4 * tokens * seqs * factor * factor * width,
-            bytes_accessed=4 * inner * tokens * width,
-            transcendentals=0,
-        ),
-        name="mix",
-    )(left, right, output_weight)
-
-    held, order = item[None], [0]
-    bit = count // 2
-    while bit > 1:
-        came = swap(held, bit)
-        new = [k ^ bit for k in order]
-        if bit == 4:
-            came, y, z = lax.optimization_barrier((came, y, z))
-        if bit > 2:
-            held, order = jnp.concatenate([held, came], axis=0), order + new
-        bit //= 2
-    pieces = [held, came, swap(held, 1), swap(came, 1)]
-    orders = [order, new, [k ^ 1 for k in order], [k ^ 1 for k in new]]
+        name="first_half",
+    )(row, pairwise_state, aux, held[0], early[0], held[1], early[1])
+    *came, z, wide, state, aux = lax.optimization_barrier((*came, z, wide, state, aux))
+    late = [swap(x, 1) for x in came]
 
     tiles = lax.all_to_all(tiles, "row", split_axis=0, concat_axis=0, tiled=True)
 
     block = 2
-    pair_next, columns = pl.pallas_call(
-        functools.partial(pair_kernel, orders),
+    pair_next, columns, _ = pl.pallas_call(
+        functools.partial(pair_kernel, [[r, [k ^ 1 for k in r]] for r in new]),
         grid=(tokens // block,),
         out_shape=(
             jax.ShapeDtypeStruct((tokens, total, width), BF16),
             jax.ShapeDtypeStruct((tokens, total, width), F32),
+            jax.ShapeDtypeStruct((2, total * half, 2 * seqs), F32),
         ),
         in_specs=[whole(SMEM), whole(VMEM), pl.BlockSpec((block, total, width), lambda g: (g, 0, 0))]
-        + [whole(VMEM)] * 6,
-        out_specs=(pl.BlockSpec((block, total, width), lambda g: (g, 0, 0)),) * 2,
-        scratch_shapes=[
-            VMEM((total * half, 2 * seqs), F32),
-            VMEM((2, total, inner), BF16),
-        ],
-        compiler_params=params(24),
+        + [whole(VMEM)] * 7,
+        out_specs=(pl.BlockSpec((block, total, width), lambda g: (g, 0, 0)),) * 2 + (whole(VMEM),),
+        scratch_shapes=[VMEM((2, total, inner), BF16)],
+        input_output_aliases={5: 2},
+        compiler_params=params(16),
         cost_estimate=pl.CostEstimate(
             flops=4 * total * inner * tokens * width,
             bytes_accessed=4 * inner * tokens * width + 8 * tokens * total * width,
             transcendentals=0,
         ),
         name="pair",
-    )(row, aux, pairwise_state, y, z, *pieces)
+    )(row, aux, state, y, z, wide, came[0], late[0], came[1], late[1])
 
     block = 4
     out = pl.pallas_call(

time: 56.7 us -> 61.8 us (1.090)
  starting transfers between devices: 12.6 us -> 19.2 us
  Pallas kernels: 18.4 us -> 21.8 us
  local copies, waits for them, and re-layouts: 4.8 us -> 1.91 us
  other arithmetic: 1.85 us -> 0 us
    ppermute x5 -> x12, starting transfers between devices: 6.97 us -> 11.8 us  [swap(): return lax.ppermute(array, 'row', [(r, r ^ bit) for r in range(count)])]
    pallas_call x2 -> x5, Pallas kernels: 11.5 us -> 15.1 us  [the longest x2 8.89 us: mixed(): pl.pallas_call(functools.partial(mix_kernel, strided), out_shape=jax.Shap...]
    unnamed x14 -> x18, local copies, waits for them, and re-layouts: 4.8 us -> 1.91 us
    concatenate x2 -> x0, other arithmetic: 1.85 us -> none  [body(): held, order = (jnp.concatenate([held, came], axis=0), order + new)]
    all_to_all x1, starting transfers between devices: 5.61 us -> 7.4 us  [body(): lax.all_to_all(tiles, 'row', split_axis=0, concat_axis=0, tiled=True)]
    ppermute x5 -> x12, waiting for transfers between devices: 17.9 us -> 17.8 us  [swap(): return lax.ppermute(array, 'row', [(r, r ^ bit) for r in range(count)])]
  transfers between devices with their start and end apart: 6 -> 13, of which waited for: 3 -> 5; matrix products, arithmetic and copies ran while one was open for 2% -> 0% of each run, Pallas kernels for 21% -> 24%
where the time goes in v5:
time: 61.8 us; the launch traced here: 61.5 us
  Pallas kernels  21.8 us (35%)
  starting transfers between devices  19.2 us (31%)
  waiting for transfers between devices  17.8 us (29%)
  local copies, waits for them, and re-layouts  1.91 us (3%)
  between operations  0.81 us (1%)
    ppermute x12, waiting for transfers between devices, swap(): return lax.ppermute(array, 'row', [(r, r ^ bit) for r in range(count)])  17.8 us
    ppermute x12, starting transfers between devices, swap(): return lax.ppermute(array, 'row', [(r, r ^ bit) for r in range(count)])  11.8 us
    pallas_call x2, Pallas kernels, mixed(): pl.pallas_call(functools.partial(mix_kernel, strided), out_shape=jax.Shap...  8.89 us
    all_to_all x1, starting transfers between devices, body(): lax.all_to_all(tiles, 'row', split_axis=0, concat_axis=0, tiled=True)  7.4 us
    pallas_call x1, Pallas kernels, body(): pl.pallas_call(functools.partial(pair_kernel, [[r, [k ^ 1 for k in r]] fo...  5.98 us
    pallas_call x1, Pallas kernels, body(): pl.pallas_call(gate_kernel, grid=(tokens // block,), out_shape=jax.ShapeD...  3.59 us
    pallas_call x1, Pallas kernels, body(): pl.pallas_call(prepare_kernel, out_shape=(jax.ShapeDtypeStruct((tokens *...  3.18 us
    unnamed x18, local copies, waits for them, and re-layouts  1.91 us
  transfers between devices with their start and end apart: 13, of which 5 were waited for; matrix products, arithmetic and copies ran while one was open for 0% of the time, Pallas kernels for 24%

profile of v5, /device:TPU:0, one launch (start us, length us, event | category | flops | bytes accessed | tf_op | source)
XLA Modules:
  0.0 61.5 jit_solution(12515509077641689944)
XLA Ops:
  0.6 3.2 %prepare.1 = (bf16[768,32]{1,0:T(8,128)(2,1)}, bf16[768,32]{1,0:T(8,128)(2,1)}, bf16[1,12,16,128]{3,2,1,0:T(8,128)(2,1)}, bf16[1,12,16,128]{3,2,1,0:T(8,128)(2,1...) custom-call(s32[1]{0:T(128)} %bitcast.row_ref, s32[192]{0:T(256)} %depth_hbm.1, ...), custom_call_target="tpu_custom_call" | custom-call | tf_op jit(solution)/shard_map/prepare/pallas_call | solution.py:293
  3.8 7.4 %all-to-all-start = ((bf16[16,144,128]{2,1,0:T(8,128)(2,1)}), bf16[16,144,128]{2,1,0:T(8,128)(2,1)S(1)}, u32[]{:S(2)}, u32[]{:S(2)}) async-start(bf16[16,144,128]{2,1,0:T(8,128)(2,1)} %get-tuple-element.47), calls=%async_computation | async-start | bytes 1179648 | tf_op jit(solution)/shard_map/all_to_all | solution.py:402
  11.2 2.8 %collective-permute-start = (bf16[1,12,16,128]{3,2,1,0:T(8,128)(2,1)}, bf16[1,12,16,128]{3,2,1,0:T(8,128)(2,1)S(1)}, u32[]{:S(2)}, u32[]{:S(2)}) collective-permute-start(bf16[1,12,16,128]{3,2,1,0:T(8,128)(2,1)} %get-tuple-element.25.refs_0_), channel_id=1, source_target_pairs={{0,8},{1,9},{2,10},{3,11},{4,12},{5,13},{6,14},{7,15},{8,0},{9,1},... | collective-permute-start | bytes 147464 | tf_op jit(solution)/shard_map/ppermute | solution.py:290
  14.1 1.5 %collective-permute-start.3 = (bf16[1,12,16,128]{3,2,1,0:T(8,128)(2,1)}, bf16[1,12,16,128]{3,2,1,0:T(8,128)(2,1)S(1)}, u32[]{:S(2)}, u32[]{:S(2)}) collective-permute-start(bf16[1,12,16,128]{3,2,1,0:T(8,128)(2,1)} %get-tuple-element.26.refs_4_), channel_id=1, source_target_pairs={{0,2},{1,3},{2,0},{3,1},{4,6},{5,7},{6,4},{7,5},{8,10},{9,11},{10,... | collective-permute-start | bytes 147464 | tf_op jit(solution)/shard_map/ppermute | solution.py:290
  15.5 14.5 %collective-permute-done.refs_1_ = bf16[1,12,16,128]{3,2,1,0:T(8,128)(2,1)S(1)} collective-permute-done((bf16[1,12,16,128]{3,2,1,0:T(8,128)(2,1)}, bf16[1,12,16,128]{3,2,1,0:T(8,128)(2,1)S(1)}, u32[]{:S(2)}, u32[]{:S(2)}) %collective-permute-start) | collective-permute-done | bytes 49184 | tf_op jit(solution)/shard_map/ppermute | solution.py:290
  30.1 0.0 collective-permute-start.2
  30.1 0.0 collective-permute-done.3.refs_5_
  30.1 2.0 %collective-permute-start.4 = (bf16[1,12,16,128]{3,2,1,0:T(8,128)(2,1)S(1)}, bf16[1,12,16,128]{3,2,1,0:T(8,128)(2,1)S(1)}, u32[]{:S(2)}, u32[]{:S(2)}) collective-permute-start(bf16[1,12,16,128]{3,2,1,0:T(8,128)(2,1)S(1)} %collective-permute-done.3.refs_5_), channel_id=1, source_target_pairs={{0,8},{1,9},{2,10},{3,11},{4,12},{5,13},{6,14},{7,15},{8,0},{9,1},... | collective-permute-start | bytes 147464 | tf_op jit(solution)/shard_map/ppermute | solution.py:290
  32.1 0.0 collective-permute-start.1
  32.1 2.9 %collective-permute-start.5 = (bf16[1,12,16,128]{3,2,1,0:T(8,128)(2,1)}, bf16[1,12,16,128]{3,2,1,0:T(8,128)(2,1)S(1)}, u32[]{:S(2)}, u32[]{:S(2)}) collective-permute-start(bf16[1,12,16,128]{3,2,1,0:T(8,128)(2,1)} %get-tuple-element.26.refs_4_), channel_id=1, source_target_pairs={{0,8},{1,9},{2,10},{3,11},{4,12},{5,13},{6,14},{7,15},{8,0},{9,1},... | collective-permute-start | bytes 147464 | tf_op jit(solution)/shard_map/ppermute | solution.py:290
  35.0 0.0 copy-start.1
  35.0 0.9 %copy-done.1 = bf16[1024,128]{1,0:T(8,128)(2,1)S(1)} copy-done((bf16[1024,128]{1,0:T(8,128)(2,1)S(1)}, bf16[1024,128]{1,0:T(8,128)(2,1)}, u32[]{:S(2)}) %copy-start.1) | copy-done | bytes 262168
  36.0 0.0 copy-start.5
  36.0 0.9 %copy-done.5 = bf16[768,32]{1,0:T(8,128)(2,1)S(1)} copy-done((bf16[768,32]{1,0:T(8,128)(2,1)S(1)}, bf16[768,32]{1,0:T(8,128)(2,1)}, u32[]{:S(2)}) %copy-start.5) | copy-done | bytes 49176
  36.9 0.0 copy-start.7
  36.9 0.0 copy-start.8
  36.9 0.0 copy-start.2
  36.9 0.0 copy-start.4
  36.9 4.5 %mix.2.y_ref = bf16[6,2048,256]{2,1,0:T(8,128)(2,1)S(1)} custom-call(bf16[768,32]{1,0:T(8,128)(2,1)S(1)} %copy-done.5, bf16[1024,128]{1,0:T(8,128)(2,1)S(1)} %copy-done.1), custom_call_target="tpu_custom_call" | custom-call | flops 201326592 | bytes 6291456 | tf_op jit(solution)/shard_map/mix/pallas_call | solution.py:343
  41.4 0.0 collective-permute-done.2.refs_3_
  41.5 0.0 collective-permute-done.4.refs_7_
  41.5 0.0 collective-permute-done.1.refs_2_
  41.5 0.0 collective-permute-done.5.refs_6_
  41.5 0.0 copy-done.7
  41.5 0.0 copy-done.8
  41.5 0.1 collective-permute-start.8
  41.6 0.5 collective-permute-start.9
  42.1 1.5 %collective-permute-start.6 = (bf16[4,12,16,128]{3,2,1,0:T(8,128)(2,1)S(1)}, bf16[4,12,16,128]{3,2,1,0:T(8,128)(2,1)S(1)}, u32[]{:S(2)}, u32[]{:S(2)}) collective-permute-start(bf16[4,12,16,128]{3,2,1,0:T(8,128)(2,1)S(1)} %get-tuple-element.30.rest_0_), channel_id=1, source_target_pairs={{0,2},{1,3},{2,0},{3,1},{4,6},{5,7},{6,4},{7,5},{8,10},{9,11},{10,... | collective-permute-start | bytes 589832 | tf_op jit(solution)/shard_map/ppermute | solution.py:290
  43.6 0.0 collective-permute-start.7
  43.6 0.0 copy-done.2
  43.6 0.0 copy-done.4
  43.6 0.0 copy-start
  43.6 0.0 copy-start.3
  43.6 4.3 %mix.3.z_ref = bf16[6,2048,256]{2,1,0:T(8,128)(2,1)S(1)} custom-call(bf16[768,32]{1,0:T(8,128)(2,1)S(1)} %copy-done.4, bf16[1024,128]{1,0:T(8,128)(2,1)S(1)} %copy-done.2), custom_call_target="tpu_custom_call" | custom-call | flops 201326592 | bytes 6291456 | tf_op jit(solution)/shard_map/mix/pallas_call | solution.py:343
  48.0 0.0 collective-permute-done.8.rest_1_
  48.0 0.0 collective-permute-done.9.rest_3_
  48.0 0.0 copy-done
  48.0 0.0 copy-done.3
  48.0 0.2 first_half.1
  48.2 0.8 %collective-permute-done.6.rest_0_ = bf16[4,12,16,128]{3,2,1,0:T(8,128)(2,1)S(1)} collective-permute-done((bf16[4,12,16,128]{3,2,1,0:T(8,128)(2,1)S(1)}, bf16[4,12,16,128]{3,2,1,0:T(8,128)(2,1)S(1)}, u32[]{:S(2)}, u32[]{:S(2)}) %collective-permute-start.6) | collective-permute-done | bytes 196640 | tf_op jit(solution)/shard_map/ppermute | solution.py:290
  49.0 1.2 %collective-permute-done.7.rest_2_ = bf16[4,12,16,128]{3,2,1,0:T(8,128)(2,1)S(1)} collective-permute-done((bf16[4,12,16,128]{3,2,1,0:T(8,128)(2,1)S(1)}, bf16[4,12,16,128]{3,2,1,0:T(8,128)(2,1)S(1)}, u32[]{:S(2)}, u32[]{:S(2)}) %collective-permute-start.7) | collective-permute-done | bytes 196640 | tf_op jit(solution)/shard_map/ppermute | solution.py:290
  50.2 0.0 copy-start.6
  50.2 0.0 collective-permute-start.10
  50.2 0.5 collective-permute-start.11
  50.7 0.9 %collective-permute-done.10.rest_1_ = bf16[4,12,16,128]{3,2,1,0:T(8,128)(2,1)S(1)} collective-permute-done((bf16[4,12,16,128]{3,2,1,0:T(8,128)(2,1)S(1)}, bf16[4,12,16,128]{3,2,1,0:T(8,128)(2,1)S(1)}, u32[]{:S(2)}, u32[]{:S(2)}) %collective-permute-start.10) | collective-permute-done | bytes 196640 | tf_op jit(solution)/shard_map/ppermute | solution.py:290
  51.7 0.3 collective-permute-done.11.rest_3_
  51.9 6.0 %pair.1 = (bf16[12,192,128]{2,1,0:T(8,128)(2,1)}, f32[12,192,128]{2,1,0:T(8,128)S(1)}, f32[2,3072,128]{2,1,0:T(8,128)S(1)}) custom-call(s32[1]{0:T(128)} %bitcast.row_ref, f32[424,128]{1,0:T(8,128)S(1)} %get-tuple-element.37.aux_ref, bf16[12,192,128]{2,1,0:T(8,128)(2,1)S(1)} %get-tuple-element.38.state_ref, ...), custom_call_target="tpu_custom_call", output_to_operand_aliasing={{2}: (5, {})} | custom-call | flops 2415919104 | bytes 14942208 | tf_op jit(solution)/shard_map/pair/pallas_call | solution.py:405
  57.9 0.0 all-to-all-done.tiles_ref
  57.9 0.0 copy-done.6
  57.9 3.6 %gate.1 = bf16[12,192,256]{2,1,0:T(8,128)(2,1)} custom-call(f32[424,128]{1,0:T(8,128)S(1)} %get-tuple-element.37.aux_ref, f32[12,192,128]{2,1,0:T(8,128)S(1)} %get-tuple-element.45.col_ref, bf16[2,128,256]{2,1,0:T(8,128)(2,1)S(1)} %copy-done.6, bf16[16,144,128]{2,1,0:T(8,128)(2,1)S(1)} %all-to-all-done.tiles_ref), custom_call_target="tpu_custom_call" | custom-call | flops 301989888 | bytes 2949120 | tf_op jit(solution)/shard_map/gate/pallas_call | solution.py:428
  (1 shorter events, 0.0 us)
Async XLA Ops:
  3.8 54.1 %all-to-all-start = ((bf16[16,144,128]{2,1,0:T(8,128)(2,1)}), bf16[16,144,128]{2,1,0:T(8,128)(2,1)S(1)}, u32[]{:S(2)}, u32[]{:S(2)}) async-start(bf16[16,144,128]{2,1,0:T(8,128)(2,1)} %get-tuple-element.47), calls=%async_computation | async-start | bytes 1179648 | tf_op jit(solution)/shard_map/all_to_all | solution.py:402
  11.2 18.8 %collective-permute-start = (bf16[1,12,16,128]{3,2,1,0:T(8,128)(2,1)}, bf16[1,12,16,128]{3,2,1,0:T(8,128)(2,1)S(1)}, u32[]{:S(2)}, u32[]{:S(2)}) collective-permute-start(bf16[1,12,16,128]{3,2,1,0:T(8,128)(2,1)} %get-tuple-element.25.refs_0_), channel_id=1, source_target_pairs={{0,8},{1,9},{2,10},{3,11},{4,12},{5,13},{6,14},{7,15},{8,0},{9,1},... | collective-permute-start | bytes 147464 | tf_op jit(solution)/shard_map/ppermute | solution.py:290
  14.1 16.0 %collective-permute-start.3 = (bf16[1,12,16,128]{3,2,1,0:T(8,128)(2,1)}, bf16[1,12,16,128]{3,2,1,0:T(8,128)(2,1)S(1)}, u32[]{:S(2)}, u32[]{:S(2)}) collective-permute-start(bf16[1,12,16,128]{3,2,1,0:T(8,128)(2,1)} %get-tuple-element.26.refs_4_), channel_id=1, source_target_pairs={{0,2},{1,3},{2,0},{3,1},{4,6},{5,7},{6,4},{7,5},{8,10},{9,11},{10,... | collective-permute-start | bytes 147464 | tf_op jit(solution)/shard_map/ppermute | solution.py:290
  30.1 11.4 %collective-permute-start.2 = (bf16[1,12,16,128]{3,2,1,0:T(8,128)(2,1)S(1)}, bf16[1,12,16,128]{3,2,1,0:T(8,128)(2,1)S(1)}, u32[]{:S(2)}, u32[]{:S(2)}) collective-permute-start(bf16[1,12,16,128]{3,2,1,0:T(8,128)(2,1)S(1)} %collective-permute-done.refs_1_), channel_id=1, source_target_pairs={{0,4},{1,5},{2,6},{3,7},{4,0},{5,1},{6,2},{7,3},{8,12},{9,13},{10,... | collective-permute-start | bytes 147464 | tf_op jit(solution)/shard_map/ppermute | solution.py:290
  30.1 11.4 %collective-permute-start.4 = (bf16[1,12,16,128]{3,2,1,0:T(8,128)(2,1)S(1)}, bf16[1,12,16,128]{3,2,1,0:T(8,128)(2,1)S(1)}, u32[]{:S(2)}, u32[]{:S(2)}) collective-permute-start(bf16[1,12,16,128]{3,2,1,0:T(8,128)(2,1)S(1)} %collective-permute-done.3.refs_5_), channel_id=1, source_target_pairs={{0,8},{1,9},{2,10},{3,11},{4,12},{5,13},{6,14},{7,15},{8,0},{9,1},... | collective-permute-start | bytes 147464 | tf_op jit(solution)/shard_map/ppermute | solution.py:290
  32.1 9.4 %collective-permute-start.1 = (bf16[1,12,16,128]{3,2,1,0:T(8,128)(2,1)}, bf16[1,12,16,128]{3,2,1,0:T(8,128)(2,1)S(1)}, u32[]{:S(2)}, u32[]{:S(2)}) collective-permute-start(bf16[1,12,16,128]{3,2,1,0:T(8,128)(2,1)} %get-tuple-element.25.refs_0_), channel_id=1, source_target_pairs={{0,4},{1,5},{2,6},{3,7},{4,0},{5,1},{6,2},{7,3},{8,12},{9,13},{10,... | collective-permute-start | bytes 147464 | tf_op jit(solution)/shard_map/ppermute | solution.py:290
  32.1 9.4 %collective-permute-start.5 = (bf16[1,12,16,128]{3,2,1,0:T(8,128)(2,1)}, bf16[1,12,16,128]{3,2,1,0:T(8,128)(2,1)S(1)}, u32[]{:S(2)}, u32[]{:S(2)}) collective-permute-start(bf16[1,12,16,128]{3,2,1,0:T(8,128)(2,1)} %get-tuple-element.26.refs_4_), channel_id=1, source_target_pairs={{0,8},{1,9},{2,10},{3,11},{4,12},{5,13},{6,14},{7,15},{8,0},{9,1},... | collective-permute-start | bytes 147464 | tf_op jit(solution)/shard_map/ppermute | solution.py:290
  35.0 0.9 %copy-start.1 = (bf16[1024,128]{1,0:T(8,128)(2,1)S(1)}, bf16[1024,128]{1,0:T(8,128)(2,1)}, u32[]{:S(2)}) copy-start(bf16[1024,128]{1,0:T(8,128)(2,1)} %weight_ref.3) | copy-start | bytes 786436
  36.0 0.9 %copy-start.5 = (bf16[768,32]{1,0:T(8,128)(2,1)S(1)}, bf16[768,32]{1,0:T(8,128)(2,1)}, u32[]{:S(2)}) copy-start(bf16[768,32]{1,0:T(8,128)(2,1)} %get-tuple-element.27.lhs_ref) | copy-start | bytes 147460
  36.9 4.6 %copy-start.7 = (bf16[1,12,16,128]{3,2,1,0:T(8,128)(2,1)S(1)}, bf16[1,12,16,128]{3,2,1,0:T(8,128)(2,1)}, u32[]{:S(2)}) copy-start(bf16[1,12,16,128]{3,2,1,0:T(8,128)(2,1)} %get-tuple-element.25.refs_0_) | copy-start | bytes 147460
  36.9 4.6 %copy-start.8 = (bf16[1,12,16,128]{3,2,1,0:T(8,128)(2,1)S(1)}, bf16[1,12,16,128]{3,2,1,0:T(8,128)(2,1)}, u32[]{:S(2)}) copy-start(bf16[1,12,16,128]{3,2,1,0:T(8,128)(2,1)} %get-tuple-element.26.refs_4_) | copy-start | bytes 147460
  36.9 6.7 %copy-start.2 = (bf16[1024,128]{1,0:T(8,128)(2,1)S(1)}, bf16[1024,128]{1,0:T(8,128)(2,1)}, u32[]{:S(2)}) copy-start(bf16[1024,128]{1,0:T(8,128)(2,1)} %weight_ref.3) | copy-start | bytes 786436
  36.9 6.7 %copy-start.4 = (bf16[768,32]{1,0:T(8,128)(2,1)S(1)}, bf16[768,32]{1,0:T(8,128)(2,1)}, u32[]{:S(2)}) copy-start(bf16[768,32]{1,0:T(8,128)(2,1)} %get-tuple-element.32.lhs_ref) | copy-start | bytes 147460
  41.5 6.4 %collective-permute-start.8 = (bf16[4,12,16,128]{3,2,1,0:T(8,128)(2,1)S(1)}, bf16[4,12,16,128]{3,2,1,0:T(8,128)(2,1)S(1)}, u32[]{:S(2)}, u32[]{:S(2)}) collective-permute-start(bf16[4,12,16,128]{3,2,1,0:T(8,128)(2,1)S(1)} %get-tuple-element.30.rest_0_), channel_id=1, source_target_pairs={{0,1},{1,0},{2,3},{3,2},{4,5},{5,4},{6,7},{7,6},{8,9},{9,8},{10,11... | collective-permute-start | bytes 589832 | tf_op jit(solution)/shard_map/ppermute | solution.py:290
  41.6 6.4 %collective-permute-start.9 = (bf16[4,12,16,128]{3,2,1,0:T(8,128)(2,1)S(1)}, bf16[4,12,16,128]{3,2,1,0:T(8,128)(2,1)S(1)}, u32[]{:S(2)}, u32[]{:S(2)}) collective-permute-start(bf16[4,12,16,128]{3,2,1,0:T(8,128)(2,1)S(1)} %get-tuple-element.31.rest_2_), channel_id=1, source_target_pairs={{0,1},{1,0},{2,3},{3,2},{4,5},{5,4},{6,7},{7,6},{8,9},{9,8},{10,11... | collective-permute-start | bytes 589832 | tf_op jit(solution)/shard_map/ppermute | solution.py:290
  42.1 6.9 %collective-permute-start.6 = (bf16[4,12,16,128]{3,2,1,0:T(8,128)(2,1)S(1)}, bf16[4,12,16,128]{3,2,1,0:T(8,128)(2,1)S(1)}, u32[]{:S(2)}, u32[]{:S(2)}) collective-permute-start(bf16[4,12,16,128]{3,2,1,0:T(8,128)(2,1)S(1)} %get-tuple-element.30.rest_0_), channel_id=1, source_target_pairs={{0,2},{1,3},{2,0},{3,1},{4,6},{5,7},{6,4},{7,5},{8,10},{9,11},{10,... | collective-permute-start | bytes 589832 | tf_op jit(solution)/shard_map/ppermute | solution.py:290
  43.6 6.6 %collective-permute-start.7 = (bf16[4,12,16,128]{3,2,1,0:T(8,128)(2,1)S(1)}, bf16[4,12,16,128]{3,2,1,0:T(8,128)(2,1)S(1)}, u32[]{:S(2)}, u32[]{:S(2)}) collective-permute-start(bf16[4,12,16,128]{3,2,1,0:T(8,128)(2,1)S(1)} %get-tuple-element.31.rest_2_), channel_id=1, source_target_pairs={{0,4},{1,5},{2,6},{3,7},{4,0},{5,1},{6,2},{7,3},{8,12},{9,13},{10,... | collective-permute-start | bytes 589832 | tf_op jit(solution)/shard_map/ppermute | solution.py:290
  43.6 4.4 %copy-start = (bf16[12,192,128]{2,1,0:T(8,128)(2,1)S(1)}, bf16[12,192,128]{2,1,0:T(8,128)(2,1)}, u32[]{:S(2)}) copy-start(bf16[12,192,128]{2,1,0:T(8,128)(2,1)} %state_ref.1) | copy-start | bytes 1769476
  43.6 4.4 %copy-start.3 = (f32[424,128]{1,0:T(8,128)S(1)}, f32[424,128]{1,0:T(8,128)}, u32[]{:S(2)}) copy-start(f32[424,128]{1,0:T(8,128)} %get-tuple-element.33.aux_ref) | copy-start | bytes 651268
  50.2 7.7 %copy-start.6 = (bf16[2,128,256]{2,1,0:T(8,128)(2,1)S(1)}, bf16[2,128,256]{2,1,0:T(8,128)(2,1)}, u32[]{:S(2)}) copy-start(bf16[2,128,256]{2,1,0:T(8,128)(2,1)} %get-tuple-element.46.gates_ref) | copy-start | bytes 393220
  50.2 1.4 %collective-permute-start.10 = (bf16[4,12,16,128]{3,2,1,0:T(8,128)(2,1)S(1)}, bf16[4,12,16,128]{3,2,1,0:T(8,128)(2,1)S(1)}, u32[]{:S(2)}, u32[]{:S(2)}) collective-permute-start(bf16[4,12,16,128]{3,2,1,0:T(8,128)(2,1)S(1)} %collective-permute-done.6.rest_0_), channel_id=1, source_target_pairs={{0,1},{1,0},{2,3},{3,2},{4,5},{5,4},{6,7},{7,6},{8,9},{9,8},{10,11... | collective-permute-start | bytes 589832 | tf_op jit(solution)/shard_map/ppermute | solution.py:290
  50.2 1.7 %collective-permute-start.11 = (bf16[4,12,16,128]{3,2,1,0:T(8,128)(2,1)S(1)}, bf16[4,12,16,128]{3,2,1,0:T(8,128)(2,1)S(1)}, u32[]{:S(2)}, u32[]{:S(2)}) collective-permute-start(bf16[4,12,16,128]{3,2,1,0:T(8,128)(2,1)S(1)} %collective-permute-done.7.rest_2_), channel_id=1, source_target_pairs={{0,1},{1,0},{2,3},{3,2},{4,5},{5,4},{6,7},{7,6},{8,9},{9,8},{10,11... | collective-permute-start | bytes 589832 | tf_op jit(solution)/shard_map/ppermute | solution.py:290

commit v6 on v5

v6 whole, which is shorter than its diff:
```python
import functools

import jax
import jax.numpy as jnp
from jax import lax
from jax.experimental import pallas as pl
from jax.experimental.pallas import tpu as pltpu
from jax.sharding import PartitionSpec as P

F32 = jnp.float32
BF16 = jnp.bfloat16
NT = (((1,), (1,)), ((), ()))
VMEM = pltpu.VMEM
SMEM = pltpu.SMEM
HBM = pltpu.HBM
LANES = 128


def whole(space):
    return pl.BlockSpec(memory_space=space)


def params(mib):
    return pltpu.CompilerParams(vmem_limit_bytes=mib * 1024 * 1024)


def fetch(sems, *pairs):
    copies = [pltpu.make_async_copy(a, b, sems.at[n]) for n, (a, b) in enumerate(pairs)]
    for copy in copies:
        copy.start()
    return copies


def finish(copies):
    for copy in copies:
        copy.wait()


def prepare_kernel(
    row_ref, depth_hbm, hom_hbm, scale_hbm, shift_hbm, src_hbm, tgt_hbm, depth_row_hbm, chain_hbm, chain_row_hbm,
    match_hbm, bias_hbm, gain_hbm, move_hbm, proj_hbm, gate_hbm,
    left_ref, front_ref, back_ref, aux_ref, gates_ref,
    depth_ref, hom_ref, scale_ref, shift_ref, both_ref, depth_row_ref, chain_ref, chain_row_ref, vec_ref, tmp_ref, sems,
):
    tokens, seqs, feats = hom_ref.shape
    pair_width = aux_ref.shape[1]
    total = depth_ref.shape[0]
    width = src_hbm.shape[0]
    half = width // 2
    gated = proj_hbm.shape[1]
    first_copies = fetch(
        sems,
        (hom_hbm, hom_ref),
        (depth_hbm, depth_ref),
        (scale_hbm, scale_ref),
        (shift_hbm, shift_ref),
        (src_hbm, both_ref.at[0:width]),
        (tgt_hbm, both_ref.at[width : 2 * width]),
        (chain_hbm, chain_ref),
        (depth_row_hbm, depth_row_ref),
        (chain_row_hbm, chain_row_ref),
        (match_hbm, vec_ref.at[0]),
        (bias_hbm, vec_ref.at[1]),
        (gain_hbm, vec_ref.at[2]),
        (move_hbm, vec_ref.at[3]),
        (proj_hbm, gates_ref.at[0]),
        (gate_hbm, gates_ref.at[1]),
    )
    finish(first_copies[:6])
    values = hom_ref[...].reshape(tokens * seqs, feats)
    ones = jnp.full((feats, feats), 1.0 / feats, BF16)
    centre = values.astype(F32) - jnp.dot(values, ones, preferred_element_type=F32)
    square = centre * centre
    high = square.astype(BF16)
    low = (square - high.astype(F32)).astype(BF16)
    spread = jnp.dot(high, ones, preferred_element_type=F32) + jnp.dot(
        low, ones, preferred_element_type=F32
    )
    normed = (centre * lax.rsqrt(spread + 1e-05) * scale_ref[...] + shift_ref[...]).astype(BF16)
    turned = lax.dot_general(both_ref[width : 2 * width], normed, NT, preferred_element_type=F32)
    plain = lax.dot_general(normed, both_ref[0:width], NT, preferred_element_type=F32)
    first = row_ref[0] * tokens
    row_pos = lax.broadcasted_iota(jnp.int32, (seqs, width), 0)
    lane = lax.broadcasted_iota(jnp.int32, (half, 2 * seqs), 1)
    seq_pos = jnp.where(lane < seqs, lane, lane - seqs)
    part = half // 2
    for n in range(tokens):
        depth = depth_ref[first + n]
        rows = slice(n * seqs, (n + 1) * seqs)
        left_ref[rows] = jnp.where(row_pos < depth, plain[rows], 0.0).astype(BF16)
        joint = jnp.concatenate([turned[0:half, rows], turned[half:width, rows]], axis=1)
        joint = jnp.where(seq_pos < depth, joint, 0.0)
        for side in (0, 1):
            tmp_ref[side, n * part : (n + 1) * part] = joint[side * part : (side + 1) * part]
    front_ref[0] = tmp_ref[0].astype(BF16)
    back_ref[0] = tmp_ref[1].astype(BF16)

    finish(first_copies[6:])
    same = lax.broadcasted_iota(jnp.int32, (total, total), 0) == lax.broadcasted_iota(
        jnp.int32, (total, total), 1
    )
    fill = jnp.ones((total, pair_width), BF16)

    def column(ref):
        diagonal = jnp.where(same, ref[...].astype(F32), 0.0).astype(BF16)
        return jnp.dot(diagonal, fill, preferred_element_type=F32)

    aux_ref[0:total] = 1.0 / jnp.maximum(column(depth_row_ref), 1.0)
    aux_ref[total : 2 * total] = column(chain_row_ref)
    for n in range(tokens):
        own = jnp.full((1, pair_width), depth_ref[first + n], jnp.int32).astype(F32)
        aux_ref[2 * total + n : 2 * total + n + 1] = 1.0 / jnp.maximum(own, 1.0)
        label = jnp.full((1, pair_width), chain_ref[first + n], jnp.int32).astype(F32)
        aux_ref[2 * total + 16 + n : 2 * total + 17 + n] = label
    for n in range(4):
        aux_ref[2 * total + 32 + n : 2 * total + 33 + n] = vec_ref[n]


def mix_kernel(strided, lhs_ref, weight_ref, out_ref, wide_ref):
    factor = lhs_ref.shape[1]
    half = factor // 2
    seqs = out_ref.shape[1] // factor
    width = weight_ref.shape[1]
    tokens = lhs_ref.shape[0] // seqs
    wide_ref[...] = weight_ref[...].astype(F32)

    def one(q, carry):
        if strided:
            pair = [wide_ref[pl.ds(q + t * half, factor, stride=factor), :] for t in (0, 1)]
        else:
            pair = [
                wide_ref[pl.ds(pl.multiple_of((q + t * half) * factor, factor), factor), :] for t in (0, 1)
            ]
        rhs = jnp.concatenate(pair, axis=1).astype(BF16)
        mixed = jnp.dot(lhs_ref[...], rhs, preferred_element_type=F32).astype(BF16)
        for n in range(tokens):
            rows = slice(n * seqs, (n + 1) * seqs)
            cols = slice(n % 2 * width, (n % 2 + 1) * width)
            for t in (0, 1):
                spot = pl.ds(pl.multiple_of((2 * q + t) * seqs, seqs), seqs)
                out_ref[n // 2, spot, cols] = mixed[rows, t * width : (t + 1) * width]
        return carry

    lax.fori_loop(0, half, one, 0)


def join_kernel(*refs):
    per = (len(refs) - 2) // 2
    for side in (0, 1):
        spot = 0
        for piece in refs[side * per : (side + 1) * per]:
            refs[2 * per + side][spot : spot + piece.shape[0]] = piece[...]
            spot += piece.shape[0]


def spread_items(row, wide_ref, sides):
    for side, pieces in enumerate(sides):
        for piece, ks in pieces:
            size = piece.shape[1]
            for m, k in enumerate(ks):
                spot = pl.ds(pl.multiple_of((row ^ k) * size, size), size)
                wide_ref[side, spot, :] = piece[m].astype(F32)


def first_half_kernel(orders, row_ref, state_ref, aux_ref, *rest):
    pieces, (wide_ref, state_out, aux_out) = rest[:-3], rest[-3:]
    per = len(pieces) // 2
    state_out[...] = state_ref[...]
    aux_out[...] = aux_ref[...]
    spread_items(
        row_ref[0], wide_ref, [list(zip(pieces[s * per : (s + 1) * per], orders[s])) for s in (0, 1)]
    )


def pair_kernel(orders, row_ref, aux_ref, state_ref, y_ref, wide_in, *rest):
    pieces, (next_ref, same_ref, cross_ref, wide_ref, lhs_ref, msg_ref) = rest[:-6], rest[-6:]
    step = pl.program_id(0)
    block, total, width = state_ref.shape
    lanes = pieces[0].shape[2]
    per = len(pieces) // 2
    count = msg_ref.shape[0]
    tokens = total // count
    groups = wide_ref.shape[1] // total

    @pl.when(step == 0)
    def _():
        spread_items(
            row_ref[0], wide_ref, [list(zip(pieces[s * per : (s + 1) * per], orders[s])) for s in (0, 1)]
        )

        def one(q, carry):
            for side in (0, 1):
                cols = pl.ds(pl.multiple_of((side * groups + q) * lanes, lanes), lanes)
                lhs_ref[:, cols] = wide_ref[side, pl.ds(q, total, stride=groups), :].astype(BF16)
            return carry

        lax.fori_loop(0, groups, one, 0, unroll=2)

    base = 2 * total
    match = aux_ref[base + 32 : base + 33]
    bias = aux_ref[base + 33 : base + 34]
    prod = jnp.dot(lhs_ref[...], y_ref[step], preferred_element_type=F32)
    done = []
    for t in range(block):
        own = step * block + t
        inv_own = aux_ref[pl.ds(base + own, 1)]
        label = aux_ref[pl.ds(base + 16 + own, 1)]
        extra = jnp.where(aux_ref[total:base] == label, match, 0.0) + bias
        value = prod[:, t * width : (t + 1) * width] * jnp.maximum(aux_ref[0:total], inv_own) + extra
        value = state_ref[t].astype(F32) + value
        next_ref[t] = value.astype(BF16)
        done.append(value)
    size = block * tokens
    for d in range(count):
        rows = slice(d * tokens, (d + 1) * tokens)
        msg_ref[d, pl.ds(pl.multiple_of(step * size, size), size), :] = jnp.concatenate(
            [value[rows] for value in done], axis=0
        )

    for core in (0, 1):

        @pl.when((step == pl.num_programs(0) - 1) & ((row_ref[0] & 1) == core))
        def _():
            for d in range(count):
                (same_ref if (d & 1) == core else cross_ref)[d // 2] = msg_ref[d].astype(BF16)


def pack_kernel(row_ref, same_ref, crossed_ref, *outs):
    chip = row_ref[0] >> 1
    for core in (0, 1):

        @pl.when((row_ref[0] & 1) == core)
        def _():
            for k, out_ref in enumerate(outs):
                out_ref[core] = same_ref[chip ^ k]
                out_ref[1 - core] = crossed_ref[chip ^ k]


def gate_kernel(row_ref, aux_ref, gates_ref, *rest):
    tiles, (out_ref, wide_ref) = rest[:-2], rest[-2:]
    step = pl.program_id(0)
    block, total = out_ref.shape[:2]
    rows, width = tiles[0].shape[1:]
    tokens = total // (2 * len(tiles))

    @pl.when(step == 0)
    def _():
        chip = row_ref[0] >> 1
        for k, tile in enumerate(tiles):
            for core in (0, 1):
                spot = pl.ds(pl.multiple_of(((chip ^ k) * 2 + core) * rows, rows), rows)
                wide_ref[spot, :] = tile[core].astype(F32)

    gain = aux_ref[2 * total + 34 : 2 * total + 35]
    shift = aux_ref[2 * total + 35 : 2 * total + 36]
    ones = jnp.full((width, width), 1.0 / width, BF16)
    none = jnp.zeros((width, width), BF16)
    means = jnp.concatenate(
        [jnp.concatenate([ones, none], axis=1), jnp.concatenate([none, ones], axis=1)], axis=0
    )
    for t in range(0, block, 2):
        pair = jnp.concatenate(
            [wide_ref[pl.ds(step * block + t + u, total, stride=tokens), :] for u in (0, 1)], axis=1
        )
        centre = pair - jnp.dot(pair.astype(BF16), means, preferred_element_type=F32)
        square = (centre * centre).astype(BF16)
        spread = jnp.dot(square, means, preferred_element_type=F32)
        scaled = centre * lax.rsqrt(spread + 1e-05)
        for u in (0, 1):
            normed = scaled[:, u * width : (u + 1) * width] * gain + shift
            normed = normed.astype(BF16)
            projected = jnp.dot(normed, gates_ref[0], preferred_element_type=F32)
            gating = jnp.dot(normed, gates_ref[1], preferred_element_type=F32)
            out_ref[t + u] = (projected * (0.5 + 0.5 * jnp.tanh(0.5 * gating))).astype(BF16)


def fixed(*shape):
    return pl.BlockSpec(shape, lambda g: (0,) * len(shape))


def body(
    pairwise_state,
    homolog_embedding,
    alignment_depth,
    chain_labels,
    homolog_layer_scale,
    homolog_layer_shift,
    outer_source_matrix,
    outer_target_matrix,
    output_weight,
    output_bias,
    chain_match,
    pairwise_norm_gain,
    pairwise_norm_bias,
    input_projection_weight,
    input_gate_weight,
    *,
    count,
):
    tokens, total, width = pairwise_state.shape
    seqs, _, feats = homolog_embedding.shape
    factor = outer_source_matrix.shape[1]
    half = factor // 2
    inner = factor * seqs
    gated = input_projection_weight.shape[1]
    row = lax.axis_index("row").astype(jnp.int32).reshape(1)

    def swap(array, bit):
        return lax.ppermute(array, "row", [(r, r ^ bit) for r in range(count)])

    aux_rows = 2 * total + 40
    part = tokens * half // 2
    left, front, back, aux, gates = pl.pallas_call(
        prepare_kernel,
        out_shape=(
            jax.ShapeDtypeStruct((tokens * seqs, factor), BF16),
            jax.ShapeDtypeStruct((1, part, 2 * seqs), BF16),
            jax.ShapeDtypeStruct((1, part, 2 * seqs), BF16),
            jax.ShapeDtypeStruct((aux_rows, width), F32),
            jax.ShapeDtypeStruct((2, width, gated), BF16),
        ),
        in_specs=[whole(SMEM)] + [whole(HBM)] * 15,
        out_specs=(whole(VMEM),) * 5,
        scratch_shapes=[
            SMEM((total,), jnp.int32),
            VMEM((tokens, seqs, feats), BF16),
            VMEM((1, feats), F32),
            VMEM((1, feats), F32),
            VMEM((2 * factor, feats), BF16),
            VMEM((1, total), jnp.int32),
            SMEM((total,), jnp.int32),
            VMEM((1, total), jnp.int32),
            VMEM((4, 1, width), F32),
            VMEM((2, part, 2 * seqs), F32),
            pltpu.SemaphoreType.DMA((15,)),
        ],
        name="prepare",
    )(
        row,
        alignment_depth,
        homolog_embedding.transpose(1, 0, 2),
        homolog_layer_scale.reshape(1, feats),
        homolog_layer_shift.reshape(1, feats),
        outer_source_matrix.T,
        outer_target_matrix.T,
        alignment_depth.reshape(1, total),
        chain_labels,
        chain_labels.reshape(1, total),
        chain_match.reshape(1, width),
        output_bias.reshape(1, width),
        pairwise_norm_gain.reshape(1, width),
        pairwise_norm_bias.reshape(1, width),
        input_projection_weight,
        input_gate_weight,
    )

    def joined(fronts, backs):
        shape = (sum(x.shape[0] for x in fronts), part, 2 * seqs)
        return pl.pallas_call(
            join_kernel,
            out_shape=(jax.ShapeDtypeStruct(shape, BF16),) * 2,
            in_specs=[whole(VMEM)] * (2 * len(fronts)),
            out_specs=(whole(VMEM),) * 2,
            compiler_params=params(16),
            name="join",
        )(*fronts, *backs)

    bits = [1 << n for n in range(1, count.bit_length() - 1)][::-1]
    turns = [bits, bits[-1:] + bits[:-1]]
    own = [front, back]
    far = [swap(x, t[0]) for x, t in zip(own, turns)]
    near = [swap(x, t[1]) for x, t in zip(own, turns)]
    both = [swap(x, t[1]) for x, t in zip(far, turns)]
    held = joined(*[[own[s], far[s], near[s], both[s]] for s in (0, 1)])
    ranks = [[0, t[0], t[1], t[0] ^ t[1]] for t in turns]
    for n in range(2, len(bits)):
        came = [swap(x, t[n]) for x, t in zip(held, turns)]
        new = [[k ^ t[n] for k in r] for r, t in zip(ranks, turns)]
        if n + 1 < len(bits):
            held = joined(*[[held[s], came[s]] for s in (0, 1)])
            ranks = [r + m for r, m in zip(ranks, new)]
    early = [swap(x, 1) for x in held]
    y = pl.pallas_call(
        functools.partial(mix_kernel, True),
        out_shape=jax.ShapeDtypeStruct((tokens // 2, inner, 2 * width), BF16),
        in_specs=[whole(VMEM), whole(VMEM)],
        out_specs=whole(VMEM),
        scratch_shapes=[VMEM((factor * factor, width), F32)],
        compiler_params=params(16),
        cost_estimate=pl.CostEstimate(
            flops=2 * tokens * seqs * factor * factor * width,
            bytes_accessed=2 * inner * tokens * width,
            transcendentals=0,
        ),
        name="mix",
    )(left, output_weight)
    wide, state, aux = pl.pallas_call(
        functools.partial(first_half_kernel, [[r, [k ^ 1 for k in r]] for r in ranks]),
        out_shape=(
            jax.ShapeDtypeStruct((2, count * part, 2 * seqs), F32),
            jax.ShapeDtypeStruct((tokens, total, width), BF16),
            jax.ShapeDtypeStruct((aux_rows, width), F32),
        ),
        in_specs=[whole(SMEM)] + [whole(VMEM)] * 6,
        out_specs=(whole(VMEM),) * 3,
        compiler_params=params(16),
        name="first_half",
    )(row, pairwise_state, aux, held[0], early[0], held[1], early[1])
    *came, y, wide, state, aux = lax.optimization_barrier((*came, y, wide, state, aux))
    late = [swap(x, 1) for x in came]

    block = 2
    chips = count // 2
    tile = tokens * tokens
    pair_next, same, cross, _ = pl.pallas_call(
        functools.partial(pair_kernel, [[r, [k ^ 1 for k in r]] for r in new]),
        grid=(tokens // block,),
        out_shape=(
            jax.ShapeDtypeStruct((tokens, total, width), BF16),
            jax.ShapeDtypeStruct((chips, tile, width), BF16),
            jax.ShapeDtypeStruct((chips, tile, width), BF16),
            jax.ShapeDtypeStruct((2, count * part, 2 * seqs), F32),
        ),
        in_specs=[whole(SMEM), whole(VMEM), pl.BlockSpec((block, total, width), lambda g: (g, 0, 0))]
        + [whole(VMEM)] * 6,
        out_specs=(pl.BlockSpec((block, total, width), lambda g: (g, 0, 0)),) + (whole(VMEM),) * 3,
        scratch_shapes=[VMEM((total, inner), BF16), VMEM((count, tile, width), F32)],
        input_output_aliases={4: 3},
        compiler_params=params(16),
        cost_estimate=pl.CostEstimate(
            flops=2 * total * inner * tokens * width,
            bytes_accessed=2 * inner * tokens * width + 8 * tokens * total * width,
            transcendentals=0,
        ),
        name="pair",
    )(row, aux, state, y, wide, came[0], late[0], came[1], late[1])

    crossed = swap(cross, 1)
    tiles = pl.pallas_call(
        pack_kernel,
        out_shape=(jax.ShapeDtypeStruct((2, tile, width), BF16),) * chips,
        in_specs=[whole(SMEM), whole(VMEM), whole(VMEM)],
        out_specs=(whole(VMEM),) * chips,
        compiler_params=params(16),
        name="pack",
    )(row, same, crossed)
    tiles = [tiles[0]] + [swap(tiles[k], 2 * k) for k in range(1, chips)]

    block = 4
    out = pl.pallas_call(
        gate_kernel,
        grid=(tokens // block,),
        out_shape=jax.ShapeDtypeStruct((tokens, total, gated), BF16),
        in_specs=[whole(SMEM)] + [whole(VMEM)] * (2 + chips),
        out_specs=pl.BlockSpec((block, total, gated), lambda j: (j, 0, 0)),
        scratch_shapes=[VMEM((count * tile, width), F32)],
        compiler_params=params(24),
        cost_estimate=pl.CostEstimate(
            flops=4 * tokens * total * width * gated,
            bytes_accessed=tokens * total * (2 * gated + 6 * width),
            transcendentals=tokens * total * gated,
        ),
        name="gate",
    )(row, aux, gates, *tiles)
    return pair_next, out.transpose(1, 0, 2)


def solution(mesh):
    return jax.shard_map(
        functools.partial(body, count=mesh.shape["row"]),
        mesh=mesh,
        in_specs=(
            P(("groups", "row"), None, None),
            P(None, ("groups", "row"), None),
            P("groups"),
            P("groups"),
        )
        + (P(),) * 11,
        out_specs=(P(("groups", "row"), None, None), P("groups", "row", None)),
        check_vma=False,
    )
```

time: 61.8 us -> 56.6 us (0.916)
  waiting for transfers between devices: 17.8 us -> 9.94 us
  starting transfers between devices: 19.2 us -> 26.5 us
  Pallas kernels: 21.8 us -> 15.3 us
  local copies, waits for them, and re-layouts: 1.91 us -> 3.36 us
    ppermute x12 -> x20, starting transfers between devices: 11.8 us -> 26.5 us  [swap(): return lax.ppermute(array, 'row', [(r, r ^ bit) for r in range(count)])]
    ppermute x12 -> x20, waiting for transfers between devices: 17.8 us -> 9.94 us  [swap(): return lax.ppermute(array, 'row', [(r, r ^ bit) for r in range(count)])]
    all_to_all x1 -> x0, starting transfers between devices: 7.4 us -> none  [body(): lax.all_to_all(tiles, 'row', split_axis=0, concat_axis=0, tiled=True)]
    pallas_call x2, Pallas kernels: 8.89 us -> 4.59 us  [the longest x1 4.55 us: body(): pl.pallas_call(functools.partial(mix_kernel, True), out_shape=jax.ShapeDt...]
    pallas_call x1, Pallas kernels: 5.98 us -> 4.14 us  [body(): pl.pallas_call(functools.partial(pair_kernel, [[r, [k ^ 1 for k in r]] fo...]
    unnamed x18 -> x14, local copies, waits for them, and re-layouts: 1.91 us -> 3.36 us
  transfers between devices with their start and end apart: 13 -> 20, of which waited for: 5 -> 8; matrix products, arithmetic and copies ran while one was open for 0% -> 0% of each run, Pallas kernels for 24% -> 8%
where the time goes in v6:
time: 56.6 us; the launch traced here: 55.8 us
  starting transfers between devices  26.5 us (47%)
  Pallas kernels  15.3 us (27%)
  waiting for transfers between devices  9.94 us (18%)
  local copies, waits for them, and re-layouts  3.36 us (6%)
  between operations  0.77 us (1%)
    ppermute x20, starting transfers between devices, swap(): return lax.ppermute(array, 'row', [(r, r ^ bit) for r in range(count)])  26.5 us
    ppermute x20, waiting for transfers between devices, swap(): return lax.ppermute(array, 'row', [(r, r ^ bit) for r in range(count)])  9.94 us
    pallas_call x1, Pallas kernels, body(): pl.pallas_call(functools.partial(mix_kernel, True), out_shape=jax.ShapeDt...  4.55 us
    pallas_call x1, Pallas kernels, body(): pl.pallas_call(functools.partial(pair_kernel, [[r, [k ^ 1 for k in r]] fo...  4.14 us
    pallas_call x1, Pallas kernels, body(): pl.pallas_call(gate_kernel, grid=(tokens // block,), out_shape=jax.ShapeD...  3.63 us
    unnamed x14, local copies, waits for them, and re-layouts  3.36 us
    pallas_call x1, Pallas kernels, body(): pl.pallas_call(prepare_kernel, out_shape=(jax.ShapeDtypeStruct((tokens *...  2.77 us
  transfers between devices with their start and end apart: 20, of which 8 were waited for; matrix products, arithmetic and copies ran while one was open for 0% of the time, Pallas kernels for 8%

profile of v6, /device:TPU:0, one launch (start us, length us, event | category | flops | bytes accessed | tf_op | source)
XLA Modules:
  0.0 55.8 jit_solution(6826391722941437116)
XLA Ops:
  0.6 2.8 %prepare.1 = (bf16[768,32]{1,0:T(8,128)(2,1)}, bf16[1,96,128]{2,1,0:T(8,128)(2,1)}, bf16[1,96,128]{2,1,0:T(8,128)(2,1)}, f32[424,128]{1,0:T(8,128)}, bf16[2,128,256]{2,1,0:T(8,128)(2,1)}) custom-call(s32[1]{0:T(128)} %bitcast.row_ref, s32[192]{0:T(256)} %depth_hbm.1, bf16[12,64,64]{2,1,0:T(8,128)(2,1)} %bitcast.14, f32[1,64]{1,0:T(1,128)} %bitcast.19, ...), custom_call_target="tpu_custom_call" | custom-call | tf_op jit(solution)/shard_map/prepare/pallas_call | solution.py:313
  3.4 4.1 %collective-permute-start = (bf16[1,96,128]{2,1,0:T(8,128)(2,1)}, bf16[1,96,128]{2,1,0:T(8,128)(2,1)S(1)}, u32[]{:S(2)}, u32[]{:S(2)}) collective-permute-start(bf16[1,96,128]{2,1,0:T(8,128)(2,1)} %get-tuple-element.29.refs_0_), channel_id=1, source_target_pairs={{0,8},{1,9},{2,10},{3,11},{4,12},{5,13},{6,14},{7,15},{8,0},{9,1},... | collective-permute-start | bytes 73736 | tf_op jit(solution)/shard_map/ppermute | solution.py:309
  7.5 1.5 %collective-permute-start.3 = (bf16[1,96,128]{2,1,0:T(8,128)(2,1)}, bf16[1,96,128]{2,1,0:T(8,128)(2,1)S(1)}, u32[]{:S(2)}, u32[]{:S(2)}) collective-permute-start(bf16[1,96,128]{2,1,0:T(8,128)(2,1)} %get-tuple-element.30.refs_4_), channel_id=1, source_target_pairs={{0,2},{1,3},{2,0},{3,1},{4,6},{5,7},{6,4},{7,5},{8,10},{9,11},{10,... | collective-permute-start | bytes 73736 | tf_op jit(solution)/shard_map/ppermute | solution.py:309
  9.0 1.6 %collective-permute-start.1 = (bf16[1,96,128]{2,1,0:T(8,128)(2,1)}, bf16[1,96,128]{2,1,0:T(8,128)(2,1)S(1)}, u32[]{:S(2)}, u32[]{:S(2)}) collective-permute-start(bf16[1,96,128]{2,1,0:T(8,128)(2,1)} %get-tuple-element.29.refs_0_), channel_id=1, source_target_pairs={{0,4},{1,5},{2,6},{3,7},{4,0},{5,1},{6,2},{7,3},{8,12},{9,13},{10,... | collective-permute-start | bytes 73736 | tf_op jit(solution)/shard_map/ppermute | solution.py:309
  10.6 0.3 collective-permute-start.4
  11.0 0.0 collective-permute-done.refs_1_
  11.0 0.5 collective-permute-start.2
  11.4 0.1 collective-permute-done.3.refs_5_
  11.6 2.7 %collective-permute-start.5 = (bf16[1,96,128]{2,1,0:T(8,128)(2,1)S(1)}, bf16[1,96,128]{2,1,0:T(8,128)(2,1)S(1)}, u32[]{:S(2)}, u32[]{:S(2)}) collective-permute-start(bf16[1,96,128]{2,1,0:T(8,128)(2,1)S(1)} %collective-permute-done.3.refs_5_), channel_id=1, source_target_pairs={{0,8},{1,9},{2,10},{3,11},{4,12},{5,13},{6,14},{7,15},{8,0},{9,1},... | collective-permute-start | bytes 73736 | tf_op jit(solution)/shard_map/ppermute | solution.py:309
  14.2 0.0 collective-permute-done.1.refs_2_
  14.2 1.5 %collective-permute-done.4.refs_6_ = bf16[1,96,128]{2,1,0:T(8,128)(2,1)S(1)} collective-permute-done((bf16[1,96,128]{2,1,0:T(8,128)(2,1)}, bf16[1,96,128]{2,1,0:T(8,128)(2,1)S(1)}, u32[]{:S(2)}, u32[]{:S(2)}) %collective-permute-start.4) | collective-permute-done | bytes 24608 | tf_op jit(solution)/shard_map/ppermute | solution.py:309
  15.7 0.0 collective-permute-done.2.refs_3_
  15.7 0.6 %collective-permute-done.5.refs_7_ = bf16[1,96,128]{2,1,0:T(8,128)(2,1)S(1)} collective-permute-done((bf16[1,96,128]{2,1,0:T(8,128)(2,1)S(1)}, bf16[1,96,128]{2,1,0:T(8,128)(2,1)S(1)}, u32[]{:S(2)}, u32[]{:S(2)}) %collective-permute-start.5) | collective-permute-done | bytes 24608 | tf_op jit(solution)/shard_map/ppermute | solution.py:309
  16.3 0.0 copy-start.5
  16.3 0.7 %copy-done.5 = bf16[1,96,128]{2,1,0:T(8,128)(2,1)S(1)} copy-done((bf16[1,96,128]{2,1,0:T(8,128)(2,1)S(1)}, bf16[1,96,128]{2,1,0:T(8,128)(2,1)}, u32[]{:S(2)}) %copy-start.5) | copy-done | bytes 24600
  17.0 0.0 copy-start.6
  17.0 0.7 %copy-done.6 = bf16[1,96,128]{2,1,0:T(8,128)(2,1)S(1)} copy-done((bf16[1,96,128]{2,1,0:T(8,128)(2,1)S(1)}, bf16[1,96,128]{2,1,0:T(8,128)(2,1)}, u32[]{:S(2)}) %copy-start.6) | copy-done | bytes 24600
  17.8 0.1 collective-permute-start.8
  17.9 0.5 collective-permute-start.9
  18.4 1.5 %collective-permute-start.6 = (bf16[4,96,128]{2,1,0:T(8,128)(2,1)S(1)}, bf16[4,96,128]{2,1,0:T(8,128)(2,1)S(1)}, u32[]{:S(2)}, u32[]{:S(2)}) collective-permute-start(bf16[4,96,128]{2,1,0:T(8,128)(2,1)S(1)} %get-tuple-element.31.rest_0_), channel_id=1, source_target_pairs={{0,2},{1,3},{2,0},{3,1},{4,6},{5,7},{6,4},{7,5},{8,10},{9,11},{10,... | collective-permute-start | bytes 294920 | tf_op jit(solution)/shard_map/ppermute | solution.py:309
  19.9 1.6 %collective-permute-start.7 = (bf16[4,96,128]{2,1,0:T(8,128)(2,1)S(1)}, bf16[4,96,128]{2,1,0:T(8,128)(2,1)S(1)}, u32[]{:S(2)}, u32[]{:S(2)}) collective-permute-start(bf16[4,96,128]{2,1,0:T(8,128)(2,1)S(1)} %get-tuple-element.32.rest_2_), channel_id=1, source_target_pairs={{0,4},{1,5},{2,6},{3,7},{4,0},{5,1},{6,2},{7,3},{8,12},{9,13},{10,... | collective-permute-start | bytes 294920 | tf_op jit(solution)/shard_map/ppermute | solution.py:309
  21.4 0.0 copy-start.1
  21.4 0.9 %copy-done.1 = bf16[1024,128]{1,0:T(8,128)(2,1)S(1)} copy-done((bf16[1024,128]{1,0:T(8,128)(2,1)S(1)}, bf16[1024,128]{1,0:T(8,128)(2,1)}, u32[]{:S(2)}) %copy-start.1) | copy-done | bytes 262168
  22.4 0.0 copy-start.3
  22.4 0.9 %copy-done.3 = bf16[768,32]{1,0:T(8,128)(2,1)S(1)} copy-done((bf16[768,32]{1,0:T(8,128)(2,1)S(1)}, bf16[768,32]{1,0:T(8,128)(2,1)}, u32[]{:S(2)}) %copy-start.3) | copy-done | bytes 49176
  23.3 0.0 copy-start
  23.3 0.0 copy-start.2
  23.3 4.5 %mix.1.y_ref = bf16[6,2048,256]{2,1,0:T(8,128)(2,1)S(1)} custom-call(bf16[768,32]{1,0:T(8,128)(2,1)S(1)} %copy-done.3, bf16[1024,128]{1,0:T(8,128)(2,1)S(1)} %copy-done.1), custom_call_target="tpu_custom_call" | custom-call | flops 201326592 | bytes 6291456 | tf_op jit(solution)/shard_map/mix/pallas_call | solution.py:383
  27.9 0.0 collective-permute-done.8.rest_1_
  27.9 0.0 collective-permute-done.9.rest_3_
  27.9 0.0 copy-done
  27.9 0.0 copy-done.2
  27.9 0.1 first_half.1
  28.0 0.0 collective-permute-done.6.rest_0_
  28.1 0.0 collective-permute-done.7.rest_2_
  28.1 0.0 copy-start.4
  28.1 0.1 collective-permute-start.10
  28.2 0.5 collective-permute-start.11
  28.7 0.8 %collective-permute-done.10.rest_1_ = bf16[4,96,128]{2,1,0:T(8,128)(2,1)S(1)} collective-permute-done((bf16[4,96,128]{2,1,0:T(8,128)(2,1)S(1)}, bf16[4,96,128]{2,1,0:T(8,128)(2,1)S(1)}, u32[]{:S(2)}, u32[]{:S(2)}) %collective-permute-start.10) | collective-permute-done | bytes 98336 | tf_op jit(solution)/shard_map/ppermute | solution.py:309
  29.4 0.2 collective-permute-done.11.rest_3_
  29.6 4.1 %pair.1 = (bf16[12,192,128]{2,1,0:T(8,128)(2,1)}, bf16[8,144,128]{2,1,0:T(8,128)(2,1)S(1)}, bf16[8,144,128]{2,1,0:T(8,128)(2,1)S(1)}, f32[2,1536,128]{2,1,0:T(8,128)S(1)}) custom-call(s32[1]{0:T(128)} %bitcast.row_ref, f32[424,128]{1,0:T(8,128)S(1)} %get-tuple-element.38.aux_ref, ...), custom_call_target="tpu_custom_call", output_to_operand_aliasing={{3}: (4, {})} | custom-call | flops 1207959552 | bytes 8650752 | tf_op jit(solution)/shard_map/pair/pallas_call | solution.py:415
  33.7 0.4 collective-permute-start.12
  34.1 1.2 %collective-permute-done.12.crossed_ref = bf16[8,144,128]{2,1,0:T(8,128)(2,1)S(1)} collective-permute-done((bf16[8,144,128]{2,1,0:T(8,128)(2,1)S(1)}, bf16[8,144,128]{2,1,0:T(8,128)(2,1)S(1)}, u32[]{:S(2)}, u32[]{:S(2)}) %collective-permute-start.12) | collective-permute-done | bytes 294944 | tf_op jit(solution)/shard_map/ppermute | solution.py:309
  35.4 0.6 %collective-permute-start.13 = (bf16[2,144,128]{2,1,0:T(8,128)(2,1)S(1)}, bf16[2,144,128]{2,1,0:T(8,128)(2,1)S(1)}, u32[]{:S(2)}, u32[]{:S(2)}) collective-permute-start(bf16[2,144,128]{2,1,0:T(8,128)(2,1)S(1)} %get-tuple-element.49), channel_id=1, source_target_pairs={{0,2},{1,3},{2,0},{3,1},{4,6},{5,7},{6,4},{7,5},{8,10},{9,11},{10,... | collective-permute-start | bytes 221192 | tf_op jit(solution)/shard_map/ppermute | solution.py:309
  36.0 0.4 collective-permute-start.14
  36.4 2.5 %collective-permute-start.15 = (bf16[2,144,128]{2,1,0:T(8,128)(2,1)S(1)}, bf16[2,144,128]{2,1,0:T(8,128)(2,1)S(1)}, u32[]{:S(2)}, u32[]{:S(2)}) collective-permute-start(bf16[2,144,128]{2,1,0:T(8,128)(2,1)S(1)} %get-tuple-element.51), channel_id=1, source_target_pairs={{0,6},{1,7},{2,4},{3,5},{4,2},{5,3},{6,0},{7,1},{8,14},{9,15},{10,... | collective-permute-start | bytes 221192 | tf_op jit(solution)/shard_map/ppermute | solution.py:309
  38.9 1.4 %collective-permute-start.16 = (bf16[2,144,128]{2,1,0:T(8,128)(2,1)S(1)}, bf16[2,144,128]{2,1,0:T(8,128)(2,1)S(1)}, u32[]{:S(2)}, u32[]{:S(2)}) collective-permute-start(bf16[2,144,128]{2,1,0:T(8,128)(2,1)S(1)} %get-tuple-element.52), channel_id=1, source_target_pairs={{0,8},{1,9},{2,10},{3,11},{4,12},{5,13},{6,14},{7,15},{8,0},{9,1},... | collective-permute-start | bytes 221192 | tf_op jit(solution)/shard_map/ppermute | solution.py:309
  40.4 1.5 %collective-permute-start.17 = (bf16[2,144,128]{2,1,0:T(8,128)(2,1)S(1)}, bf16[2,144,128]{2,1,0:T(8,128)(2,1)S(1)}, u32[]{:S(2)}, u32[]{:S(2)}) collective-permute-start(bf16[2,144,128]{2,1,0:T(8,128)(2,1)S(1)} %get-tuple-element.53), channel_id=1, source_target_pairs={{0,10},{1,11},{2,8},{3,9},{4,14},{5,15},{6,12},{7,13},{8,2},{9,3},... | collective-permute-start | bytes 221192 | tf_op jit(solution)/shard_map/ppermute | solution.py:309
  41.8 0.0 collective-permute-done.13.rest_1_
  41.8 2.7 %collective-permute-start.18 = (bf16[2,144,128]{2,1,0:T(8,128)(2,1)S(1)}, bf16[2,144,128]{2,1,0:T(8,128)(2,1)S(1)}, u32[]{:S(2)}, u32[]{:S(2)}) collective-permute-start(bf16[2,144,128]{2,1,0:T(8,128)(2,1)S(1)} %get-tuple-element.54), channel_id=1, source_target_pairs={{0,12},{1,13},{2,14},{3,15},{4,8},{5,9},{6,10},{7,11},{8,4},{9,5},... | collective-permute-start | bytes 221192 | tf_op jit(solution)/shard_map/ppermute | solution.py:309
  44.5 0.0 collective-permute-done.14.rest_2_
  44.5 2.1 %collective-permute-start.19 = (bf16[2,144,128]{2,1,0:T(8,128)(2,1)S(1)}, bf16[2,144,128]{2,1,0:T(8,128)(2,1)S(1)}, u32[]{:S(2)}, u32[]{:S(2)}) collective-permute-start(bf16[2,144,128]{2,1,0:T(8,128)(2,1)S(1)} %get-tuple-element.55), channel_id=1, source_target_pairs={{0,14},{1,15},{2,12},{3,13},{4,10},{5,11},{6,8},{7,9},{8,6},{9,7},... | collective-permute-start | bytes 221192 | tf_op jit(solution)/shard_map/ppermute | solution.py:309
  46.6 0.0 collective-permute-done.15.rest_3_
  46.6 3.5 %collective-permute-done.16.rest_4_ = bf16[2,144,128]{2,1,0:T(8,128)(2,1)S(1)} collective-permute-done((bf16[2,144,128]{2,1,0:T(8,128)(2,1)S(1)}, bf16[2,144,128]{2,1,0:T(8,128)(2,1)S(1)}, u32[]{:S(2)}, u32[]{:S(2)}) %collective-permute-start.16) | collective-permute-done | bytes 73760 | tf_op jit(solution)/shard_map/ppermute | solution.py:309
  50.0 2.1 %collective-permute-done.17.rest_5_ = bf16[2,144,128]{2,1,0:T(8,128)(2,1)S(1)} collective-permute-done((bf16[2,144,128]{2,1,0:T(8,128)(2,1)S(1)}, bf16[2,144,128]{2,1,0:T(8,128)(2,1)S(1)}, u32[]{:S(2)}, u32[]{:S(2)}) %collective-permute-start.17) | collective-permute-done | bytes 73760 | tf_op jit(solution)/shard_map/ppermute | solution.py:309
  52.2 0.0 collective-permute-done.18.rest_6_
  52.2 0.0 collective-permute-done.19.rest_7_
  52.2 0.0 copy-done.4
  52.2 3.6 %gate.1 = bf16[12,192,256]{2,1,0:T(8,128)(2,1)} custom-call(s32[1]{0:T(128)} %bitcast.row_ref, f32[424,128]{1,0:T(8,128)S(1)} %get-tuple-element.38.aux_ref, bf16[2,128,256]{2,1,0:T(8,128)(2,1)S(1)} %copy-done.4, bf16[2,144,128]{2,1,0:T(8,128)(2,1)S(1)} %get-tuple-element.48.rest_0_, bf16[2,144,128]{2,1,0:T(8,128)(2,1)S(1)} %collective-permute-done.13.rest_1_, ...), custom_call_target="tpu_custom_call" | custom-call | flops 301989888 | bytes 2949120 | tf_op jit(solution)/shard_map/gate/pallas_call | solution.py:450
  (2 shorter events, 0.1 us)
Async XLA Ops:
  3.4 7.5 %collective-permute-start = (bf16[1,96,128]{2,1,0:T(8,128)(2,1)}, bf16[1,96,128]{2,1,0:T(8,128)(2,1)S(1)}, u32[]{:S(2)}, u32[]{:S(2)}) collective-permute-start(bf16[1,96,128]{2,1,0:T(8,128)(2,1)} %get-tuple-element.29.refs_0_), channel_id=1, source_target_pairs={{0,8},{1,9},{2,10},{3,11},{4,12},{5,13},{6,14},{7,15},{8,0},{9,1},... | collective-permute-start | bytes 73736 | tf_op jit(solution)/shard_map/ppermute | solution.py:309
  7.5 4.0 %collective-permute-start.3 = (bf16[1,96,128]{2,1,0:T(8,128)(2,1)}, bf16[1,96,128]{2,1,0:T(8,128)(2,1)S(1)}, u32[]{:S(2)}, u32[]{:S(2)}) collective-permute-start(bf16[1,96,128]{2,1,0:T(8,128)(2,1)} %get-tuple-element.30.refs_4_), channel_id=1, source_target_pairs={{0,2},{1,3},{2,0},{3,1},{4,6},{5,7},{6,4},{7,5},{8,10},{9,11},{10,... | collective-permute-start | bytes 73736 | tf_op jit(solution)/shard_map/ppermute | solution.py:309
  9.0 5.2 %collective-permute-start.1 = (bf16[1,96,128]{2,1,0:T(8,128)(2,1)}, bf16[1,96,128]{2,1,0:T(8,128)(2,1)S(1)}, u32[]{:S(2)}, u32[]{:S(2)}) collective-permute-start(bf16[1,96,128]{2,1,0:T(8,128)(2,1)} %get-tuple-element.29.refs_0_), channel_id=1, source_target_pairs={{0,4},{1,5},{2,6},{3,7},{4,0},{5,1},{6,2},{7,3},{8,12},{9,13},{10,... | collective-permute-start | bytes 73736 | tf_op jit(solution)/shard_map/ppermute | solution.py:309
  10.6 5.1 %collective-permute-start.4 = (bf16[1,96,128]{2,1,0:T(8,128)(2,1)}, bf16[1,96,128]{2,1,0:T(8,128)(2,1)S(1)}, u32[]{:S(2)}, u32[]{:S(2)}) collective-permute-start(bf16[1,96,128]{2,1,0:T(8,128)(2,1)} %get-tuple-element.30.refs_4_), channel_id=1, source_target_pairs={{0,8},{1,9},{2,10},{3,11},{4,12},{5,13},{6,14},{7,15},{8,0},{9,1},... | collective-permute-start | bytes 73736 | tf_op jit(solution)/shard_map/ppermute | solution.py:309
  11.0 4.7 %collective-permute-start.2 = (bf16[1,96,128]{2,1,0:T(8,128)(2,1)S(1)}, bf16[1,96,128]{2,1,0:T(8,128)(2,1)S(1)}, u32[]{:S(2)}, u32[]{:S(2)}) collective-permute-start(bf16[1,96,128]{2,1,0:T(8,128)(2,1)S(1)} %collective-permute-done.refs_1_), channel_id=1, source_target_pairs={{0,4},{1,5},{2,6},{3,7},{4,0},{5,1},{6,2},{7,3},{8,12},{9,13},{10,... | collective-permute-start | bytes 73736 | tf_op jit(solution)/shard_map/ppermute | solution.py:309
  11.6 4.7 %collective-permute-start.5 = (bf16[1,96,128]{2,1,0:T(8,128)(2,1)S(1)}, bf16[1,96,128]{2,1,0:T(8,128)(2,1)S(1)}, u32[]{:S(2)}, u32[]{:S(2)}) collective-permute-start(bf16[1,96,128]{2,1,0:T(8,128)(2,1)S(1)} %collective-permute-done.3.refs_5_), channel_id=1, source_target_pairs={{0,8},{1,9},{2,10},{3,11},{4,12},{5,13},{6,14},{7,15},{8,0},{9,1},... | collective-permute-start | bytes 73736 | tf_op jit(solution)/shard_map/ppermute | solution.py:309
  16.3 0.7 %copy-start.5 = (bf16[1,96,128]{2,1,0:T(8,128)(2,1)S(1)}, bf16[1,96,128]{2,1,0:T(8,128)(2,1)}, u32[]{:S(2)}) copy-start(bf16[1,96,128]{2,1,0:T(8,128)(2,1)} %get-tuple-element.29.refs_0_) | copy-start | bytes 73732
  17.0 0.7 %copy-start.6 = (bf16[1,96,128]{2,1,0:T(8,128)(2,1)S(1)}, bf16[1,96,128]{2,1,0:T(8,128)(2,1)}, u32[]{:S(2)}) copy-start(bf16[1,96,128]{2,1,0:T(8,128)(2,1)} %get-tuple-element.30.refs_4_) | copy-start | bytes 73732
  17.8 10.1 %collective-permute-start.8 = (bf16[4,96,128]{2,1,0:T(8,128)(2,1)S(1)}, bf16[4,96,128]{2,1,0:T(8,128)(2,1)S(1)}, u32[]{:S(2)}, u32[]{:S(2)}) collective-permute-start(bf16[4,96,128]{2,1,0:T(8,128)(2,1)S(1)} %get-tuple-element.31.rest_0_), channel_id=1, source_target_pairs={{0,1},{1,0},{2,3},{3,2},{4,5},{5,4},{6,7},{7,6},{8,9},{9,8},{10,11... | collective-permute-start | bytes 294920 | tf_op jit(solution)/shard_map/ppermute | solution.py:309
  17.9 10.0 %collective-permute-start.9 = (bf16[4,96,128]{2,1,0:T(8,128)(2,1)S(1)}, bf16[4,96,128]{2,1,0:T(8,128)(2,1)S(1)}, u32[]{:S(2)}, u32[]{:S(2)}) collective-permute-start(bf16[4,96,128]{2,1,0:T(8,128)(2,1)S(1)} %get-tuple-element.32.rest_2_), channel_id=1, source_target_pairs={{0,1},{1,0},{2,3},{3,2},{4,5},{5,4},{6,7},{7,6},{8,9},{9,8},{10,11... | collective-permute-start | bytes 294920 | tf_op jit(solution)/shard_map/ppermute | solution.py:309
  18.4 9.7 %collective-permute-start.6 = (bf16[4,96,128]{2,1,0:T(8,128)(2,1)S(1)}, bf16[4,96,128]{2,1,0:T(8,128)(2,1)S(1)}, u32[]{:S(2)}, u32[]{:S(2)}) collective-permute-start(bf16[4,96,128]{2,1,0:T(8,128)(2,1)S(1)} %get-tuple-element.31.rest_0_), channel_id=1, source_target_pairs={{0,2},{1,3},{2,0},{3,1},{4,6},{5,7},{6,4},{7,5},{8,10},{9,11},{10,... | collective-permute-start | bytes 294920 | tf_op jit(solution)/shard_map/ppermute | solution.py:309
  19.9 8.2 %collective-permute-start.7 = (bf16[4,96,128]{2,1,0:T(8,128)(2,1)S(1)}, bf16[4,96,128]{2,1,0:T(8,128)(2,1)S(1)}, u32[]{:S(2)}, u32[]{:S(2)}) collective-permute-start(bf16[4,96,128]{2,1,0:T(8,128)(2,1)S(1)} %get-tuple-element.32.rest_2_), channel_id=1, source_target_pairs={{0,4},{1,5},{2,6},{3,7},{4,0},{5,1},{6,2},{7,3},{8,12},{9,13},{10,... | collective-permute-start | bytes 294920 | tf_op jit(solution)/shard_map/ppermute | solution.py:309
  21.4 0.9 %copy-start.1 = (bf16[1024,128]{1,0:T(8,128)(2,1)S(1)}, bf16[1024,128]{1,0:T(8,128)(2,1)}, u32[]{:S(2)}) copy-start(bf16[1024,128]{1,0:T(8,128)(2,1)} %weight_ref.1) | copy-start | bytes 786436
  22.4 0.9 %copy-start.3 = (bf16[768,32]{1,0:T(8,128)(2,1)S(1)}, bf16[768,32]{1,0:T(8,128)(2,1)}, u32[]{:S(2)}) copy-start(bf16[768,32]{1,0:T(8,128)(2,1)} %get-tuple-element.33.lhs_ref) | copy-start | bytes 147460
  23.3 4.6 %copy-start = (bf16[12,192,128]{2,1,0:T(8,128)(2,1)S(1)}, bf16[12,192,128]{2,1,0:T(8,128)(2,1)}, u32[]{:S(2)}) copy-start(bf16[12,192,128]{2,1,0:T(8,128)(2,1)} %state_ref.1) | copy-start | bytes 1769476
  23.3 4.6 %copy-start.2 = (f32[424,128]{1,0:T(8,128)S(1)}, f32[424,128]{1,0:T(8,128)}, u32[]{:S(2)}) copy-start(f32[424,128]{1,0:T(8,128)} %get-tuple-element.34.aux_ref) | copy-start | bytes 651268
  28.1 24.1 %copy-start.4 = (bf16[2,128,256]{2,1,0:T(8,128)(2,1)S(1)}, bf16[2,128,256]{2,1,0:T(8,128)(2,1)}, u32[]{:S(2)}) copy-start(bf16[2,128,256]{2,1,0:T(8,128)(2,1)} %get-tuple-element.45.gates_ref) | copy-start | bytes 393220
  28.1 1.4 %collective-permute-start.10 = (bf16[4,96,128]{2,1,0:T(8,128)(2,1)S(1)}, bf16[4,96,128]{2,1,0:T(8,128)(2,1)S(1)}, u32[]{:S(2)}, u32[]{:S(2)}) collective-permute-start(bf16[4,96,128]{2,1,0:T(8,128)(2,1)S(1)} %collective-permute-done.6.rest_0_), channel_id=1, source_target_pairs={{0,1},{1,0},{2,3},{3,2},{4,5},{5,4},{6,7},{7,6},{8,9},{9,8},{10,11... | collective-permute-start | bytes 294920 | tf_op jit(solution)/shard_map/ppermute | solution.py:309
  28.2 1.4 %collective-permute-start.11 = (bf16[4,96,128]{2,1,0:T(8,128)(2,1)S(1)}, bf16[4,96,128]{2,1,0:T(8,128)(2,1)S(1)}, u32[]{:S(2)}, u32[]{:S(2)}) collective-permute-start(bf16[4,96,128]{2,1,0:T(8,128)(2,1)S(1)} %collective-permute-done.7.rest_2_), channel_id=1, source_target_pairs={{0,1},{1,0},{2,3},{3,2},{4,5},{5,4},{6,7},{7,6},{8,9},{9,8},{10,11... | collective-permute-start | bytes 294920 | tf_op jit(solution)/shard_map/ppermute | solution.py:309
  33.7 1.6 %collective-permute-start.12 = (bf16[8,144,128]{2,1,0:T(8,128)(2,1)S(1)}, bf16[8,144,128]{2,1,0:T(8,128)(2,1)S(1)}, u32[]{:S(2)}, u32[]{:S(2)}) collective-permute-start(bf16[8,144,128]{2,1,0:T(8,128)(2,1)S(1)} %get-tuple-element.47), channel_id=1, source_target_pairs={{0,1},{1,0},{2,3},{3,2},{4,5},{5,4},{6,7},{7,6},{8,9},{9,8},{10,11... | collective-permute-start | bytes 884744 | tf_op jit(solution)/shard_map/ppermute | solution.py:309
  35.4 6.4 %collective-permute-start.13 = (bf16[2,144,128]{2,1,0:T(8,128)(2,1)S(1)}, bf16[2,144,128]{2,1,0:T(8,128)(2,1)S(1)}, u32[]{:S(2)}, u32[]{:S(2)}) collective-permute-start(bf16[2,144,128]{2,1,0:T(8,128)(2,1)S(1)} %get-tuple-element.49), channel_id=1, source_target_pairs={{0,2},{1,3},{2,0},{3,1},{4,6},{5,7},{6,4},{7,5},{8,10},{9,11},{10,... | collective-permute-start | bytes 221192 | tf_op jit(solution)/shard_map/ppermute | solution.py:309
  36.0 8.5 %collective-permute-start.14 = (bf16[2,144,128]{2,1,0:T(8,128)(2,1)S(1)}, bf16[2,144,128]{2,1,0:T(8,128)(2,1)S(1)}, u32[]{:S(2)}, u32[]{:S(2)}) collective-permute-start(bf16[2,144,128]{2,1,0:T(8,128)(2,1)S(1)} %get-tuple-element.50), channel_id=1, source_target_pairs={{0,4},{1,5},{2,6},{3,7},{4,0},{5,1},{6,2},{7,3},{8,12},{9,13},{10,... | collective-permute-start | bytes 221192 | tf_op jit(solution)/shard_map/ppermute | solution.py:309
  36.4 10.2 %collective-permute-start.15 = (bf16[2,144,128]{2,1,0:T(8,128)(2,1)S(1)}, bf16[2,144,128]{2,1,0:T(8,128)(2,1)S(1)}, u32[]{:S(2)}, u32[]{:S(2)}) collective-permute-start(bf16[2,144,128]{2,1,0:T(8,128)(2,1)S(1)} %get-tuple-element.51), channel_id=1, source_target_pairs={{0,6},{1,7},{2,4},{3,5},{4,2},{5,3},{6,0},{7,1},{8,14},{9,15},{10,... | collective-permute-start | bytes 221192 | tf_op jit(solution)/shard_map/ppermute | solution.py:309
  38.9 11.1 %collective-permute-start.16 = (bf16[2,144,128]{2,1,0:T(8,128)(2,1)S(1)}, bf16[2,144,128]{2,1,0:T(8,128)(2,1)S(1)}, u32[]{:S(2)}, u32[]{:S(2)}) collective-permute-start(bf16[2,144,128]{2,1,0:T(8,128)(2,1)S(1)} %get-tuple-element.52), channel_id=1, source_target_pairs={{0,8},{1,9},{2,10},{3,11},{4,12},{5,13},{6,14},{7,15},{8,0},{9,1},... | collective-permute-start | bytes 221192 | tf_op jit(solution)/shard_map/ppermute | solution.py:309
  40.4 11.8 %collective-permute-start.17 = (bf16[2,144,128]{2,1,0:T(8,128)(2,1)S(1)}, bf16[2,144,128]{2,1,0:T(8,128)(2,1)S(1)}, u32[]{:S(2)}, u32[]{:S(2)}) collective-permute-start(bf16[2,144,128]{2,1,0:T(8,128)(2,1)S(1)} %get-tuple-element.53), channel_id=1, source_target_pairs={{0,10},{1,11},{2,8},{3,9},{4,14},{5,15},{6,12},{7,13},{8,2},{9,3},... | collective-permute-start | bytes 221192 | tf_op jit(solution)/shard_map/ppermute | solution.py:309
  41.8 10.4 %collective-permute-start.18 = (bf16[2,144,128]{2,1,0:T(8,128)(2,1)S(1)}, bf16[2,144,128]{2,1,0:T(8,128)(2,1)S(1)}, u32[]{:S(2)}, u32[]{:S(2)}) collective-permute-start(bf16[2,144,128]{2,1,0:T(8,128)(2,1)S(1)} %get-tuple-element.54), channel_id=1, source_target_pairs={{0,12},{1,13},{2,14},{3,15},{4,8},{5,9},{6,10},{7,11},{8,4},{9,5},... | collective-permute-start | bytes 221192 | tf_op jit(solution)/shard_map/ppermute | solution.py:309
  44.5 7.7 %collective-permute-start.19 = (bf16[2,144,128]{2,1,0:T(8,128)(2,1)S(1)}, bf16[2,144,128]{2,1,0:T(8,128)(2,1)S(1)}, u32[]{:S(2)}, u32[]{:S(2)}) collective-permute-start(bf16[2,144,128]{2,1,0:T(8,128)(2,1)S(1)} %get-tuple-element.55), channel_id=1, source_target_pairs={{0,14},{1,15},{2,12},{3,13},{4,10},{5,11},{6,8},{7,9},{8,6},{9,7},... | collective-permute-start | bytes 221192 | tf_op jit(solution)/shard_map/ppermute | solution.py:309

commit v7 on v6

--- a/solution.py
+++ b/solution.py
@@ -38,9 +38,9 @@
 
 def prepare_kernel(
     row_ref, depth_hbm, hom_hbm, scale_hbm, shift_hbm, src_hbm, tgt_hbm, depth_row_hbm, chain_hbm, chain_row_hbm,
-    match_hbm, bias_hbm, gain_hbm, move_hbm, proj_hbm, gate_hbm,
-    left_ref, front_ref, back_ref, aux_ref, gates_ref,
-    depth_ref, hom_ref, scale_ref, shift_ref, both_ref, depth_row_ref, chain_ref, chain_row_ref, vec_ref, tmp_ref, sems,
+    match_hbm, bias_hbm, gain_hbm, move_hbm, proj_hbm, gate_hbm, weight_hbm,
+    mix_ref, item_ref, aux_ref, gates_ref,
+    depth_ref, hom_ref, scale_ref, shift_ref, both_ref, depth_row_ref, chain_ref, chain_row_ref, vec_ref, sems,
 ):
     tokens, seqs, feats = hom_ref.shape
     pair_width = aux_ref.shape[1]
@@ -65,6 +65,7 @@
         (move_hbm, vec_ref.at[3]),
         (proj_hbm, gates_ref.at[0]),
         (gate_hbm, gates_ref.at[1]),
+        (weight_hbm, mix_ref.at[tokens * seqs : tokens * seqs + width * width]),
     )
     finish(first_copies[:6])
     values = hom_ref[...].reshape(tokens * seqs, feats)
@@ -83,17 +84,12 @@
     row_pos = lax.broadcasted_iota(jnp.int32, (seqs, width), 0)
     lane = lax.broadcasted_iota(jnp.int32, (half, 2 * seqs), 1)
     seq_pos = jnp.where(lane < seqs, lane, lane - seqs)
-    part = half // 2
     for n in range(tokens):
         depth = depth_ref[first + n]
         rows = slice(n * seqs, (n + 1) * seqs)
-        left_ref[rows] = jnp.where(row_pos < depth, plain[rows], 0.0).astype(BF16)
+        mix_ref[rows, 0:width] = jnp.where(row_pos < depth, plain[rows], 0.0).astype(BF16)
         joint = jnp.concatenate([turned[0:half, rows], turned[half:width, rows]], axis=1)
-        joint = jnp.where(seq_pos < depth, joint, 0.0)
-        for side in (0, 1):
-            tmp_ref[side, n * part : (n + 1) * part] = joint[side * part : (side + 1) * part]
-    front_ref[0] = tmp_ref[0].astype(BF16)
-    back_ref[0] = tmp_ref[1].astype(BF16)
+        item_ref[0, n * half : (n + 1) * half] = jnp.where(seq_pos < depth, joint, 0.0).astype(BF16)
 
     finish(first_copies[6:])
     same = lax.broadcasted_iota(jnp.int32, (total, total), 0) == lax.broadcasted_iota(
@@ -116,23 +112,18 @@
         aux_ref[2 * total + 32 + n : 2 * total + 33 + n] = vec_ref[n]
 
 
-def mix_kernel(strided, lhs_ref, weight_ref, out_ref, wide_ref):
-    factor = lhs_ref.shape[1]
+def mix_kernel(factor, mix_ref, out_ref, wide_ref):
     half = factor // 2
     seqs = out_ref.shape[1] // factor
-    width = weight_ref.shape[1]
-    tokens = lhs_ref.shape[0] // seqs
-    wide_ref[...] = weight_ref[...].astype(F32)
+    width = mix_ref.shape[1]
+    lefts = mix_ref.shape[0] - factor * factor
+    tokens = lefts // seqs
+    wide_ref[...] = mix_ref[lefts : lefts + factor * factor].astype(F32)
 
     def one(q, carry):
-        if strided:
-            pair = [wide_ref[pl.ds(q + t * half, factor, stride=factor), :] for t in (0, 1)]
-        else:
-            pair = [
-                wide_ref[pl.ds(pl.multiple_of((q + t * half) * factor, factor), factor), :] for t in (0, 1)
-            ]
+        pair = [wide_ref[pl.ds(q + t * half, factor, stride=factor), :] for t in (0, 1)]
         rhs = jnp.concatenate(pair, axis=1).astype(BF16)
-        mixed = jnp.dot(lhs_ref[...], rhs, preferred_element_type=F32).astype(BF16)
+        mixed = jnp.dot(mix_ref[0:lefts, 0:factor], rhs, preferred_element_type=F32).astype(BF16)
         for n in range(tokens):
             rows = slice(n * seqs, (n + 1) * seqs)
             cols = slice(n % 2 * width, (n % 2 + 1) * width)
@@ -141,35 +132,29 @@
                 out_ref[n // 2, spot, cols] = mixed[rows, t * width : (t + 1) * width]
         return carry
 
-    lax.fori_loop(0, half, one, 0)
+    lax.fori_loop(0, half, one, 0, unroll=4)
 
 
 def join_kernel(*refs):
-    per = (len(refs) - 2) // 2
-    for side in (0, 1):
-        spot = 0
-        for piece in refs[side * per : (side + 1) * per]:
-            refs[2 * per + side][spot : spot + piece.shape[0]] = piece[...]
-            spot += piece.shape[0]
-
-
-def spread_items(row, wide_ref, sides):
-    for side, pieces in enumerate(sides):
-        for piece, ks in pieces:
-            size = piece.shape[1]
-            for m, k in enumerate(ks):
-                spot = pl.ds(pl.multiple_of((row ^ k) * size, size), size)
-                wide_ref[side, spot, :] = piece[m].astype(F32)
+    spot = 0
+    for piece in refs[:-1]:
+        refs[-1][spot : spot + piece.shape[0]] = piece[...]
+        spot += piece.shape[0]
+
+
+def spread_items(row, wide_ref, pieces, orders):
+    for piece, ks in zip(pieces, orders):
+        size = piece.shape[1]
+        for m, k in enumerate(ks):
+            spot = pl.ds(pl.multiple_of((row ^ k) * size, size), size)
+            wide_ref[spot, :] = piece[m].astype(F32)
 
 
 def first_half_kernel(orders, row_ref, state_ref, aux_ref, *rest):
     pieces, (wide_ref, state_out, aux_out) = rest[:-3], rest[-3:]
-    per = len(pieces) // 2
     state_out[...] = state_ref[...]
     aux_out[...] = aux_ref[...]
-    spread_items(
-        row_ref[0], wide_ref, [list(zip(pieces[s * per : (s + 1) * per], orders[s])) for s in (0, 1)]
-    )
+    spread_items(row_ref[0], wide_ref, pieces, orders)
 
 
 def pair_kernel(orders, row_ref, aux_ref, state_ref, y_ref, wide_in, *rest):
@@ -177,24 +162,20 @@
     step = pl.program_id(0)
     block, total, width = state_ref.shape
     lanes = pieces[0].shape[2]
-    per = len(pieces) // 2
     count = msg_ref.shape[0]
     tokens = total // count
-    groups = wide_ref.shape[1] // total
+    groups = wide_ref.shape[0] // total
 
     @pl.when(step == 0)
     def _():
-        spread_items(
-            row_ref[0], wide_ref, [list(zip(pieces[s * per : (s + 1) * per], orders[s])) for s in (0, 1)]
-        )
+        spread_items(row_ref[0], wide_ref, pieces, orders)
 
         def one(q, carry):
-            for side in (0, 1):
-                cols = pl.ds(pl.multiple_of((side * groups + q) * lanes, lanes), lanes)
-                lhs_ref[:, cols] = wide_ref[side, pl.ds(q, total, stride=groups), :].astype(BF16)
+            cols = pl.ds(pl.multiple_of(q * lanes, lanes), lanes)
+            lhs_ref[:, cols] = wide_ref[pl.ds(q, total, stride=groups), :].astype(BF16)
             return carry
 
-        lax.fori_loop(0, groups, one, 0, unroll=2)
+        lax.fori_loop(0, groups, one, 0, unroll=4)
 
     base = 2 * total
     match = aux_ref[base + 32 : base + 33]
@@ -309,18 +290,18 @@
         return lax.ppermute(array, "row", [(r, r ^ bit) for r in range(count)])
 
     aux_rows = 2 * total + 40
-    part = tokens * half // 2
-    left, front, back, aux, gates = pl.pallas_call(
+    part = tokens * half
+    mix_rows = tokens * seqs + factor * factor
+    to_mix, item, aux, gates = pl.pallas_call(
         prepare_kernel,
         out_shape=(
-            jax.ShapeDtypeStruct((tokens * seqs, factor), BF16),
-            jax.ShapeDtypeStruct((1, part, 2 * seqs), BF16),
+            jax.ShapeDtypeStruct((mix_rows, width), BF16),
             jax.ShapeDtypeStruct((1, part, 2 * seqs), BF16),
             jax.ShapeDtypeStruct((aux_rows, width), F32),
             jax.ShapeDtypeStruct((2, width, gated), BF16),
         ),
-        in_specs=[whole(SMEM)] + [whole(HBM)] * 15,
-        out_specs=(whole(VMEM),) * 5,
+        in_specs=[whole(SMEM)] + [whole(HBM)] * 16,
+        out_specs=(whole(VMEM),) * 4,
         scratch_shapes=[
             SMEM((total,), jnp.int32),
             VMEM((tokens, seqs, feats), BF16),
@@ -331,8 +312,7 @@
             SMEM((total,), jnp.int32),
             VMEM((1, total), jnp.int32),
             VMEM((4, 1, width), F32),
-            VMEM((2, part, 2 * seqs), F32),
-            pltpu.SemaphoreType.DMA((15,)),
+            pltpu.SemaphoreType.DMA((16,)),
         ],
         name="prepare",
     )(
@@ -352,38 +332,13 @@
         pairwise_norm_bias.reshape(1, width),
         input_projection_weight,
         input_gate_weight,
-    )
-
-    def joined(fronts, backs):
-        shape = (sum(x.shape[0] for x in fronts), part, 2 * seqs)
-        return pl.pallas_call(
-            join_kernel,
-            out_shape=(jax.ShapeDtypeStruct(shape, BF16),) * 2,
-            in_specs=[whole(VMEM)] * (2 * len(fronts)),
-            out_specs=(whole(VMEM),) * 2,
-            compiler_params=params(16),
-            name="join",
-        )(*fronts, *backs)
-
-    bits = [1 << n for n in range(1, count.bit_length() - 1)][::-1]
-    turns = [bits, bits[-1:] + bits[:-1]]
-    own = [front, back]
-    far = [swap(x, t[0]) for x, t in zip(own, turns)]
-    near = [swap(x, t[1]) for x, t in zip(own, turns)]
-    both = [swap(x, t[1]) for x, t in zip(far, turns)]
-    held = joined(*[[own[s], far[s], near[s], both[s]] for s in (0, 1)])
-    ranks = [[0, t[0], t[1], t[0] ^ t[1]] for t in turns]
-    for n in range(2, len(bits)):
-        came = [swap(x, t[n]) for x, t in zip(held, turns)]
-        new = [[k ^ t[n] for k in r] for r, t in zip(ranks, turns)]
-        if n + 1 < len(bits):
-            held = joined(*[[held[s], came[s]] for s in (0, 1)])
-            ranks = [r + m for r, m in zip(ranks, new)]
-    early = [swap(x, 1) for x in held]
+        output_weight,
+    )
+
     y = pl.pallas_call(
-        functools.partial(mix_kernel, True),
+        functools.partial(mix_kernel, factor),
         out_shape=jax.ShapeDtypeStruct((tokens // 2, inner, 2 * width), BF16),
-        in_specs=[whole(VMEM), whole(VMEM)],
+        in_specs=[whole(VMEM)],
         out_specs=whole(VMEM),
         scratch_shapes=[VMEM((factor * factor, width), F32)],
         compiler_params=params(16),
@@ -393,36 +348,55 @@
             transcendentals=0,
         ),
         name="mix",
-    )(left, output_weight)
+    )(to_mix)
+
+    def joined(*pieces):
+        return pl.pallas_call(
+            join_kernel,
+            out_shape=jax.ShapeDtypeStruct((sum(x.shape[0] for x in pieces), part, 2 * seqs), BF16),
+            in_specs=[whole(VMEM)] * len(pieces),
+            out_specs=whole(VMEM),
+            compiler_params=params(16),
+            name="join",
+        )(*pieces)
+
+    held, ranks = item, [0]
+    bit = count // 2
+    while bit > 1:
+        came, new = swap(held, bit), [k ^ bit for k in ranks]
+        if bit > 2:
+            held, ranks = joined(held, came), ranks + new
+        bit //= 2
+    early = swap(held, 1)
     wide, state, aux = pl.pallas_call(
-        functools.partial(first_half_kernel, [[r, [k ^ 1 for k in r]] for r in ranks]),
+        functools.partial(first_half_kernel, [ranks, [k ^ 1 for k in ranks]]),
         out_shape=(
-            jax.ShapeDtypeStruct((2, count * part, 2 * seqs), F32),
+            jax.ShapeDtypeStruct((count * part, 2 * seqs), F32),
             jax.ShapeDtypeStruct((tokens, total, width), BF16),
             jax.ShapeDtypeStruct((aux_rows, width), F32),
         ),
-        in_specs=[whole(SMEM)] + [whole(VMEM)] * 6,
+        in_specs=[whole(SMEM)] + [whole(VMEM)] * 4,
         out_specs=(whole(VMEM),) * 3,
         compiler_params=params(16),
         name="first_half",
-    )(row, pairwise_state, aux, held[0], early[0], held[1], early[1])
-    *came, y, wide, state, aux = lax.optimization_barrier((*came, y, wide, state, aux))
-    late = [swap(x, 1) for x in came]
+    )(row, pairwise_state, aux, held, early)
+    came, y, wide, state, aux = lax.optimization_barrier((came, y, wide, state, aux))
+    late = swap(came, 1)
 
     block = 2
     chips = count // 2
     tile = tokens * tokens
     pair_next, same, cross, _ = pl.pallas_call(
-        functools.partial(pair_kernel, [[r, [k ^ 1 for k in r]] for r in new]),
+        functools.partial(pair_kernel, [new, [k ^ 1 for k in new]]),
         grid=(tokens // block,),
         out_shape=(
             jax.ShapeDtypeStruct((tokens, total, width), BF16),
             jax.ShapeDtypeStruct((chips, tile, width), BF16),
             jax.ShapeDtypeStruct((chips, tile, width), BF16),
-            jax.ShapeDtypeStruct((2, count * part, 2 * seqs), F32),
+            jax.ShapeDtypeStruct((count * part, 2 * seqs), F32),
         ),
         in_specs=[whole(SMEM), whole(VMEM), pl.BlockSpec((block, total, width), lambda g: (g, 0, 0))]
-        + [whole(VMEM)] * 6,
+        + [whole(VMEM)] * 4,
         out_specs=(pl.BlockSpec((block, total, width), lambda g: (g, 0, 0)),) + (whole(VMEM),) * 3,
         scratch_shapes=[VMEM((total, inner), BF16), VMEM((count, tile, width), F32)],
         input_output_aliases={4: 3},
@@ -433,7 +407,7 @@
             transcendentals=0,
         ),
         name="pair",
-    )(row, aux, state, y, wide, came[0], late[0], came[1], late[1])
+    )(row, aux, state, y, wide, came, late)
 
     crossed = swap(cross, 1)
     tiles = pl.pallas_call(
@@ -444,7 +418,8 @@
         compiler_params=params(16),
         name="pack",
     )(row, same, crossed)
-    tiles = [tiles[0]] + [swap(tiles[k], 2 * k) for k in range(1, chips)]
+    moved = {k: swap(tiles[k], 2 * k) for k in range(chips - 1, 0, -1)}
+    tiles = [tiles[0]] + [moved[k] for k in range(1, chips)]
 
     block = 4
     out = pl.pallas_call(

time: 56.6 us -> 53.3 us (0.942)
  waiting for transfers between devices: 9.94 us -> 17.7 us
  starting transfers between devices: 26.5 us -> 18.8 us
  Pallas kernels: 15.3 us -> 13.7 us
  local copies, waits for them, and re-layouts: 3.36 us -> 1.83 us
    ppermute x20 -> x13, waiting for transfers between devices: 9.94 us -> 17.7 us  [swap(): return lax.ppermute(array, 'row', [(r, r ^ bit) for r in range(count)])]
    ppermute x20 -> x13, starting transfers between devices: 26.5 us -> 18.8 us  [swap(): return lax.ppermute(array, 'row', [(r, r ^ bit) for r in range(count)])]
    unnamed x14 -> x10, local copies, waits for them, and re-layouts: 3.36 us -> 1.83 us
    pallas_call x5 -> x6, Pallas kernels: 11.6 us -> 10.1 us  [the longest x1 4.44 us: body(): pl.pallas_call(functools.partial(pair_kernel, [new, [k ^ 1 for k in new]]...]
  transfers between devices with their start and end apart: 20 -> 13, of which waited for: 8 -> 6; matrix products, arithmetic and copies ran while one was open for 0% -> 0% of each run, Pallas kernels for 8% -> 5%
where the time goes in v7:
time: 53.3 us; the launch traced here: 52.8 us
  starting transfers between devices  18.8 us (35%)
  waiting for transfers between devices  17.7 us (33%)
  Pallas kernels  13.7 us (26%)
  local copies, waits for them, and re-layouts  1.83 us (3%)
  between operations  0.73 us (1%)
    ppermute x13, starting transfers between devices, swap(): return lax.ppermute(array, 'row', [(r, r ^ bit) for r in range(count)])  18.8 us
    ppermute x13, waiting for transfers between devices, swap(): return lax.ppermute(array, 'row', [(r, r ^ bit) for r in range(count)])  17.7 us
    pallas_call x1, Pallas kernels, body(): pl.pallas_call(functools.partial(pair_kernel, [new, [k ^ 1 for k in new]]...  4.44 us
    pallas_call x1, Pallas kernels, body(): pl.pallas_call(gate_kernel, grid=(tokens // block,), out_shape=jax.ShapeD...  3.61 us
    pallas_call x1, Pallas kernels, body(): pl.pallas_call(prepare_kernel, out_shape=(jax.ShapeDtypeStruct((mix_rows,...  2.77 us
    pallas_call x1, Pallas kernels, body(): pl.pallas_call(functools.partial(mix_kernel, factor), out_shape=jax.Shape...  2.74 us
    unnamed x10, local copies, waits for them, and re-layouts  1.83 us
  transfers between devices with their start and end apart: 13, of which 6 were waited for; matrix products, arithmetic and copies ran while one was open for 0% of the time, Pallas kernels for 5%

profile of v7, /device:TPU:0, one launch (start us, length us, event | category | flops | bytes accessed | tf_op | source)
XLA Modules:
  0.0 52.8 jit_solution(3490674284262928875)
XLA Ops:
  0.6 2.8 %prepare.1 = (bf16[1792,128]{1,0:T(8,128)(2,1)}, bf16[1,192,128]{2,1,0:T(8,128)(2,1)}, f32[424,128]{1,0:T(8,128)}, bf16[2,128,256]{2,1,0:T(8,128)(2,1)}) custom-call(s32[1]{0:T(128)} %bitcast.row_ref, s32[192]{0:T(256)} %depth_hbm.1, bf16[12,64,64]{2,1,0:T(8,128)(2,1)} %bitcast.14, f32[1,64]{1,0:T(1,128)} %bitcast.19, f32[1,64]{1,0:T(1,128)} %bitcast.20, ...), custom_call_target="tpu_custom_call" | custom-call | tf_op jit(solution)/shard_map/prepare/pallas_call | solution.py:295
  3.4 4.1 %collective-permute-start = (bf16[1,192,128]{2,1,0:T(8,128)(2,1)}, bf16[1,192,128]{2,1,0:T(8,128)(2,1)S(1)}, u32[]{:S(2)}, u32[]{:S(2)}) collective-permute-start(bf16[1,192,128]{2,1,0:T(8,128)(2,1)} %get-tuple-element.25.refs_0_), channel_id=1, source_target_pairs={{0,8},{1,9},{2,10},{3,11},{4,12},{5,13},{6,14},{7,15},{8,0},{9,1},... | collective-permute-start | bytes 147464 | tf_op jit(solution)/shard_map/ppermute | solution.py:290
  7.5 2.8 %collective-permute-done.refs_1_ = bf16[1,192,128]{2,1,0:T(8,128)(2,1)S(1)} collective-permute-done((bf16[1,192,128]{2,1,0:T(8,128)(2,1)}, bf16[1,192,128]{2,1,0:T(8,128)(2,1)S(1)}, u32[]{:S(2)}, u32[]{:S(2)}) %collective-permute-start) | collective-permute-done | bytes 49184 | tf_op jit(solution)/shard_map/ppermute | solution.py:290
  10.3 0.0 copy-start.4
  10.3 0.8 %copy-done.4 = bf16[1,192,128]{2,1,0:T(8,128)(2,1)S(1)} copy-done((bf16[1,192,128]{2,1,0:T(8,128)(2,1)S(1)}, bf16[1,192,128]{2,1,0:T(8,128)(2,1)}, u32[]{:S(2)}) %copy-start.4) | copy-done | bytes 49176
  11.1 1.4 %collective-permute-start.1 = (bf16[2,192,128]{2,1,0:T(8,128)(2,1)S(1)}, bf16[2,192,128]{2,1,0:T(8,128)(2,1)S(1)}, u32[]{:S(2)}, u32[]{:S(2)}) collective-permute-start(bf16[2,192,128]{2,1,0:T(8,128)(2,1)S(1)} %join.2.refs_0_), channel_id=1, source_target_pairs={{0,4},{1,5},{2,6},{3,7},{4,0},{5,1},{6,2},{7,3},{8,12},{9,13},{10,... | collective-permute-start | bytes 294920 | tf_op jit(solution)/shard_map/ppermute | solution.py:290
  12.6 3.2 %collective-permute-done.1.refs_1_ = bf16[2,192,128]{2,1,0:T(8,128)(2,1)S(1)} collective-permute-done((bf16[2,192,128]{2,1,0:T(8,128)(2,1)S(1)}, bf16[2,192,128]{2,1,0:T(8,128)(2,1)S(1)}, u32[]{:S(2)}, u32[]{:S(2)}) %collective-permute-start.1) | collective-permute-done | bytes 98336 | tf_op jit(solution)/shard_map/ppermute | solution.py:290
  15.8 0.1 collective-permute-start.3
  15.9 1.8 %collective-permute-start.2 = (bf16[4,192,128]{2,1,0:T(8,128)(2,1)S(1)}, bf16[4,192,128]{2,1,0:T(8,128)(2,1)S(1)}, u32[]{:S(2)}, u32[]{:S(2)}) collective-permute-start(bf16[4,192,128]{2,1,0:T(8,128)(2,1)S(1)} %join.3.rest_0_), channel_id=1, source_target_pairs={{0,2},{1,3},{2,0},{3,1},{4,6},{5,7},{6,4},{7,5},{8,10},{9,11},{10,... | collective-permute-start | bytes 589832 | tf_op jit(solution)/shard_map/ppermute | solution.py:290
  17.7 0.0 copy-start.1
  17.7 1.0 %copy-done.1 = bf16[1792,128]{1,0:T(8,128)(2,1)S(1)} copy-done((bf16[1792,128]{1,0:T(8,128)(2,1)S(1)}, bf16[1792,128]{1,0:T(8,128)(2,1)}, u32[]{:S(2)}) %copy-start.1) | copy-done | bytes 458776
  18.7 0.0 copy-start
  18.7 0.0 copy-start.2
  18.7 2.7 %mix.1.y_ref = bf16[6,2048,256]{2,1,0:T(8,128)(2,1)S(1)} custom-call(bf16[1792,128]{1,0:T(8,128)(2,1)S(1)} %copy-done.1), custom_call_target="tpu_custom_call" | custom-call | flops 201326592 | bytes 6291456 | tf_op jit(solution)/shard_map/mix/pallas_call | solution.py:338
  21.5 0.0 collective-permute-done.3.rest_1_
  21.5 0.0 copy-done
  21.5 0.0 copy-done.2
  21.5 0.1 first_half.1
  21.6 1.6 %collective-permute-done.2.rest_0_ = bf16[4,192,128]{2,1,0:T(8,128)(2,1)S(1)} collective-permute-done((bf16[4,192,128]{2,1,0:T(8,128)(2,1)S(1)}, bf16[4,192,128]{2,1,0:T(8,128)(2,1)S(1)}, u32[]{:S(2)}, u32[]{:S(2)}) %collective-permute-start.2) | collective-permute-done | bytes 196640 | tf_op jit(solution)/shard_map/ppermute | solution.py:290
  23.2 0.0 copy-start.3
  23.2 0.0 collective-permute-start.4
  23.2 1.4 %collective-permute-done.4.rest_1_ = bf16[4,192,128]{2,1,0:T(8,128)(2,1)S(1)} collective-permute-done((bf16[4,192,128]{2,1,0:T(8,128)(2,1)S(1)}, bf16[4,192,128]{2,1,0:T(8,128)(2,1)S(1)}, u32[]{:S(2)}, u32[]{:S(2)}) %collective-permute-start.4) | collective-permute-done | bytes 196640 | tf_op jit(solution)/shard_map/ppermute | solution.py:290
  24.7 4.4 %pair.1 = (bf16[12,192,128]{2,1,0:T(8,128)(2,1)}, bf16[8,144,128]{2,1,0:T(8,128)(2,1)S(1)}, bf16[8,144,128]{2,1,0:T(8,128)(2,1)S(1)}, f32[3072,128]{1,0:T(8,128)S(1)}) custom-call(s32[1]{0:T(128)} %bitcast.row_ref, f32[424,128]{1,0:T(8,128)S(1)} %get-tuple-element.31.aux_ref, ...), custom_call_target="tpu_custom_call", output_to_operand_aliasing={{3}: (4, {})} | custom-call | flops 1207959552 | bytes 8650752 | tf_op jit(solution)/shard_map/pair/pallas_call | solution.py:389
  29.1 0.1 collective-permute-start.5
  29.2 1.5 %collective-permute-done.5.crossed_ref = bf16[8,144,128]{2,1,0:T(8,128)(2,1)S(1)} collective-permute-done((bf16[8,144,128]{2,1,0:T(8,128)(2,1)S(1)}, bf16[8,144,128]{2,1,0:T(8,128)(2,1)S(1)}, u32[]{:S(2)}, u32[]{:S(2)}) %collective-permute-start.5) | collective-permute-done | bytes 294944 | tf_op jit(solution)/shard_map/ppermute | solution.py:290
  30.7 1.8 %collective-permute-start.6 = (bf16[2,144,128]{2,1,0:T(8,128)(2,1)S(1)}, bf16[2,144,128]{2,1,0:T(8,128)(2,1)S(1)}, u32[]{:S(2)}, u32[]{:S(2)}) collective-permute-start(bf16[2,144,128]{2,1,0:T(8,128)(2,1)S(1)} %get-tuple-element.41), channel_id=1, source_target_pairs={{0,2},{1,3},{2,0},{3,1},{4,6},{5,7},{6,4},{7,5},{8,10},{9,11},{10,... | collective-permute-start | bytes 221192 | tf_op jit(solution)/shard_map/ppermute | solution.py:290
  32.5 1.2 %collective-permute-start.7 = (bf16[2,144,128]{2,1,0:T(8,128)(2,1)S(1)}, bf16[2,144,128]{2,1,0:T(8,128)(2,1)S(1)}, u32[]{:S(2)}, u32[]{:S(2)}) collective-permute-start(bf16[2,144,128]{2,1,0:T(8,128)(2,1)S(1)} %get-tuple-element.42), channel_id=1, source_target_pairs={{0,4},{1,5},{2,6},{3,7},{4,0},{5,1},{6,2},{7,3},{8,12},{9,13},{10,... | collective-permute-start | bytes 221192 | tf_op jit(solution)/shard_map/ppermute | solution.py:290
  33.7 0.6 %collective-permute-start.8 = (bf16[2,144,128]{2,1,0:T(8,128)(2,1)S(1)}, bf16[2,144,128]{2,1,0:T(8,128)(2,1)S(1)}, u32[]{:S(2)}, u32[]{:S(2)}) collective-permute-start(bf16[2,144,128]{2,1,0:T(8,128)(2,1)S(1)} %get-tuple-element.43), channel_id=1, source_target_pairs={{0,6},{1,7},{2,4},{3,5},{4,2},{5,3},{6,0},{7,1},{8,14},{9,15},{10,... | collective-permute-start | bytes 221192 | tf_op jit(solution)/shard_map/ppermute | solution.py:290
  34.3 2.4 %collective-permute-start.9 = (bf16[2,144,128]{2,1,0:T(8,128)(2,1)S(1)}, bf16[2,144,128]{2,1,0:T(8,128)(2,1)S(1)}, u32[]{:S(2)}, u32[]{:S(2)}) collective-permute-start(bf16[2,144,128]{2,1,0:T(8,128)(2,1)S(1)} %get-tuple-element.44), channel_id=1, source_target_pairs={{0,8},{1,9},{2,10},{3,11},{4,12},{5,13},{6,14},{7,15},{8,0},{9,1},... | collective-permute-start | bytes 221192 | tf_op jit(solution)/shard_map/ppermute | solution.py:290
  36.7 1.7 %collective-permute-start.10 = (bf16[2,144,128]{2,1,0:T(8,128)(2,1)S(1)}, bf16[2,144,128]{2,1,0:T(8,128)(2,1)S(1)}, u32[]{:S(2)}, u32[]{:S(2)}) collective-permute-start(bf16[2,144,128]{2,1,0:T(8,128)(2,1)S(1)} %get-tuple-element.45), channel_id=1, source_target_pairs={{0,10},{1,11},{2,8},{3,9},{4,14},{5,15},{6,12},{7,13},{8,2},{9,3},... | collective-permute-start | bytes 221192 | tf_op jit(solution)/shard_map/ppermute | solution.py:290
  38.4 0.0 collective-permute-done.6.rest_1_
  38.4 3.6 %collective-permute-start.11 = (bf16[2,144,128]{2,1,0:T(8,128)(2,1)S(1)}, bf16[2,144,128]{2,1,0:T(8,128)(2,1)S(1)}, u32[]{:S(2)}, u32[]{:S(2)}) collective-permute-start(bf16[2,144,128]{2,1,0:T(8,128)(2,1)S(1)} %get-tuple-element.46), channel_id=1, source_target_pairs={{0,12},{1,13},{2,14},{3,15},{4,8},{5,9},{6,10},{7,11},{8,4},{9,5},... | collective-permute-start | bytes 221192 | tf_op jit(solution)/shard_map/ppermute | solution.py:290
  42.0 0.0 collective-permute-done.7.rest_2_
  42.0 0.0 collective-permute-start.12
  42.0 0.0 collective-permute-done.8.rest_3_
  42.0 0.0 collective-permute-done.9.rest_4_
  42.0 7.2 %collective-permute-done.10.rest_5_ = bf16[2,144,128]{2,1,0:T(8,128)(2,1)S(1)} collective-permute-done((bf16[2,144,128]{2,1,0:T(8,128)(2,1)S(1)}, bf16[2,144,128]{2,1,0:T(8,128)(2,1)S(1)}, u32[]{:S(2)}, u32[]{:S(2)}) %collective-permute-start.10) | collective-permute-done | bytes 73760 | tf_op jit(solution)/shard_map/ppermute | solution.py:290
  49.2 0.0 collective-permute-done.11.rest_6_
  49.2 0.0 collective-permute-done.12.rest_7_
  49.2 0.0 copy-done.3
  49.2 3.6 %gate.1 = bf16[12,192,256]{2,1,0:T(8,128)(2,1)} custom-call(s32[1]{0:T(128)} %bitcast.row_ref, f32[424,128]{1,0:T(8,128)S(1)} %get-tuple-element.31.aux_ref, bf16[2,128,256]{2,1,0:T(8,128)(2,1)S(1)} %copy-done.3, bf16[2,144,128]{2,1,0:T(8,128)(2,1)S(1)} %get-tuple-element.40.rest_0_, bf16[2,144,128]{2,1,0:T(8,128)(2,1)S(1)} %collective-permute-done.6.rest_1_, ...), custom_call_target="tpu_custom_call" | custom-call | flops 301989888 | bytes 2949120 | tf_op jit(solution)/shard_map/gate/pallas_call | solution.py:425
  (3 shorter events, 0.1 us)
Async XLA Ops:
  3.4 6.9 %collective-permute-start = (bf16[1,192,128]{2,1,0:T(8,128)(2,1)}, bf16[1,192,128]{2,1,0:T(8,128)(2,1)S(1)}, u32[]{:S(2)}, u32[]{:S(2)}) collective-permute-start(bf16[1,192,128]{2,1,0:T(8,128)(2,1)} %get-tuple-element.25.refs_0_), channel_id=1, source_target_pairs={{0,8},{1,9},{2,10},{3,11},{4,12},{5,13},{6,14},{7,15},{8,0},{9,1},... | collective-permute-start | bytes 147464 | tf_op jit(solution)/shard_map/ppermute | solution.py:290
  10.3 0.8 %copy-start.4 = (bf16[1,192,128]{2,1,0:T(8,128)(2,1)S(1)}, bf16[1,192,128]{2,1,0:T(8,128)(2,1)}, u32[]{:S(2)}) copy-start(bf16[1,192,128]{2,1,0:T(8,128)(2,1)} %get-tuple-element.25.refs_0_) | copy-start | bytes 147460
  11.1 4.7 %collective-permute-start.1 = (bf16[2,192,128]{2,1,0:T(8,128)(2,1)S(1)}, bf16[2,192,128]{2,1,0:T(8,128)(2,1)S(1)}, u32[]{:S(2)}, u32[]{:S(2)}) collective-permute-start(bf16[2,192,128]{2,1,0:T(8,128)(2,1)S(1)} %join.2.refs_0_), channel_id=1, source_target_pairs={{0,4},{1,5},{2,6},{3,7},{4,0},{5,1},{6,2},{7,3},{8,12},{9,13},{10,... | collective-permute-start | bytes 294920 | tf_op jit(solution)/shard_map/ppermute | solution.py:290
  15.8 5.6 %collective-permute-start.3 = (bf16[4,192,128]{2,1,0:T(8,128)(2,1)S(1)}, bf16[4,192,128]{2,1,0:T(8,128)(2,1)S(1)}, u32[]{:S(2)}, u32[]{:S(2)}) collective-permute-start(bf16[4,192,128]{2,1,0:T(8,128)(2,1)S(1)} %join.3.rest_0_), channel_id=1, source_target_pairs={{0,1},{1,0},{2,3},{3,2},{4,5},{5,4},{6,7},{7,6},{8,9},{9,8},{10,11... | collective-permute-start | bytes 589832 | tf_op jit(solution)/shard_map/ppermute | solution.py:290
  15.9 7.3 %collective-permute-start.2 = (bf16[4,192,128]{2,1,0:T(8,128)(2,1)S(1)}, bf16[4,192,128]{2,1,0:T(8,128)(2,1)S(1)}, u32[]{:S(2)}, u32[]{:S(2)}) collective-permute-start(bf16[4,192,128]{2,1,0:T(8,128)(2,1)S(1)} %join.3.rest_0_), channel_id=1, source_target_pairs={{0,2},{1,3},{2,0},{3,1},{4,6},{5,7},{6,4},{7,5},{8,10},{9,11},{10,... | collective-permute-start | bytes 589832 | tf_op jit(solution)/shard_map/ppermute | solution.py:290
  17.7 1.0 %copy-start.1 = (bf16[1792,128]{1,0:T(8,128)(2,1)S(1)}, bf16[1792,128]{1,0:T(8,128)(2,1)}, u32[]{:S(2)}) copy-start(bf16[1792,128]{1,0:T(8,128)(2,1)} %get-tuple-element.26.mix_ref) | copy-start | bytes 1376260
  18.7 2.8 %copy-start = (bf16[12,192,128]{2,1,0:T(8,128)(2,1)S(1)}, bf16[12,192,128]{2,1,0:T(8,128)(2,1)}, u32[]{:S(2)}) copy-start(bf16[12,192,128]{2,1,0:T(8,128)(2,1)} %state_ref.1) | copy-start | bytes 1769476
  18.7 2.8 %copy-start.2 = (f32[424,128]{1,0:T(8,128)S(1)}, f32[424,128]{1,0:T(8,128)}, u32[]{:S(2)}) copy-start(f32[424,128]{1,0:T(8,128)} %get-tuple-element.27.aux_ref) | copy-start | bytes 651268
  23.2 26.0 %copy-start.3 = (bf16[2,128,256]{2,1,0:T(8,128)(2,1)S(1)}, bf16[2,128,256]{2,1,0:T(8,128)(2,1)}, u32[]{:S(2)}) copy-start(bf16[2,128,256]{2,1,0:T(8,128)(2,1)} %get-tuple-element.37.gates_ref) | copy-start | bytes 393220
  23.2 1.4 %collective-permute-start.4 = (bf16[4,192,128]{2,1,0:T(8,128)(2,1)S(1)}, bf16[4,192,128]{2,1,0:T(8,128)(2,1)S(1)}, u32[]{:S(2)}, u32[]{:S(2)}) collective-permute-start(bf16[4,192,128]{2,1,0:T(8,128)(2,1)S(1)} %collective-permute-done.2.rest_0_), channel_id=1, source_target_pairs={{0,1},{1,0},{2,3},{3,2},{4,5},{5,4},{6,7},{7,6},{8,9},{9,8},{10,11... | collective-permute-start | bytes 589832 | tf_op jit(solution)/shard_map/ppermute | solution.py:290
  29.1 1.6 %collective-permute-start.5 = (bf16[8,144,128]{2,1,0:T(8,128)(2,1)S(1)}, bf16[8,144,128]{2,1,0:T(8,128)(2,1)S(1)}, u32[]{:S(2)}, u32[]{:S(2)}) collective-permute-start(bf16[8,144,128]{2,1,0:T(8,128)(2,1)S(1)} %get-tuple-element.39), channel_id=1, source_target_pairs={{0,1},{1,0},{2,3},{3,2},{4,5},{5,4},{6,7},{7,6},{8,9},{9,8},{10,11... | collective-permute-start | bytes 884744 | tf_op jit(solution)/shard_map/ppermute | solution.py:290
  30.7 7.6 %collective-permute-start.6 = (bf16[2,144,128]{2,1,0:T(8,128)(2,1)S(1)}, bf16[2,144,128]{2,1,0:T(8,128)(2,1)S(1)}, u32[]{:S(2)}, u32[]{:S(2)}) collective-permute-start(bf16[2,144,128]{2,1,0:T(8,128)(2,1)S(1)} %get-tuple-element.41), channel_id=1, source_target_pairs={{0,2},{1,3},{2,0},{3,1},{4,6},{5,7},{6,4},{7,5},{8,10},{9,11},{10,... | collective-permute-start | bytes 221192 | tf_op jit(solution)/shard_map/ppermute | solution.py:290
  32.5 9.5 %collective-permute-start.7 = (bf16[2,144,128]{2,1,0:T(8,128)(2,1)S(1)}, bf16[2,144,128]{2,1,0:T(8,128)(2,1)S(1)}, u32[]{:S(2)}, u32[]{:S(2)}) collective-permute-start(bf16[2,144,128]{2,1,0:T(8,128)(2,1)S(1)} %get-tuple-element.42), channel_id=1, source_target_pairs={{0,4},{1,5},{2,6},{3,7},{4,0},{5,1},{6,2},{7,3},{8,12},{9,13},{10,... | collective-permute-start | bytes 221192 | tf_op jit(solution)/shard_map/ppermute | solution.py:290
  33.7 8.3 %collective-permute-start.8 = (bf16[2,144,128]{2,1,0:T(8,128)(2,1)S(1)}, bf16[2,144,128]{2,1,0:T(8,128)(2,1)S(1)}, u32[]{:S(2)}, u32[]{:S(2)}) collective-permute-start(bf16[2,144,128]{2,1,0:T(8,128)(2,1)S(1)} %get-tuple-element.43), channel_id=1, source_target_pairs={{0,6},{1,7},{2,4},{3,5},{4,2},{5,3},{6,0},{7,1},{8,14},{9,15},{10,... | collective-permute-start | bytes 221192 | tf_op jit(solution)/shard_map/ppermute | solution.py:290
  34.3 7.7 %collective-permute-start.9 = (bf16[2,144,128]{2,1,0:T(8,128)(2,1)S(1)}, bf16[2,144,128]{2,1,0:T(8,128)(2,1)S(1)}, u32[]{:S(2)}, u32[]{:S(2)}) collective-permute-start(bf16[2,144,128]{2,1,0:T(8,128)(2,1)S(1)} %get-tuple-element.44), channel_id=1, source_target_pairs={{0,8},{1,9},{2,10},{3,11},{4,12},{5,13},{6,14},{7,15},{8,0},{9,1},... | collective-permute-start | bytes 221192 | tf_op jit(solution)/shard_map/ppermute | solution.py:290
  36.7 12.5 %collective-permute-start.10 = (bf16[2,144,128]{2,1,0:T(8,128)(2,1)S(1)}, bf16[2,144,128]{2,1,0:T(8,128)(2,1)S(1)}, u32[]{:S(2)}, u32[]{:S(2)}) collective-permute-start(bf16[2,144,128]{2,1,0:T(8,128)(2,1)S(1)} %get-tuple-element.45), channel_id=1, source_target_pairs={{0,10},{1,11},{2,8},{3,9},{4,14},{5,15},{6,12},{7,13},{8,2},{9,3},... | collective-permute-start | bytes 221192 | tf_op jit(solution)/shard_map/ppermute | solution.py:290
  38.4 10.8 %collective-permute-start.11 = (bf16[2,144,128]{2,1,0:T(8,128)(2,1)S(1)}, bf16[2,144,128]{2,1,0:T(8,128)(2,1)S(1)}, u32[]{:S(2)}, u32[]{:S(2)}) collective-permute-start(bf16[2,144,128]{2,1,0:T(8,128)(2,1)S(1)} %get-tuple-element.46), channel_id=1, source_target_pairs={{0,12},{1,13},{2,14},{3,15},{4,8},{5,9},{6,10},{7,11},{8,4},{9,5},... | collective-permute-start | bytes 221192 | tf_op jit(solution)/shard_map/ppermute | solution.py:290
  42.0 7.2 %collective-permute-start.12 = (bf16[2,144,128]{2,1,0:T(8,128)(2,1)S(1)}, bf16[2,144,128]{2,1,0:T(8,128)(2,1)S(1)}, u32[]{:S(2)}, u32[]{:S(2)}) collective-permute-start(bf16[2,144,128]{2,1,0:T(8,128)(2,1)S(1)} %get-tuple-element.47), channel_id=1, source_target_pairs={{0,14},{1,15},{2,12},{3,13},{4,10},{5,11},{6,8},{7,9},{8,6},{9,7},... | collective-permute-start | bytes 221192 | tf_op jit(solution)/shard_map/ppermute | solution.py:290

commit v8 on v7

--- a/solution.py
+++ b/solution.py
@@ -360,34 +360,30 @@
             name="join",
         )(*pieces)
 
-    held, ranks = item, [0]
-    bit = count // 2
-    while bit > 1:
-        came, new = swap(held, bit), [k ^ bit for k in ranks]
-        if bit > 2:
-            held, ranks = joined(held, came), ranks + new
-        bit //= 2
-    early = swap(held, 1)
+    chips = count // 2
+    turn = [2 * k for k in range(chips - 1, 0, -1)]
+    direct = [swap(item, k) for k in turn]
+    early = swap(item, 1)
+    *direct, y = lax.optimization_barrier((*direct, y))
+    held = joined(*direct)
+    late = swap(held, 1)
     wide, state, aux = pl.pallas_call(
-        functools.partial(first_half_kernel, [ranks, [k ^ 1 for k in ranks]]),
+        functools.partial(first_half_kernel, [turn, [0], [1]]),
         out_shape=(
             jax.ShapeDtypeStruct((count * part, 2 * seqs), F32),
             jax.ShapeDtypeStruct((tokens, total, width), BF16),
             jax.ShapeDtypeStruct((aux_rows, width), F32),
         ),
-        in_specs=[whole(SMEM)] + [whole(VMEM)] * 4,
+        in_specs=[whole(SMEM)] + [whole(VMEM)] * 5,
         out_specs=(whole(VMEM),) * 3,
         compiler_params=params(16),
         name="first_half",
-    )(row, pairwise_state, aux, held, early)
-    came, y, wide, state, aux = lax.optimization_barrier((came, y, wide, state, aux))
-    late = swap(came, 1)
+    )(row, pairwise_state, aux, held, item, early)
 
     block = 2
-    chips = count // 2
     tile = tokens * tokens
     pair_next, same, cross, _ = pl.pallas_call(
-        functools.partial(pair_kernel, [new, [k ^ 1 for k in new]]),
+        functools.partial(pair_kernel, [[k ^ 1 for k in turn]]),
         grid=(tokens // block,),
         out_shape=(
             jax.ShapeDtypeStruct((tokens, total, width), BF16),
@@ -396,7 +392,7 @@
             jax.ShapeDtypeStruct((count * part, 2 * seqs), F32),
         ),
         in_specs=[whole(SMEM), whole(VMEM), pl.BlockSpec((block, total, width), lambda g: (g, 0, 0))]
-        + [whole(VMEM)] * 4,
+        + [whole(VMEM)] * 3,
         out_specs=(pl.BlockSpec((block, total, width), lambda g: (g, 0, 0)),) + (whole(VMEM),) * 3,
         scratch_shapes=[VMEM((total, inner), BF16), VMEM((count, tile, width), F32)],
         input_output_aliases={4: 3},
@@ -407,7 +403,7 @@
             transcendentals=0,
         ),
         name="pair",
-    )(row, aux, state, y, wide, came, late)
+    )(row, aux, state, y, wide, late)
 
     crossed = swap(cross, 1)
     tiles = pl.pallas_call(

time: 53.3 us -> 51.3 us (0.962)
  waiting for transfers between devices: 17.7 us -> 11.1 us
  starting transfers between devices: 18.8 us -> 24.4 us
  local copies, waits for them, and re-layouts: 1.83 us -> 1.03 us
    ppermute x13 -> x17, waiting for transfers between devices: 17.7 us -> 11.1 us  [swap(): return lax.ppermute(array, 'row', [(r, r ^ bit) for r in range(count)])]
    ppermute x13 -> x17, starting transfers between devices: 18.8 us -> 24.4 us  [swap(): return lax.ppermute(array, 'row', [(r, r ^ bit) for r in range(count)])]
    unnamed x10, local copies, waits for them, and re-layouts: 1.83 us -> 1.03 us
  transfers between devices with their start and end apart: 13 -> 17, of which waited for: 6 -> 5; matrix products, arithmetic and copies ran while one was open for 0% -> 0% of each run, Pallas kernels for 5% -> 6%
where the time goes in v8:
time: 51.3 us; the launch traced here: 51.1 us
  starting transfers between devices  24.4 us (48%)
  Pallas kernels  13.8 us (27%)
  waiting for transfers between devices  11.1 us (22%)
  local copies, waits for them, and re-layouts  1.03 us (2%)
  between operations  0.76 us (1%)
    ppermute x17, starting transfers between devices, swap(): return lax.ppermute(array, 'row', [(r, r ^ bit) for r in range(count)])  24.4 us
    ppermute x17, waiting for transfers between devices, swap(): return lax.ppermute(array, 'row', [(r, r ^ bit) for r in range(count)])  11.1 us
    pallas_call x1, Pallas kernels, body(): pl.pallas_call(functools.partial(pair_kernel, [[k ^ 1 for k in turn]]), g...  4.46 us
    pallas_call x1, Pallas kernels, body(): pl.pallas_call(gate_kernel, grid=(tokens // block,), out_shape=jax.ShapeD...  3.61 us
    pallas_call x1, Pallas kernels, body(): pl.pallas_call(prepare_kernel, out_shape=(jax.ShapeDtypeStruct((mix_rows,...  2.77 us
    pallas_call x1, Pallas kernels, body(): pl.pallas_call(functools.partial(mix_kernel, factor), out_shape=jax.Shape...  2.74 us
    unnamed x10, local copies, waits for them, and re-layouts  1.03 us
  transfers between devices with their start and end apart: 17, of which 5 were waited for; matrix products, arithmetic and copies ran while one was open for 0% of the time, Pallas kernels for 6%

profile of v8, /device:TPU:0, one launch (start us, length us, event | category | flops | bytes accessed | tf_op | source)
XLA Modules:
  0.0 51.1 jit_solution(16361192929164563592)
XLA Ops:
  0.6 2.8 %prepare.1 = (bf16[1792,128]{1,0:T(8,128)(2,1)}, bf16[1,192,128]{2,1,0:T(8,128)(2,1)}, f32[424,128]{1,0:T(8,128)}, bf16[2,128,256]{2,1,0:T(8,128)(2,1)}) custom-call(s32[1]{0:T(128)} %bitcast.row_ref, s32[192]{0:T(256)} %depth_hbm.1, bf16[12,64,64]{2,1,0:T(8,128)(2,1)} %bitcast.14, f32[1,64]{1,0:T(1,128)} %bitcast.19, f32[1,64]{1,0:T(1,128)} %bitcast.20, ...), custom_call_target="tpu_custom_call" | custom-call | tf_op jit(solution)/shard_map/prepare/pallas_call | solution.py:295
  3.4 3.0 %collective-permute-start.6 = (bf16[1,192,128]{2,1,0:T(8,128)(2,1)}, bf16[1,192,128]{2,1,0:T(8,128)(2,1)S(1)}, u32[]{:S(2)}, u32[]{:S(2)}) collective-permute-start(bf16[1,192,128]{2,1,0:T(8,128)(2,1)} %get-tuple-element.29.rest_1_), channel_id=1, source_target_pairs={{0,2},{1,3},{2,0},{3,1},{4,6},{5,7},{6,4},{7,5},{8,10},{9,11},{10,... | collective-permute-start | bytes 147464 | tf_op jit(solution)/shard_map/ppermute | solution.py:290
  6.5 1.6 %collective-permute-start.5 = (bf16[1,192,128]{2,1,0:T(8,128)(2,1)}, bf16[1,192,128]{2,1,0:T(8,128)(2,1)S(1)}, u32[]{:S(2)}, u32[]{:S(2)}) collective-permute-start(bf16[1,192,128]{2,1,0:T(8,128)(2,1)} %get-tuple-element.29.rest_1_), channel_id=1, source_target_pairs={{0,4},{1,5},{2,6},{3,7},{4,0},{5,1},{6,2},{7,3},{8,12},{9,13},{10,... | collective-permute-start | bytes 147464 | tf_op jit(solution)/shard_map/ppermute | solution.py:290
  8.0 0.0 collective-permute-start.4
  8.0 3.0 %collective-permute-start.3 = (bf16[1,192,128]{2,1,0:T(8,128)(2,1)}, bf16[1,192,128]{2,1,0:T(8,128)(2,1)S(1)}, u32[]{:S(2)}, u32[]{:S(2)}) collective-permute-start(bf16[1,192,128]{2,1,0:T(8,128)(2,1)} %get-tuple-element.29.rest_1_), channel_id=1, source_target_pairs={{0,8},{1,9},{2,10},{3,11},{4,12},{5,13},{6,14},{7,15},{8,0},{9,1},... | collective-permute-start | bytes 147464 | tf_op jit(solution)/shard_map/ppermute | solution.py:290
  11.0 1.3 %collective-permute-start.2 = (bf16[1,192,128]{2,1,0:T(8,128)(2,1)}, bf16[1,192,128]{2,1,0:T(8,128)(2,1)S(1)}, u32[]{:S(2)}, u32[]{:S(2)}) collective-permute-start(bf16[1,192,128]{2,1,0:T(8,128)(2,1)} %get-tuple-element.29.rest_1_), channel_id=1, source_target_pairs={{0,10},{1,11},{2,8},{3,9},{4,14},{5,15},{6,12},{7,13},{8,2},{9,3},... | collective-permute-start | bytes 147464 | tf_op jit(solution)/shard_map/ppermute | solution.py:290
  12.3 0.0 collective-permute-done.6.refs_6_
  12.3 3.6 %collective-permute-start.1 = (bf16[1,192,128]{2,1,0:T(8,128)(2,1)}, bf16[1,192,128]{2,1,0:T(8,128)(2,1)S(1)}, u32[]{:S(2)}, u32[]{:S(2)}) collective-permute-start(bf16[1,192,128]{2,1,0:T(8,128)(2,1)} %get-tuple-element.29.rest_1_), channel_id=1, source_target_pairs={{0,12},{1,13},{2,14},{3,15},{4,8},{5,9},{6,10},{7,11},{8,4},{9,5},... | collective-permute-start | bytes 147464 | tf_op jit(solution)/shard_map/ppermute | solution.py:290
  15.9 0.0 collective-permute-done.5.refs_5_
  15.9 0.0 collective-permute-start
  15.9 0.0 copy-start.1
  15.9 1.0 %copy-done.1 = bf16[1792,128]{1,0:T(8,128)(2,1)S(1)} copy-done((bf16[1792,128]{1,0:T(8,128)(2,1)S(1)}, bf16[1792,128]{1,0:T(8,128)(2,1)}, u32[]{:S(2)}) %copy-start.1) | copy-done | bytes 458776
  16.9 0.0 copy-start.4
  16.9 0.0 copy-start
  16.9 0.0 copy-start.2
  16.9 2.7 %mix.1.y_ref = bf16[6,2048,256]{2,1,0:T(8,128)(2,1)S(1)} custom-call(bf16[1792,128]{1,0:T(8,128)(2,1)S(1)} %copy-done.1), custom_call_target="tpu_custom_call" | custom-call | flops 201326592 | bytes 6291456 | tf_op jit(solution)/shard_map/mix/pallas_call | solution.py:338
  19.7 0.0 collective-permute-done.4.refs_4_
  19.7 0.0 collective-permute-done.3.refs_3_
  19.7 0.0 collective-permute-done.2.refs_2_
  19.7 0.0 collective-permute-done.1.refs_1_
  19.7 3.2 %collective-permute-done.refs_0_ = bf16[1,192,128]{2,1,0:T(8,128)(2,1)S(1)} collective-permute-done((bf16[1,192,128]{2,1,0:T(8,128)(2,1)}, bf16[1,192,128]{2,1,0:T(8,128)(2,1)S(1)}, u32[]{:S(2)}, u32[]{:S(2)}) %collective-permute-start) | collective-permute-done | bytes 49184 | tf_op jit(solution)/shard_map/ppermute | solution.py:290
  22.9 0.1 collective-permute-start.8
  23.0 0.0 copy-done.4
  23.0 0.5 collective-permute-start.7
  23.5 1.2 %collective-permute-done.7.rest_2_ = bf16[1,192,128]{2,1,0:T(8,128)(2,1)S(1)} collective-permute-done((bf16[1,192,128]{2,1,0:T(8,128)(2,1)S(1)}, bf16[1,192,128]{2,1,0:T(8,128)(2,1)S(1)}, u32[]{:S(2)}, u32[]{:S(2)}) %collective-permute-start.7) | collective-permute-done | bytes 49184 | tf_op jit(solution)/shard_map/ppermute | solution.py:290
  24.7 0.0 copy-done
  24.7 0.0 copy-done.2
  24.7 0.1 first_half.1
  24.8 0.0 collective-permute-done.8.rest_0_
  24.9 0.0 copy-start.3
  24.9 4.5 %pair.1 = (bf16[12,192,128]{2,1,0:T(8,128)(2,1)}, bf16[8,144,128]{2,1,0:T(8,128)(2,1)S(1)}, bf16[8,144,128]{2,1,0:T(8,128)(2,1)S(1)}, f32[3072,128]{1,0:T(8,128)S(1)}) custom-call(s32[1]{0:T(128)} %bitcast.row_ref, f32[424,128]{1,0:T(8,128)S(1)} %get-tuple-element.38.aux_ref, ...), custom_call_target="tpu_custom_call", output_to_operand_aliasing={{3}: (4, {})} | custom-call | flops 1207959552 | bytes 8650752 | tf_op jit(solution)/shard_map/pair/pallas_call | solution.py:385
  29.3 0.1 collective-permute-start.9
  29.5 1.4 %collective-permute-done.9.crossed_ref = bf16[8,144,128]{2,1,0:T(8,128)(2,1)S(1)} collective-permute-done((bf16[8,144,128]{2,1,0:T(8,128)(2,1)S(1)}, bf16[8,144,128]{2,1,0:T(8,128)(2,1)S(1)}, u32[]{:S(2)}, u32[]{:S(2)}) %collective-permute-start.9) | collective-permute-done | bytes 294944 | tf_op jit(solution)/shard_map/ppermute | solution.py:290
  31.0 0.6 %collective-permute-start.10 = (bf16[2,144,128]{2,1,0:T(8,128)(2,1)S(1)}, bf16[2,144,128]{2,1,0:T(8,128)(2,1)S(1)}, u32[]{:S(2)}, u32[]{:S(2)}) collective-permute-start(bf16[2,144,128]{2,1,0:T(8,128)(2,1)S(1)} %get-tuple-element.47), channel_id=1, source_target_pairs={{0,2},{1,3},{2,0},{3,1},{4,6},{5,7},{6,4},{7,5},{8,10},{9,11},{10,... | collective-permute-start | bytes 221192 | tf_op jit(solution)/shard_map/ppermute | solution.py:290
  31.5 0.0 collective-permute-start.11
  31.5 3.0 %collective-permute-start.12 = (bf16[2,144,128]{2,1,0:T(8,128)(2,1)S(1)}, bf16[2,144,128]{2,1,0:T(8,128)(2,1)S(1)}, u32[]{:S(2)}, u32[]{:S(2)}) collective-permute-start(bf16[2,144,128]{2,1,0:T(8,128)(2,1)S(1)} %get-tuple-element.49), channel_id=1, source_target_pairs={{0,6},{1,7},{2,4},{3,5},{4,2},{5,3},{6,0},{7,1},{8,14},{9,15},{10,... | collective-permute-start | bytes 221192 | tf_op jit(solution)/shard_map/ppermute | solution.py:290
  34.5 0.2 collective-permute-start.13
  34.7 2.7 %collective-permute-start.14 = (bf16[2,144,128]{2,1,0:T(8,128)(2,1)S(1)}, bf16[2,144,128]{2,1,0:T(8,128)(2,1)S(1)}, u32[]{:S(2)}, u32[]{:S(2)}) collective-permute-start(bf16[2,144,128]{2,1,0:T(8,128)(2,1)S(1)} %get-tuple-element.51), channel_id=1, source_target_pairs={{0,10},{1,11},{2,8},{3,9},{4,14},{5,15},{6,12},{7,13},{8,2},{9,3},... | collective-permute-start | bytes 221192 | tf_op jit(solution)/shard_map/ppermute | solution.py:290
  37.4 0.0 collective-permute-done.10.rest_1_
  37.4 1.6 %collective-permute-start.15 = (bf16[2,144,128]{2,1,0:T(8,128)(2,1)S(1)}, bf16[2,144,128]{2,1,0:T(8,128)(2,1)S(1)}, u32[]{:S(2)}, u32[]{:S(2)}) collective-permute-start(bf16[2,144,128]{2,1,0:T(8,128)(2,1)S(1)} %get-tuple-element.52), channel_id=1, source_target_pairs={{0,12},{1,13},{2,14},{3,15},{4,8},{5,9},{6,10},{7,11},{8,4},{9,5},... | collective-permute-start | bytes 221192 | tf_op jit(solution)/shard_map/ppermute | solution.py:290
  39.0 0.0 collective-permute-done.11.rest_2_
  39.0 3.1 %collective-permute-start.16 = (bf16[2,144,128]{2,1,0:T(8,128)(2,1)S(1)}, bf16[2,144,128]{2,1,0:T(8,128)(2,1)S(1)}, u32[]{:S(2)}, u32[]{:S(2)}) collective-permute-start(bf16[2,144,128]{2,1,0:T(8,128)(2,1)S(1)} %get-tuple-element.53), channel_id=1, source_target_pairs={{0,14},{1,15},{2,12},{3,13},{4,10},{5,11},{6,8},{7,9},{8,6},{9,7},... | collective-permute-start | bytes 221192 | tf_op jit(solution)/shard_map/ppermute | solution.py:290
  42.2 0.0 collective-permute-done.12.rest_3_
  42.2 3.4 %collective-permute-done.13.rest_4_ = bf16[2,144,128]{2,1,0:T(8,128)(2,1)S(1)} collective-permute-done((bf16[2,144,128]{2,1,0:T(8,128)(2,1)S(1)}, bf16[2,144,128]{2,1,0:T(8,128)(2,1)S(1)}, u32[]{:S(2)}, u32[]{:S(2)}) %collective-permute-start.13) | collective-permute-done | bytes 73760 | tf_op jit(solution)/shard_map/ppermute | solution.py:290
  45.6 1.9 %collective-permute-done.14.rest_5_ = bf16[2,144,128]{2,1,0:T(8,128)(2,1)S(1)} collective-permute-done((bf16[2,144,128]{2,1,0:T(8,128)(2,1)S(1)}, bf16[2,144,128]{2,1,0:T(8,128)(2,1)S(1)}, u32[]{:S(2)}, u32[]{:S(2)}) %collective-permute-start.14) | collective-permute-done | bytes 73760 | tf_op jit(solution)/shard_map/ppermute | solution.py:290
  47.5 0.0 collective-permute-done.15.rest_6_
  47.5 0.0 collective-permute-done.16.rest_7_
  47.5 0.0 copy-done.3
  47.5 3.6 %gate.1 = bf16[12,192,256]{2,1,0:T(8,128)(2,1)} custom-call(s32[1]{0:T(128)} %bitcast.row_ref, f32[424,128]{1,0:T(8,128)S(1)} %get-tuple-element.38.aux_ref, bf16[2,128,256]{2,1,0:T(8,128)(2,1)S(1)} %copy-done.3, bf16[2,144,128]{2,1,0:T(8,128)(2,1)S(1)} %get-tuple-element.46.rest_0_, bf16[2,144,128]{2,1,0:T(8,128)(2,1)S(1)} %collective-permute-done.10.rest_1_, ...), custom_call_target="tpu_custom_call" | custom-call | flops 301989888 | bytes 2949120 | tf_op jit(solution)/shard_map/gate/pallas_call | solution.py:421
  (2 shorter events, 0.1 us)
Async XLA Ops:
  3.4 8.9 %collective-permute-start.6 = (bf16[1,192,128]{2,1,0:T(8,128)(2,1)}, bf16[1,192,128]{2,1,0:T(8,128)(2,1)S(1)}, u32[]{:S(2)}, u32[]{:S(2)}) collective-permute-start(bf16[1,192,128]{2,1,0:T(8,128)(2,1)} %get-tuple-element.29.rest_1_), channel_id=1, source_target_pairs={{0,2},{1,3},{2,0},{3,1},{4,6},{5,7},{6,4},{7,5},{8,10},{9,11},{10,... | collective-permute-start | bytes 147464 | tf_op jit(solution)/shard_map/ppermute | solution.py:290
  6.5 9.5 %collective-permute-start.5 = (bf16[1,192,128]{2,1,0:T(8,128)(2,1)}, bf16[1,192,128]{2,1,0:T(8,128)(2,1)S(1)}, u32[]{:S(2)}, u32[]{:S(2)}) collective-permute-start(bf16[1,192,128]{2,1,0:T(8,128)(2,1)} %get-tuple-element.29.rest_1_), channel_id=1, source_target_pairs={{0,4},{1,5},{2,6},{3,7},{4,0},{5,1},{6,2},{7,3},{8,12},{9,13},{10,... | collective-permute-start | bytes 147464 | tf_op jit(solution)/shard_map/ppermute | solution.py:290
  8.0 11.7 %collective-permute-start.4 = (bf16[1,192,128]{2,1,0:T(8,128)(2,1)}, bf16[1,192,128]{2,1,0:T(8,128)(2,1)S(1)}, u32[]{:S(2)}, u32[]{:S(2)}) collective-permute-start(bf16[1,192,128]{2,1,0:T(8,128)(2,1)} %get-tuple-element.29.rest_1_), channel_id=1, source_target_pairs={{0,6},{1,7},{2,4},{3,5},{4,2},{5,3},{6,0},{7,1},{8,14},{9,15},{10,... | collective-permute-start | bytes 147464 | tf_op jit(solution)/shard_map/ppermute | solution.py:290
  8.0 11.7 %collective-permute-start.3 = (bf16[1,192,128]{2,1,0:T(8,128)(2,1)}, bf16[1,192,128]{2,1,0:T(8,128)(2,1)S(1)}, u32[]{:S(2)}, u32[]{:S(2)}) collective-permute-start(bf16[1,192,128]{2,1,0:T(8,128)(2,1)} %get-tuple-element.29.rest_1_), channel_id=1, source_target_pairs={{0,8},{1,9},{2,10},{3,11},{4,12},{5,13},{6,14},{7,15},{8,0},{9,1},... | collective-permute-start | bytes 147464 | tf_op jit(solution)/shard_map/ppermute | solution.py:290
  11.0 8.7 %collective-permute-start.2 = (bf16[1,192,128]{2,1,0:T(8,128)(2,1)}, bf16[1,192,128]{2,1,0:T(8,128)(2,1)S(1)}, u32[]{:S(2)}, u32[]{:S(2)}) collective-permute-start(bf16[1,192,128]{2,1,0:T(8,128)(2,1)} %get-tuple-element.29.rest_1_), channel_id=1, source_target_pairs={{0,10},{1,11},{2,8},{3,9},{4,14},{5,15},{6,12},{7,13},{8,2},{9,3},... | collective-permute-start | bytes 147464 | tf_op jit(solution)/shard_map/ppermute | solution.py:290
  12.3 7.4 %collective-permute-start.1 = (bf16[1,192,128]{2,1,0:T(8,128)(2,1)}, bf16[1,192,128]{2,1,0:T(8,128)(2,1)S(1)}, u32[]{:S(2)}, u32[]{:S(2)}) collective-permute-start(bf16[1,192,128]{2,1,0:T(8,128)(2,1)} %get-tuple-element.29.rest_1_), channel_id=1, source_target_pairs={{0,12},{1,13},{2,14},{3,15},{4,8},{5,9},{6,10},{7,11},{8,4},{9,5},... | collective-permute-start | bytes 147464 | tf_op jit(solution)/shard_map/ppermute | solution.py:290
  15.9 7.0 %collective-permute-start = (bf16[1,192,128]{2,1,0:T(8,128)(2,1)}, bf16[1,192,128]{2,1,0:T(8,128)(2,1)S(1)}, u32[]{:S(2)}, u32[]{:S(2)}) collective-permute-start(bf16[1,192,128]{2,1,0:T(8,128)(2,1)} %get-tuple-element.29.rest_1_), channel_id=1, source_target_pairs={{0,14},{1,15},{2,12},{3,13},{4,10},{5,11},{6,8},{7,9},{8,6},{9,7},... | collective-permute-start | bytes 147464 | tf_op jit(solution)/shard_map/ppermute | solution.py:290
  15.9 1.0 %copy-start.1 = (bf16[1792,128]{1,0:T(8,128)(2,1)S(1)}, bf16[1792,128]{1,0:T(8,128)(2,1)}, u32[]{:S(2)}) copy-start(bf16[1792,128]{1,0:T(8,128)(2,1)} %get-tuple-element.30.mix_ref) | copy-start | bytes 1376260
  16.9 6.1 %copy-start.4 = (bf16[1,192,128]{2,1,0:T(8,128)(2,1)S(1)}, bf16[1,192,128]{2,1,0:T(8,128)(2,1)}, u32[]{:S(2)}) copy-start(bf16[1,192,128]{2,1,0:T(8,128)(2,1)} %get-tuple-element.29.rest_1_) | copy-start | bytes 147460
  16.9 7.8 %copy-start = (bf16[12,192,128]{2,1,0:T(8,128)(2,1)S(1)}, bf16[12,192,128]{2,1,0:T(8,128)(2,1)}, u32[]{:S(2)}) copy-start(bf16[12,192,128]{2,1,0:T(8,128)(2,1)} %state_ref.1) | copy-start | bytes 1769476
  16.9 7.8 %copy-start.2 = (f32[424,128]{1,0:T(8,128)S(1)}, f32[424,128]{1,0:T(8,128)}, u32[]{:S(2)}) copy-start(f32[424,128]{1,0:T(8,128)} %get-tuple-element.28.aux_ref) | copy-start | bytes 651268
  22.9 1.9 %collective-permute-start.8 = (bf16[7,192,128]{2,1,0:T(8,128)(2,1)S(1)}, bf16[7,192,128]{2,1,0:T(8,128)(2,1)S(1)}, u32[]{:S(2)}, u32[]{:S(2)}) collective-permute-start(bf16[7,192,128]{2,1,0:T(8,128)(2,1)S(1)} %join.1.rest_0_), channel_id=1, source_target_pairs={{0,1},{1,0},{2,3},{3,2},{4,5},{5,4},{6,7},{7,6},{8,9},{9,8},{10,11... | collective-permute-start | bytes 1032200 | tf_op jit(solution)/shard_map/ppermute | solution.py:290
  23.0 1.7 %collective-permute-start.7 = (bf16[1,192,128]{2,1,0:T(8,128)(2,1)S(1)}, bf16[1,192,128]{2,1,0:T(8,128)(2,1)S(1)}, u32[]{:S(2)}, u32[]{:S(2)}) collective-permute-start(bf16[1,192,128]{2,1,0:T(8,128)(2,1)S(1)} %copy-done.4), channel_id=1, source_target_pairs={{0,1},{1,0},{2,3},{3,2},{4,5},{5,4},{6,7},{7,6},{8,9},{9,8},{10,11... | collective-permute-start | bytes 147464 | tf_op jit(solution)/shard_map/ppermute | solution.py:290
  24.9 22.6 %copy-start.3 = (bf16[2,128,256]{2,1,0:T(8,128)(2,1)S(1)}, bf16[2,128,256]{2,1,0:T(8,128)(2,1)}, u32[]{:S(2)}) copy-start(bf16[2,128,256]{2,1,0:T(8,128)(2,1)} %get-tuple-element.43.gates_ref) | copy-start | bytes 393220
  29.3 1.6 %collective-permute-start.9 = (bf16[8,144,128]{2,1,0:T(8,128)(2,1)S(1)}, bf16[8,144,128]{2,1,0:T(8,128)(2,1)S(1)}, u32[]{:S(2)}, u32[]{:S(2)}) collective-permute-start(bf16[8,144,128]{2,1,0:T(8,128)(2,1)S(1)} %get-tuple-element.45), channel_id=1, source_target_pairs={{0,1},{1,0},{2,3},{3,2},{4,5},{5,4},{6,7},{7,6},{8,9},{9,8},{10,11... | collective-permute-start | bytes 884744 | tf_op jit(solution)/shard_map/ppermute | solution.py:290
  31.0 6.4 %collective-permute-start.10 = (bf16[2,144,128]{2,1,0:T(8,128)(2,1)S(1)}, bf16[2,144,128]{2,1,0:T(8,128)(2,1)S(1)}, u32[]{:S(2)}, u32[]{:S(2)}) collective-permute-start(bf16[2,144,128]{2,1,0:T(8,128)(2,1)S(1)} %get-tuple-element.47), channel_id=1, source_target_pairs={{0,2},{1,3},{2,0},{3,1},{4,6},{5,7},{6,4},{7,5},{8,10},{9,11},{10,... | collective-permute-start | bytes 221192 | tf_op jit(solution)/shard_map/ppermute | solution.py:290
  31.5 7.5 %collective-permute-start.11 = (bf16[2,144,128]{2,1,0:T(8,128)(2,1)S(1)}, bf16[2,144,128]{2,1,0:T(8,128)(2,1)S(1)}, u32[]{:S(2)}, u32[]{:S(2)}) collective-permute-start(bf16[2,144,128]{2,1,0:T(8,128)(2,1)S(1)} %get-tuple-element.48), channel_id=1, source_target_pairs={{0,4},{1,5},{2,6},{3,7},{4,0},{5,1},{6,2},{7,3},{8,12},{9,13},{10,... | collective-permute-start | bytes 221192 | tf_op jit(solution)/shard_map/ppermute | solution.py:290
  31.5 10.6 %collective-permute-start.12 = (bf16[2,144,128]{2,1,0:T(8,128)(2,1)S(1)}, bf16[2,144,128]{2,1,0:T(8,128)(2,1)S(1)}, u32[]{:S(2)}, u32[]{:S(2)}) collective-permute-start(bf16[2,144,128]{2,1,0:T(8,128)(2,1)S(1)} %get-tuple-element.49), channel_id=1, source_target_pairs={{0,6},{1,7},{2,4},{3,5},{4,2},{5,3},{6,0},{7,1},{8,14},{9,15},{10,... | collective-permute-start | bytes 221192 | tf_op jit(solution)/shard_map/ppermute | solution.py:290
  34.5 11.1 %collective-permute-start.13 = (bf16[2,144,128]{2,1,0:T(8,128)(2,1)S(1)}, bf16[2,144,128]{2,1,0:T(8,128)(2,1)S(1)}, u32[]{:S(2)}, u32[]{:S(2)}) collective-permute-start(bf16[2,144,128]{2,1,0:T(8,128)(2,1)S(1)} %get-tuple-element.50), channel_id=1, source_target_pairs={{0,8},{1,9},{2,10},{3,11},{4,12},{5,13},{6,14},{7,15},{8,0},{9,1},... | collective-permute-start | bytes 221192 | tf_op jit(solution)/shard_map/ppermute | solution.py:290
  34.7 12.8 %collective-permute-start.14 = (bf16[2,144,128]{2,1,0:T(8,128)(2,1)S(1)}, bf16[2,144,128]{2,1,0:T(8,128)(2,1)S(1)}, u32[]{:S(2)}, u32[]{:S(2)}) collective-permute-start(bf16[2,144,128]{2,1,0:T(8,128)(2,1)S(1)} %get-tuple-element.51), channel_id=1, source_target_pairs={{0,10},{1,11},{2,8},{3,9},{4,14},{5,15},{6,12},{7,13},{8,2},{9,3},... | collective-permute-start | bytes 221192 | tf_op jit(solution)/shard_map/ppermute | solution.py:290
  37.4 10.1 %collective-permute-start.15 = (bf16[2,144,128]{2,1,0:T(8,128)(2,1)S(1)}, bf16[2,144,128]{2,1,0:T(8,128)(2,1)S(1)}, u32[]{:S(2)}, u32[]{:S(2)}) collective-permute-start(bf16[2,144,128]{2,1,0:T(8,128)(2,1)S(1)} %get-tuple-element.52), channel_id=1, source_target_pairs={{0,12},{1,13},{2,14},{3,15},{4,8},{5,9},{6,10},{7,11},{8,4},{9,5},... | collective-permute-start | bytes 221192 | tf_op jit(solution)/shard_map/ppermute | solution.py:290
  39.0 8.4 %collective-permute-start.16 = (bf16[2,144,128]{2,1,0:T(8,128)(2,1)S(1)}, bf16[2,144,128]{2,1,0:T(8,128)(2,1)S(1)}, u32[]{:S(2)}, u32[]{:S(2)}) collective-permute-start(bf16[2,144,128]{2,1,0:T(8,128)(2,1)S(1)} %get-tuple-element.53), channel_id=1, source_target_pairs={{0,14},{1,15},{2,12},{3,13},{4,10},{5,11},{6,8},{7,9},{8,6},{9,7},... | collective-permute-start | bytes 221192 | tf_op jit(solution)/shard_map/ppermute | solution.py:290

commit v9 on v8

--- a/solution.py
+++ b/solution.py
@@ -158,11 +158,11 @@
 
 
 def pair_kernel(orders, row_ref, aux_ref, state_ref, y_ref, wide_in, *rest):
-    pieces, (next_ref, same_ref, cross_ref, wide_ref, lhs_ref, msg_ref) = rest[:-6], rest[-6:]
+    pieces, (next_ref, same_ref, cross_ref, wide_ref, lhs_ref) = rest[:-5], rest[-5:]
     step = pl.program_id(0)
     block, total, width = state_ref.shape
     lanes = pieces[0].shape[2]
-    count = msg_ref.shape[0]
+    count = 2 * same_ref.shape[0]
     tokens = total // count
     groups = wide_ref.shape[0] // total
 
@@ -180,30 +180,28 @@
     base = 2 * total
     match = aux_ref[base + 32 : base + 33]
     bias = aux_ref[base + 33 : base + 34]
-    prod = jnp.dot(lhs_ref[...], y_ref[step], preferred_element_type=F32)
     done = []
     for t in range(block):
+        if t % 2 == 0:
+            prod = jnp.dot(lhs_ref[...], y_ref[step * (block // 2) + t // 2], preferred_element_type=F32)
         own = step * block + t
         inv_own = aux_ref[pl.ds(base + own, 1)]
         label = aux_ref[pl.ds(base + 16 + own, 1)]
         extra = jnp.where(aux_ref[total:base] == label, match, 0.0) + bias
-        value = prod[:, t * width : (t + 1) * width] * jnp.maximum(aux_ref[0:total], inv_own) + extra
+        value = prod[:, t % 2 * width : (t % 2 + 1) * width] * jnp.maximum(aux_ref[0:total], inv_own) + extra
         value = state_ref[t].astype(F32) + value
         next_ref[t] = value.astype(BF16)
         done.append(value)
     size = block * tokens
-    for d in range(count):
-        rows = slice(d * tokens, (d + 1) * tokens)
-        msg_ref[d, pl.ds(pl.multiple_of(step * size, size), size), :] = jnp.concatenate(
-            [value[rows] for value in done], axis=0
-        )
-
+    spot = pl.ds(pl.multiple_of(step * size, size), size)
     for core in (0, 1):
 
-        @pl.when((step == pl.num_programs(0) - 1) & ((row_ref[0] & 1) == core))
+        @pl.when((row_ref[0] & 1) == core)
         def _():
             for d in range(count):
-                (same_ref if (d & 1) == core else cross_ref)[d // 2] = msg_ref[d].astype(BF16)
+                rows = slice(d * tokens, (d + 1) * tokens)
+                tile = jnp.concatenate([value[rows] for value in done], axis=0).astype(BF16)
+                (same_ref if (d & 1) == core else cross_ref)[d // 2, spot, :] = tile
 
 
 def pack_kernel(row_ref, same_ref, crossed_ref, *outs):
@@ -239,20 +237,28 @@
     means = jnp.concatenate(
         [jnp.concatenate([ones, none], axis=1), jnp.concatenate([none, ones], axis=1)], axis=0
     )
-    for t in range(0, block, 2):
-        pair = jnp.concatenate(
-            [wide_ref[pl.ds(step * block + t + u, total, stride=tokens), :] for u in (0, 1)], axis=1
-        )
-        centre = pair - jnp.dot(pair.astype(BF16), means, preferred_element_type=F32)
-        square = (centre * centre).astype(BF16)
-        spread = jnp.dot(square, means, preferred_element_type=F32)
-        scaled = centre * lax.rsqrt(spread + 1e-05)
-        for u in (0, 1):
-            normed = scaled[:, u * width : (u + 1) * width] * gain + shift
-            normed = normed.astype(BF16)
-            projected = jnp.dot(normed, gates_ref[0], preferred_element_type=F32)
-            gating = jnp.dot(normed, gates_ref[1], preferred_element_type=F32)
-            out_ref[t + u] = (projected * (0.5 + 0.5 * jnp.tanh(0.5 * gating))).astype(BF16)
+    weights = jnp.concatenate([gates_ref[0], gates_ref[1]], axis=1)
+    gated = gates_ref.shape[2]
+    pair = jnp.concatenate(
+        [
+            jnp.concatenate(
+                [wide_ref[pl.ds(step * block + t + u, total, stride=tokens), :] for u in (0, 1)], axis=1
+            )
+            for t in range(0, block, 2)
+        ],
+        axis=0,
+    )
+    centre = pair - jnp.dot(pair.astype(BF16), means, preferred_element_type=F32)
+    square = (centre * centre).astype(BF16)
+    spread = jnp.dot(square, means, preferred_element_type=F32)
+    scaled = centre * lax.rsqrt(spread + 1e-05)
+    scaled = jnp.concatenate([scaled[:, 0:width], scaled[:, width : 2 * width]], axis=0)
+    normed = (scaled * gain + shift).astype(BF16)
+    mixed = jnp.dot(normed, weights, preferred_element_type=F32)
+    result = (mixed[:, 0:gated] * (0.5 + 0.5 * jnp.tanh(0.5 * mixed[:, gated : 2 * gated]))).astype(BF16)
+    for t in range(block):
+        first = (t % 2 * (block // 2) + t // 2) * total
+        out_ref[t] = result[first : first + total]
 
 
 def fixed(*shape):
@@ -361,14 +367,16 @@
         )(*pieces)
 
     chips = count // 2
-    turn = [2 * k for k in range(chips - 1, 0, -1)]
+    turn = [4 * k for k in range(count // 4 - 1, 0, -1)]
     direct = [swap(item, k) for k in turn]
-    early = swap(item, 1)
-    *direct, y = lax.optimization_barrier((*direct, y))
-    held = joined(*direct)
-    late = swap(held, 1)
+    held = joined(item, *direct)
+    turn = [0] + turn
+    came = swap(held, 2)
+    early = swap(held, 1)
+    came, y = lax.optimization_barrier((came, y))
+    late = swap(came, 1)
     wide, state, aux = pl.pallas_call(
-        functools.partial(first_half_kernel, [turn, [0], [1]]),
+        functools.partial(first_half_kernel, [turn, [k ^ 1 for k in turn], [k ^ 2 for k in turn]]),
         out_shape=(
             jax.ShapeDtypeStruct((count * part, 2 * seqs), F32),
             jax.ShapeDtypeStruct((tokens, total, width), BF16),
@@ -378,12 +386,12 @@
         out_specs=(whole(VMEM),) * 3,
         compiler_params=params(16),
         name="first_half",
-    )(row, pairwise_state, aux, held, item, early)
-
-    block = 2
+    )(row, pairwise_state, aux, held, early, came)
+
+    block = 4
     tile = tokens * tokens
     pair_next, same, cross, _ = pl.pallas_call(
-        functools.partial(pair_kernel, [[k ^ 1 for k in turn]]),
+        functools.partial(pair_kernel, [[k ^ 3 for k in turn]]),
         grid=(tokens // block,),
         out_shape=(
             jax.ShapeDtypeStruct((tokens, total, width), BF16),
@@ -394,7 +402,7 @@
         in_specs=[whole(SMEM), whole(VMEM), pl.BlockSpec((block, total, width), lambda g: (g, 0, 0))]
         + [whole(VMEM)] * 3,
         out_specs=(pl.BlockSpec((block, total, width), lambda g: (g, 0, 0)),) + (whole(VMEM),) * 3,
-        scratch_shapes=[VMEM((total, inner), BF16), VMEM((count, tile, width), F32)],
+        scratch_shapes=[VMEM((total, inner), BF16)],
         input_output_aliases={4: 3},
         compiler_params=params(16),
         cost_estimate=pl.CostEstimate(

time: 51.3 us -> 48.7 us (0.949)
  starting transfers between devices: 24.4 us -> 18.9 us
  waiting for transfers between devices: 11.1 us -> 14.9 us
  Pallas kernels: 13.8 us -> 12 us
  local copies, waits for them, and re-layouts: 1.03 us -> 1.83 us
    ppermute x17 -> x14, starting transfers between devices: 24.4 us -> 18.9 us  [swap(): return lax.ppermute(array, 'row', [(r, r ^ bit) for r in range(count)])]
    ppermute x17 -> x14, waiting for transfers between devices: 11.1 us -> 14.9 us  [swap(): return lax.ppermute(array, 'row', [(r, r ^ bit) for r in range(count)])]
    pallas_call x2, Pallas kernels: 4.58 us -> 3.61 us  [the longest x1 3.47 us: body(): pl.pallas_call(functools.partial(pair_kernel, [[k ^ 3 for k in turn]]), g...]
    unnamed x10, local copies, waits for them, and re-layouts: 1.03 us -> 1.83 us
    pallas_call x1, Pallas kernels: 3.61 us -> 2.88 us  [body(): pl.pallas_call(gate_kernel, grid=(tokens // block,), out_shape=jax.ShapeD...]
  transfers between devices with their start and end apart: 17 -> 14, of which waited for: 5 -> 8; matrix products, arithmetic and copies ran while one was open for 0% -> 0% of each run, Pallas kernels for 6% -> 6%
where the time goes in v9:
time: 48.7 us; the launch traced here: 48.4 us
  starting transfers between devices  18.9 us (39%)
  waiting for transfers between devices  14.9 us (31%)
  Pallas kernels  12 us (25%)
  local copies, waits for them, and re-layouts  1.83 us (4%)
  between operations  0.7 us (1%)
    ppermute x14, starting transfers between devices, swap(): return lax.ppermute(array, 'row', [(r, r ^ bit) for r in range(count)])  18.9 us
    ppermute x14, waiting for transfers between devices, swap(): return lax.ppermute(array, 'row', [(r, r ^ bit) for r in range(count)])  14.9 us
    pallas_call x1, Pallas kernels, body(): pl.pallas_call(functools.partial(pair_kernel, [[k ^ 3 for k in turn]]), g...  3.47 us
    pallas_call x1, Pallas kernels, body(): pl.pallas_call(gate_kernel, grid=(tokens // block,), out_shape=jax.ShapeD...  2.88 us
    pallas_call x1, Pallas kernels, body(): pl.pallas_call(prepare_kernel, out_shape=(jax.ShapeDtypeStruct((mix_rows,...  2.77 us
    pallas_call x1, Pallas kernels, body(): pl.pallas_call(functools.partial(mix_kernel, factor), out_shape=jax.Shape...  2.74 us
    unnamed x10, local copies, waits for them, and re-layouts  1.83 us
  transfers between devices with their start and end apart: 14, of which 8 were waited for; matrix products, arithmetic and copies ran while one was open for 0% of the time, Pallas kernels for 6%

profile of v9, /device:TPU:0, one launch (start us, length us, event | category | flops | bytes accessed | tf_op | source)
XLA Modules:
  0.0 48.4 jit_solution(15040598398006662293)
XLA Ops:
  0.6 2.8 %prepare.1 = (bf16[1792,128]{1,0:T(8,128)(2,1)}, bf16[1,192,128]{2,1,0:T(8,128)(2,1)}, f32[424,128]{1,0:T(8,128)}, bf16[2,128,256]{2,1,0:T(8,128)(2,1)}) custom-call(s32[1]{0:T(128)} %bitcast.row_ref, s32[192]{0:T(256)} %depth_hbm.1, bf16[12,64,64]{2,1,0:T(8,128)(2,1)} %bitcast.14, f32[1,64]{1,0:T(1,128)} %bitcast.19, f32[1,64]{1,0:T(1,128)} %bitcast.20, ...), custom_call_target="tpu_custom_call" | custom-call | tf_op jit(solution)/shard_map/prepare/pallas_call | solution.py:301
  3.4 3.1 %collective-permute-start.2 = (bf16[1,192,128]{2,1,0:T(8,128)(2,1)}, bf16[1,192,128]{2,1,0:T(8,128)(2,1)S(1)}, u32[]{:S(2)}, u32[]{:S(2)}) collective-permute-start(bf16[1,192,128]{2,1,0:T(8,128)(2,1)} %get-tuple-element.23.refs_0_), channel_id=1, source_target_pairs={{0,4},{1,5},{2,6},{3,7},{4,0},{5,1},{6,2},{7,3},{8,12},{9,13},{10,... | collective-permute-start | bytes 147464 | tf_op jit(solution)/shard_map/ppermute | solution.py:296
  6.5 2.6 %collective-permute-start.1 = (bf16[1,192,128]{2,1,0:T(8,128)(2,1)}, bf16[1,192,128]{2,1,0:T(8,128)(2,1)S(1)}, u32[]{:S(2)}, u32[]{:S(2)}) collective-permute-start(bf16[1,192,128]{2,1,0:T(8,128)(2,1)} %get-tuple-element.23.refs_0_), channel_id=1, source_target_pairs={{0,8},{1,9},{2,10},{3,11},{4,12},{5,13},{6,14},{7,15},{8,0},{9,1},... | collective-permute-start | bytes 147464 | tf_op jit(solution)/shard_map/ppermute | solution.py:296
  9.1 0.0 collective-permute-start
  9.1 0.0 collective-permute-done.2.refs_3_
  9.1 3.5 %collective-permute-done.1.refs_2_ = bf16[1,192,128]{2,1,0:T(8,128)(2,1)S(1)} collective-permute-done((bf16[1,192,128]{2,1,0:T(8,128)(2,1)}, bf16[1,192,128]{2,1,0:T(8,128)(2,1)S(1)}, u32[]{:S(2)}, u32[]{:S(2)}) %collective-permute-start.1) | collective-permute-done | bytes 49184 | tf_op jit(solution)/shard_map/ppermute | solution.py:296
  12.6 2.6 %collective-permute-done.refs_1_ = bf16[1,192,128]{2,1,0:T(8,128)(2,1)S(1)} collective-permute-done((bf16[1,192,128]{2,1,0:T(8,128)(2,1)}, bf16[1,192,128]{2,1,0:T(8,128)(2,1)S(1)}, u32[]{:S(2)}, u32[]{:S(2)}) %collective-permute-start) | collective-permute-done | bytes 49184 | tf_op jit(solution)/shard_map/ppermute | solution.py:296
  15.2 0.0 copy-start.4
  15.2 0.8 %copy-done.4 = bf16[1,192,128]{2,1,0:T(8,128)(2,1)S(1)} copy-done((bf16[1,192,128]{2,1,0:T(8,128)(2,1)S(1)}, bf16[1,192,128]{2,1,0:T(8,128)(2,1)}, u32[]{:S(2)}) %copy-start.4) | copy-done | bytes 49176
  16.0 1.6 %collective-permute-start.4 = (bf16[4,192,128]{2,1,0:T(8,128)(2,1)S(1)}, bf16[4,192,128]{2,1,0:T(8,128)(2,1)S(1)}, u32[]{:S(2)}, u32[]{:S(2)}) collective-permute-start(bf16[4,192,128]{2,1,0:T(8,128)(2,1)S(1)} %join.1.rest_0_), channel_id=1, source_target_pairs={{0,2},{1,3},{2,0},{3,1},{4,6},{5,7},{6,4},{7,5},{8,10},{9,11},{10,... | collective-permute-start | bytes 589832 | tf_op jit(solution)/shard_map/ppermute | solution.py:296
  17.6 0.0 copy-start.1
  17.6 1.0 %copy-done.1 = bf16[1792,128]{1,0:T(8,128)(2,1)S(1)} copy-done((bf16[1792,128]{1,0:T(8,128)(2,1)S(1)}, bf16[1792,128]{1,0:T(8,128)(2,1)}, u32[]{:S(2)}) %copy-start.1) | copy-done | bytes 458776
  18.6 0.0 copy-start
  18.6 0.0 copy-start.2
  18.6 2.7 %mix.1.y_ref = bf16[6,2048,256]{2,1,0:T(8,128)(2,1)S(1)} custom-call(bf16[1792,128]{1,0:T(8,128)(2,1)S(1)} %copy-done.1), custom_call_target="tpu_custom_call" | custom-call | flops 201326592 | bytes 6291456 | tf_op jit(solution)/shard_map/mix/pallas_call | solution.py:344
  21.4 0.1 collective-permute-start.3
  21.4 0.3 collective-permute-done.4.rest_2_
  21.7 0.2 collective-permute-start.5
  21.9 0.9 %collective-permute-done.3.rest_1_ = bf16[4,192,128]{2,1,0:T(8,128)(2,1)S(1)} collective-permute-done((bf16[4,192,128]{2,1,0:T(8,128)(2,1)S(1)}, bf16[4,192,128]{2,1,0:T(8,128)(2,1)S(1)}, u32[]{:S(2)}, u32[]{:S(2)}) %collective-permute-start.3) | collective-permute-done | bytes 196640 | tf_op jit(solution)/shard_map/ppermute | solution.py:296
  22.9 0.0 copy-done
  22.9 0.0 copy-done.2
  22.9 0.1 first_half.1
  23.0 0.2 collective-permute-done.5.rest_0_
  23.2 0.0 copy-start.3
  23.2 3.5 %pair.1 = (bf16[12,192,128]{2,1,0:T(8,128)(2,1)}, bf16[8,144,128]{2,1,0:T(8,128)(2,1)S(1)}, bf16[8,144,128]{2,1,0:T(8,128)(2,1)S(1)}, f32[3072,128]{1,0:T(8,128)S(1)}) custom-call(s32[1]{0:T(128)} %bitcast.row_ref, f32[424,128]{1,0:T(8,128)S(1)} %get-tuple-element.26.aux_ref, ...), custom_call_target="tpu_custom_call", output_to_operand_aliasing={{3}: (4, {})} | custom-call | flops 1207959552 | bytes 8650752 | tf_op jit(solution)/shard_map/pair/pallas_call | solution.py:393
  26.7 0.2 collective-permute-start.6
  26.9 1.4 %collective-permute-done.6.crossed_ref = bf16[8,144,128]{2,1,0:T(8,128)(2,1)S(1)} collective-permute-done((bf16[8,144,128]{2,1,0:T(8,128)(2,1)S(1)}, bf16[8,144,128]{2,1,0:T(8,128)(2,1)S(1)}, u32[]{:S(2)}, u32[]{:S(2)}) %collective-permute-start.6) | collective-permute-done | bytes 294944 | tf_op jit(solution)/shard_map/ppermute | solution.py:296
  28.3 1.6 %collective-permute-start.7 = (bf16[2,144,128]{2,1,0:T(8,128)(2,1)S(1)}, bf16[2,144,128]{2,1,0:T(8,128)(2,1)S(1)}, u32[]{:S(2)}, u32[]{:S(2)}) collective-permute-start(bf16[2,144,128]{2,1,0:T(8,128)(2,1)S(1)} %get-tuple-element.35), channel_id=1, source_target_pairs={{0,2},{1,3},{2,0},{3,1},{4,6},{5,7},{6,4},{7,5},{8,10},{9,11},{10,... | collective-permute-start | bytes 221192 | tf_op jit(solution)/shard_map/ppermute | solution.py:296
  29.9 0.0 collective-permute-start.8
  29.9 2.0 %collective-permute-start.9 = (bf16[2,144,128]{2,1,0:T(8,128)(2,1)S(1)}, bf16[2,144,128]{2,1,0:T(8,128)(2,1)S(1)}, u32[]{:S(2)}, u32[]{:S(2)}) collective-permute-start(bf16[2,144,128]{2,1,0:T(8,128)(2,1)S(1)} %get-tuple-element.37), channel_id=1, source_target_pairs={{0,6},{1,7},{2,4},{3,5},{4,2},{5,3},{6,0},{7,1},{8,14},{9,15},{10,... | collective-permute-start | bytes 221192 | tf_op jit(solution)/shard_map/ppermute | solution.py:296
  31.9 0.4 collective-permute-start.10
  32.2 3.5 %collective-permute-start.11 = (bf16[2,144,128]{2,1,0:T(8,128)(2,1)S(1)}, bf16[2,144,128]{2,1,0:T(8,128)(2,1)S(1)}, u32[]{:S(2)}, u32[]{:S(2)}) collective-permute-start(bf16[2,144,128]{2,1,0:T(8,128)(2,1)S(1)} %get-tuple-element.39), channel_id=1, source_target_pairs={{0,10},{1,11},{2,8},{3,9},{4,14},{5,15},{6,12},{7,13},{8,2},{9,3},... | collective-permute-start | bytes 221192 | tf_op jit(solution)/shard_map/ppermute | solution.py:296
  35.7 0.0 collective-permute-done.7.rest_1_
  35.7 0.8 %collective-permute-start.12 = (bf16[2,144,128]{2,1,0:T(8,128)(2,1)S(1)}, bf16[2,144,128]{2,1,0:T(8,128)(2,1)S(1)}, u32[]{:S(2)}, u32[]{:S(2)}) collective-permute-start(bf16[2,144,128]{2,1,0:T(8,128)(2,1)S(1)} %get-tuple-element.40), channel_id=1, source_target_pairs={{0,12},{1,13},{2,14},{3,15},{4,8},{5,9},{6,10},{7,11},{8,4},{9,5},... | collective-permute-start | bytes 221192 | tf_op jit(solution)/shard_map/ppermute | solution.py:296
  36.5 0.0 collective-permute-done.8.rest_2_
  36.5 3.0 %collective-permute-start.13 = (bf16[2,144,128]{2,1,0:T(8,128)(2,1)S(1)}, bf16[2,144,128]{2,1,0:T(8,128)(2,1)S(1)}, u32[]{:S(2)}, u32[]{:S(2)}) collective-permute-start(bf16[2,144,128]{2,1,0:T(8,128)(2,1)S(1)} %get-tuple-element.41), channel_id=1, source_target_pairs={{0,14},{1,15},{2,12},{3,13},{4,10},{5,11},{6,8},{7,9},{8,6},{9,7},... | collective-permute-start | bytes 221192 | tf_op jit(solution)/shard_map/ppermute | solution.py:296
  39.5 0.0 collective-permute-done.9.rest_3_
  39.5 3.8 %collective-permute-done.10.rest_4_ = bf16[2,144,128]{2,1,0:T(8,128)(2,1)S(1)} collective-permute-done((bf16[2,144,128]{2,1,0:T(8,128)(2,1)S(1)}, bf16[2,144,128]{2,1,0:T(8,128)(2,1)S(1)}, u32[]{:S(2)}, u32[]{:S(2)}) %collective-permute-start.10) | collective-permute-done | bytes 73760 | tf_op jit(solution)/shard_map/ppermute | solution.py:296
  43.3 2.2 %collective-permute-done.11.rest_5_ = bf16[2,144,128]{2,1,0:T(8,128)(2,1)S(1)} collective-permute-done((bf16[2,144,128]{2,1,0:T(8,128)(2,1)S(1)}, bf16[2,144,128]{2,1,0:T(8,128)(2,1)S(1)}, u32[]{:S(2)}, u32[]{:S(2)}) %collective-permute-start.11) | collective-permute-done | bytes 73760 | tf_op jit(solution)/shard_map/ppermute | solution.py:296
  45.5 0.0 collective-permute-done.12.rest_6_
  45.5 0.0 collective-permute-done.13.rest_7_
  45.5 0.0 copy-done.3
  45.5 2.9 %gate.1 = bf16[12,192,256]{2,1,0:T(8,128)(2,1)} custom-call(s32[1]{0:T(128)} %bitcast.row_ref, f32[424,128]{1,0:T(8,128)S(1)} %get-tuple-element.26.aux_ref, bf16[2,128,256]{2,1,0:T(8,128)(2,1)S(1)} %copy-done.3, bf16[2,144,128]{2,1,0:T(8,128)(2,1)S(1)} %get-tuple-element.34.rest_0_, bf16[2,144,128]{2,1,0:T(8,128)(2,1)S(1)} %collective-permute-done.7.rest_1_, ...), custom_call_target="tpu_custom_call" | custom-call | flops 301989888 | bytes 2949120 | tf_op jit(solution)/shard_map/gate/pallas_call | solution.py:429
  (2 shorter events, 0.1 us)
Async XLA Ops:
  3.4 5.7 %collective-permute-start.2 = (bf16[1,192,128]{2,1,0:T(8,128)(2,1)}, bf16[1,192,128]{2,1,0:T(8,128)(2,1)S(1)}, u32[]{:S(2)}, u32[]{:S(2)}) collective-permute-start(bf16[1,192,128]{2,1,0:T(8,128)(2,1)} %get-tuple-element.23.refs_0_), channel_id=1, source_target_pairs={{0,4},{1,5},{2,6},{3,7},{4,0},{5,1},{6,2},{7,3},{8,12},{9,13},{10,... | collective-permute-start | bytes 147464 | tf_op jit(solution)/shard_map/ppermute | solution.py:296
  6.5 6.1 %collective-permute-start.1 = (bf16[1,192,128]{2,1,0:T(8,128)(2,1)}, bf16[1,192,128]{2,1,0:T(8,128)(2,1)S(1)}, u32[]{:S(2)}, u32[]{:S(2)}) collective-permute-start(bf16[1,192,128]{2,1,0:T(8,128)(2,1)} %get-tuple-element.23.refs_0_), channel_id=1, source_target_pairs={{0,8},{1,9},{2,10},{3,11},{4,12},{5,13},{6,14},{7,15},{8,0},{9,1},... | collective-permute-start | bytes 147464 | tf_op jit(solution)/shard_map/ppermute | solution.py:296
  9.1 6.1 %collective-permute-start = (bf16[1,192,128]{2,1,0:T(8,128)(2,1)}, bf16[1,192,128]{2,1,0:T(8,128)(2,1)S(1)}, u32[]{:S(2)}, u32[]{:S(2)}) collective-permute-start(bf16[1,192,128]{2,1,0:T(8,128)(2,1)} %get-tuple-element.23.refs_0_), channel_id=1, source_target_pairs={{0,12},{1,13},{2,14},{3,15},{4,8},{5,9},{6,10},{7,11},{8,4},{9,5},... | collective-permute-start | bytes 147464 | tf_op jit(solution)/shard_map/ppermute | solution.py:296
  15.2 0.8 %copy-start.4 = (bf16[1,192,128]{2,1,0:T(8,128)(2,1)S(1)}, bf16[1,192,128]{2,1,0:T(8,128)(2,1)}, u32[]{:S(2)}) copy-start(bf16[1,192,128]{2,1,0:T(8,128)(2,1)} %get-tuple-element.23.refs_0_) | copy-start | bytes 147460
  16.0 5.7 %collective-permute-start.4 = (bf16[4,192,128]{2,1,0:T(8,128)(2,1)S(1)}, bf16[4,192,128]{2,1,0:T(8,128)(2,1)S(1)}, u32[]{:S(2)}, u32[]{:S(2)}) collective-permute-start(bf16[4,192,128]{2,1,0:T(8,128)(2,1)S(1)} %join.1.rest_0_), channel_id=1, source_target_pairs={{0,2},{1,3},{2,0},{3,1},{4,6},{5,7},{6,4},{7,5},{8,10},{9,11},{10,... | collective-permute-start | bytes 589832 | tf_op jit(solution)/shard_map/ppermute | solution.py:296
  17.6 1.0 %copy-start.1 = (bf16[1792,128]{1,0:T(8,128)(2,1)S(1)}, bf16[1792,128]{1,0:T(8,128)(2,1)}, u32[]{:S(2)}) copy-start(bf16[1792,128]{1,0:T(8,128)(2,1)} %get-tuple-element.24.mix_ref) | copy-start | bytes 1376260
  18.6 4.3 %copy-start = (bf16[12,192,128]{2,1,0:T(8,128)(2,1)S(1)}, bf16[12,192,128]{2,1,0:T(8,128)(2,1)}, u32[]{:S(2)}) copy-start(bf16[12,192,128]{2,1,0:T(8,128)(2,1)} %state_ref.1) | copy-start | bytes 1769476
  18.6 4.3 %copy-start.2 = (f32[424,128]{1,0:T(8,128)S(1)}, f32[424,128]{1,0:T(8,128)}, u32[]{:S(2)}) copy-start(f32[424,128]{1,0:T(8,128)} %get-tuple-element.22.aux_ref) | copy-start | bytes 651268
  21.4 1.5 %collective-permute-start.3 = (bf16[4,192,128]{2,1,0:T(8,128)(2,1)S(1)}, bf16[4,192,128]{2,1,0:T(8,128)(2,1)S(1)}, u32[]{:S(2)}, u32[]{:S(2)}) collective-permute-start(bf16[4,192,128]{2,1,0:T(8,128)(2,1)S(1)} %join.1.rest_0_), channel_id=1, source_target_pairs={{0,1},{1,0},{2,3},{3,2},{4,5},{5,4},{6,7},{7,6},{8,9},{9,8},{10,11... | collective-permute-start | bytes 589832 | tf_op jit(solution)/shard_map/ppermute | solution.py:296
  21.7 1.4 %collective-permute-start.5 = (bf16[4,192,128]{2,1,0:T(8,128)(2,1)S(1)}, bf16[4,192,128]{2,1,0:T(8,128)(2,1)S(1)}, u32[]{:S(2)}, u32[]{:S(2)}) collective-permute-start(bf16[4,192,128]{2,1,0:T(8,128)(2,1)S(1)} %collective-permute-done.4.rest_2_), channel_id=1, source_target_pairs={{0,1},{1,0},{2,3},{3,2},{4,5},{5,4},{6,7},{7,6},{8,9},{9,8},{10,11... | collective-permute-start | bytes 589832 | tf_op jit(solution)/shard_map/ppermute | solution.py:296
  23.2 22.3 %copy-start.3 = (bf16[2,128,256]{2,1,0:T(8,128)(2,1)S(1)}, bf16[2,128,256]{2,1,0:T(8,128)(2,1)}, u32[]{:S(2)}) copy-start(bf16[2,128,256]{2,1,0:T(8,128)(2,1)} %get-tuple-element.31.gates_ref) | copy-start | bytes 393220
  26.7 1.6 %collective-permute-start.6 = (bf16[8,144,128]{2,1,0:T(8,128)(2,1)S(1)}, bf16[8,144,128]{2,1,0:T(8,128)(2,1)S(1)}, u32[]{:S(2)}, u32[]{:S(2)}) collective-permute-start(bf16[8,144,128]{2,1,0:T(8,128)(2,1)S(1)} %get-tuple-element.33), channel_id=1, source_target_pairs={{0,1},{1,0},{2,3},{3,2},{4,5},{5,4},{6,7},{7,6},{8,9},{9,8},{10,11... | collective-permute-start | bytes 884744 | tf_op jit(solution)/shard_map/ppermute | solution.py:296
  28.3 7.4 %collective-permute-start.7 = (bf16[2,144,128]{2,1,0:T(8,128)(2,1)S(1)}, bf16[2,144,128]{2,1,0:T(8,128)(2,1)S(1)}, u32[]{:S(2)}, u32[]{:S(2)}) collective-permute-start(bf16[2,144,128]{2,1,0:T(8,128)(2,1)S(1)} %get-tuple-element.35), channel_id=1, source_target_pairs={{0,2},{1,3},{2,0},{3,1},{4,6},{5,7},{6,4},{7,5},{8,10},{9,11},{10,... | collective-permute-start | bytes 221192 | tf_op jit(solution)/shard_map/ppermute | solution.py:296
  29.9 6.6 %collective-permute-start.8 = (bf16[2,144,128]{2,1,0:T(8,128)(2,1)S(1)}, bf16[2,144,128]{2,1,0:T(8,128)(2,1)S(1)}, u32[]{:S(2)}, u32[]{:S(2)}) collective-permute-start(bf16[2,144,128]{2,1,0:T(8,128)(2,1)S(1)} %get-tuple-element.36), channel_id=1, source_target_pairs={{0,4},{1,5},{2,6},{3,7},{4,0},{5,1},{6,2},{7,3},{8,12},{9,13},{10,... | collective-permute-start | bytes 221192 | tf_op jit(solution)/shard_map/ppermute | solution.py:296
  29.9 9.6 %collective-permute-start.9 = (bf16[2,144,128]{2,1,0:T(8,128)(2,1)S(1)}, bf16[2,144,128]{2,1,0:T(8,128)(2,1)S(1)}, u32[]{:S(2)}, u32[]{:S(2)}) collective-permute-start(bf16[2,144,128]{2,1,0:T(8,128)(2,1)S(1)} %get-tuple-element.37), channel_id=1, source_target_pairs={{0,6},{1,7},{2,4},{3,5},{4,2},{5,3},{6,0},{7,1},{8,14},{9,15},{10,... | collective-permute-start | bytes 221192 | tf_op jit(solution)/shard_map/ppermute | solution.py:296
  31.9 11.5 %collective-permute-start.10 = (bf16[2,144,128]{2,1,0:T(8,128)(2,1)S(1)}, bf16[2,144,128]{2,1,0:T(8,128)(2,1)S(1)}, u32[]{:S(2)}, u32[]{:S(2)}) collective-permute-start(bf16[2,144,128]{2,1,0:T(8,128)(2,1)S(1)} %get-tuple-element.38), channel_id=1, source_target_pairs={{0,8},{1,9},{2,10},{3,11},{4,12},{5,13},{6,14},{7,15},{8,0},{9,1},... | collective-permute-start | bytes 221192 | tf_op jit(solution)/shard_map/ppermute | solution.py:296
  32.2 13.3 %collective-permute-start.11 = (bf16[2,144,128]{2,1,0:T(8,128)(2,1)S(1)}, bf16[2,144,128]{2,1,0:T(8,128)(2,1)S(1)}, u32[]{:S(2)}, u32[]{:S(2)}) collective-permute-start(bf16[2,144,128]{2,1,0:T(8,128)(2,1)S(1)} %get-tuple-element.39), channel_id=1, source_target_pairs={{0,10},{1,11},{2,8},{3,9},{4,14},{5,15},{6,12},{7,13},{8,2},{9,3},... | collective-permute-start | bytes 221192 | tf_op jit(solution)/shard_map/ppermute | solution.py:296
  35.7 9.8 %collective-permute-start.12 = (bf16[2,144,128]{2,1,0:T(8,128)(2,1)S(1)}, bf16[2,144,128]{2,1,0:T(8,128)(2,1)S(1)}, u32[]{:S(2)}, u32[]{:S(2)}) collective-permute-start(bf16[2,144,128]{2,1,0:T(8,128)(2,1)S(1)} %get-tuple-element.40), channel_id=1, source_target_pairs={{0,12},{1,13},{2,14},{3,15},{4,8},{5,9},{6,10},{7,11},{8,4},{9,5},... | collective-permute-start | bytes 221192 | tf_op jit(solution)/shard_map/ppermute | solution.py:296
  36.5 9.0 %collective-permute-start.13 = (bf16[2,144,128]{2,1,0:T(8,128)(2,1)S(1)}, bf16[2,144,128]{2,1,0:T(8,128)(2,1)S(1)}, u32[]{:S(2)}, u32[]{:S(2)}) collective-permute-start(bf16[2,144,128]{2,1,0:T(8,128)(2,1)S(1)} %get-tuple-element.41), channel_id=1, source_target_pairs={{0,14},{1,15},{2,12},{3,13},{4,10},{5,11},{6,8},{7,9},{8,6},{9,7},... | collective-permute-start | bytes 221192 | tf_op jit(solution)/shard_map/ppermute | solution.py:296

commit v10 on v9

--- a/solution.py
+++ b/solution.py
@@ -38,8 +38,8 @@
 
 def prepare_kernel(
     row_ref, depth_hbm, hom_hbm, scale_hbm, shift_hbm, src_hbm, tgt_hbm, depth_row_hbm, chain_hbm, chain_row_hbm,
-    match_hbm, bias_hbm, gain_hbm, move_hbm, proj_hbm, gate_hbm, weight_hbm,
-    mix_ref, item_ref, aux_ref, gates_ref,
+    match_hbm, bias_hbm, gain_hbm, move_hbm, proj_hbm, gate_hbm,
+    left_ref, item_ref, aux_ref, gates_ref,
     depth_ref, hom_ref, scale_ref, shift_ref, both_ref, depth_row_ref, chain_ref, chain_row_ref, vec_ref, sems,
 ):
     tokens, seqs, feats = hom_ref.shape
@@ -65,7 +65,6 @@
         (move_hbm, vec_ref.at[3]),
         (proj_hbm, gates_ref.at[0]),
         (gate_hbm, gates_ref.at[1]),
-        (weight_hbm, mix_ref.at[tokens * seqs : tokens * seqs + width * width]),
     )
     finish(first_copies[:6])
     values = hom_ref[...].reshape(tokens * seqs, feats)
@@ -87,7 +86,7 @@
     for n in range(tokens):
         depth = depth_ref[first + n]
         rows = slice(n * seqs, (n + 1) * seqs)
-        mix_ref[rows, 0:width] = jnp.where(row_pos < depth, plain[rows], 0.0).astype(BF16)
+        left_ref[rows] = jnp.where(row_pos < depth, plain[rows], 0.0).astype(BF16)
         joint = jnp.concatenate([turned[0:half, rows], turned[half:width, rows]], axis=1)
         item_ref[0, n * half : (n + 1) * half] = jnp.where(seq_pos < depth, joint, 0.0).astype(BF16)
 
@@ -112,18 +111,18 @@
         aux_ref[2 * total + 32 + n : 2 * total + 33 + n] = vec_ref[n]
 
 
-def mix_kernel(factor, mix_ref, out_ref, wide_ref):
+def mix_kernel(left_ref, weight_ref, out_ref, wide_ref):
+    factor = left_ref.shape[1]
     half = factor // 2
     seqs = out_ref.shape[1] // factor
-    width = mix_ref.shape[1]
-    lefts = mix_ref.shape[0] - factor * factor
-    tokens = lefts // seqs
-    wide_ref[...] = mix_ref[lefts : lefts + factor * factor].astype(F32)
+    width = weight_ref.shape[1]
+    tokens = left_ref.shape[0] // seqs
+    wide_ref[...] = weight_ref[...].astype(F32)
 
     def one(q, carry):
         pair = [wide_ref[pl.ds(q + t * half, factor, stride=factor), :] for t in (0, 1)]
         rhs = jnp.concatenate(pair, axis=1).astype(BF16)
-        mixed = jnp.dot(mix_ref[0:lefts, 0:factor], rhs, preferred_element_type=F32).astype(BF16)
+        mixed = jnp.dot(left_ref[...], rhs, preferred_element_type=F32).astype(BF16)
         for n in range(tokens):
             rows = slice(n * seqs, (n + 1) * seqs)
             cols = slice(n % 2 * width, (n % 2 + 1) * width)
@@ -297,16 +296,15 @@
 
     aux_rows = 2 * total + 40
     part = tokens * half
-    mix_rows = tokens * seqs + factor * factor
-    to_mix, item, aux, gates = pl.pallas_call(
+    left, item, aux, gates = pl.pallas_call(
         prepare_kernel,
         out_shape=(
-            jax.ShapeDtypeStruct((mix_rows, width), BF16),
+            jax.ShapeDtypeStruct((tokens * seqs, factor), BF16),
             jax.ShapeDtypeStruct((1, part, 2 * seqs), BF16),
             jax.ShapeDtypeStruct((aux_rows, width), F32),
             jax.ShapeDtypeStruct((2, width, gated), BF16),
         ),
-        in_specs=[whole(SMEM)] + [whole(HBM)] * 16,
+        in_specs=[whole(SMEM)] + [whole(HBM)] * 15,
         out_specs=(whole(VMEM),) * 4,
         scratch_shapes=[
             SMEM((total,), jnp.int32),
@@ -318,7 +316,7 @@
             SMEM((total,), jnp.int32),
             VMEM((1, total), jnp.int32),
             VMEM((4, 1, width), F32),
-            pltpu.SemaphoreType.DMA((16,)),
+            pltpu.SemaphoreType.DMA((15,)),
         ],
         name="prepare",
     )(
@@ -338,13 +336,12 @@
         pairwise_norm_bias.reshape(1, width),
         input_projection_weight,
         input_gate_weight,
-        output_weight,
     )
 
     y = pl.pallas_call(
-        functools.partial(mix_kernel, factor),
+        mix_kernel,
         out_shape=jax.ShapeDtypeStruct((tokens // 2, inner, 2 * width), BF16),
-        in_specs=[whole(VMEM)],
+        in_specs=[whole(VMEM)] * 2,
         out_specs=whole(VMEM),
         scratch_shapes=[VMEM((factor * factor, width), F32)],
         compiler_params=params(16),
@@ -354,7 +351,7 @@
             transcendentals=0,
         ),
         name="mix",
-    )(to_mix)
+    )(left, output_weight)
 
     def joined(*pieces):
         return pl.pallas_call(
@@ -369,29 +366,34 @@
     chips = count // 2
     turn = [4 * k for k in range(count // 4 - 1, 0, -1)]
     direct = [swap(item, k) for k in turn]
-    held = joined(item, *direct)
-    turn = [0] + turn
+    own_came = swap(item, 2)
+    own_early = swap(item, 1)
+    *direct, own_came, own_early = lax.optimization_barrier((*direct, own_came, own_early))
+    held = joined(*direct)
     came = swap(held, 2)
     early = swap(held, 1)
     came, y = lax.optimization_barrier((came, y))
+    own_late = swap(own_came, 1)
     late = swap(came, 1)
     wide, state, aux = pl.pallas_call(
-        functools.partial(first_half_kernel, [turn, [k ^ 1 for k in turn], [k ^ 2 for k in turn]]),
+        functools.partial(
+            first_half_kernel, [[0], [1], [2], turn, [k ^ 1 for k in turn], [k ^ 2 for k in turn]]
+        ),
         out_shape=(
             jax.ShapeDtypeStruct((count * part, 2 * seqs), F32),
             jax.ShapeDtypeStruct((tokens, total, width), BF16),
             jax.ShapeDtypeStruct((aux_rows, width), F32),
         ),
-        in_specs=[whole(SMEM)] + [whole(VMEM)] * 5,
+        in_specs=[whole(SMEM)] + [whole(VMEM)] * 8,
         out_specs=(whole(VMEM),) * 3,
         compiler_params=params(16),
         name="first_half",
-    )(row, pairwise_state, aux, held, early, came)
+    )(row, pairwise_state, aux, item, own_early, own_came, held, early, came)
 
     block = 4
     tile = tokens * tokens
     pair_next, same, cross, _ = pl.pallas_call(
-        functools.partial(pair_kernel, [[k ^ 3 for k in turn]]),
+        functools.partial(pair_kernel, [[3], [k ^ 3 for k in turn]]),
         grid=(tokens // block,),
         out_shape=(
             jax.ShapeDtypeStruct((tokens, total, width), BF16),
@@ -400,7 +402,7 @@
             jax.ShapeDtypeStruct((count * part, 2 * seqs), F32),
         ),
         in_specs=[whole(SMEM), whole(VMEM), pl.BlockSpec((block, total, width), lambda g: (g, 0, 0))]
-        + [whole(VMEM)] * 3,
+        + [whole(VMEM)] * 4,
         out_specs=(pl.BlockSpec((block, total, width), lambda g: (g, 0, 0)),) + (whole(VMEM),) * 3,
         scratch_shapes=[VMEM((total, inner), BF16)],
         input_output_aliases={4: 3},
@@ -411,7 +413,7 @@
             transcendentals=0,
         ),
         name="pair",
-    )(row, aux, state, y, wide, late)
+    )(row, aux, state, y, wide, own_late, late)
 
     crossed = swap(cross, 1)
     tiles = pl.pallas_call(

time: 48.7 us -> 49.5 us (1.016)
  starting transfers between devices: 18.9 us -> 20.1 us
    ppermute x14 -> x17, starting transfers between devices: 18.9 us -> 20.1 us  [swap(): return lax.ppermute(array, 'row', [(r, r ^ bit) for r in range(count)])]
    ppermute x14 -> x17, waiting for transfers between devices: 14.9 us -> 14.5 us  [swap(): return lax.ppermute(array, 'row', [(r, r ^ bit) for r in range(count)])]
    unnamed x10 -> x12, local copies, waits for them, and re-layouts: 1.83 us -> 1.89 us
  transfers between devices with their start and end apart: 14 -> 17, of which waited for: 8 -> 6; matrix products, arithmetic and copies ran while one was open for 0% -> 0% of each run, Pallas kernels for 6% -> 6%
where the time goes in v10:
time: 49.5 us; the launch traced here: 49.3 us
  starting transfers between devices  20.1 us (41%)
  waiting for transfers between devices  14.5 us (29%)
  Pallas kernels  12 us (24%)
  local copies, waits for them, and re-layouts  1.89 us (4%)
  between operations  0.72 us (1%)
    ppermute x17, starting transfers between devices, swap(): return lax.ppermute(array, 'row', [(r, r ^ bit) for r in range(count)])  20.1 us
    ppermute x17, waiting for transfers between devices, swap(): return lax.ppermute(array, 'row', [(r, r ^ bit) for r in range(count)])  14.5 us
    pallas_call x1, Pallas kernels, body(): pl.pallas_call(functools.partial(pair_kernel, [[3], [k ^ 3 for k in turn]...  3.48 us
    pallas_call x1, Pallas kernels, body(): pl.pallas_call(gate_kernel, grid=(tokens // block,), out_shape=jax.ShapeD...  2.87 us
    pallas_call x1, Pallas kernels, body(): pl.pallas_call(mix_kernel, out_shape=jax.ShapeDtypeStruct((tokens // 2, i...  2.74 us
    pallas_call x1, Pallas kernels, body(): pl.pallas_call(prepare_kernel, out_shape=(jax.ShapeDtypeStruct((tokens *...  2.73 us
    unnamed x12, local copies, waits for them, and re-layouts  1.89 us
  transfers between devices with their start and end apart: 17, of which 6 were waited for; matrix products, arithmetic and copies ran while one was open for 0% of the time, Pallas kernels for 6%

profile of v10, /device:TPU:0, one launch (start us, length us, event | category | flops | bytes accessed | tf_op | source)
XLA Modules:
  0.0 49.3 jit_solution(2673232339160637417)
XLA Ops:
  0.6 2.7 %prepare.1 = (bf16[768,32]{1,0:T(8,128)(2,1)}, bf16[1,192,128]{2,1,0:T(8,128)(2,1)}, f32[424,128]{1,0:T(8,128)}, bf16[2,128,256]{2,1,0:T(8,128)(2,1)}) custom-call(s32[1]{0:T(128)} %bitcast.row_ref, s32[192]{0:T(256)} %depth_hbm.1, bf16[12,64,64]{2,1,0:T(8,128)(2,1)} %bitcast.14, f32[1,64]{1,0:T(1,128)} %bitcast.19, f32[1,64]{1,0:T(1,128)} %bitcast.20, ...), custom_call_target="tpu_custom_call" | custom-call | tf_op jit(solution)/shard_map/prepare/pallas_call | solution.py:299
  3.4 0.5 %collective-permute-start.4 = (bf16[1,192,128]{2,1,0:T(8,128)(2,1)}, bf16[1,192,128]{2,1,0:T(8,128)(2,1)S(1)}, u32[]{:S(2)}, u32[]{:S(2)}) collective-permute-start(bf16[1,192,128]{2,1,0:T(8,128)(2,1)} %get-tuple-element.28.rest_0_), channel_id=1, source_target_pairs={{0,1},{1,0},{2,3},{3,2},{4,5},{5,4},{6,7},{7,6},{8,9},{9,8},{10,11... | collective-permute-start | bytes 147464 | tf_op jit(solution)/shard_map/ppermute | solution.py:295
  3.9 2.6 %collective-permute-start.3 = (bf16[1,192,128]{2,1,0:T(8,128)(2,1)}, bf16[1,192,128]{2,1,0:T(8,128)(2,1)S(1)}, u32[]{:S(2)}, u32[]{:S(2)}) collective-permute-start(bf16[1,192,128]{2,1,0:T(8,128)(2,1)} %get-tuple-element.28.rest_0_), channel_id=1, source_target_pairs={{0,2},{1,3},{2,0},{3,1},{4,6},{5,7},{6,4},{7,5},{8,10},{9,11},{10,... | collective-permute-start | bytes 147464 | tf_op jit(solution)/shard_map/ppermute | solution.py:295
  6.5 1.6 %collective-permute-start.2 = (bf16[1,192,128]{2,1,0:T(8,128)(2,1)}, bf16[1,192,128]{2,1,0:T(8,128)(2,1)S(1)}, u32[]{:S(2)}, u32[]{:S(2)}) collective-permute-start(bf16[1,192,128]{2,1,0:T(8,128)(2,1)} %get-tuple-element.28.rest_0_), channel_id=1, source_target_pairs={{0,4},{1,5},{2,6},{3,7},{4,0},{5,1},{6,2},{7,3},{8,12},{9,13},{10,... | collective-permute-start | bytes 147464 | tf_op jit(solution)/shard_map/ppermute | solution.py:295
  8.1 2.6 %collective-permute-start.1 = (bf16[1,192,128]{2,1,0:T(8,128)(2,1)}, bf16[1,192,128]{2,1,0:T(8,128)(2,1)S(1)}, u32[]{:S(2)}, u32[]{:S(2)}) collective-permute-start(bf16[1,192,128]{2,1,0:T(8,128)(2,1)} %get-tuple-element.28.rest_0_), channel_id=1, source_target_pairs={{0,8},{1,9},{2,10},{3,11},{4,12},{5,13},{6,14},{7,15},{8,0},{9,1},... | collective-permute-start | bytes 147464 | tf_op jit(solution)/shard_map/ppermute | solution.py:295
  10.7 0.2 collective-permute-start
  10.9 0.0 collective-permute-done.4.rest_1_
  10.9 0.0 collective-permute-done.3.rest_2_
  10.9 0.0 collective-permute-done.2.refs_2_
  10.9 3.3 %collective-permute-done.1.refs_1_ = bf16[1,192,128]{2,1,0:T(8,128)(2,1)S(1)} collective-permute-done((bf16[1,192,128]{2,1,0:T(8,128)(2,1)}, bf16[1,192,128]{2,1,0:T(8,128)(2,1)S(1)}, u32[]{:S(2)}, u32[]{:S(2)}) %collective-permute-start.1) | collective-permute-done | bytes 49184 | tf_op jit(solution)/shard_map/ppermute | solution.py:295
  14.2 2.6 %collective-permute-done.refs_0_ = bf16[1,192,128]{2,1,0:T(8,128)(2,1)S(1)} collective-permute-done((bf16[1,192,128]{2,1,0:T(8,128)(2,1)}, bf16[1,192,128]{2,1,0:T(8,128)(2,1)S(1)}, u32[]{:S(2)}, u32[]{:S(2)}) %collective-permute-start) | collective-permute-done | bytes 49184 | tf_op jit(solution)/shard_map/ppermute | solution.py:295
  16.8 0.6 %collective-permute-start.6 = (bf16[3,192,128]{2,1,0:T(8,128)(2,1)S(1)}, bf16[3,192,128]{2,1,0:T(8,128)(2,1)S(1)}, u32[]{:S(2)}, u32[]{:S(2)}) collective-permute-start(bf16[3,192,128]{2,1,0:T(8,128)(2,1)S(1)} %join.1.rest_3_), channel_id=1, source_target_pairs={{0,2},{1,3},{2,0},{3,1},{4,6},{5,7},{6,4},{7,5},{8,10},{9,11},{10,... | collective-permute-start | bytes 442376 | tf_op jit(solution)/shard_map/ppermute | solution.py:295
  17.3 0.0 collective-permute-start.5
  17.3 0.0 copy-start.1
  17.3 0.9 %copy-done.1 = bf16[1024,128]{1,0:T(8,128)(2,1)S(1)} copy-done((bf16[1024,128]{1,0:T(8,128)(2,1)S(1)}, bf16[1024,128]{1,0:T(8,128)(2,1)}, u32[]{:S(2)}) %copy-start.1) | copy-done | bytes 262168
  18.3 0.0 copy-start.3
  18.3 0.9 %copy-done.3 = bf16[768,32]{1,0:T(8,128)(2,1)S(1)} copy-done((bf16[768,32]{1,0:T(8,128)(2,1)S(1)}, bf16[768,32]{1,0:T(8,128)(2,1)}, u32[]{:S(2)}) %copy-start.3) | copy-done | bytes 49176
  19.2 0.0 copy-start
  19.2 0.0 copy-start.2
  19.2 0.0 copy-start.5
  19.2 2.7 %mix.1.y_ref = bf16[6,2048,256]{2,1,0:T(8,128)(2,1)S(1)} custom-call(bf16[768,32]{1,0:T(8,128)(2,1)S(1)} %copy-done.3, bf16[1024,128]{1,0:T(8,128)(2,1)S(1)} %copy-done.1), custom_call_target="tpu_custom_call" | custom-call | flops 201326592 | bytes 6291456 | tf_op jit(solution)/shard_map/mix/pallas_call | solution.py:341
  22.0 0.0 collective-permute-done.6.rest_5_
  22.0 0.6 %collective-permute-start.8 = (bf16[3,192,128]{2,1,0:T(8,128)(2,1)S(1)}, bf16[3,192,128]{2,1,0:T(8,128)(2,1)S(1)}, u32[]{:S(2)}, u32[]{:S(2)}) collective-permute-start(bf16[3,192,128]{2,1,0:T(8,128)(2,1)S(1)} %collective-permute-done.6.rest_5_), channel_id=1, source_target_pairs={{0,1},{1,0},{2,3},{3,2},{4,5},{5,4},{6,7},{7,6},{8,9},{9,8},{10,11... | collective-permute-start | bytes 442376 | tf_op jit(solution)/shard_map/ppermute | solution.py:295
  22.6 0.1 collective-permute-start.7
  22.6 0.0 collective-permute-done.5.rest_4_
  22.6 0.0 copy-done
  22.6 0.0 copy-done.2
  22.7 0.0 copy-done.5
  22.7 0.1 first_half.1
  22.8 1.0 %collective-permute-done.7.rest_0_ = bf16[1,192,128]{2,1,0:T(8,128)(2,1)S(1)} collective-permute-done((bf16[1,192,128]{2,1,0:T(8,128)(2,1)S(1)}, bf16[1,192,128]{2,1,0:T(8,128)(2,1)S(1)}, u32[]{:S(2)}, u32[]{:S(2)}) %collective-permute-start.7) | collective-permute-done | bytes 49184 | tf_op jit(solution)/shard_map/ppermute | solution.py:295
  23.8 0.0 collective-permute-done.8.rest_1_
  23.8 0.0 copy-start.4
  23.8 3.5 %pair.1 = (bf16[12,192,128]{2,1,0:T(8,128)(2,1)}, bf16[8,144,128]{2,1,0:T(8,128)(2,1)S(1)}, bf16[8,144,128]{2,1,0:T(8,128)(2,1)S(1)}, f32[3072,128]{1,0:T(8,128)S(1)}) custom-call(s32[1]{0:T(128)} %bitcast.row_ref, f32[424,128]{1,0:T(8,128)S(1)} %get-tuple-element.36.aux_ref, ...), custom_call_target="tpu_custom_call", output_to_operand_aliasing={{3}: (4, {})} | custom-call | flops 1207959552 | bytes 8650752 | tf_op jit(solution)/shard_map/pair/pallas_call | solution.py:395
  27.3 0.2 collective-permute-start.9
  27.5 1.4 %collective-permute-done.9.crossed_ref = bf16[8,144,128]{2,1,0:T(8,128)(2,1)S(1)} collective-permute-done((bf16[8,144,128]{2,1,0:T(8,128)(2,1)S(1)}, bf16[8,144,128]{2,1,0:T(8,128)(2,1)S(1)}, u32[]{:S(2)}, u32[]{:S(2)}) %collective-permute-start.9) | collective-permute-done | bytes 294944 | tf_op jit(solution)/shard_map/ppermute | solution.py:295
  28.9 1.6 %collective-permute-start.10 = (bf16[2,144,128]{2,1,0:T(8,128)(2,1)S(1)}, bf16[2,144,128]{2,1,0:T(8,128)(2,1)S(1)}, u32[]{:S(2)}, u32[]{:S(2)}) collective-permute-start(bf16[2,144,128]{2,1,0:T(8,128)(2,1)S(1)} %get-tuple-element.45), channel_id=1, source_target_pairs={{0,2},{1,3},{2,0},{3,1},{4,6},{5,7},{6,4},{7,5},{8,10},{9,11},{10,... | collective-permute-start | bytes 221192 | tf_op jit(solution)/shard_map/ppermute | solution.py:295
  30.5 0.0 collective-permute-start.11
  30.5 2.0 %collective-permute-start.12 = (bf16[2,144,128]{2,1,0:T(8,128)(2,1)S(1)}, bf16[2,144,128]{2,1,0:T(8,128)(2,1)S(1)}, u32[]{:S(2)}, u32[]{:S(2)}) collective-permute-start(bf16[2,144,128]{2,1,0:T(8,128)(2,1)S(1)} %get-tuple-element.47), channel_id=1, source_target_pairs={{0,6},{1,7},{2,4},{3,5},{4,2},{5,3},{6,0},{7,1},{8,14},{9,15},{10,... | collective-permute-start | bytes 221192 | tf_op jit(solution)/shard_map/ppermute | solution.py:295
  32.5 0.7 %collective-permute-start.13 = (bf16[2,144,128]{2,1,0:T(8,128)(2,1)S(1)}, bf16[2,144,128]{2,1,0:T(8,128)(2,1)S(1)}, u32[]{:S(2)}, u32[]{:S(2)}) collective-permute-start(bf16[2,144,128]{2,1,0:T(8,128)(2,1)S(1)} %get-tuple-element.48), channel_id=1, source_target_pairs={{0,8},{1,9},{2,10},{3,11},{4,12},{5,13},{6,14},{7,15},{8,0},{9,1},... | collective-permute-start | bytes 221192 | tf_op jit(solution)/shard_map/ppermute | solution.py:295
  33.1 3.2 %collective-permute-start.14 = (bf16[2,144,128]{2,1,0:T(8,128)(2,1)S(1)}, bf16[2,144,128]{2,1,0:T(8,128)(2,1)S(1)}, u32[]{:S(2)}, u32[]{:S(2)}) collective-permute-start(bf16[2,144,128]{2,1,0:T(8,128)(2,1)S(1)} %get-tuple-element.49), channel_id=1, source_target_pairs={{0,10},{1,11},{2,8},{3,9},{4,14},{5,15},{6,12},{7,13},{8,2},{9,3},... | collective-permute-start | bytes 221192 | tf_op jit(solution)/shard_map/ppermute | solution.py:295
  36.4 0.0 collective-permute-done.10.rest_1_
  36.4 1.1 %collective-permute-start.15 = (bf16[2,144,128]{2,1,0:T(8,128)(2,1)S(1)}, bf16[2,144,128]{2,1,0:T(8,128)(2,1)S(1)}, u32[]{:S(2)}, u32[]{:S(2)}) collective-permute-start(bf16[2,144,128]{2,1,0:T(8,128)(2,1)S(1)} %get-tuple-element.50), channel_id=1, source_target_pairs={{0,12},{1,13},{2,14},{3,15},{4,8},{5,9},{6,10},{7,11},{8,4},{9,5},... | collective-permute-start | bytes 221192 | tf_op jit(solution)/shard_map/ppermute | solution.py:295
  37.4 0.0 collective-permute-done.11.rest_2_
  37.4 2.7 %collective-permute-start.16 = (bf16[2,144,128]{2,1,0:T(8,128)(2,1)S(1)}, bf16[2,144,128]{2,1,0:T(8,128)(2,1)S(1)}, u32[]{:S(2)}, u32[]{:S(2)}) collective-permute-start(bf16[2,144,128]{2,1,0:T(8,128)(2,1)S(1)} %get-tuple-element.51), channel_id=1, source_target_pairs={{0,14},{1,15},{2,12},{3,13},{4,10},{5,11},{6,8},{7,9},{8,6},{9,7},... | collective-permute-start | bytes 221192 | tf_op jit(solution)/shard_map/ppermute | solution.py:295
  40.1 0.0 collective-permute-done.12.rest_3_
  40.1 4.0 %collective-permute-done.13.rest_4_ = bf16[2,144,128]{2,1,0:T(8,128)(2,1)S(1)} collective-permute-done((bf16[2,144,128]{2,1,0:T(8,128)(2,1)S(1)}, bf16[2,144,128]{2,1,0:T(8,128)(2,1)S(1)}, u32[]{:S(2)}, u32[]{:S(2)}) %collective-permute-start.13) | collective-permute-done | bytes 73760 | tf_op jit(solution)/shard_map/ppermute | solution.py:295
  44.1 2.3 %collective-permute-done.14.rest_5_ = bf16[2,144,128]{2,1,0:T(8,128)(2,1)S(1)} collective-permute-done((bf16[2,144,128]{2,1,0:T(8,128)(2,1)S(1)}, bf16[2,144,128]{2,1,0:T(8,128)(2,1)S(1)}, u32[]{:S(2)}, u32[]{:S(2)}) %collective-permute-start.14) | collective-permute-done | bytes 73760 | tf_op jit(solution)/shard_map/ppermute | solution.py:295
  46.4 0.0 collective-permute-done.15.rest_6_
  46.4 0.0 collective-permute-done.16.rest_7_
  46.4 0.0 copy-done.4
  46.4 2.9 %gate.1 = bf16[12,192,256]{2,1,0:T(8,128)(2,1)} custom-call(s32[1]{0:T(128)} %bitcast.row_ref, f32[424,128]{1,0:T(8,128)S(1)} %get-tuple-element.36.aux_ref, bf16[2,128,256]{2,1,0:T(8,128)(2,1)S(1)} %copy-done.4, bf16[2,144,128]{2,1,0:T(8,128)(2,1)S(1)} %get-tuple-element.44.rest_0_, bf16[2,144,128]{2,1,0:T(8,128)(2,1)S(1)} %collective-permute-done.10.rest_1_, ...), custom_call_target="tpu_custom_call" | custom-call | flops 301989888 | bytes 2949120 | tf_op jit(solution)/shard_map/gate/pallas_call | solution.py:431
  (2 shorter events, 0.1 us)
Async XLA Ops:
  3.4 7.5 %collective-permute-start.4 = (bf16[1,192,128]{2,1,0:T(8,128)(2,1)}, bf16[1,192,128]{2,1,0:T(8,128)(2,1)S(1)}, u32[]{:S(2)}, u32[]{:S(2)}) collective-permute-start(bf16[1,192,128]{2,1,0:T(8,128)(2,1)} %get-tuple-element.28.rest_0_), channel_id=1, source_target_pairs={{0,1},{1,0},{2,3},{3,2},{4,5},{5,4},{6,7},{7,6},{8,9},{9,8},{10,11... | collective-permute-start | bytes 147464 | tf_op jit(solution)/shard_map/ppermute | solution.py:295
  3.9 7.0 %collective-permute-start.3 = (bf16[1,192,128]{2,1,0:T(8,128)(2,1)}, bf16[1,192,128]{2,1,0:T(8,128)(2,1)S(1)}, u32[]{:S(2)}, u32[]{:S(2)}) collective-permute-start(bf16[1,192,128]{2,1,0:T(8,128)(2,1)} %get-tuple-element.28.rest_0_), channel_id=1, source_target_pairs={{0,2},{1,3},{2,0},{3,1},{4,6},{5,7},{6,4},{7,5},{8,10},{9,11},{10,... | collective-permute-start | bytes 147464 | tf_op jit(solution)/shard_map/ppermute | solution.py:295
  6.5 4.4 %collective-permute-start.2 = (bf16[1,192,128]{2,1,0:T(8,128)(2,1)}, bf16[1,192,128]{2,1,0:T(8,128)(2,1)S(1)}, u32[]{:S(2)}, u32[]{:S(2)}) collective-permute-start(bf16[1,192,128]{2,1,0:T(8,128)(2,1)} %get-tuple-element.28.rest_0_), channel_id=1, source_target_pairs={{0,4},{1,5},{2,6},{3,7},{4,0},{5,1},{6,2},{7,3},{8,12},{9,13},{10,... | collective-permute-start | bytes 147464 | tf_op jit(solution)/shard_map/ppermute | solution.py:295
  8.1 6.1 %collective-permute-start.1 = (bf16[1,192,128]{2,1,0:T(8,128)(2,1)}, bf16[1,192,128]{2,1,0:T(8,128)(2,1)S(1)}, u32[]{:S(2)}, u32[]{:S(2)}) collective-permute-start(bf16[1,192,128]{2,1,0:T(8,128)(2,1)} %get-tuple-element.28.rest_0_), channel_id=1, source_target_pairs={{0,8},{1,9},{2,10},{3,11},{4,12},{5,13},{6,14},{7,15},{8,0},{9,1},... | collective-permute-start | bytes 147464 | tf_op jit(solution)/shard_map/ppermute | solution.py:295
  10.7 6.1 %collective-permute-start = (bf16[1,192,128]{2,1,0:T(8,128)(2,1)}, bf16[1,192,128]{2,1,0:T(8,128)(2,1)S(1)}, u32[]{:S(2)}, u32[]{:S(2)}) collective-permute-start(bf16[1,192,128]{2,1,0:T(8,128)(2,1)} %get-tuple-element.28.rest_0_), channel_id=1, source_target_pairs={{0,12},{1,13},{2,14},{3,15},{4,8},{5,9},{6,10},{7,11},{8,4},{9,5},... | collective-permute-start | bytes 147464 | tf_op jit(solution)/shard_map/ppermute | solution.py:295
  16.8 5.2 %collective-permute-start.6 = (bf16[3,192,128]{2,1,0:T(8,128)(2,1)S(1)}, bf16[3,192,128]{2,1,0:T(8,128)(2,1)S(1)}, u32[]{:S(2)}, u32[]{:S(2)}) collective-permute-start(bf16[3,192,128]{2,1,0:T(8,128)(2,1)S(1)} %join.1.rest_3_), channel_id=1, source_target_pairs={{0,2},{1,3},{2,0},{3,1},{4,6},{5,7},{6,4},{7,5},{8,10},{9,11},{10,... | collective-permute-start | bytes 442376 | tf_op jit(solution)/shard_map/ppermute | solution.py:295
  17.3 5.3 %collective-permute-start.5 = (bf16[3,192,128]{2,1,0:T(8,128)(2,1)S(1)}, bf16[3,192,128]{2,1,0:T(8,128)(2,1)S(1)}, u32[]{:S(2)}, u32[]{:S(2)}) collective-permute-start(bf16[3,192,128]{2,1,0:T(8,128)(2,1)S(1)} %join.1.rest_3_), channel_id=1, source_target_pairs={{0,1},{1,0},{2,3},{3,2},{4,5},{5,4},{6,7},{7,6},{8,9},{9,8},{10,11... | collective-permute-start | bytes 442376 | tf_op jit(solution)/shard_map/ppermute | solution.py:295
  17.3 1.0 %copy-start.1 = (bf16[1024,128]{1,0:T(8,128)(2,1)S(1)}, bf16[1024,128]{1,0:T(8,128)(2,1)}, u32[]{:S(2)}) copy-start(bf16[1024,128]{1,0:T(8,128)(2,1)} %weight_ref.1) | copy-start | bytes 786436
  18.3 0.9 %copy-start.3 = (bf16[768,32]{1,0:T(8,128)(2,1)S(1)}, bf16[768,32]{1,0:T(8,128)(2,1)}, u32[]{:S(2)}) copy-start(bf16[768,32]{1,0:T(8,128)(2,1)} %get-tuple-element.34.left_ref) | copy-start | bytes 147460
  19.2 3.4 %copy-start = (bf16[12,192,128]{2,1,0:T(8,128)(2,1)S(1)}, bf16[12,192,128]{2,1,0:T(8,128)(2,1)}, u32[]{:S(2)}) copy-start(bf16[12,192,128]{2,1,0:T(8,128)(2,1)} %state_ref.1) | copy-start | bytes 1769476
  19.2 3.4 %copy-start.2 = (f32[424,128]{1,0:T(8,128)S(1)}, f32[424,128]{1,0:T(8,128)}, u32[]{:S(2)}) copy-start(f32[424,128]{1,0:T(8,128)} %get-tuple-element.27.aux_ref) | copy-start | bytes 651268
  19.2 3.4 %copy-start.5 = (bf16[1,192,128]{2,1,0:T(8,128)(2,1)S(1)}, bf16[1,192,128]{2,1,0:T(8,128)(2,1)}, u32[]{:S(2)}) copy-start(bf16[1,192,128]{2,1,0:T(8,128)(2,1)} %get-tuple-element.28.rest_0_) | copy-start | bytes 147460
  22.0 1.8 %collective-permute-start.8 = (bf16[3,192,128]{2,1,0:T(8,128)(2,1)S(1)}, bf16[3,192,128]{2,1,0:T(8,128)(2,1)S(1)}, u32[]{:S(2)}, u32[]{:S(2)}) collective-permute-start(bf16[3,192,128]{2,1,0:T(8,128)(2,1)S(1)} %collective-permute-done.6.rest_5_), channel_id=1, source_target_pairs={{0,1},{1,0},{2,3},{3,2},{4,5},{5,4},{6,7},{7,6},{8,9},{9,8},{10,11... | collective-permute-start | bytes 442376 | tf_op jit(solution)/shard_map/ppermute | solution.py:295
  22.6 1.2 %collective-permute-start.7 = (bf16[1,192,128]{2,1,0:T(8,128)(2,1)S(1)}, bf16[1,192,128]{2,1,0:T(8,128)(2,1)S(1)}, u32[]{:S(2)}, u32[]{:S(2)}) collective-permute-start(bf16[1,192,128]{2,1,0:T(8,128)(2,1)S(1)} %collective-permute-done.3.rest_2_), channel_id=1, source_target_pairs={{0,1},{1,0},{2,3},{3,2},{4,5},{5,4},{6,7},{7,6},{8,9},{9,8},{10,11... | collective-permute-start | bytes 147464 | tf_op jit(solution)/shard_map/ppermute | solution.py:295
  23.8 22.6 %copy-start.4 = (bf16[2,128,256]{2,1,0:T(8,128)(2,1)S(1)}, bf16[2,128,256]{2,1,0:T(8,128)(2,1)}, u32[]{:S(2)}) copy-start(bf16[2,128,256]{2,1,0:T(8,128)(2,1)} %get-tuple-element.41.gates_ref) | copy-start | bytes 393220
  27.3 1.6 %collective-permute-start.9 = (bf16[8,144,128]{2,1,0:T(8,128)(2,1)S(1)}, bf16[8,144,128]{2,1,0:T(8,128)(2,1)S(1)}, u32[]{:S(2)}, u32[]{:S(2)}) collective-permute-start(bf16[8,144,128]{2,1,0:T(8,128)(2,1)S(1)} %get-tuple-element.43), channel_id=1, source_target_pairs={{0,1},{1,0},{2,3},{3,2},{4,5},{5,4},{6,7},{7,6},{8,9},{9,8},{10,11... | collective-permute-start | bytes 884744 | tf_op jit(solution)/shard_map/ppermute | solution.py:295
  28.9 7.4 %collective-permute-start.10 = (bf16[2,144,128]{2,1,0:T(8,128)(2,1)S(1)}, bf16[2,144,128]{2,1,0:T(8,128)(2,1)S(1)}, u32[]{:S(2)}, u32[]{:S(2)}) collective-permute-start(bf16[2,144,128]{2,1,0:T(8,128)(2,1)S(1)} %get-tuple-element.45), channel_id=1, source_target_pairs={{0,2},{1,3},{2,0},{3,1},{4,6},{5,7},{6,4},{7,5},{8,10},{9,11},{10,... | collective-permute-start | bytes 221192 | tf_op jit(solution)/shard_map/ppermute | solution.py:295
  30.5 6.9 %collective-permute-start.11 = (bf16[2,144,128]{2,1,0:T(8,128)(2,1)S(1)}, bf16[2,144,128]{2,1,0:T(8,128)(2,1)S(1)}, u32[]{:S(2)}, u32[]{:S(2)}) collective-permute-start(bf16[2,144,128]{2,1,0:T(8,128)(2,1)S(1)} %get-tuple-element.46), channel_id=1, source_target_pairs={{0,4},{1,5},{2,6},{3,7},{4,0},{5,1},{6,2},{7,3},{8,12},{9,13},{10,... | collective-permute-start | bytes 221192 | tf_op jit(solution)/shard_map/ppermute | solution.py:295
  30.5 9.6 %collective-permute-start.12 = (bf16[2,144,128]{2,1,0:T(8,128)(2,1)S(1)}, bf16[2,144,128]{2,1,0:T(8,128)(2,1)S(1)}, u32[]{:S(2)}, u32[]{:S(2)}) collective-permute-start(bf16[2,144,128]{2,1,0:T(8,128)(2,1)S(1)} %get-tuple-element.47), channel_id=1, source_target_pairs={{0,6},{1,7},{2,4},{3,5},{4,2},{5,3},{6,0},{7,1},{8,14},{9,15},{10,... | collective-permute-start | bytes 221192 | tf_op jit(solution)/shard_map/ppermute | solution.py:295
  32.5 11.6 %collective-permute-start.13 = (bf16[2,144,128]{2,1,0:T(8,128)(2,1)S(1)}, bf16[2,144,128]{2,1,0:T(8,128)(2,1)S(1)}, u32[]{:S(2)}, u32[]{:S(2)}) collective-permute-start(bf16[2,144,128]{2,1,0:T(8,128)(2,1)S(1)} %get-tuple-element.48), channel_id=1, source_target_pairs={{0,8},{1,9},{2,10},{3,11},{4,12},{5,13},{6,14},{7,15},{8,0},{9,1},... | collective-permute-start | bytes 221192 | tf_op jit(solution)/shard_map/ppermute | solution.py:295
  33.1 13.3 %collective-permute-start.14 = (bf16[2,144,128]{2,1,0:T(8,128)(2,1)S(1)}, bf16[2,144,128]{2,1,0:T(8,128)(2,1)S(1)}, u32[]{:S(2)}, u32[]{:S(2)}) collective-permute-start(bf16[2,144,128]{2,1,0:T(8,128)(2,1)S(1)} %get-tuple-element.49), channel_id=1, source_target_pairs={{0,10},{1,11},{2,8},{3,9},{4,14},{5,15},{6,12},{7,13},{8,2},{9,3},... | collective-permute-start | bytes 221192 | tf_op jit(solution)/shard_map/ppermute | solution.py:295
  36.4 10.1 %collective-permute-start.15 = (bf16[2,144,128]{2,1,0:T(8,128)(2,1)S(1)}, bf16[2,144,128]{2,1,0:T(8,128)(2,1)S(1)}, u32[]{:S(2)}, u32[]{:S(2)}) collective-permute-start(bf16[2,144,128]{2,1,0:T(8,128)(2,1)S(1)} %get-tuple-element.50), channel_id=1, source_target_pairs={{0,12},{1,13},{2,14},{3,15},{4,8},{5,9},{6,10},{7,11},{8,4},{9,5},... | collective-permute-start | bytes 221192 | tf_op jit(solution)/shard_map/ppermute | solution.py:295
  37.4 9.0 %collective-permute-start.16 = (bf16[2,144,128]{2,1,0:T(8,128)(2,1)S(1)}, bf16[2,144,128]{2,1,0:T(8,128)(2,1)S(1)}, u32[]{:S(2)}, u32[]{:S(2)}) collective-permute-start(bf16[2,144,128]{2,1,0:T(8,128)(2,1)S(1)} %get-tuple-element.51), channel_id=1, source_target_pairs={{0,14},{1,15},{2,12},{3,13},{4,10},{5,11},{6,8},{7,9},{8,6},{9,7},... | collective-permute-start | bytes 221192 | tf_op jit(solution)/shard_map/ppermute | solution.py:295

commit v11 on v9

--- a/solution.py
+++ b/solution.py
@@ -142,11 +142,15 @@
         spot += piece.shape[0]
 
 
+def by_core(row, pair):
+    return jnp.where((row & 1) == 1, pair[1], pair[0])
+
+
 def spread_items(row, wide_ref, pieces, orders):
-    for piece, ks in zip(pieces, orders):
+    for piece, pairs in zip(pieces, orders):
         size = piece.shape[1]
-        for m, k in enumerate(ks):
-            spot = pl.ds(pl.multiple_of((row ^ k) * size, size), size)
+        for m, pair in enumerate(pairs):
+            spot = pl.ds(pl.multiple_of((row ^ by_core(row, pair)) * size, size), size)
             wide_ref[spot, :] = piece[m].astype(F32)
 
 
@@ -204,18 +208,18 @@
                 (same_ref if (d & 1) == core else cross_ref)[d // 2, spot, :] = tile
 
 
-def pack_kernel(row_ref, same_ref, crossed_ref, *outs):
+def pack_kernel(pairs, row_ref, same_ref, crossed_ref, *outs):
     chip = row_ref[0] >> 1
     for core in (0, 1):
 
         @pl.when((row_ref[0] & 1) == core)
         def _():
-            for k, out_ref in enumerate(outs):
-                out_ref[core] = same_ref[chip ^ k]
-                out_ref[1 - core] = crossed_ref[chip ^ k]
-
-
-def gate_kernel(row_ref, aux_ref, gates_ref, *rest):
+            for pair, out_ref in zip(pairs, outs):
+                out_ref[core] = same_ref[chip ^ pair[core]]
+                out_ref[1 - core] = crossed_ref[chip ^ pair[core]]
+
+
+def gate_kernel(pairs, row_ref, aux_ref, gates_ref, *rest):
     tiles, (out_ref, wide_ref) = rest[:-2], rest[-2:]
     step = pl.program_id(0)
     block, total = out_ref.shape[:2]
@@ -225,9 +229,10 @@
     @pl.when(step == 0)
     def _():
         chip = row_ref[0] >> 1
-        for k, tile in enumerate(tiles):
+        for pair, tile in zip(pairs, tiles):
+            source = chip ^ by_core(row_ref[0], pair)
             for core in (0, 1):
-                spot = pl.ds(pl.multiple_of(((chip ^ k) * 2 + core) * rows, rows), rows)
+                spot = pl.ds(pl.multiple_of((source * 2 + core) * rows, rows), rows)
                 wide_ref[spot, :] = tile[core].astype(F32)
 
     gain = aux_ref[2 * total + 34 : 2 * total + 35]
@@ -292,8 +297,13 @@
     gated = input_projection_weight.shape[1]
     row = lax.axis_index("row").astype(jnp.int32).reshape(1)
 
-    def swap(array, bit):
-        return lax.ppermute(array, "row", [(r, r ^ bit) for r in range(count)])
+    def swap(array, bits):
+        bits = bits if isinstance(bits, tuple) else (bits, bits)
+        return lax.ppermute(array, "row", [(r, r ^ bits[r & 1]) for r in range(count)])
+
+    def staggered(items):
+        cut = (len(items) + 1) // 2
+        return list(zip(items, items[cut:] + items[:cut]))
 
     aux_rows = 2 * total + 40
     part = tokens * half
@@ -367,31 +377,41 @@
         )(*pieces)
 
     chips = count // 2
-    turn = [4 * k for k in range(count // 4 - 1, 0, -1)]
-    direct = [swap(item, k) for k in turn]
-    held = joined(item, *direct)
-    turn = [0] + turn
+    turn = staggered([4 * k for k in range(count // 4 - 1, 0, -1)])
+    direct = [swap(item, pair) for pair in turn]
+    own_came = swap(item, 2)
+    own_early = swap(item, 1)
+    *direct, own_came, own_early = lax.optimization_barrier((*direct, own_came, own_early))
+    held = joined(*direct)
     came = swap(held, 2)
-    early = swap(held, 1)
+    kept, y = lax.optimization_barrier((held, y))
+    early = swap(kept, 1)
     came, y = lax.optimization_barrier((came, y))
+    own_late = swap(own_came, 1)
     late = swap(came, 1)
+
+    def ranks(bits):
+        return [(a ^ bits, b ^ bits) if bits in (0, 2) else (b ^ bits, a ^ bits) for a, b in turn]
+
     wide, state, aux = pl.pallas_call(
-        functools.partial(first_half_kernel, [turn, [k ^ 1 for k in turn], [k ^ 2 for k in turn]]),
+        functools.partial(
+            first_half_kernel, [[(0, 0)], [(1, 1)], [(2, 2)], ranks(0), ranks(1), ranks(2)]
+        ),
         out_shape=(
             jax.ShapeDtypeStruct((count * part, 2 * seqs), F32),
             jax.ShapeDtypeStruct((tokens, total, width), BF16),
             jax.ShapeDtypeStruct((aux_rows, width), F32),
         ),
-        in_specs=[whole(SMEM)] + [whole(VMEM)] * 5,
+        in_specs=[whole(SMEM)] + [whole(VMEM)] * 8,
         out_specs=(whole(VMEM),) * 3,
         compiler_params=params(16),
         name="first_half",
-    )(row, pairwise_state, aux, held, early, came)
+    )(row, pairwise_state, aux, item, own_early, own_came, held, early, came)
 
     block = 4
     tile = tokens * tokens
     pair_next, same, cross, _ = pl.pallas_call(
-        functools.partial(pair_kernel, [[k ^ 3 for k in turn]]),
+        functools.partial(pair_kernel, [[(3, 3)], ranks(3)]),
         grid=(tokens // block,),
         out_shape=(
             jax.ShapeDtypeStruct((tokens, total, width), BF16),
@@ -400,7 +420,7 @@
             jax.ShapeDtypeStruct((count * part, 2 * seqs), F32),
         ),
         in_specs=[whole(SMEM), whole(VMEM), pl.BlockSpec((block, total, width), lambda g: (g, 0, 0))]
-        + [whole(VMEM)] * 3,
+        + [whole(VMEM)] * 4,
         out_specs=(pl.BlockSpec((block, total, width), lambda g: (g, 0, 0)),) + (whole(VMEM),) * 3,
         scratch_shapes=[VMEM((total, inner), BF16)],
         input_output_aliases={4: 3},
@@ -411,23 +431,23 @@
             transcendentals=0,
         ),
         name="pair",
-    )(row, aux, state, y, wide, late)
+    )(row, aux, state, y, wide, own_late, late)
 
     crossed = swap(cross, 1)
+    sends = [(0, 0)] + staggered(list(range(chips - 1, 0, -1)))
     tiles = pl.pallas_call(
-        pack_kernel,
+        functools.partial(pack_kernel, sends),
         out_shape=(jax.ShapeDtypeStruct((2, tile, width), BF16),) * chips,
         in_specs=[whole(SMEM), whole(VMEM), whole(VMEM)],
         out_specs=(whole(VMEM),) * chips,
         compiler_params=params(16),
         name="pack",
     )(row, same, crossed)
-    moved = {k: swap(tiles[k], 2 * k) for k in range(chips - 1, 0, -1)}
-    tiles = [tiles[0]] + [moved[k] for k in range(1, chips)]
+    tiles = [tiles[0]] + [swap(t, (2 * a, 2 * b)) for t, (a, b) in zip(tiles[1:], sends[1:])]
 
     block = 4
     out = pl.pallas_call(
-        gate_kernel,
+        functools.partial(gate_kernel, sends),
         grid=(tokens // block,),
         out_shape=jax.ShapeDtypeStruct((tokens, total, gated), BF16),
         in_specs=[whole(SMEM)] + [whole(VMEM)] * (2 + chips),

time: 48.7 us -> 47.7 us (0.979)
  waiting for transfers between devices: 14.9 us -> 13 us
  starting transfers between devices: 18.9 us -> 20.1 us
  local copies, waits for them, and re-layouts: 1.83 us -> 1.03 us
    ppermute x14 -> x17, waiting for transfers between devices: 14.9 us -> 13 us  [swap(): lax.ppermute(array, 'row', [(r, r ^ bits[r & 1]) for r in range(count)])]
    ppermute x14 -> x17, starting transfers between devices: 18.9 us -> 20.1 us  [swap(): lax.ppermute(array, 'row', [(r, r ^ bits[r & 1]) for r in range(count)])]
    unnamed x10, local copies, waits for them, and re-layouts: 1.83 us -> 1.03 us
  transfers between devices with their start and end apart: 14 -> 17, of which waited for: 8 -> 9; matrix products, arithmetic and copies ran while one was open for 0% -> 0% of each run, Pallas kernels for 6% -> 6%
where the time goes in v11:
time: 47.7 us; the launch traced here: 46.9 us
  starting transfers between devices  20.1 us (42%)
  waiting for transfers between devices  13 us (27%)
  Pallas kernels  12.1 us (25%)
  local copies, waits for them, and re-layouts  1.03 us (2%)
  between operations  0.72 us (2%)
    ppermute x17, starting transfers between devices, swap(): lax.ppermute(array, 'row', [(r, r ^ bits[r & 1]) for r in range(count)])  20.1 us
    ppermute x17, waiting for transfers between devices, swap(): lax.ppermute(array, 'row', [(r, r ^ bits[r & 1]) for r in range(count)])  13 us
    pallas_call x1, Pallas kernels, body(): pl.pallas_call(functools.partial(pair_kernel, [[(3, 3)], ranks(3)]), grid...  3.47 us
    pallas_call x1, Pallas kernels, body(): pl.pallas_call(functools.partial(gate_kernel, sends), grid=(tokens // blo...  2.88 us
    pallas_call x1, Pallas kernels, body(): pl.pallas_call(prepare_kernel, out_shape=(jax.ShapeDtypeStruct((mix_rows,...  2.77 us
    pallas_call x1, Pallas kernels, body(): pl.pallas_call(functools.partial(mix_kernel, factor), out_shape=jax.Shape...  2.74 us
    unnamed x10, local copies, waits for them, and re-layouts  1.03 us
  transfers between devices with their start and end apart: 17, of which 9 were waited for; matrix products, arithmetic and copies ran while one was open for 0% of the time, Pallas kernels for 6%

profile of v11, /device:TPU:0, one launch (start us, length us, event | category | flops | bytes accessed | tf_op | source)
XLA Modules:
  0.0 46.9 jit_solution(3470197930991415559)
XLA Ops:
  0.6 2.8 %prepare.1 = (bf16[1792,128]{1,0:T(8,128)(2,1)}, bf16[1,192,128]{2,1,0:T(8,128)(2,1)}, f32[424,128]{1,0:T(8,128)}, bf16[2,128,256]{2,1,0:T(8,128)(2,1)}) custom-call(s32[1]{0:T(128)} %bitcast.row_ref, s32[192]{0:T(256)} %depth_hbm.1, bf16[12,64,64]{2,1,0:T(8,128)(2,1)} %bitcast.14, f32[1,64]{1,0:T(1,128)} %bitcast.19, f32[1,64]{1,0:T(1,128)} %bitcast.20, ...), custom_call_target="tpu_custom_call" | custom-call | tf_op jit(solution)/shard_map/prepare/pallas_call | solution.py:311
  3.4 0.5 %collective-permute-start.4 = (bf16[1,192,128]{2,1,0:T(8,128)(2,1)}, bf16[1,192,128]{2,1,0:T(8,128)(2,1)S(1)}, u32[]{:S(2)}, u32[]{:S(2)}) collective-permute-start(bf16[1,192,128]{2,1,0:T(8,128)(2,1)} %get-tuple-element.30.rest_0_), channel_id=1, source_target_pairs={{0,1},{1,0},{2,3},{3,2},{4,5},{5,4},{6,7},{7,6},{8,9},{9,8},{10,11... | collective-permute-start | bytes 147464 | tf_op jit(solution)/shard_map/ppermute | solution.py:302
  3.9 2.6 %collective-permute-start.3 = (bf16[1,192,128]{2,1,0:T(8,128)(2,1)}, bf16[1,192,128]{2,1,0:T(8,128)(2,1)S(1)}, u32[]{:S(2)}, u32[]{:S(2)}) collective-permute-start(bf16[1,192,128]{2,1,0:T(8,128)(2,1)} %get-tuple-element.30.rest_0_), channel_id=1, source_target_pairs={{0,2},{1,3},{2,0},{3,1},{4,6},{5,7},{6,4},{7,5},{8,10},{9,11},{10,... | collective-permute-start | bytes 147464 | tf_op jit(solution)/shard_map/ppermute | solution.py:302
  6.5 1.6 %collective-permute-start.2 = (bf16[1,192,128]{2,1,0:T(8,128)(2,1)}, bf16[1,192,128]{2,1,0:T(8,128)(2,1)S(1)}, u32[]{:S(2)}, u32[]{:S(2)}) collective-permute-start(bf16[1,192,128]{2,1,0:T(8,128)(2,1)} %get-tuple-element.30.rest_0_), channel_id=1, source_target_pairs={{0,4},{1,9},{2,6},{3,11},{4,0},{5,13},{6,2},{7,15},{8,12},{9,1},{1... | collective-permute-start | bytes 147464 | tf_op jit(solution)/shard_map/ppermute | solution.py:302
  8.1 2.6 %collective-permute-start.1 = (bf16[1,192,128]{2,1,0:T(8,128)(2,1)}, bf16[1,192,128]{2,1,0:T(8,128)(2,1)S(1)}, u32[]{:S(2)}, u32[]{:S(2)}) collective-permute-start(bf16[1,192,128]{2,1,0:T(8,128)(2,1)} %get-tuple-element.30.rest_0_), channel_id=1, source_target_pairs={{0,8},{1,13},{2,10},{3,15},{4,12},{5,9},{6,14},{7,11},{8,0},{9,5},... | collective-permute-start | bytes 147464 | tf_op jit(solution)/shard_map/ppermute | solution.py:302
  10.7 0.2 collective-permute-start
  10.9 0.0 collective-permute-done.4.rest_1_
  10.9 0.0 collective-permute-done.3.rest_2_
  10.9 0.4 collective-permute-done.2.refs_2_
  11.4 3.5 %collective-permute-done.1.refs_1_ = bf16[1,192,128]{2,1,0:T(8,128)(2,1)S(1)} collective-permute-done((bf16[1,192,128]{2,1,0:T(8,128)(2,1)}, bf16[1,192,128]{2,1,0:T(8,128)(2,1)S(1)}, u32[]{:S(2)}, u32[]{:S(2)}) %collective-permute-start.1) | collective-permute-done | bytes 49184 | tf_op jit(solution)/shard_map/ppermute | solution.py:302
  14.8 2.0 %collective-permute-done.refs_0_ = bf16[1,192,128]{2,1,0:T(8,128)(2,1)S(1)} collective-permute-done((bf16[1,192,128]{2,1,0:T(8,128)(2,1)}, bf16[1,192,128]{2,1,0:T(8,128)(2,1)S(1)}, u32[]{:S(2)}, u32[]{:S(2)}) %collective-permute-start) | collective-permute-done | bytes 49184 | tf_op jit(solution)/shard_map/ppermute | solution.py:302
  16.8 0.6 %collective-permute-start.6 = (bf16[3,192,128]{2,1,0:T(8,128)(2,1)S(1)}, bf16[3,192,128]{2,1,0:T(8,128)(2,1)S(1)}, u32[]{:S(2)}, u32[]{:S(2)}) collective-permute-start(bf16[3,192,128]{2,1,0:T(8,128)(2,1)S(1)} %join.1.rest_3_), channel_id=1, source_target_pairs={{0,2},{1,3},{2,0},{3,1},{4,6},{5,7},{6,4},{7,5},{8,10},{9,11},{10,... | collective-permute-start | bytes 442376 | tf_op jit(solution)/shard_map/ppermute | solution.py:302
  17.4 0.0 copy-start.1
  17.4 1.0 %copy-done.1 = bf16[1792,128]{1,0:T(8,128)(2,1)S(1)} copy-done((bf16[1792,128]{1,0:T(8,128)(2,1)S(1)}, bf16[1792,128]{1,0:T(8,128)(2,1)}, u32[]{:S(2)}) %copy-start.1) | copy-done | bytes 458776
  18.4 0.0 copy-start
  18.4 0.0 copy-start.2
  18.4 0.0 copy-start.4
  18.4 2.7 %mix.1.y_ref = bf16[6,2048,256]{2,1,0:T(8,128)(2,1)S(1)} custom-call(bf16[1792,128]{1,0:T(8,128)(2,1)S(1)} %copy-done.1), custom_call_target="tpu_custom_call" | custom-call | flops 201326592 | bytes 6291456 | tf_op jit(solution)/shard_map/mix/pallas_call | solution.py:354
  21.2 0.1 collective-permute-start.5
  21.2 0.8 %collective-permute-done.6.rest_5_ = bf16[3,192,128]{2,1,0:T(8,128)(2,1)S(1)} collective-permute-done((bf16[3,192,128]{2,1,0:T(8,128)(2,1)S(1)}, bf16[3,192,128]{2,1,0:T(8,128)(2,1)S(1)}, u32[]{:S(2)}, u32[]{:S(2)}) %collective-permute-start.6) | collective-permute-done | bytes 147488 | tf_op jit(solution)/shard_map/ppermute | solution.py:302
  22.0 0.0 collective-permute-start.8
  22.0 0.5 %collective-permute-start.7 = (bf16[1,192,128]{2,1,0:T(8,128)(2,1)S(1)}, bf16[1,192,128]{2,1,0:T(8,128)(2,1)S(1)}, u32[]{:S(2)}, u32[]{:S(2)}) collective-permute-start(bf16[1,192,128]{2,1,0:T(8,128)(2,1)S(1)} %collective-permute-done.3.rest_2_), channel_id=1, source_target_pairs={{0,1},{1,0},{2,3},{3,2},{4,5},{5,4},{6,7},{7,6},{8,9},{9,8},{10,11... | collective-permute-start | bytes 147464 | tf_op jit(solution)/shard_map/ppermute | solution.py:302
  22.5 0.1 collective-permute-done.5.rest_4_
  22.6 0.0 copy-done
  22.6 0.0 copy-done.2
  22.6 0.0 copy-done.4
  22.6 0.1 first_half.1
  22.7 0.7 %collective-permute-done.7.rest_0_ = bf16[1,192,128]{2,1,0:T(8,128)(2,1)S(1)} collective-permute-done((bf16[1,192,128]{2,1,0:T(8,128)(2,1)S(1)}, bf16[1,192,128]{2,1,0:T(8,128)(2,1)S(1)}, u32[]{:S(2)}, u32[]{:S(2)}) %collective-permute-start.7) | collective-permute-done | bytes 49184 | tf_op jit(solution)/shard_map/ppermute | solution.py:302
  23.5 0.0 collective-permute-done.8.rest_1_
  23.5 0.0 copy-start.3
  23.5 3.5 %pair.1 = (bf16[12,192,128]{2,1,0:T(8,128)(2,1)}, bf16[8,144,128]{2,1,0:T(8,128)(2,1)S(1)}, bf16[8,144,128]{2,1,0:T(8,128)(2,1)S(1)}, f32[3072,128]{1,0:T(8,128)S(1)}) custom-call(s32[1]{0:T(128)} %bitcast.row_ref, f32[424,128]{1,0:T(8,128)S(1)} %get-tuple-element.40.aux_ref, ...), custom_call_target="tpu_custom_call", output_to_operand_aliasing={{3}: (4, {})} | custom-call | flops 1207959552 | bytes 8650752 | tf_op jit(solution)/shard_map/pair/pallas_call | solution.py:413
  26.9 0.3 collective-permute-start.9
  27.2 1.3 %collective-permute-done.9.crossed_ref = bf16[8,144,128]{2,1,0:T(8,128)(2,1)S(1)} collective-permute-done((bf16[8,144,128]{2,1,0:T(8,128)(2,1)S(1)}, bf16[8,144,128]{2,1,0:T(8,128)(2,1)S(1)}, u32[]{:S(2)}, u32[]{:S(2)}) %collective-permute-start.9) | collective-permute-done | bytes 294944 | tf_op jit(solution)/shard_map/ppermute | solution.py:302
  28.6 1.4 %collective-permute-start.10 = (bf16[2,144,128]{2,1,0:T(8,128)(2,1)S(1)}, bf16[2,144,128]{2,1,0:T(8,128)(2,1)S(1)}, u32[]{:S(2)}, u32[]{:S(2)}) collective-permute-start(bf16[2,144,128]{2,1,0:T(8,128)(2,1)S(1)} %get-tuple-element.49), channel_id=1, source_target_pairs={{0,14},{1,7},{2,12},{3,5},{4,10},{5,3},{6,8},{7,1},{8,6},{9,15},{1... | collective-permute-start | bytes 221192 | tf_op jit(solution)/shard_map/ppermute | solution.py:302
  29.9 3.0 %collective-permute-start.11 = (bf16[2,144,128]{2,1,0:T(8,128)(2,1)S(1)}, bf16[2,144,128]{2,1,0:T(8,128)(2,1)S(1)}, u32[]{:S(2)}, u32[]{:S(2)}) collective-permute-start(bf16[2,144,128]{2,1,0:T(8,128)(2,1)S(1)} %get-tuple-element.50), channel_id=1, source_target_pairs={{0,12},{1,5},{2,14},{3,7},{4,8},{5,1},{6,10},{7,3},{8,4},{9,13},{1... | collective-permute-start | bytes 221192 | tf_op jit(solution)/shard_map/ppermute | solution.py:302
  32.9 0.0 collective-permute-start.12
  32.9 3.4 %collective-permute-start.13 = (bf16[2,144,128]{2,1,0:T(8,128)(2,1)S(1)}, bf16[2,144,128]{2,1,0:T(8,128)(2,1)S(1)}, u32[]{:S(2)}, u32[]{:S(2)}) collective-permute-start(bf16[2,144,128]{2,1,0:T(8,128)(2,1)S(1)} %get-tuple-element.52), channel_id=1, source_target_pairs={{0,8},{1,15},{2,10},{3,13},{4,12},{5,11},{6,14},{7,9},{8,0},{9,7},... | collective-permute-start | bytes 221192 | tf_op jit(solution)/shard_map/ppermute | solution.py:302
  36.3 0.0 collective-permute-start.14
  36.3 0.0 collective-permute-done.10.rest_1_
  36.3 2.5 %collective-permute-start.15 = (bf16[2,144,128]{2,1,0:T(8,128)(2,1)S(1)}, bf16[2,144,128]{2,1,0:T(8,128)(2,1)S(1)}, u32[]{:S(2)}, u32[]{:S(2)}) collective-permute-start(bf16[2,144,128]{2,1,0:T(8,128)(2,1)S(1)} %get-tuple-element.54), channel_id=1, source_target_pairs={{0,4},{1,11},{2,6},{3,9},{4,0},{5,15},{6,2},{7,13},{8,12},{9,3},{1... | collective-permute-start | bytes 221192 | tf_op jit(solution)/shard_map/ppermute | solution.py:302
  38.8 0.0 collective-permute-done.11.rest_2_
  38.8 1.0 %collective-permute-start.16 = (bf16[2,144,128]{2,1,0:T(8,128)(2,1)S(1)}, bf16[2,144,128]{2,1,0:T(8,128)(2,1)S(1)}, u32[]{:S(2)}, u32[]{:S(2)}) collective-permute-start(bf16[2,144,128]{2,1,0:T(8,128)(2,1)S(1)} %get-tuple-element.55), channel_id=1, source_target_pairs={{0,2},{1,9},{2,0},{3,11},{4,6},{5,13},{6,4},{7,15},{8,10},{9,1},{1... | collective-permute-start | bytes 221192 | tf_op jit(solution)/shard_map/ppermute | solution.py:302
  39.8 3.1 %collective-permute-done.12.rest_3_ = bf16[2,144,128]{2,1,0:T(8,128)(2,1)S(1)} collective-permute-done((bf16[2,144,128]{2,1,0:T(8,128)(2,1)S(1)}, bf16[2,144,128]{2,1,0:T(8,128)(2,1)S(1)}, u32[]{:S(2)}, u32[]{:S(2)}) %collective-permute-start.12) | collective-permute-done | bytes 73760 | tf_op jit(solution)/shard_map/ppermute | solution.py:302
  42.9 1.1 %collective-permute-done.13.rest_4_ = bf16[2,144,128]{2,1,0:T(8,128)(2,1)S(1)} collective-permute-done((bf16[2,144,128]{2,1,0:T(8,128)(2,1)S(1)}, bf16[2,144,128]{2,1,0:T(8,128)(2,1)S(1)}, u32[]{:S(2)}, u32[]{:S(2)}) %collective-permute-start.13) | collective-permute-done | bytes 73760 | tf_op jit(solution)/shard_map/ppermute | solution.py:302
  44.0 0.0 collective-permute-done.14.rest_5_
  44.0 0.0 collective-permute-done.15.rest_6_
  44.0 0.0 collective-permute-done.16.rest_7_
  44.0 0.0 copy-done.3
  44.1 2.9 %gate.1 = bf16[12,192,256]{2,1,0:T(8,128)(2,1)} custom-call(s32[1]{0:T(128)} %bitcast.row_ref, f32[424,128]{1,0:T(8,128)S(1)} %get-tuple-element.40.aux_ref, bf16[2,128,256]{2,1,0:T(8,128)(2,1)S(1)} %copy-done.3, bf16[2,144,128]{2,1,0:T(8,128)(2,1)S(1)} %get-tuple-element.48.rest_0_, bf16[2,144,128]{2,1,0:T(8,128)(2,1)S(1)} %collective-permute-done.10.rest_1_, ...), custom_call_target="tpu_custom_call" | custom-call | flops 301989888 | bytes 2949120 | tf_op jit(solution)/shard_map/gate/pallas_call | solution.py:449
  (2 shorter events, 0.1 us)
Async XLA Ops:
  3.4 7.5 %collective-permute-start.4 = (bf16[1,192,128]{2,1,0:T(8,128)(2,1)}, bf16[1,192,128]{2,1,0:T(8,128)(2,1)S(1)}, u32[]{:S(2)}, u32[]{:S(2)}) collective-permute-start(bf16[1,192,128]{2,1,0:T(8,128)(2,1)} %get-tuple-element.30.rest_0_), channel_id=1, source_target_pairs={{0,1},{1,0},{2,3},{3,2},{4,5},{5,4},{6,7},{7,6},{8,9},{9,8},{10,11... | collective-permute-start | bytes 147464 | tf_op jit(solution)/shard_map/ppermute | solution.py:302
  3.9 7.0 %collective-permute-start.3 = (bf16[1,192,128]{2,1,0:T(8,128)(2,1)}, bf16[1,192,128]{2,1,0:T(8,128)(2,1)S(1)}, u32[]{:S(2)}, u32[]{:S(2)}) collective-permute-start(bf16[1,192,128]{2,1,0:T(8,128)(2,1)} %get-tuple-element.30.rest_0_), channel_id=1, source_target_pairs={{0,2},{1,3},{2,0},{3,1},{4,6},{5,7},{6,4},{7,5},{8,10},{9,11},{10,... | collective-permute-start | bytes 147464 | tf_op jit(solution)/shard_map/ppermute | solution.py:302
  6.5 4.8 %collective-permute-start.2 = (bf16[1,192,128]{2,1,0:T(8,128)(2,1)}, bf16[1,192,128]{2,1,0:T(8,128)(2,1)S(1)}, u32[]{:S(2)}, u32[]{:S(2)}) collective-permute-start(bf16[1,192,128]{2,1,0:T(8,128)(2,1)} %get-tuple-element.30.rest_0_), channel_id=1, source_target_pairs={{0,4},{1,9},{2,6},{3,11},{4,0},{5,13},{6,2},{7,15},{8,12},{9,1},{1... | collective-permute-start | bytes 147464 | tf_op jit(solution)/shard_map/ppermute | solution.py:302
  8.1 6.7 %collective-permute-start.1 = (bf16[1,192,128]{2,1,0:T(8,128)(2,1)}, bf16[1,192,128]{2,1,0:T(8,128)(2,1)S(1)}, u32[]{:S(2)}, u32[]{:S(2)}) collective-permute-start(bf16[1,192,128]{2,1,0:T(8,128)(2,1)} %get-tuple-element.30.rest_0_), channel_id=1, source_target_pairs={{0,8},{1,13},{2,10},{3,15},{4,12},{5,9},{6,14},{7,11},{8,0},{9,5},... | collective-permute-start | bytes 147464 | tf_op jit(solution)/shard_map/ppermute | solution.py:302
  10.7 6.1 %collective-permute-start = (bf16[1,192,128]{2,1,0:T(8,128)(2,1)}, bf16[1,192,128]{2,1,0:T(8,128)(2,1)S(1)}, u32[]{:S(2)}, u32[]{:S(2)}) collective-permute-start(bf16[1,192,128]{2,1,0:T(8,128)(2,1)} %get-tuple-element.30.rest_0_), channel_id=1, source_target_pairs={{0,12},{1,5},{2,14},{3,7},{4,8},{5,1},{6,10},{7,3},{8,4},{9,13},{1... | collective-permute-start | bytes 147464 | tf_op jit(solution)/shard_map/ppermute | solution.py:302
  16.8 5.2 %collective-permute-start.6 = (bf16[3,192,128]{2,1,0:T(8,128)(2,1)S(1)}, bf16[3,192,128]{2,1,0:T(8,128)(2,1)S(1)}, u32[]{:S(2)}, u32[]{:S(2)}) collective-permute-start(bf16[3,192,128]{2,1,0:T(8,128)(2,1)S(1)} %join.1.rest_3_), channel_id=1, source_target_pairs={{0,2},{1,3},{2,0},{3,1},{4,6},{5,7},{6,4},{7,5},{8,10},{9,11},{10,... | collective-permute-start | bytes 442376 | tf_op jit(solution)/shard_map/ppermute | solution.py:302
  17.4 1.0 %copy-start.1 = (bf16[1792,128]{1,0:T(8,128)(2,1)S(1)}, bf16[1792,128]{1,0:T(8,128)(2,1)}, u32[]{:S(2)}) copy-start(bf16[1792,128]{1,0:T(8,128)(2,1)} %get-tuple-element.36.mix_ref) | copy-start | bytes 1376260
  18.4 4.2 %copy-start = (bf16[12,192,128]{2,1,0:T(8,128)(2,1)S(1)}, bf16[12,192,128]{2,1,0:T(8,128)(2,1)}, u32[]{:S(2)}) copy-start(bf16[12,192,128]{2,1,0:T(8,128)(2,1)} %state_ref.1) | copy-start | bytes 1769476
  18.4 4.2 %copy-start.2 = (f32[424,128]{1,0:T(8,128)S(1)}, f32[424,128]{1,0:T(8,128)}, u32[]{:S(2)}) copy-start(f32[424,128]{1,0:T(8,128)} %get-tuple-element.29.aux_ref) | copy-start | bytes 651268
  18.4 4.2 %copy-start.4 = (bf16[1,192,128]{2,1,0:T(8,128)(2,1)S(1)}, bf16[1,192,128]{2,1,0:T(8,128)(2,1)}, u32[]{:S(2)}) copy-start(bf16[1,192,128]{2,1,0:T(8,128)(2,1)} %get-tuple-element.30.rest_0_) | copy-start | bytes 147460
  21.2 1.4 %collective-permute-start.5 = (bf16[3,192,128]{2,1,0:T(8,128)(2,1)S(1)}, bf16[3,192,128]{2,1,0:T(8,128)(2,1)S(1)}, u32[]{:S(2)}, u32[]{:S(2)}) collective-permute-start(bf16[3,192,128]{2,1,0:T(8,128)(2,1)S(1)} %join.1.rest_3_), channel_id=1, source_target_pairs={{0,1},{1,0},{2,3},{3,2},{4,5},{5,4},{6,7},{7,6},{8,9},{9,8},{10,11... | collective-permute-start | bytes 442376 | tf_op jit(solution)/shard_map/ppermute | solution.py:302
  22.0 1.4 %collective-permute-start.8 = (bf16[3,192,128]{2,1,0:T(8,128)(2,1)S(1)}, bf16[3,192,128]{2,1,0:T(8,128)(2,1)S(1)}, u32[]{:S(2)}, u32[]{:S(2)}) collective-permute-start(bf16[3,192,128]{2,1,0:T(8,128)(2,1)S(1)} %collective-permute-done.6.rest_5_), channel_id=1, source_target_pairs={{0,1},{1,0},{2,3},{3,2},{4,5},{5,4},{6,7},{7,6},{8,9},{9,8},{10,11... | collective-permute-start | bytes 442376 | tf_op jit(solution)/shard_map/ppermute | solution.py:302
  22.0 1.4 %collective-permute-start.7 = (bf16[1,192,128]{2,1,0:T(8,128)(2,1)S(1)}, bf16[1,192,128]{2,1,0:T(8,128)(2,1)S(1)}, u32[]{:S(2)}, u32[]{:S(2)}) collective-permute-start(bf16[1,192,128]{2,1,0:T(8,128)(2,1)S(1)} %collective-permute-done.3.rest_2_), channel_id=1, source_target_pairs={{0,1},{1,0},{2,3},{3,2},{4,5},{5,4},{6,7},{7,6},{8,9},{9,8},{10,11... | collective-permute-start | bytes 147464 | tf_op jit(solution)/shard_map/ppermute | solution.py:302
  23.5 20.6 %copy-start.3 = (bf16[2,128,256]{2,1,0:T(8,128)(2,1)S(1)}, bf16[2,128,256]{2,1,0:T(8,128)(2,1)}, u32[]{:S(2)}) copy-start(bf16[2,128,256]{2,1,0:T(8,128)(2,1)} %get-tuple-element.45.gates_ref) | copy-start | bytes 393220
  26.9 1.6 %collective-permute-start.9 = (bf16[8,144,128]{2,1,0:T(8,128)(2,1)S(1)}, bf16[8,144,128]{2,1,0:T(8,128)(2,1)S(1)}, u32[]{:S(2)}, u32[]{:S(2)}) collective-permute-start(bf16[8,144,128]{2,1,0:T(8,128)(2,1)S(1)} %get-tuple-element.47), channel_id=1, source_target_pairs={{0,1},{1,0},{2,3},{3,2},{4,5},{5,4},{6,7},{7,6},{8,9},{9,8},{10,11... | collective-permute-start | bytes 884744 | tf_op jit(solution)/shard_map/ppermute | solution.py:302
  28.6 7.7 %collective-permute-start.10 = (bf16[2,144,128]{2,1,0:T(8,128)(2,1)S(1)}, bf16[2,144,128]{2,1,0:T(8,128)(2,1)S(1)}, u32[]{:S(2)}, u32[]{:S(2)}) collective-permute-start(bf16[2,144,128]{2,1,0:T(8,128)(2,1)S(1)} %get-tuple-element.49), channel_id=1, source_target_pairs={{0,14},{1,7},{2,12},{3,5},{4,10},{5,3},{6,8},{7,1},{8,6},{9,15},{1... | collective-permute-start | bytes 221192 | tf_op jit(solution)/shard_map/ppermute | solution.py:302
  29.9 8.8 %collective-permute-start.11 = (bf16[2,144,128]{2,1,0:T(8,128)(2,1)S(1)}, bf16[2,144,128]{2,1,0:T(8,128)(2,1)S(1)}, u32[]{:S(2)}, u32[]{:S(2)}) collective-permute-start(bf16[2,144,128]{2,1,0:T(8,128)(2,1)S(1)} %get-tuple-element.50), channel_id=1, source_target_pairs={{0,12},{1,5},{2,14},{3,7},{4,8},{5,1},{6,10},{7,3},{8,4},{9,13},{1... | collective-permute-start | bytes 221192 | tf_op jit(solution)/shard_map/ppermute | solution.py:302
  32.9 10.0 %collective-permute-start.12 = (bf16[2,144,128]{2,1,0:T(8,128)(2,1)S(1)}, bf16[2,144,128]{2,1,0:T(8,128)(2,1)S(1)}, u32[]{:S(2)}, u32[]{:S(2)}) collective-permute-start(bf16[2,144,128]{2,1,0:T(8,128)(2,1)S(1)} %get-tuple-element.51), channel_id=1, source_target_pairs={{0,10},{1,3},{2,8},{3,1},{4,14},{5,7},{6,12},{7,5},{8,2},{9,11},{1... | collective-permute-start | bytes 221192 | tf_op jit(solution)/shard_map/ppermute | solution.py:302
  32.9 11.1 %collective-permute-start.13 = (bf16[2,144,128]{2,1,0:T(8,128)(2,1)S(1)}, bf16[2,144,128]{2,1,0:T(8,128)(2,1)S(1)}, u32[]{:S(2)}, u32[]{:S(2)}) collective-permute-start(bf16[2,144,128]{2,1,0:T(8,128)(2,1)S(1)} %get-tuple-element.52), channel_id=1, source_target_pairs={{0,8},{1,15},{2,10},{3,13},{4,12},{5,11},{6,14},{7,9},{8,0},{9,7},... | collective-permute-start | bytes 221192 | tf_op jit(solution)/shard_map/ppermute | solution.py:302
  36.3 7.7 %collective-permute-start.14 = (bf16[2,144,128]{2,1,0:T(8,128)(2,1)S(1)}, bf16[2,144,128]{2,1,0:T(8,128)(2,1)S(1)}, u32[]{:S(2)}, u32[]{:S(2)}) collective-permute-start(bf16[2,144,128]{2,1,0:T(8,128)(2,1)S(1)} %get-tuple-element.53), channel_id=1, source_target_pairs={{0,6},{1,13},{2,4},{3,15},{4,2},{5,9},{6,0},{7,11},{8,14},{9,5},{1... | collective-permute-start | bytes 221192 | tf_op jit(solution)/shard_map/ppermute | solution.py:302
  36.3 7.7 %collective-permute-start.15 = (bf16[2,144,128]{2,1,0:T(8,128)(2,1)S(1)}, bf16[2,144,128]{2,1,0:T(8,128)(2,1)S(1)}, u32[]{:S(2)}, u32[]{:S(2)}) collective-permute-start(bf16[2,144,128]{2,1,0:T(8,128)(2,1)S(1)} %get-tuple-element.54), channel_id=1, source_target_pairs={{0,4},{1,11},{2,6},{3,9},{4,0},{5,15},{6,2},{7,13},{8,12},{9,3},{1... | collective-permute-start | bytes 221192 | tf_op jit(solution)/shard_map/ppermute | solution.py:302
  38.8 5.3 %collective-permute-start.16 = (bf16[2,144,128]{2,1,0:T(8,128)(2,1)S(1)}, bf16[2,144,128]{2,1,0:T(8,128)(2,1)S(1)}, u32[]{:S(2)}, u32[]{:S(2)}) collective-permute-start(bf16[2,144,128]{2,1,0:T(8,128)(2,1)S(1)} %get-tuple-element.55), channel_id=1, source_target_pairs={{0,2},{1,9},{2,0},{3,11},{4,6},{5,13},{6,4},{7,15},{8,10},{9,1},{1... | collective-permute-start | bytes 221192 | tf_op jit(solution)/shard_map/ppermute | solution.py:302

commit v12 on v11

--- a/solution.py
+++ b/solution.py
@@ -219,22 +219,12 @@
                 out_ref[1 - core] = crossed_ref[chip ^ pair[core]]
 
 
-def gate_kernel(pairs, row_ref, aux_ref, gates_ref, *rest):
-    tiles, (out_ref, wide_ref) = rest[:-2], rest[-2:]
-    step = pl.program_id(0)
-    block, total = out_ref.shape[:2]
+def gate_kernel(groups, row_ref, aux_ref, gates_ref, *rest):
+    tiles, (out_hbm, wide_ref, done_ref, sems) = rest[: 2 * len(groups)], rest[-4:]
+    tokens, total, gated = out_hbm.shape
     rows, width = tiles[0].shape[1:]
-    tokens = total // (2 * len(tiles))
-
-    @pl.when(step == 0)
-    def _():
-        chip = row_ref[0] >> 1
-        for pair, tile in zip(pairs, tiles):
-            source = chip ^ by_core(row_ref[0], pair)
-            for core in (0, 1):
-                spot = pl.ds(pl.multiple_of((source * 2 + core) * rows, rows), rows)
-                wide_ref[spot, :] = tile[core].astype(F32)
-
+    chip = row_ref[0] >> 1
+    band = 4 * tokens
     gain = aux_ref[2 * total + 34 : 2 * total + 35]
     shift = aux_ref[2 * total + 35 : 2 * total + 36]
     ones = jnp.full((width, width), 1.0 / width, BF16)
@@ -243,27 +233,38 @@
         [jnp.concatenate([ones, none], axis=1), jnp.concatenate([none, ones], axis=1)], axis=0
     )
     weights = jnp.concatenate([gates_ref[0], gates_ref[1]], axis=1)
-    gated = gates_ref.shape[2]
-    pair = jnp.concatenate(
-        [
-            jnp.concatenate(
-                [wide_ref[pl.ds(step * block + t + u, total, stride=tokens), :] for u in (0, 1)], axis=1
+    copies = []
+    for n, pairs in enumerate(groups):
+        for m, pair in enumerate(pairs):
+            source = chip ^ by_core(row_ref[0], pair)
+            for core in (0, 1):
+                spot = pl.ds(pl.multiple_of(((source & 1) * 2 + core) * rows, rows), rows)
+                wide_ref[n, spot, :] = tiles[2 * n + m][core].astype(F32)
+        place = source >> 1
+        parts = [wide_ref[n, pl.ds(j, band, stride=tokens), :] for j in range(tokens)]
+        half = tokens // 2
+        pair = jnp.concatenate(
+            [jnp.concatenate(parts[:half], axis=0), jnp.concatenate(parts[half:], axis=0)], axis=1
+        )
+        centre = pair - jnp.dot(pair.astype(BF16), means, preferred_element_type=F32)
+        square = (centre * centre).astype(BF16)
+        spread = jnp.dot(square, means, preferred_element_type=F32)
+        scaled = centre * lax.rsqrt(spread + 1e-05)
+        scaled = jnp.concatenate([scaled[:, 0:width], scaled[:, width : 2 * width]], axis=0)
+        normed = (scaled * gain + shift).astype(BF16)
+        mixed = jnp.dot(normed, weights, preferred_element_type=F32)
+        result = (mixed[:, 0:gated] * (0.5 + 0.5 * jnp.tanh(0.5 * mixed[:, gated : 2 * gated]))).astype(BF16)
+        for j in range(tokens):
+            done_ref[n, j] = result[j * band : (j + 1) * band]
+        copies.append(
+            pltpu.make_async_copy(
+                done_ref.at[n],
+                out_hbm.at[:, pl.ds(pl.multiple_of(place * band, band), band), :],
+                sems.at[n],
             )
-            for t in range(0, block, 2)
-        ],
-        axis=0,
-    )
-    centre = pair - jnp.dot(pair.astype(BF16), means, preferred_element_type=F32)
-    square = (centre * centre).astype(BF16)
-    spread = jnp.dot(square, means, preferred_element_type=F32)
-    scaled = centre * lax.rsqrt(spread + 1e-05)
-    scaled = jnp.concatenate([scaled[:, 0:width], scaled[:, width : 2 * width]], axis=0)
-    normed = (scaled * gain + shift).astype(BF16)
-    mixed = jnp.dot(normed, weights, preferred_element_type=F32)
-    result = (mixed[:, 0:gated] * (0.5 + 0.5 * jnp.tanh(0.5 * mixed[:, gated : 2 * gated]))).astype(BF16)
-    for t in range(block):
-        first = (t % 2 * (block // 2) + t // 2) * total
-        out_ref[t] = result[first : first + total]
+        )
+        copies[-1].start()
+    finish(copies)
 
 
 def fixed(*shape):
@@ -434,7 +435,12 @@
     )(row, aux, state, y, wide, own_late, late)
 
     crossed = swap(cross, 1)
-    sends = [(0, 0)] + staggered(list(range(chips - 1, 0, -1)))
+    others = staggered([(k, k - 1) for k in range(chips - 1, 1, -2)])
+    others = [[(a[m], b[m]) for m in (0, 1)] for a, b in others]
+    cut = (len(others) + 1) // 2
+    first, last = others[:cut], [[(0, 0), (1, 1)]] + others[cut:]
+    sends = [(0, 0)] + [pair for group in first for pair in group] + [(1, 1)]
+    sends += [pair for group in others[cut:] for pair in group]
     tiles = pl.pallas_call(
         functools.partial(pack_kernel, sends),
         out_shape=(jax.ShapeDtypeStruct((2, tile, width), BF16),) * chips,
@@ -445,22 +451,31 @@
     )(row, same, crossed)
     tiles = [tiles[0]] + [swap(t, (2 * a, 2 * b)) for t, (a, b) in zip(tiles[1:], sends[1:])]
 
-    block = 4
-    out = pl.pallas_call(
-        functools.partial(gate_kernel, sends),
-        grid=(tokens // block,),
-        out_shape=jax.ShapeDtypeStruct((tokens, total, gated), BF16),
-        in_specs=[whole(SMEM)] + [whole(VMEM)] * (2 + chips),
-        out_specs=pl.BlockSpec((block, total, gated), lambda j: (j, 0, 0)),
-        scratch_shapes=[VMEM((count * tile, width), F32)],
-        compiler_params=params(24),
-        cost_estimate=pl.CostEstimate(
-            flops=4 * tokens * total * width * gated,
-            bytes_accessed=tokens * total * (2 * gated + 6 * width),
-            transcendentals=tokens * total * gated,
-        ),
-        name="gate",
-    )(row, aux, gates, *tiles)
+    by_send = dict(zip(sends, tiles))
+
+    def gate(groups, name, *before):
+        given = [by_send[pair] for group in groups for pair in group]
+        return pl.pallas_call(
+            functools.partial(gate_kernel, groups),
+            out_shape=jax.ShapeDtypeStruct((tokens, total, gated), BF16),
+            in_specs=[whole(SMEM)] + [whole(VMEM)] * (2 + len(given)) + [whole(HBM)] * len(before),
+            out_specs=whole(HBM),
+            scratch_shapes=[
+                VMEM((len(groups), 4 * tile, width), F32),
+                VMEM((len(groups), tokens, 4 * tokens, gated), BF16),
+                pltpu.SemaphoreType.DMA((len(groups),)),
+            ],
+            input_output_aliases={3 + len(given): 0} if before else {},
+            compiler_params=params(24),
+            cost_estimate=pl.CostEstimate(
+                flops=2 * tokens * total * width * gated,
+                bytes_accessed=tokens * total * (gated + 3 * width),
+                transcendentals=tokens * total * gated // 2,
+            ),
+            name=name,
+        )(row, aux, gates, *given, *before)
+
+    out = gate(last, "gate_last", gate(first, "gate_first"))
     return pair_next, out.transpose(1, 0, 2)
 
 

time: 47.7 us -> 47.9 us (level); the launches traced: 46.9 us -> 47.7 us
  Pallas kernels: 12.1 us -> 12.7 us
    pallas_call x1 -> x2, Pallas kernels: 2.88 us -> 3.49 us  [gate(): pl.pallas_call(functools.partial(gate_kernel, groups), out_shape=jax.Shap...]
  transfers between devices with their start and end apart: 17 -> 17, of which waited for: 9 -> 9; matrix products, arithmetic and copies ran while one was open for 0% -> 0% of each run, Pallas kernels for 6% -> 10%
where the time goes in v12:
time: 47.9 us; the launch traced here: 47.7 us
  starting transfers between devices  20.1 us (42%)
  waiting for transfers between devices  13.2 us (28%)
  Pallas kernels  12.7 us (27%)
  local copies, waits for them, and re-layouts  1.03 us (2%)
  between operations  0.74 us (2%)
    ppermute x17, starting transfers between devices, swap(): lax.ppermute(array, 'row', [(r, r ^ bits[r & 1]) for r in range(count)])  20.1 us
    ppermute x17, waiting for transfers between devices, swap(): lax.ppermute(array, 'row', [(r, r ^ bits[r & 1]) for r in range(count)])  13.2 us
    pallas_call x2, Pallas kernels, gate(): pl.pallas_call(functools.partial(gate_kernel, groups), out_shape=jax.Shap...  3.49 us
    pallas_call x1, Pallas kernels, body(): pl.pallas_call(functools.partial(pair_kernel, [[(3, 3)], ranks(3)]), grid...  3.47 us
    pallas_call x1, Pallas kernels, body(): pl.pallas_call(prepare_kernel, out_shape=(jax.ShapeDtypeStruct((mix_rows,...  2.77 us
    pallas_call x1, Pallas kernels, body(): pl.pallas_call(functools.partial(mix_kernel, factor), out_shape=jax.Shape...  2.74 us
    unnamed x10, local copies, waits for them, and re-layouts  1.03 us
  transfers between devices with their start and end apart: 17, of which 9 were waited for; matrix products, arithmetic and copies ran while one was open for 0% of the time, Pallas kernels for 10%

profile of v12, /device:TPU:0, one launch (start us, length us, event | category | flops | bytes accessed | tf_op | source)
XLA Modules:
  0.0 47.7 jit_solution(11768882846801346623)
XLA Ops:
  0.6 2.8 %prepare.1 = (bf16[1792,128]{1,0:T(8,128)(2,1)}, bf16[1,192,128]{2,1,0:T(8,128)(2,1)}, f32[424,128]{1,0:T(8,128)}, bf16[2,128,256]{2,1,0:T(8,128)(2,1)}) custom-call(s32[1]{0:T(128)} %bitcast.row_ref, s32[192]{0:T(256)} %depth_hbm.1, bf16[12,64,64]{2,1,0:T(8,128)(2,1)} %bitcast.14, f32[1,64]{1,0:T(1,128)} %bitcast.19, f32[1,64]{1,0:T(1,128)} %bitcast.20, ...), custom_call_target="tpu_custom_call" | custom-call | tf_op jit(solution)/shard_map/prepare/pallas_call | solution.py:312
  3.4 0.5 %collective-permute-start.4 = (bf16[1,192,128]{2,1,0:T(8,128)(2,1)}, bf16[1,192,128]{2,1,0:T(8,128)(2,1)S(1)}, u32[]{:S(2)}, u32[]{:S(2)}) collective-permute-start(bf16[1,192,128]{2,1,0:T(8,128)(2,1)} %get-tuple-element.30.rest_0_), channel_id=1, source_target_pairs={{0,1},{1,0},{2,3},{3,2},{4,5},{5,4},{6,7},{7,6},{8,9},{9,8},{10,11... | collective-permute-start | bytes 147464 | tf_op jit(solution)/shard_map/ppermute | solution.py:303
  3.9 2.6 %collective-permute-start.3 = (bf16[1,192,128]{2,1,0:T(8,128)(2,1)}, bf16[1,192,128]{2,1,0:T(8,128)(2,1)S(1)}, u32[]{:S(2)}, u32[]{:S(2)}) collective-permute-start(bf16[1,192,128]{2,1,0:T(8,128)(2,1)} %get-tuple-element.30.rest_0_), channel_id=1, source_target_pairs={{0,2},{1,3},{2,0},{3,1},{4,6},{5,7},{6,4},{7,5},{8,10},{9,11},{10,... | collective-permute-start | bytes 147464 | tf_op jit(solution)/shard_map/ppermute | solution.py:303
  6.5 1.6 %collective-permute-start.2 = (bf16[1,192,128]{2,1,0:T(8,128)(2,1)}, bf16[1,192,128]{2,1,0:T(8,128)(2,1)S(1)}, u32[]{:S(2)}, u32[]{:S(2)}) collective-permute-start(bf16[1,192,128]{2,1,0:T(8,128)(2,1)} %get-tuple-element.30.rest_0_), channel_id=1, source_target_pairs={{0,4},{1,9},{2,6},{3,11},{4,0},{5,13},{6,2},{7,15},{8,12},{9,1},{1... | collective-permute-start | bytes 147464 | tf_op jit(solution)/shard_map/ppermute | solution.py:303
  8.1 2.6 %collective-permute-start.1 = (bf16[1,192,128]{2,1,0:T(8,128)(2,1)}, bf16[1,192,128]{2,1,0:T(8,128)(2,1)S(1)}, u32[]{:S(2)}, u32[]{:S(2)}) collective-permute-start(bf16[1,192,128]{2,1,0:T(8,128)(2,1)} %get-tuple-element.30.rest_0_), channel_id=1, source_target_pairs={{0,8},{1,13},{2,10},{3,15},{4,12},{5,9},{6,14},{7,11},{8,0},{9,5},... | collective-permute-start | bytes 147464 | tf_op jit(solution)/shard_map/ppermute | solution.py:303
  10.7 0.2 collective-permute-start
  10.9 0.0 collective-permute-done.4.rest_1_
  10.9 0.0 collective-permute-done.3.rest_2_
  10.9 0.4 collective-permute-done.2.refs_2_
  11.4 3.5 %collective-permute-done.1.refs_1_ = bf16[1,192,128]{2,1,0:T(8,128)(2,1)S(1)} collective-permute-done((bf16[1,192,128]{2,1,0:T(8,128)(2,1)}, bf16[1,192,128]{2,1,0:T(8,128)(2,1)S(1)}, u32[]{:S(2)}, u32[]{:S(2)}) %collective-permute-start.1) | collective-permute-done | bytes 49184 | tf_op jit(solution)/shard_map/ppermute | solution.py:303
  14.8 2.0 %collective-permute-done.refs_0_ = bf16[1,192,128]{2,1,0:T(8,128)(2,1)S(1)} collective-permute-done((bf16[1,192,128]{2,1,0:T(8,128)(2,1)}, bf16[1,192,128]{2,1,0:T(8,128)(2,1)S(1)}, u32[]{:S(2)}, u32[]{:S(2)}) %collective-permute-start) | collective-permute-done | bytes 49184 | tf_op jit(solution)/shard_map/ppermute | solution.py:303
  16.8 0.6 %collective-permute-start.6 = (bf16[3,192,128]{2,1,0:T(8,128)(2,1)S(1)}, bf16[3,192,128]{2,1,0:T(8,128)(2,1)S(1)}, u32[]{:S(2)}, u32[]{:S(2)}) collective-permute-start(bf16[3,192,128]{2,1,0:T(8,128)(2,1)S(1)} %join.1.rest_3_), channel_id=1, source_target_pairs={{0,2},{1,3},{2,0},{3,1},{4,6},{5,7},{6,4},{7,5},{8,10},{9,11},{10,... | collective-permute-start | bytes 442376 | tf_op jit(solution)/shard_map/ppermute | solution.py:303
  17.4 0.0 copy-start.2
  17.4 1.0 %copy-done.2 = bf16[1792,128]{1,0:T(8,128)(2,1)S(1)} copy-done((bf16[1792,128]{1,0:T(8,128)(2,1)S(1)}, bf16[1792,128]{1,0:T(8,128)(2,1)}, u32[]{:S(2)}) %copy-start.2) | copy-done | bytes 458776
  18.4 0.0 copy-start
  18.4 0.0 copy-start.3
  18.4 0.0 copy-start.4
  18.4 2.7 %mix.1.y_ref = bf16[6,2048,256]{2,1,0:T(8,128)(2,1)S(1)} custom-call(bf16[1792,128]{1,0:T(8,128)(2,1)S(1)} %copy-done.2), custom_call_target="tpu_custom_call" | custom-call | flops 201326592 | bytes 6291456 | tf_op jit(solution)/shard_map/mix/pallas_call | solution.py:355
  21.2 0.1 collective-permute-start.5
  21.2 0.8 %collective-permute-done.6.rest_5_ = bf16[3,192,128]{2,1,0:T(8,128)(2,1)S(1)} collective-permute-done((bf16[3,192,128]{2,1,0:T(8,128)(2,1)S(1)}, bf16[3,192,128]{2,1,0:T(8,128)(2,1)S(1)}, u32[]{:S(2)}, u32[]{:S(2)}) %collective-permute-start.6) | collective-permute-done | bytes 147488 | tf_op jit(solution)/shard_map/ppermute | solution.py:303
  22.0 0.0 collective-permute-start.8
  22.0 0.5 %collective-permute-start.7 = (bf16[1,192,128]{2,1,0:T(8,128)(2,1)S(1)}, bf16[1,192,128]{2,1,0:T(8,128)(2,1)S(1)}, u32[]{:S(2)}, u32[]{:S(2)}) collective-permute-start(bf16[1,192,128]{2,1,0:T(8,128)(2,1)S(1)} %collective-permute-done.3.rest_2_), channel_id=1, source_target_pairs={{0,1},{1,0},{2,3},{3,2},{4,5},{5,4},{6,7},{7,6},{8,9},{9,8},{10,11... | collective-permute-start | bytes 147464 | tf_op jit(solution)/shard_map/ppermute | solution.py:303
  22.5 0.1 collective-permute-done.5.rest_4_
  22.6 0.0 copy-done
  22.6 0.0 copy-done.3
  22.6 0.0 copy-done.4
  22.6 0.1 first_half.1
  22.7 0.7 %collective-permute-done.7.rest_0_ = bf16[1,192,128]{2,1,0:T(8,128)(2,1)S(1)} collective-permute-done((bf16[1,192,128]{2,1,0:T(8,128)(2,1)S(1)}, bf16[1,192,128]{2,1,0:T(8,128)(2,1)S(1)}, u32[]{:S(2)}, u32[]{:S(2)}) %collective-permute-start.7) | collective-permute-done | bytes 49184 | tf_op jit(solution)/shard_map/ppermute | solution.py:303
  23.5 0.0 collective-permute-done.8.rest_1_
  23.5 0.0 copy-start.1
  23.5 3.5 %pair.1 = (bf16[12,192,128]{2,1,0:T(8,128)(2,1)}, bf16[8,144,128]{2,1,0:T(8,128)(2,1)S(1)}, bf16[8,144,128]{2,1,0:T(8,128)(2,1)S(1)}, f32[3072,128]{1,0:T(8,128)S(1)}) custom-call(s32[1]{0:T(128)} %bitcast.row_ref, f32[424,128]{1,0:T(8,128)S(1)} %get-tuple-element.40.aux_ref, ...), custom_call_target="tpu_custom_call", output_to_operand_aliasing={{3}: (4, {})} | custom-call | flops 1207959552 | bytes 8650752 | tf_op jit(solution)/shard_map/pair/pallas_call | solution.py:414
  26.9 0.3 collective-permute-start.9
  27.2 1.3 %collective-permute-done.9.crossed_ref = bf16[8,144,128]{2,1,0:T(8,128)(2,1)S(1)} collective-permute-done((bf16[8,144,128]{2,1,0:T(8,128)(2,1)S(1)}, bf16[8,144,128]{2,1,0:T(8,128)(2,1)S(1)}, u32[]{:S(2)}, u32[]{:S(2)}) %collective-permute-start.9) | collective-permute-done | bytes 294944 | tf_op jit(solution)/shard_map/ppermute | solution.py:303
  28.6 1.4 %collective-permute-start.13 = (bf16[2,144,128]{2,1,0:T(8,128)(2,1)S(1)}, bf16[2,144,128]{2,1,0:T(8,128)(2,1)S(1)}, u32[]{:S(2)}, u32[]{:S(2)}) collective-permute-start(bf16[2,144,128]{2,1,0:T(8,128)(2,1)S(1)} %get-tuple-element.52), channel_id=1, source_target_pairs={{0,14},{1,7},{2,12},{3,5},{4,10},{5,3},{6,8},{7,1},{8,6},{9,15},{1... | collective-permute-start | bytes 221192 | tf_op jit(solution)/shard_map/ppermute | solution.py:303
  29.9 3.0 %collective-permute-start.14 = (bf16[2,144,128]{2,1,0:T(8,128)(2,1)S(1)}, bf16[2,144,128]{2,1,0:T(8,128)(2,1)S(1)}, u32[]{:S(2)}, u32[]{:S(2)}) collective-permute-start(bf16[2,144,128]{2,1,0:T(8,128)(2,1)S(1)} %get-tuple-element.53), channel_id=1, source_target_pairs={{0,12},{1,5},{2,14},{3,7},{4,8},{5,1},{6,10},{7,3},{8,4},{9,13},{1... | collective-permute-start | bytes 221192 | tf_op jit(solution)/shard_map/ppermute | solution.py:303
  32.9 0.0 collective-permute-start.15
  32.9 3.4 %collective-permute-start.16 = (bf16[2,144,128]{2,1,0:T(8,128)(2,1)S(1)}, bf16[2,144,128]{2,1,0:T(8,128)(2,1)S(1)}, u32[]{:S(2)}, u32[]{:S(2)}) collective-permute-start(bf16[2,144,128]{2,1,0:T(8,128)(2,1)S(1)} %get-tuple-element.55), channel_id=1, source_target_pairs={{0,8},{1,13},{2,10},{3,15},{4,12},{5,9},{6,14},{7,11},{8,0},{9,5},... | collective-permute-start | bytes 221192 | tf_op jit(solution)/shard_map/ppermute | solution.py:303
  36.3 1.0 %collective-permute-start.10 = (bf16[2,144,128]{2,1,0:T(8,128)(2,1)S(1)}, bf16[2,144,128]{2,1,0:T(8,128)(2,1)S(1)}, u32[]{:S(2)}, u32[]{:S(2)}) collective-permute-start(bf16[2,144,128]{2,1,0:T(8,128)(2,1)S(1)} %get-tuple-element.49), channel_id=1, source_target_pairs={{0,2},{1,3},{2,0},{3,1},{4,6},{5,7},{6,4},{7,5},{8,10},{9,11},{10,... | collective-permute-start | bytes 221192 | tf_op jit(solution)/shard_map/ppermute | solution.py:303
  37.3 0.0 collective-permute-done.13.rest_0_
  37.3 0.0 collective-permute-start.11
  37.3 0.0 collective-permute-done.14.rest_1_
  37.3 2.5 %collective-permute-start.12 = (bf16[2,144,128]{2,1,0:T(8,128)(2,1)S(1)}, bf16[2,144,128]{2,1,0:T(8,128)(2,1)S(1)}, u32[]{:S(2)}, u32[]{:S(2)}) collective-permute-start(bf16[2,144,128]{2,1,0:T(8,128)(2,1)S(1)} %get-tuple-element.51), channel_id=1, source_target_pairs={{0,4},{1,9},{2,6},{3,11},{4,0},{5,13},{6,2},{7,15},{8,12},{9,1},{1... | collective-permute-start | bytes 221192 | tf_op jit(solution)/shard_map/ppermute | solution.py:303
  39.8 3.3 %collective-permute-done.15.rest_2_ = bf16[2,144,128]{2,1,0:T(8,128)(2,1)S(1)} collective-permute-done((bf16[2,144,128]{2,1,0:T(8,128)(2,1)S(1)}, bf16[2,144,128]{2,1,0:T(8,128)(2,1)S(1)}, u32[]{:S(2)}, u32[]{:S(2)}) %collective-permute-start.15) | collective-permute-done | bytes 73760 | tf_op jit(solution)/shard_map/ppermute | solution.py:303
  43.1 1.2 %collective-permute-done.16.rest_3_ = bf16[2,144,128]{2,1,0:T(8,128)(2,1)S(1)} collective-permute-done((bf16[2,144,128]{2,1,0:T(8,128)(2,1)S(1)}, bf16[2,144,128]{2,1,0:T(8,128)(2,1)S(1)}, u32[]{:S(2)}, u32[]{:S(2)}) %collective-permute-start.16) | collective-permute-done | bytes 73760 | tf_op jit(solution)/shard_map/ppermute | solution.py:303
  44.2 0.0 copy-done.1
  44.2 1.7 %gate_first.1.rest_4_ = bf16[12,192,256]{2,1,0:T(8,128)(2,1)} custom-call(s32[1]{0:T(128)} %bitcast.row_ref, f32[424,128]{1,0:T(8,128)S(1)} %get-tuple-element.40.aux_ref, bf16[2,128,256]{2,1,0:T(8,128)(2,1)S(1)} %copy-done.1, bf16[2,144,128]{2,1,0:T(8,128)(2,1)S(1)} %collective-permute-done.13.rest_0_, ...), custom_call_target="tpu_custom_call" | custom-call | flops 150994944 | bytes 1474560 | tf_op jit(solution)/shard_map/gate_first/pallas_call | solution.py:458
  46.0 0.0 collective-permute-done.10.rest_1_
  46.0 0.0 collective-permute-done.11.rest_2_
  46.0 0.0 collective-permute-done.12.rest_3_
  46.0 1.7 %gate_last.1 = bf16[12,192,256]{2,1,0:T(8,128)(2,1)} custom-call(s32[1]{0:T(128)} %bitcast.row_ref, f32[424,128]{1,0:T(8,128)S(1)} %get-tuple-element.40.aux_ref, bf16[2,128,256]{2,1,0:T(8,128)(2,1)S(1)} %copy-done.1, bf16[2,144,128]{2,1,0:T(8,128)(2,1)S(1)} %get-tuple-element.48.rest_0_, ...), custom_call_target="tpu_custom_call", output_to_operand_aliasing={{}: (7, {})} | custom-call | flops 150994944 | bytes 1474560 | tf_op jit(solution)/shard_map/gate_last/pallas_call | solution.py:458
  (2 shorter events, 0.1 us)
Async XLA Ops:
  3.4 7.5 %collective-permute-start.4 = (bf16[1,192,128]{2,1,0:T(8,128)(2,1)}, bf16[1,192,128]{2,1,0:T(8,128)(2,1)S(1)}, u32[]{:S(2)}, u32[]{:S(2)}) collective-permute-start(bf16[1,192,128]{2,1,0:T(8,128)(2,1)} %get-tuple-element.30.rest_0_), channel_id=1, source_target_pairs={{0,1},{1,0},{2,3},{3,2},{4,5},{5,4},{6,7},{7,6},{8,9},{9,8},{10,11... | collective-permute-start | bytes 147464 | tf_op jit(solution)/shard_map/ppermute | solution.py:303
  3.9 7.0 %collective-permute-start.3 = (bf16[1,192,128]{2,1,0:T(8,128)(2,1)}, bf16[1,192,128]{2,1,0:T(8,128)(2,1)S(1)}, u32[]{:S(2)}, u32[]{:S(2)}) collective-permute-start(bf16[1,192,128]{2,1,0:T(8,128)(2,1)} %get-tuple-element.30.rest_0_), channel_id=1, source_target_pairs={{0,2},{1,3},{2,0},{3,1},{4,6},{5,7},{6,4},{7,5},{8,10},{9,11},{10,... | collective-permute-start | bytes 147464 | tf_op jit(solution)/shard_map/ppermute | solution.py:303
  6.5 4.8 %collective-permute-start.2 = (bf16[1,192,128]{2,1,0:T(8,128)(2,1)}, bf16[1,192,128]{2,1,0:T(8,128)(2,1)S(1)}, u32[]{:S(2)}, u32[]{:S(2)}) collective-permute-start(bf16[1,192,128]{2,1,0:T(8,128)(2,1)} %get-tuple-element.30.rest_0_), channel_id=1, source_target_pairs={{0,4},{1,9},{2,6},{3,11},{4,0},{5,13},{6,2},{7,15},{8,12},{9,1},{1... | collective-permute-start | bytes 147464 | tf_op jit(solution)/shard_map/ppermute | solution.py:303
  8.1 6.7 %collective-permute-start.1 = (bf16[1,192,128]{2,1,0:T(8,128)(2,1)}, bf16[1,192,128]{2,1,0:T(8,128)(2,1)S(1)}, u32[]{:S(2)}, u32[]{:S(2)}) collective-permute-start(bf16[1,192,128]{2,1,0:T(8,128)(2,1)} %get-tuple-element.30.rest_0_), channel_id=1, source_target_pairs={{0,8},{1,13},{2,10},{3,15},{4,12},{5,9},{6,14},{7,11},{8,0},{9,5},... | collective-permute-start | bytes 147464 | tf_op jit(solution)/shard_map/ppermute | solution.py:303
  10.7 6.1 %collective-permute-start = (bf16[1,192,128]{2,1,0:T(8,128)(2,1)}, bf16[1,192,128]{2,1,0:T(8,128)(2,1)S(1)}, u32[]{:S(2)}, u32[]{:S(2)}) collective-permute-start(bf16[1,192,128]{2,1,0:T(8,128)(2,1)} %get-tuple-element.30.rest_0_), channel_id=1, source_target_pairs={{0,12},{1,5},{2,14},{3,7},{4,8},{5,1},{6,10},{7,3},{8,4},{9,13},{1... | collective-permute-start | bytes 147464 | tf_op jit(solution)/shard_map/ppermute | solution.py:303
  16.8 5.2 %collective-permute-start.6 = (bf16[3,192,128]{2,1,0:T(8,128)(2,1)S(1)}, bf16[3,192,128]{2,1,0:T(8,128)(2,1)S(1)}, u32[]{:S(2)}, u32[]{:S(2)}) collective-permute-start(bf16[3,192,128]{2,1,0:T(8,128)(2,1)S(1)} %join.1.rest_3_), channel_id=1, source_target_pairs={{0,2},{1,3},{2,0},{3,1},{4,6},{5,7},{6,4},{7,5},{8,10},{9,11},{10,... | collective-permute-start | bytes 442376 | tf_op jit(solution)/shard_map/ppermute | solution.py:303
  17.4 1.0 %copy-start.2 = (bf16[1792,128]{1,0:T(8,128)(2,1)S(1)}, bf16[1792,128]{1,0:T(8,128)(2,1)}, u32[]{:S(2)}) copy-start(bf16[1792,128]{1,0:T(8,128)(2,1)} %get-tuple-element.36.mix_ref) | copy-start | bytes 1376260
  18.4 4.2 %copy-start = (bf16[12,192,128]{2,1,0:T(8,128)(2,1)S(1)}, bf16[12,192,128]{2,1,0:T(8,128)(2,1)}, u32[]{:S(2)}) copy-start(bf16[12,192,128]{2,1,0:T(8,128)(2,1)} %state_ref.1) | copy-start | bytes 1769476
  18.4 4.2 %copy-start.3 = (f32[424,128]{1,0:T(8,128)S(1)}, f32[424,128]{1,0:T(8,128)}, u32[]{:S(2)}) copy-start(f32[424,128]{1,0:T(8,128)} %get-tuple-element.29.aux_ref) | copy-start | bytes 651268
  18.4 4.2 %copy-start.4 = (bf16[1,192,128]{2,1,0:T(8,128)(2,1)S(1)}, bf16[1,192,128]{2,1,0:T(8,128)(2,1)}, u32[]{:S(2)}) copy-start(bf16[1,192,128]{2,1,0:T(8,128)(2,1)} %get-tuple-element.30.rest_0_) | copy-start | bytes 147460
  21.2 1.4 %collective-permute-start.5 = (bf16[3,192,128]{2,1,0:T(8,128)(2,1)S(1)}, bf16[3,192,128]{2,1,0:T(8,128)(2,1)S(1)}, u32[]{:S(2)}, u32[]{:S(2)}) collective-permute-start(bf16[3,192,128]{2,1,0:T(8,128)(2,1)S(1)} %join.1.rest_3_), channel_id=1, source_target_pairs={{0,1},{1,0},{2,3},{3,2},{4,5},{5,4},{6,7},{7,6},{8,9},{9,8},{10,11... | collective-permute-start | bytes 442376 | tf_op jit(solution)/shard_map/ppermute | solution.py:303
  22.0 1.4 %collective-permute-start.8 = (bf16[3,192,128]{2,1,0:T(8,128)(2,1)S(1)}, bf16[3,192,128]{2,1,0:T(8,128)(2,1)S(1)}, u32[]{:S(2)}, u32[]{:S(2)}) collective-permute-start(bf16[3,192,128]{2,1,0:T(8,128)(2,1)S(1)} %collective-permute-done.6.rest_5_), channel_id=1, source_target_pairs={{0,1},{1,0},{2,3},{3,2},{4,5},{5,4},{6,7},{7,6},{8,9},{9,8},{10,11... | collective-permute-start | bytes 442376 | tf_op jit(solution)/shard_map/ppermute | solution.py:303
  22.0 1.4 %collective-permute-start.7 = (bf16[1,192,128]{2,1,0:T(8,128)(2,1)S(1)}, bf16[1,192,128]{2,1,0:T(8,128)(2,1)S(1)}, u32[]{:S(2)}, u32[]{:S(2)}) collective-permute-start(bf16[1,192,128]{2,1,0:T(8,128)(2,1)S(1)} %collective-permute-done.3.rest_2_), channel_id=1, source_target_pairs={{0,1},{1,0},{2,3},{3,2},{4,5},{5,4},{6,7},{7,6},{8,9},{9,8},{10,11... | collective-permute-start | bytes 147464 | tf_op jit(solution)/shard_map/ppermute | solution.py:303
  23.5 20.7 %copy-start.1 = (bf16[2,128,256]{2,1,0:T(8,128)(2,1)S(1)}, bf16[2,128,256]{2,1,0:T(8,128)(2,1)}, u32[]{:S(2)}) copy-start(bf16[2,128,256]{2,1,0:T(8,128)(2,1)} %get-tuple-element.45.gates_ref) | copy-start | bytes 393220
  26.9 1.6 %collective-permute-start.9 = (bf16[8,144,128]{2,1,0:T(8,128)(2,1)S(1)}, bf16[8,144,128]{2,1,0:T(8,128)(2,1)S(1)}, u32[]{:S(2)}, u32[]{:S(2)}) collective-permute-start(bf16[8,144,128]{2,1,0:T(8,128)(2,1)S(1)} %get-tuple-element.47), channel_id=1, source_target_pairs={{0,1},{1,0},{2,3},{3,2},{4,5},{5,4},{6,7},{7,6},{8,9},{9,8},{10,11... | collective-permute-start | bytes 884744 | tf_op jit(solution)/shard_map/ppermute | solution.py:303
  28.6 8.7 %collective-permute-start.13 = (bf16[2,144,128]{2,1,0:T(8,128)(2,1)S(1)}, bf16[2,144,128]{2,1,0:T(8,128)(2,1)S(1)}, u32[]{:S(2)}, u32[]{:S(2)}) collective-permute-start(bf16[2,144,128]{2,1,0:T(8,128)(2,1)S(1)} %get-tuple-element.52), channel_id=1, source_target_pairs={{0,14},{1,7},{2,12},{3,5},{4,10},{5,3},{6,8},{7,1},{8,6},{9,15},{1... | collective-permute-start | bytes 221192 | tf_op jit(solution)/shard_map/ppermute | solution.py:303
  29.9 7.4 %collective-permute-start.14 = (bf16[2,144,128]{2,1,0:T(8,128)(2,1)S(1)}, bf16[2,144,128]{2,1,0:T(8,128)(2,1)S(1)}, u32[]{:S(2)}, u32[]{:S(2)}) collective-permute-start(bf16[2,144,128]{2,1,0:T(8,128)(2,1)S(1)} %get-tuple-element.53), channel_id=1, source_target_pairs={{0,12},{1,5},{2,14},{3,7},{4,8},{5,1},{6,10},{7,3},{8,4},{9,13},{1... | collective-permute-start | bytes 221192 | tf_op jit(solution)/shard_map/ppermute | solution.py:303
  32.9 10.1 %collective-permute-start.15 = (bf16[2,144,128]{2,1,0:T(8,128)(2,1)S(1)}, bf16[2,144,128]{2,1,0:T(8,128)(2,1)S(1)}, u32[]{:S(2)}, u32[]{:S(2)}) collective-permute-start(bf16[2,144,128]{2,1,0:T(8,128)(2,1)S(1)} %get-tuple-element.54), channel_id=1, source_target_pairs={{0,10},{1,15},{2,8},{3,13},{4,14},{5,11},{6,12},{7,9},{8,2},{9,7},... | collective-permute-start | bytes 221192 | tf_op jit(solution)/shard_map/ppermute | solution.py:303
  32.9 11.3 %collective-permute-start.16 = (bf16[2,144,128]{2,1,0:T(8,128)(2,1)S(1)}, bf16[2,144,128]{2,1,0:T(8,128)(2,1)S(1)}, u32[]{:S(2)}, u32[]{:S(2)}) collective-permute-start(bf16[2,144,128]{2,1,0:T(8,128)(2,1)S(1)} %get-tuple-element.55), channel_id=1, source_target_pairs={{0,8},{1,13},{2,10},{3,15},{4,12},{5,9},{6,14},{7,11},{8,0},{9,5},... | collective-permute-start | bytes 221192 | tf_op jit(solution)/shard_map/ppermute | solution.py:303
  36.3 9.7 %collective-permute-start.10 = (bf16[2,144,128]{2,1,0:T(8,128)(2,1)S(1)}, bf16[2,144,128]{2,1,0:T(8,128)(2,1)S(1)}, u32[]{:S(2)}, u32[]{:S(2)}) collective-permute-start(bf16[2,144,128]{2,1,0:T(8,128)(2,1)S(1)} %get-tuple-element.49), channel_id=1, source_target_pairs={{0,2},{1,3},{2,0},{3,1},{4,6},{5,7},{6,4},{7,5},{8,10},{9,11},{10,... | collective-permute-start | bytes 221192 | tf_op jit(solution)/shard_map/ppermute | solution.py:303
  37.3 8.7 %collective-permute-start.11 = (bf16[2,144,128]{2,1,0:T(8,128)(2,1)S(1)}, bf16[2,144,128]{2,1,0:T(8,128)(2,1)S(1)}, u32[]{:S(2)}, u32[]{:S(2)}) collective-permute-start(bf16[2,144,128]{2,1,0:T(8,128)(2,1)S(1)} %get-tuple-element.50), channel_id=1, source_target_pairs={{0,6},{1,11},{2,4},{3,9},{4,2},{5,15},{6,0},{7,13},{8,14},{9,3},{1... | collective-permute-start | bytes 221192 | tf_op jit(solution)/shard_map/ppermute | solution.py:303
  37.3 8.7 %collective-permute-start.12 = (bf16[2,144,128]{2,1,0:T(8,128)(2,1)S(1)}, bf16[2,144,128]{2,1,0:T(8,128)(2,1)S(1)}, u32[]{:S(2)}, u32[]{:S(2)}) collective-permute-start(bf16[2,144,128]{2,1,0:T(8,128)(2,1)S(1)} %get-tuple-element.51), channel_id=1, source_target_pairs={{0,4},{1,9},{2,6},{3,11},{4,0},{5,13},{6,2},{7,15},{8,12},{9,1},{1... | collective-permute-start | bytes 221192 | tf_op jit(solution)/shard_map/ppermute | solution.py:303

commit v13 on v12

--- a/solution.py
+++ b/solution.py
@@ -352,20 +352,21 @@
         output_weight,
     )
 
-    y = pl.pallas_call(
-        functools.partial(mix_kernel, factor),
-        out_shape=jax.ShapeDtypeStruct((tokens // 2, inner, 2 * width), BF16),
-        in_specs=[whole(VMEM)],
-        out_specs=whole(VMEM),
-        scratch_shapes=[VMEM((factor * factor, width), F32)],
-        compiler_params=params(16),
-        cost_estimate=pl.CostEstimate(
-            flops=2 * tokens * seqs * factor * factor * width,
-            bytes_accessed=2 * inner * tokens * width,
-            transcendentals=0,
-        ),
-        name="mix",
-    )(to_mix)
+    def mixed(to_mix):
+        return pl.pallas_call(
+            functools.partial(mix_kernel, factor),
+            out_shape=jax.ShapeDtypeStruct((tokens // 2, inner, 2 * width), BF16),
+            in_specs=[whole(VMEM)],
+            out_specs=whole(VMEM),
+            scratch_shapes=[VMEM((factor * factor, width), F32)],
+            compiler_params=params(16),
+            cost_estimate=pl.CostEstimate(
+                flops=2 * tokens * seqs * factor * factor * width,
+                bytes_accessed=2 * inner * tokens * width,
+                transcendentals=0,
+            ),
+            name="mix",
+        )(to_mix)
 
     def joined(*pieces):
         return pl.pallas_call(
@@ -382,12 +383,14 @@
     direct = [swap(item, pair) for pair in turn]
     own_came = swap(item, 2)
     own_early = swap(item, 1)
-    *direct, own_came, own_early = lax.optimization_barrier((*direct, own_came, own_early))
+    came = [swap(d, 2) for d in direct]
+    *direct, to_mix = lax.optimization_barrier((*direct, to_mix))
+    y = mixed(to_mix)
     held = joined(*direct)
-    came = swap(held, 2)
-    kept, y = lax.optimization_barrier((held, y))
-    early = swap(kept, 1)
-    came, y = lax.optimization_barrier((came, y))
+    held, y = lax.optimization_barrier((held, y))
+    early = swap(held, 1)
+    *came, own_came, own_early, y = lax.optimization_barrier((*came, own_came, own_early, y))
+    came = joined(*came)
     own_late = swap(own_came, 1)
     late = swap(came, 1)
 
@@ -435,8 +438,10 @@
     )(row, aux, state, y, wide, own_late, late)
 
     crossed = swap(cross, 1)
-    others = staggered([(k, k - 1) for k in range(chips - 1, 1, -2)])
-    others = [[(a[m], b[m]) for m in (0, 1)] for a, b in others]
+    falling = [(k, k - 1) for k in range(chips - 1, 1, -2)]
+    inward = [falling[m // 2] if m % 2 == 0 else falling[-1 - m // 2] for m in range(len(falling))]
+    mirrored = [inward[m ^ 1] if (m ^ 1) < len(inward) else inward[m] for m in range(len(inward))]
+    others = [[(a[m], b[m]) for m in (0, 1)] for a, b in zip(inward, mirrored)]
     cut = (len(others) + 1) // 2
     first, last = others[:cut], [[(0, 0), (1, 1)]] + others[cut:]
     sends = [(0, 0)] + [pair for group in first for pair in group] + [(1, 1)]

time: 47.9 us -> 46.1 us (0.962)
  waiting for transfers between devices: 13.2 us -> 8.98 us
  starting transfers between devices: 20.1 us -> 22.5 us
    ppermute x17 -> x19, waiting for transfers between devices: 13.2 us -> 8.98 us  [swap(): lax.ppermute(array, 'row', [(r, r ^ bits[r & 1]) for r in range(count)])]
    ppermute x17 -> x19, starting transfers between devices: 20.1 us -> 22.5 us  [swap(): lax.ppermute(array, 'row', [(r, r ^ bits[r & 1]) for r in range(count)])]
  transfers between devices with their start and end apart: 17 -> 19, of which waited for: 9 -> 9; matrix products, arithmetic and copies ran while one was open for 0% -> 0% of each run, Pallas kernels for 10% -> 10%
where the time goes in v13:
time: 46.1 us; the launch traced here: 46 us
  starting transfers between devices  22.5 us (49%)
  Pallas kernels  12.7 us (28%)
  waiting for transfers between devices  8.98 us (19%)
  local copies, waits for them, and re-layouts  1.03 us (2%)
  between operations  0.78 us (2%)
    ppermute x19, starting transfers between devices, swap(): lax.ppermute(array, 'row', [(r, r ^ bits[r & 1]) for r in range(count)])  22.5 us
    ppermute x19, waiting for transfers between devices, swap(): lax.ppermute(array, 'row', [(r, r ^ bits[r & 1]) for r in range(count)])  8.98 us
    pallas_call x2, Pallas kernels, gate(): pl.pallas_call(functools.partial(gate_kernel, groups), out_shape=jax.Shap...  3.51 us
    pallas_call x1, Pallas kernels, body(): pl.pallas_call(functools.partial(pair_kernel, [[(3, 3)], ranks(3)]), grid...  3.47 us
    pallas_call x1, Pallas kernels, body(): pl.pallas_call(prepare_kernel, out_shape=(jax.ShapeDtypeStruct((mix_rows,...  2.77 us
    pallas_call x1, Pallas kernels, mixed(): pl.pallas_call(functools.partial(mix_kernel, factor), out_shape=jax.Shape...  2.74 us
    unnamed x10, local copies, waits for them, and re-layouts  1.03 us
  transfers between devices with their start and end apart: 19, of which 9 were waited for; matrix products, arithmetic and copies ran while one was open for 0% of the time, Pallas kernels for 10%

profile of v13, /device:TPU:0, one launch (start us, length us, event | category | flops | bytes accessed | tf_op | source)
XLA Modules:
  0.0 46.0 jit_solution(4066441156629873023)
XLA Ops:
  0.6 2.8 %prepare.1 = (bf16[1792,128]{1,0:T(8,128)(2,1)}, bf16[1,192,128]{2,1,0:T(8,128)(2,1)}, f32[424,128]{1,0:T(8,128)}, bf16[2,128,256]{2,1,0:T(8,128)(2,1)}) custom-call(s32[1]{0:T(128)} %bitcast.row_ref, s32[192]{0:T(256)} %depth_hbm.1, bf16[12,64,64]{2,1,0:T(8,128)(2,1)} %bitcast.14, f32[1,64]{1,0:T(1,128)} %bitcast.19, f32[1,64]{1,0:T(1,128)} %bitcast.20, ...), custom_call_target="tpu_custom_call" | custom-call | tf_op jit(solution)/shard_map/prepare/pallas_call | solution.py:312
  3.4 3.1 %collective-permute-start.4 = (bf16[1,192,128]{2,1,0:T(8,128)(2,1)}, bf16[1,192,128]{2,1,0:T(8,128)(2,1)S(1)}, u32[]{:S(2)}, u32[]{:S(2)}) collective-permute-start(bf16[1,192,128]{2,1,0:T(8,128)(2,1)} %get-tuple-element.33.rest_0_), channel_id=1, source_target_pairs={{0,4},{1,9},{2,6},{3,11},{4,0},{5,13},{6,2},{7,15},{8,12},{9,1},{1... | collective-permute-start | bytes 147464 | tf_op jit(solution)/shard_map/ppermute | solution.py:303
  6.5 2.6 %collective-permute-start.2 = (bf16[1,192,128]{2,1,0:T(8,128)(2,1)}, bf16[1,192,128]{2,1,0:T(8,128)(2,1)S(1)}, u32[]{:S(2)}, u32[]{:S(2)}) collective-permute-start(bf16[1,192,128]{2,1,0:T(8,128)(2,1)} %get-tuple-element.33.rest_0_), channel_id=1, source_target_pairs={{0,8},{1,13},{2,10},{3,15},{4,12},{5,9},{6,14},{7,11},{8,0},{9,5},... | collective-permute-start | bytes 147464 | tf_op jit(solution)/shard_map/ppermute | solution.py:303
  9.1 0.0 collective-permute-start
  9.1 0.0 collective-permute-start.7
  9.1 1.7 %collective-permute-start.6 = (bf16[1,192,128]{2,1,0:T(8,128)(2,1)}, bf16[1,192,128]{2,1,0:T(8,128)(2,1)S(1)}, u32[]{:S(2)}, u32[]{:S(2)}) collective-permute-start(bf16[1,192,128]{2,1,0:T(8,128)(2,1)} %get-tuple-element.33.rest_0_), channel_id=1, source_target_pairs={{0,2},{1,3},{2,0},{3,1},{4,6},{5,7},{6,4},{7,5},{8,10},{9,11},{10,... | collective-permute-start | bytes 147464 | tf_op jit(solution)/shard_map/ppermute | solution.py:303
  10.8 0.0 collective-permute-done.4.refs_2_
  10.8 0.3 collective-permute-start.5
  11.1 1.9 %collective-permute-done.2.refs_1_ = bf16[1,192,128]{2,1,0:T(8,128)(2,1)S(1)} collective-permute-done((bf16[1,192,128]{2,1,0:T(8,128)(2,1)}, bf16[1,192,128]{2,1,0:T(8,128)(2,1)S(1)}, u32[]{:S(2)}, u32[]{:S(2)}) %collective-permute-start.2) | collective-permute-done | bytes 49184 | tf_op jit(solution)/shard_map/ppermute | solution.py:303
  13.0 1.5 %collective-permute-start.3 = (bf16[1,192,128]{2,1,0:T(8,128)(2,1)S(1)}, bf16[1,192,128]{2,1,0:T(8,128)(2,1)S(1)}, u32[]{:S(2)}, u32[]{:S(2)}) collective-permute-start(bf16[1,192,128]{2,1,0:T(8,128)(2,1)S(1)} %collective-permute-done.2.refs_1_), channel_id=1, source_target_pairs={{0,2},{1,3},{2,0},{3,1},{4,6},{5,7},{6,4},{7,5},{8,10},{9,11},{10,... | collective-permute-start | bytes 147464 | tf_op jit(solution)/shard_map/ppermute | solution.py:303
  14.5 0.7 %collective-permute-done.refs_0_ = bf16[1,192,128]{2,1,0:T(8,128)(2,1)S(1)} collective-permute-done((bf16[1,192,128]{2,1,0:T(8,128)(2,1)}, bf16[1,192,128]{2,1,0:T(8,128)(2,1)S(1)}, u32[]{:S(2)}, u32[]{:S(2)}) %collective-permute-start) | collective-permute-done | bytes 49184 | tf_op jit(solution)/shard_map/ppermute | solution.py:303
  15.2 1.5 %collective-permute-start.1 = (bf16[1,192,128]{2,1,0:T(8,128)(2,1)S(1)}, bf16[1,192,128]{2,1,0:T(8,128)(2,1)S(1)}, u32[]{:S(2)}, u32[]{:S(2)}) collective-permute-start(bf16[1,192,128]{2,1,0:T(8,128)(2,1)S(1)} %collective-permute-done.refs_0_), channel_id=1, source_target_pairs={{0,2},{1,3},{2,0},{3,1},{4,6},{5,7},{6,4},{7,5},{8,10},{9,11},{10,... | collective-permute-start | bytes 147464 | tf_op jit(solution)/shard_map/ppermute | solution.py:303
  16.7 0.0 copy-start.2
  16.7 1.0 %copy-done.2 = bf16[1792,128]{1,0:T(8,128)(2,1)S(1)} copy-done((bf16[1792,128]{1,0:T(8,128)(2,1)S(1)}, bf16[1792,128]{1,0:T(8,128)(2,1)}, u32[]{:S(2)}) %copy-start.2) | copy-done | bytes 458776
  17.8 0.0 copy-start
  17.8 0.0 copy-start.3
  17.8 0.0 copy-start.4
  17.8 2.7 %mix.1.y_ref = bf16[6,2048,256]{2,1,0:T(8,128)(2,1)S(1)} custom-call(bf16[1792,128]{1,0:T(8,128)(2,1)S(1)} %copy-done.2), custom_call_target="tpu_custom_call" | custom-call | flops 201326592 | bytes 6291456 | tf_op jit(solution)/shard_map/mix/pallas_call | solution.py:356
  20.5 0.0 collective-permute-done.7.rest_1_
  20.5 0.1 collective-permute-start.8
  20.6 0.0 collective-permute-done.6.rest_2_
  20.6 0.0 collective-permute-done.5.refs_2_
  20.6 0.0 collective-permute-done.3.refs_1_
  20.6 0.0 collective-permute-done.1.refs_0_
  20.7 0.5 %collective-permute-start.10 = (bf16[3,192,128]{2,1,0:T(8,128)(2,1)S(1)}, bf16[3,192,128]{2,1,0:T(8,128)(2,1)S(1)}, u32[]{:S(2)}, u32[]{:S(2)}) collective-permute-start(bf16[3,192,128]{2,1,0:T(8,128)(2,1)S(1)} %join.3.rest_5_), channel_id=1, source_target_pairs={{0,1},{1,0},{2,3},{3,2},{4,5},{5,4},{6,7},{7,6},{8,9},{9,8},{10,11... | collective-permute-start | bytes 442376 | tf_op jit(solution)/shard_map/ppermute | solution.py:303
  21.2 0.1 collective-permute-start.9
  21.3 0.7 %collective-permute-done.8.rest_4_ = bf16[3,192,128]{2,1,0:T(8,128)(2,1)S(1)} collective-permute-done((bf16[3,192,128]{2,1,0:T(8,128)(2,1)S(1)}, bf16[3,192,128]{2,1,0:T(8,128)(2,1)S(1)}, u32[]{:S(2)}, u32[]{:S(2)}) %collective-permute-start.8) | collective-permute-done | bytes 147488 | tf_op jit(solution)/shard_map/ppermute | solution.py:303
  22.0 0.0 copy-done
  22.0 0.0 copy-done.3
  22.0 0.0 copy-done.4
  22.0 0.1 first_half.1
  22.1 0.3 collective-permute-done.9.rest_0_
  22.4 0.0 collective-permute-done.10.rest_1_
  22.4 0.0 copy-start.1
  22.4 3.5 %pair.1 = (bf16[12,192,128]{2,1,0:T(8,128)(2,1)}, bf16[8,144,128]{2,1,0:T(8,128)(2,1)S(1)}, bf16[8,144,128]{2,1,0:T(8,128)(2,1)S(1)}, f32[3072,128]{1,0:T(8,128)S(1)}) custom-call(s32[1]{0:T(128)} %bitcast.row_ref, f32[424,128]{1,0:T(8,128)S(1)} %get-tuple-element.46.aux_ref, ...), custom_call_target="tpu_custom_call", output_to_operand_aliasing={{3}: (4, {})} | custom-call | flops 1207959552 | bytes 8650752 | tf_op jit(solution)/shard_map/pair/pallas_call | solution.py:417
  25.9 0.2 collective-permute-start.11
  26.1 1.4 %collective-permute-done.11.crossed_ref = bf16[8,144,128]{2,1,0:T(8,128)(2,1)S(1)} collective-permute-done((bf16[8,144,128]{2,1,0:T(8,128)(2,1)S(1)}, bf16[8,144,128]{2,1,0:T(8,128)(2,1)S(1)}, u32[]{:S(2)}, u32[]{:S(2)}) %collective-permute-start.11) | collective-permute-done | bytes 294944 | tf_op jit(solution)/shard_map/ppermute | solution.py:303
  27.5 1.3 %collective-permute-start.15 = (bf16[2,144,128]{2,1,0:T(8,128)(2,1)S(1)}, bf16[2,144,128]{2,1,0:T(8,128)(2,1)S(1)}, u32[]{:S(2)}, u32[]{:S(2)}) collective-permute-start(bf16[2,144,128]{2,1,0:T(8,128)(2,1)S(1)} %get-tuple-element.58), channel_id=1, source_target_pairs={{0,14},{1,7},{2,12},{3,5},{4,10},{5,3},{6,8},{7,1},{8,6},{9,15},{1... | collective-permute-start | bytes 221192 | tf_op jit(solution)/shard_map/ppermute | solution.py:303
  28.8 2.5 %collective-permute-start.16 = (bf16[2,144,128]{2,1,0:T(8,128)(2,1)S(1)}, bf16[2,144,128]{2,1,0:T(8,128)(2,1)S(1)}, u32[]{:S(2)}, u32[]{:S(2)}) collective-permute-start(bf16[2,144,128]{2,1,0:T(8,128)(2,1)S(1)} %get-tuple-element.59), channel_id=1, source_target_pairs={{0,12},{1,5},{2,14},{3,7},{4,8},{5,1},{6,10},{7,3},{8,4},{9,13},{1... | collective-permute-start | bytes 221192 | tf_op jit(solution)/shard_map/ppermute | solution.py:303
  31.4 0.0 collective-permute-start.17
  31.4 3.0 %collective-permute-start.18 = (bf16[2,144,128]{2,1,0:T(8,128)(2,1)S(1)}, bf16[2,144,128]{2,1,0:T(8,128)(2,1)S(1)}, u32[]{:S(2)}, u32[]{:S(2)}) collective-permute-start(bf16[2,144,128]{2,1,0:T(8,128)(2,1)S(1)} %get-tuple-element.61), channel_id=1, source_target_pairs={{0,4},{1,13},{2,6},{3,15},{4,0},{5,9},{6,2},{7,11},{8,12},{9,5},{1... | collective-permute-start | bytes 221192 | tf_op jit(solution)/shard_map/ppermute | solution.py:303
  34.4 0.5 %collective-permute-start.12 = (bf16[2,144,128]{2,1,0:T(8,128)(2,1)S(1)}, bf16[2,144,128]{2,1,0:T(8,128)(2,1)S(1)}, u32[]{:S(2)}, u32[]{:S(2)}) collective-permute-start(bf16[2,144,128]{2,1,0:T(8,128)(2,1)S(1)} %get-tuple-element.55), channel_id=1, source_target_pairs={{0,2},{1,3},{2,0},{3,1},{4,6},{5,7},{6,4},{7,5},{8,10},{9,11},{10,... | collective-permute-start | bytes 221192 | tf_op jit(solution)/shard_map/ppermute | solution.py:303
  34.9 0.1 collective-permute-done.15.rest_0_
  35.0 0.2 collective-permute-start.13
  35.2 0.3 collective-permute-done.16.rest_1_
  35.5 3.3 %collective-permute-start.14 = (bf16[2,144,128]{2,1,0:T(8,128)(2,1)S(1)}, bf16[2,144,128]{2,1,0:T(8,128)(2,1)S(1)}, u32[]{:S(2)}, u32[]{:S(2)}) collective-permute-start(bf16[2,144,128]{2,1,0:T(8,128)(2,1)S(1)} %get-tuple-element.57), channel_id=1, source_target_pairs={{0,8},{1,9},{2,10},{3,11},{4,12},{5,13},{6,14},{7,15},{8,0},{9,1},... | collective-permute-start | bytes 221192 | tf_op jit(solution)/shard_map/ppermute | solution.py:303
  38.8 0.0 collective-permute-done.17.rest_2_
  38.8 0.0 collective-permute-done.18.rest_3_
  38.8 0.0 copy-done.1
  38.8 1.8 %gate_first.1.rest_4_ = bf16[12,192,256]{2,1,0:T(8,128)(2,1)} custom-call(s32[1]{0:T(128)} %bitcast.row_ref, f32[424,128]{1,0:T(8,128)S(1)} %get-tuple-element.46.aux_ref, bf16[2,128,256]{2,1,0:T(8,128)(2,1)S(1)} %copy-done.1, bf16[2,144,128]{2,1,0:T(8,128)(2,1)S(1)} %collective-permute-done.15.rest_0_, ...), custom_call_target="tpu_custom_call" | custom-call | flops 150994944 | bytes 1474560 | tf_op jit(solution)/shard_map/gate_first/pallas_call | solution.py:463
  40.5 0.0 collective-permute-done.12.rest_1_
  40.5 2.8 %collective-permute-done.13.rest_2_ = bf16[2,144,128]{2,1,0:T(8,128)(2,1)S(1)} collective-permute-done((bf16[2,144,128]{2,1,0:T(8,128)(2,1)S(1)}, bf16[2,144,128]{2,1,0:T(8,128)(2,1)S(1)}, u32[]{:S(2)}, u32[]{:S(2)}) %collective-permute-start.13) | collective-permute-done | bytes 73760 | tf_op jit(solution)/shard_map/ppermute | solution.py:303
  43.4 0.8 %collective-permute-done.14.rest_3_ = bf16[2,144,128]{2,1,0:T(8,128)(2,1)S(1)} collective-permute-done((bf16[2,144,128]{2,1,0:T(8,128)(2,1)S(1)}, bf16[2,144,128]{2,1,0:T(8,128)(2,1)S(1)}, u32[]{:S(2)}, u32[]{:S(2)}) %collective-permute-start.14) | collective-permute-done | bytes 73760 | tf_op jit(solution)/shard_map/ppermute | solution.py:303
  44.2 1.8 %gate_last.1 = bf16[12,192,256]{2,1,0:T(8,128)(2,1)} custom-call(s32[1]{0:T(128)} %bitcast.row_ref, f32[424,128]{1,0:T(8,128)S(1)} %get-tuple-element.46.aux_ref, bf16[2,128,256]{2,1,0:T(8,128)(2,1)S(1)} %copy-done.1, bf16[2,144,128]{2,1,0:T(8,128)(2,1)S(1)} %get-tuple-element.54.rest_0_, ...), custom_call_target="tpu_custom_call", output_to_operand_aliasing={{}: (7, {})} | custom-call | flops 150994944 | bytes 1474560 | tf_op jit(solution)/shard_map/gate_last/pallas_call | solution.py:463
  (3 shorter events, 0.1 us)
Async XLA Ops:
  3.4 7.4 %collective-permute-start.4 = (bf16[1,192,128]{2,1,0:T(8,128)(2,1)}, bf16[1,192,128]{2,1,0:T(8,128)(2,1)S(1)}, u32[]{:S(2)}, u32[]{:S(2)}) collective-permute-start(bf16[1,192,128]{2,1,0:T(8,128)(2,1)} %get-tuple-element.33.rest_0_), channel_id=1, source_target_pairs={{0,4},{1,9},{2,6},{3,11},{4,0},{5,13},{6,2},{7,15},{8,12},{9,1},{1... | collective-permute-start | bytes 147464 | tf_op jit(solution)/shard_map/ppermute | solution.py:303
  6.5 6.5 %collective-permute-start.2 = (bf16[1,192,128]{2,1,0:T(8,128)(2,1)}, bf16[1,192,128]{2,1,0:T(8,128)(2,1)S(1)}, u32[]{:S(2)}, u32[]{:S(2)}) collective-permute-start(bf16[1,192,128]{2,1,0:T(8,128)(2,1)} %get-tuple-element.33.rest_0_), channel_id=1, source_target_pairs={{0,8},{1,13},{2,10},{3,15},{4,12},{5,9},{6,14},{7,11},{8,0},{9,5},... | collective-permute-start | bytes 147464 | tf_op jit(solution)/shard_map/ppermute | solution.py:303
  9.1 6.1 %collective-permute-start = (bf16[1,192,128]{2,1,0:T(8,128)(2,1)}, bf16[1,192,128]{2,1,0:T(8,128)(2,1)S(1)}, u32[]{:S(2)}, u32[]{:S(2)}) collective-permute-start(bf16[1,192,128]{2,1,0:T(8,128)(2,1)} %get-tuple-element.33.rest_0_), channel_id=1, source_target_pairs={{0,12},{1,5},{2,14},{3,7},{4,8},{5,1},{6,10},{7,3},{8,4},{9,13},{1... | collective-permute-start | bytes 147464 | tf_op jit(solution)/shard_map/ppermute | solution.py:303
  9.1 11.4 %collective-permute-start.7 = (bf16[1,192,128]{2,1,0:T(8,128)(2,1)}, bf16[1,192,128]{2,1,0:T(8,128)(2,1)S(1)}, u32[]{:S(2)}, u32[]{:S(2)}) collective-permute-start(bf16[1,192,128]{2,1,0:T(8,128)(2,1)} %get-tuple-element.33.rest_0_), channel_id=1, source_target_pairs={{0,1},{1,0},{2,3},{3,2},{4,5},{5,4},{6,7},{7,6},{8,9},{9,8},{10,11... | collective-permute-start | bytes 147464 | tf_op jit(solution)/shard_map/ppermute | solution.py:303
  9.1 11.5 %collective-permute-start.6 = (bf16[1,192,128]{2,1,0:T(8,128)(2,1)}, bf16[1,192,128]{2,1,0:T(8,128)(2,1)S(1)}, u32[]{:S(2)}, u32[]{:S(2)}) collective-permute-start(bf16[1,192,128]{2,1,0:T(8,128)(2,1)} %get-tuple-element.33.rest_0_), channel_id=1, source_target_pairs={{0,2},{1,3},{2,0},{3,1},{4,6},{5,7},{6,4},{7,5},{8,10},{9,11},{10,... | collective-permute-start | bytes 147464 | tf_op jit(solution)/shard_map/ppermute | solution.py:303
  10.8 9.8 %collective-permute-start.5 = (bf16[1,192,128]{2,1,0:T(8,128)(2,1)S(1)}, bf16[1,192,128]{2,1,0:T(8,128)(2,1)S(1)}, u32[]{:S(2)}, u32[]{:S(2)}) collective-permute-start(bf16[1,192,128]{2,1,0:T(8,128)(2,1)S(1)} %collective-permute-done.4.refs_2_), channel_id=1, source_target_pairs={{0,2},{1,3},{2,0},{3,1},{4,6},{5,7},{6,4},{7,5},{8,10},{9,11},{10,... | collective-permute-start | bytes 147464 | tf_op jit(solution)/shard_map/ppermute | solution.py:303
  13.0 7.6 %collective-permute-start.3 = (bf16[1,192,128]{2,1,0:T(8,128)(2,1)S(1)}, bf16[1,192,128]{2,1,0:T(8,128)(2,1)S(1)}, u32[]{:S(2)}, u32[]{:S(2)}) collective-permute-start(bf16[1,192,128]{2,1,0:T(8,128)(2,1)S(1)} %collective-permute-done.2.refs_1_), channel_id=1, source_target_pairs={{0,2},{1,3},{2,0},{3,1},{4,6},{5,7},{6,4},{7,5},{8,10},{9,11},{10,... | collective-permute-start | bytes 147464 | tf_op jit(solution)/shard_map/ppermute | solution.py:303
  15.2 5.4 %collective-permute-start.1 = (bf16[1,192,128]{2,1,0:T(8,128)(2,1)S(1)}, bf16[1,192,128]{2,1,0:T(8,128)(2,1)S(1)}, u32[]{:S(2)}, u32[]{:S(2)}) collective-permute-start(bf16[1,192,128]{2,1,0:T(8,128)(2,1)S(1)} %collective-permute-done.refs_0_), channel_id=1, source_target_pairs={{0,2},{1,3},{2,0},{3,1},{4,6},{5,7},{6,4},{7,5},{8,10},{9,11},{10,... | collective-permute-start | bytes 147464 | tf_op jit(solution)/shard_map/ppermute | solution.py:303
  16.7 1.0 %copy-start.2 = (bf16[1792,128]{1,0:T(8,128)(2,1)S(1)}, bf16[1792,128]{1,0:T(8,128)(2,1)}, u32[]{:S(2)}) copy-start(bf16[1792,128]{1,0:T(8,128)(2,1)} %get-tuple-element.38.mix_ref) | copy-start | bytes 1376260
  17.8 4.2 %copy-start = (bf16[12,192,128]{2,1,0:T(8,128)(2,1)S(1)}, bf16[12,192,128]{2,1,0:T(8,128)(2,1)}, u32[]{:S(2)}) copy-start(bf16[12,192,128]{2,1,0:T(8,128)(2,1)} %state_ref.1) | copy-start | bytes 1769476
  17.8 4.2 %copy-start.3 = (f32[424,128]{1,0:T(8,128)S(1)}, f32[424,128]{1,0:T(8,128)}, u32[]{:S(2)}) copy-start(f32[424,128]{1,0:T(8,128)} %get-tuple-element.32.aux_ref) | copy-start | bytes 651268
  17.8 4.2 %copy-start.4 = (bf16[1,192,128]{2,1,0:T(8,128)(2,1)S(1)}, bf16[1,192,128]{2,1,0:T(8,128)(2,1)}, u32[]{:S(2)}) copy-start(bf16[1,192,128]{2,1,0:T(8,128)(2,1)} %get-tuple-element.33.rest_0_) | copy-start | bytes 147460
  20.5 1.4 %collective-permute-start.8 = (bf16[3,192,128]{2,1,0:T(8,128)(2,1)S(1)}, bf16[3,192,128]{2,1,0:T(8,128)(2,1)S(1)}, u32[]{:S(2)}, u32[]{:S(2)}) collective-permute-start(bf16[3,192,128]{2,1,0:T(8,128)(2,1)S(1)} %join.2.rest_3_), channel_id=1, source_target_pairs={{0,1},{1,0},{2,3},{3,2},{4,5},{5,4},{6,7},{7,6},{8,9},{9,8},{10,11... | collective-permute-start | bytes 442376 | tf_op jit(solution)/shard_map/ppermute | solution.py:303
  20.7 1.8 %collective-permute-start.10 = (bf16[3,192,128]{2,1,0:T(8,128)(2,1)S(1)}, bf16[3,192,128]{2,1,0:T(8,128)(2,1)S(1)}, u32[]{:S(2)}, u32[]{:S(2)}) collective-permute-start(bf16[3,192,128]{2,1,0:T(8,128)(2,1)S(1)} %join.3.rest_5_), channel_id=1, source_target_pairs={{0,1},{1,0},{2,3},{3,2},{4,5},{5,4},{6,7},{7,6},{8,9},{9,8},{10,11... | collective-permute-start | bytes 442376 | tf_op jit(solution)/shard_map/ppermute | solution.py:303
  21.2 1.2 %collective-permute-start.9 = (bf16[1,192,128]{2,1,0:T(8,128)(2,1)S(1)}, bf16[1,192,128]{2,1,0:T(8,128)(2,1)S(1)}, u32[]{:S(2)}, u32[]{:S(2)}) collective-permute-start(bf16[1,192,128]{2,1,0:T(8,128)(2,1)S(1)} %collective-permute-done.6.rest_2_), channel_id=1, source_target_pairs={{0,1},{1,0},{2,3},{3,2},{4,5},{5,4},{6,7},{7,6},{8,9},{9,8},{10,11... | collective-permute-start | bytes 147464 | tf_op jit(solution)/shard_map/ppermute | solution.py:303
  22.4 16.3 %copy-start.1 = (bf16[2,128,256]{2,1,0:T(8,128)(2,1)S(1)}, bf16[2,128,256]{2,1,0:T(8,128)(2,1)}, u32[]{:S(2)}) copy-start(bf16[2,128,256]{2,1,0:T(8,128)(2,1)} %get-tuple-element.51.gates_ref) | copy-start | bytes 393220
  25.9 1.6 %collective-permute-start.11 = (bf16[8,144,128]{2,1,0:T(8,128)(2,1)S(1)}, bf16[8,144,128]{2,1,0:T(8,128)(2,1)S(1)}, u32[]{:S(2)}, u32[]{:S(2)}) collective-permute-start(bf16[8,144,128]{2,1,0:T(8,128)(2,1)S(1)} %get-tuple-element.53), channel_id=1, source_target_pairs={{0,1},{1,0},{2,3},{3,2},{4,5},{5,4},{6,7},{7,6},{8,9},{9,8},{10,11... | collective-permute-start | bytes 884744 | tf_op jit(solution)/shard_map/ppermute | solution.py:303
  27.5 7.4 %collective-permute-start.15 = (bf16[2,144,128]{2,1,0:T(8,128)(2,1)S(1)}, bf16[2,144,128]{2,1,0:T(8,128)(2,1)S(1)}, u32[]{:S(2)}, u32[]{:S(2)}) collective-permute-start(bf16[2,144,128]{2,1,0:T(8,128)(2,1)S(1)} %get-tuple-element.58), channel_id=1, source_target_pairs={{0,14},{1,7},{2,12},{3,5},{4,10},{5,3},{6,8},{7,1},{8,6},{9,15},{1... | collective-permute-start | bytes 221192 | tf_op jit(solution)/shard_map/ppermute | solution.py:303
  28.8 6.7 %collective-permute-start.16 = (bf16[2,144,128]{2,1,0:T(8,128)(2,1)S(1)}, bf16[2,144,128]{2,1,0:T(8,128)(2,1)S(1)}, u32[]{:S(2)}, u32[]{:S(2)}) collective-permute-start(bf16[2,144,128]{2,1,0:T(8,128)(2,1)S(1)} %get-tuple-element.59), channel_id=1, source_target_pairs={{0,12},{1,5},{2,14},{3,7},{4,8},{5,1},{6,10},{7,3},{8,4},{9,13},{1... | collective-permute-start | bytes 221192 | tf_op jit(solution)/shard_map/ppermute | solution.py:303
  31.4 7.4 %collective-permute-start.17 = (bf16[2,144,128]{2,1,0:T(8,128)(2,1)S(1)}, bf16[2,144,128]{2,1,0:T(8,128)(2,1)S(1)}, u32[]{:S(2)}, u32[]{:S(2)}) collective-permute-start(bf16[2,144,128]{2,1,0:T(8,128)(2,1)S(1)} %get-tuple-element.60), channel_id=1, source_target_pairs={{0,6},{1,15},{2,4},{3,13},{4,2},{5,11},{6,0},{7,9},{8,14},{9,7},{1... | collective-permute-start | bytes 221192 | tf_op jit(solution)/shard_map/ppermute | solution.py:303
  31.4 7.4 %collective-permute-start.18 = (bf16[2,144,128]{2,1,0:T(8,128)(2,1)S(1)}, bf16[2,144,128]{2,1,0:T(8,128)(2,1)S(1)}, u32[]{:S(2)}, u32[]{:S(2)}) collective-permute-start(bf16[2,144,128]{2,1,0:T(8,128)(2,1)S(1)} %get-tuple-element.61), channel_id=1, source_target_pairs={{0,4},{1,13},{2,6},{3,15},{4,0},{5,9},{6,2},{7,11},{8,12},{9,5},{1... | collective-permute-start | bytes 221192 | tf_op jit(solution)/shard_map/ppermute | solution.py:303
  34.4 6.2 %collective-permute-start.12 = (bf16[2,144,128]{2,1,0:T(8,128)(2,1)S(1)}, bf16[2,144,128]{2,1,0:T(8,128)(2,1)S(1)}, u32[]{:S(2)}, u32[]{:S(2)}) collective-permute-start(bf16[2,144,128]{2,1,0:T(8,128)(2,1)S(1)} %get-tuple-element.55), channel_id=1, source_target_pairs={{0,2},{1,3},{2,0},{3,1},{4,6},{5,7},{6,4},{7,5},{8,10},{9,11},{10,... | collective-permute-start | bytes 221192 | tf_op jit(solution)/shard_map/ppermute | solution.py:303
  35.0 8.4 %collective-permute-start.13 = (bf16[2,144,128]{2,1,0:T(8,128)(2,1)S(1)}, bf16[2,144,128]{2,1,0:T(8,128)(2,1)S(1)}, u32[]{:S(2)}, u32[]{:S(2)}) collective-permute-start(bf16[2,144,128]{2,1,0:T(8,128)(2,1)S(1)} %get-tuple-element.56), channel_id=1, source_target_pairs={{0,10},{1,11},{2,8},{3,9},{4,14},{5,15},{6,12},{7,13},{8,2},{9,3},... | collective-permute-start | bytes 221192 | tf_op jit(solution)/shard_map/ppermute | solution.py:303
  35.5 8.7 %collective-permute-start.14 = (bf16[2,144,128]{2,1,0:T(8,128)(2,1)S(1)}, bf16[2,144,128]{2,1,0:T(8,128)(2,1)S(1)}, u32[]{:S(2)}, u32[]{:S(2)}) collective-permute-start(bf16[2,144,128]{2,1,0:T(8,128)(2,1)S(1)} %get-tuple-element.57), channel_id=1, source_target_pairs={{0,8},{1,9},{2,10},{3,11},{4,12},{5,13},{6,14},{7,15},{8,0},{9,1},... | collective-permute-start | bytes 221192 | tf_op jit(solution)/shard_map/ppermute | solution.py:303

commit v14 on v13

--- a/solution.py
+++ b/solution.py
@@ -383,9 +383,18 @@
     direct = [swap(item, pair) for pair in turn]
     own_came = swap(item, 2)
     own_early = swap(item, 1)
+    staged = pl.pallas_call(
+        join_kernel,
+        out_shape=jax.ShapeDtypeStruct(to_mix.shape, BF16),
+        in_specs=[whole(VMEM)],
+        out_specs=whole(VMEM),
+        compiler_params=params(16),
+        name="stage",
+    )(to_mix)
+    direct[0], staged = lax.optimization_barrier((direct[0], staged))
     came = [swap(d, 2) for d in direct]
-    *direct, to_mix = lax.optimization_barrier((*direct, to_mix))
-    y = mixed(to_mix)
+    *direct, staged = lax.optimization_barrier((*direct, staged))
+    y = mixed(staged)
     held = joined(*direct)
     held, y = lax.optimization_barrier((held, y))
     early = swap(held, 1)

time: 46.1 us -> 46.2 us (level)
  waiting for transfers between devices: 8.98 us -> 7.44 us
  starting transfers between devices: 22.5 us -> 24 us
    ppermute x19, waiting for transfers between devices: 8.98 us -> 7.44 us  [swap(): lax.ppermute(array, 'row', [(r, r ^ bits[r & 1]) for r in range(count)])]
    ppermute x19, starting transfers between devices: 22.5 us -> 24 us  [swap(): lax.ppermute(array, 'row', [(r, r ^ bits[r & 1]) for r in range(count)])]
  transfers between devices with their start and end apart: 19 -> 19, of which waited for: 9 -> 8; matrix products, arithmetic and copies ran while one was open for 0% -> 0% of each run, Pallas kernels for 10% -> 10%
where the time goes in v14:
time: 46.2 us; the launch traced here: 46 us
  starting transfers between devices  24 us (52%)
  Pallas kernels  12.7 us (27%)
  waiting for transfers between devices  7.44 us (16%)
  local copies, waits for them, and re-layouts  1.04 us (2%)
  between operations  0.79 us (2%)
    ppermute x19, starting transfers between devices, swap(): lax.ppermute(array, 'row', [(r, r ^ bits[r & 1]) for r in range(count)])  24 us
    ppermute x19, waiting for transfers between devices, swap(): lax.ppermute(array, 'row', [(r, r ^ bits[r & 1]) for r in range(count)])  7.44 us
    pallas_call x2, Pallas kernels, gate(): pl.pallas_call(functools.partial(gate_kernel, groups), out_shape=jax.Shap...  3.5 us
    pallas_call x1, Pallas kernels, body(): pl.pallas_call(functools.partial(pair_kernel, [[(3, 3)], ranks(3)]), grid...  3.47 us
    pallas_call x1, Pallas kernels, body(): pl.pallas_call(prepare_kernel, out_shape=(jax.ShapeDtypeStruct((mix_rows,...  2.77 us
    pallas_call x1, Pallas kernels, mixed(): pl.pallas_call(functools.partial(mix_kernel, factor), out_shape=jax.Shape...  2.74 us
    unnamed x10, local copies, waits for them, and re-layouts  1.04 us
  transfers between devices with their start and end apart: 19, of which 8 were waited for; matrix products, arithmetic and copies ran while one was open for 0% of the time, Pallas kernels for 10%

profile of v14, /device:TPU:0, one launch (start us, length us, event | category | flops | bytes accessed | tf_op | source)
XLA Modules:
  0.0 46.0 jit_solution(15933236970482270350)
XLA Ops:
  0.6 2.8 %prepare.1 = (bf16[1792,128]{1,0:T(8,128)(2,1)}, bf16[1,192,128]{2,1,0:T(8,128)(2,1)}, f32[424,128]{1,0:T(8,128)}, bf16[2,128,256]{2,1,0:T(8,128)(2,1)}) custom-call(s32[1]{0:T(128)} %bitcast.row_ref, s32[192]{0:T(256)} %depth_hbm.1, bf16[12,64,64]{2,1,0:T(8,128)(2,1)} %bitcast.14, f32[1,64]{1,0:T(1,128)} %bitcast.19, f32[1,64]{1,0:T(1,128)} %bitcast.20, ...), custom_call_target="tpu_custom_call" | custom-call | tf_op jit(solution)/shard_map/prepare/pallas_call | solution.py:312
  3.4 5.1 %collective-permute-start = (bf16[1,192,128]{2,1,0:T(8,128)(2,1)}, bf16[1,192,128]{2,1,0:T(8,128)(2,1)S(1)}, u32[]{:S(2)}, u32[]{:S(2)}) collective-permute-start(bf16[1,192,128]{2,1,0:T(8,128)(2,1)} %get-tuple-element.35.rest_0_), channel_id=1, source_target_pairs={{0,12},{1,5},{2,14},{3,7},{4,8},{5,1},{6,10},{7,3},{8,4},{9,13},{1... | collective-permute-start | bytes 147464 | tf_op jit(solution)/shard_map/ppermute | solution.py:303
  8.5 0.0 collective-permute-start.4
  8.5 0.6 %collective-permute-start.2 = (bf16[1,192,128]{2,1,0:T(8,128)(2,1)}, bf16[1,192,128]{2,1,0:T(8,128)(2,1)S(1)}, u32[]{:S(2)}, u32[]{:S(2)}) collective-permute-start(bf16[1,192,128]{2,1,0:T(8,128)(2,1)} %get-tuple-element.35.rest_0_), channel_id=1, source_target_pairs={{0,8},{1,13},{2,10},{3,15},{4,12},{5,9},{6,14},{7,11},{8,0},{9,5},... | collective-permute-start | bytes 147464 | tf_op jit(solution)/shard_map/ppermute | solution.py:303
  9.2 0.0 collective-permute-start.7
  9.2 1.7 %collective-permute-start.6 = (bf16[1,192,128]{2,1,0:T(8,128)(2,1)}, bf16[1,192,128]{2,1,0:T(8,128)(2,1)S(1)}, u32[]{:S(2)}, u32[]{:S(2)}) collective-permute-start(bf16[1,192,128]{2,1,0:T(8,128)(2,1)} %get-tuple-element.35.rest_0_), channel_id=1, source_target_pairs={{0,2},{1,3},{2,0},{3,1},{4,6},{5,7},{6,4},{7,5},{8,10},{9,11},{10,... | collective-permute-start | bytes 147464 | tf_op jit(solution)/shard_map/ppermute | solution.py:303
  10.8 0.0 copy-start.2
  10.8 1.0 %copy-done.2 = bf16[1792,128]{1,0:T(8,128)(2,1)S(1)} copy-done((bf16[1792,128]{1,0:T(8,128)(2,1)S(1)}, bf16[1792,128]{1,0:T(8,128)(2,1)}, u32[]{:S(2)}) %copy-start.2) | copy-done | bytes 458776
  11.9 0.0 collective-permute-done.refs_0_
  11.9 0.9 %collective-permute-done.4.refs_2_ = bf16[1,192,128]{2,1,0:T(8,128)(2,1)S(1)} collective-permute-done((bf16[1,192,128]{2,1,0:T(8,128)(2,1)}, bf16[1,192,128]{2,1,0:T(8,128)(2,1)S(1)}, u32[]{:S(2)}, u32[]{:S(2)}) %collective-permute-start.4) | collective-permute-done | bytes 49184 | tf_op jit(solution)/shard_map/ppermute | solution.py:303
  12.8 1.5 %collective-permute-start.5 = (bf16[1,192,128]{2,1,0:T(8,128)(2,1)S(1)}, bf16[1,192,128]{2,1,0:T(8,128)(2,1)S(1)}, u32[]{:S(2)}, u32[]{:S(2)}) collective-permute-start(bf16[1,192,128]{2,1,0:T(8,128)(2,1)S(1)} %collective-permute-done.4.refs_2_), channel_id=1, source_target_pairs={{0,2},{1,3},{2,0},{3,1},{4,6},{5,7},{6,4},{7,5},{8,10},{9,11},{10,... | collective-permute-start | bytes 147464 | tf_op jit(solution)/shard_map/ppermute | solution.py:303
  14.4 0.0 collective-permute-done.2.refs_1_
  14.4 1.2 %collective-permute-start.3 = (bf16[1,192,128]{2,1,0:T(8,128)(2,1)S(1)}, bf16[1,192,128]{2,1,0:T(8,128)(2,1)S(1)}, u32[]{:S(2)}, u32[]{:S(2)}) collective-permute-start(bf16[1,192,128]{2,1,0:T(8,128)(2,1)S(1)} %collective-permute-done.2.refs_1_), channel_id=1, source_target_pairs={{0,2},{1,3},{2,0},{3,1},{4,6},{5,7},{6,4},{7,5},{8,10},{9,11},{10,... | collective-permute-start | bytes 147464 | tf_op jit(solution)/shard_map/ppermute | solution.py:303
  15.5 0.8 %collective-permute-start.1 = (bf16[1,192,128]{2,1,0:T(8,128)(2,1)S(1)}, bf16[1,192,128]{2,1,0:T(8,128)(2,1)S(1)}, u32[]{:S(2)}, u32[]{:S(2)}) collective-permute-start(bf16[1,192,128]{2,1,0:T(8,128)(2,1)S(1)} %collective-permute-done.refs_0_), channel_id=1, source_target_pairs={{0,2},{1,3},{2,0},{3,1},{4,6},{5,7},{6,4},{7,5},{8,10},{9,11},{10,... | collective-permute-start | bytes 147464 | tf_op jit(solution)/shard_map/ppermute | solution.py:303
  16.4 0.0 copy-start
  16.4 0.0 copy-start.3
  16.4 0.0 copy-start.4
  16.4 2.7 %mix.1.y_ref = bf16[6,2048,256]{2,1,0:T(8,128)(2,1)S(1)} custom-call(bf16[1792,128]{1,0:T(8,128)(2,1)S(1)} %stage.1.mix_ref), custom_call_target="tpu_custom_call" | custom-call | flops 201326592 | bytes 6291456 | tf_op jit(solution)/shard_map/mix/pallas_call | solution.py:356
  19.2 0.0 collective-permute-done.7.rest_1_
  19.2 0.1 collective-permute-start.8
  19.3 0.0 collective-permute-done.6.rest_2_
  19.3 0.0 collective-permute-done.5.refs_2_
  19.3 0.0 collective-permute-done.3.refs_1_
  19.3 0.3 collective-permute-done.1.refs_0_
  19.7 0.2 collective-permute-start.10
  19.9 0.3 collective-permute-start.9
  20.2 0.4 collective-permute-done.8.rest_4_
  20.6 0.0 copy-done
  20.6 0.0 copy-done.3
  20.6 0.0 copy-done.4
  20.6 0.1 first_half.1
  20.8 0.4 collective-permute-done.9.rest_0_
  21.2 0.0 collective-permute-done.10.rest_1_
  21.2 0.0 copy-start.1
  21.2 3.5 %pair.1 = (bf16[12,192,128]{2,1,0:T(8,128)(2,1)}, bf16[8,144,128]{2,1,0:T(8,128)(2,1)S(1)}, bf16[8,144,128]{2,1,0:T(8,128)(2,1)S(1)}, f32[3072,128]{1,0:T(8,128)S(1)}) custom-call(s32[1]{0:T(128)} %bitcast.row_ref, f32[424,128]{1,0:T(8,128)S(1)} %get-tuple-element.50.aux_ref, ...), custom_call_target="tpu_custom_call", output_to_operand_aliasing={{3}: (4, {})} | custom-call | flops 1207959552 | bytes 8650752 | tf_op jit(solution)/shard_map/pair/pallas_call | solution.py:426
  24.6 0.3 collective-permute-start.11
  24.9 1.3 %collective-permute-done.11.crossed_ref = bf16[8,144,128]{2,1,0:T(8,128)(2,1)S(1)} collective-permute-done((bf16[8,144,128]{2,1,0:T(8,128)(2,1)S(1)}, bf16[8,144,128]{2,1,0:T(8,128)(2,1)S(1)}, u32[]{:S(2)}, u32[]{:S(2)}) %collective-permute-start.11) | collective-permute-done | bytes 294944 | tf_op jit(solution)/shard_map/ppermute | solution.py:303
  26.3 3.0 %collective-permute-start.15 = (bf16[2,144,128]{2,1,0:T(8,128)(2,1)S(1)}, bf16[2,144,128]{2,1,0:T(8,128)(2,1)S(1)}, u32[]{:S(2)}, u32[]{:S(2)}) collective-permute-start(bf16[2,144,128]{2,1,0:T(8,128)(2,1)S(1)} %get-tuple-element.62), channel_id=1, source_target_pairs={{0,14},{1,7},{2,12},{3,5},{4,10},{5,3},{6,8},{7,1},{8,6},{9,15},{1... | collective-permute-start | bytes 221192 | tf_op jit(solution)/shard_map/ppermute | solution.py:303
  29.3 1.5 %collective-permute-start.16 = (bf16[2,144,128]{2,1,0:T(8,128)(2,1)S(1)}, bf16[2,144,128]{2,1,0:T(8,128)(2,1)S(1)}, u32[]{:S(2)}, u32[]{:S(2)}) collective-permute-start(bf16[2,144,128]{2,1,0:T(8,128)(2,1)S(1)} %get-tuple-element.63), channel_id=1, source_target_pairs={{0,12},{1,5},{2,14},{3,7},{4,8},{5,1},{6,10},{7,3},{8,4},{9,13},{1... | collective-permute-start | bytes 221192 | tf_op jit(solution)/shard_map/ppermute | solution.py:303
  30.7 0.3 collective-permute-start.17
  31.0 2.1 %collective-permute-start.18 = (bf16[2,144,128]{2,1,0:T(8,128)(2,1)S(1)}, bf16[2,144,128]{2,1,0:T(8,128)(2,1)S(1)}, u32[]{:S(2)}, u32[]{:S(2)}) collective-permute-start(bf16[2,144,128]{2,1,0:T(8,128)(2,1)S(1)} %get-tuple-element.65), channel_id=1, source_target_pairs={{0,4},{1,13},{2,6},{3,15},{4,0},{5,9},{6,2},{7,11},{8,12},{9,5},{1... | collective-permute-start | bytes 221192 | tf_op jit(solution)/shard_map/ppermute | solution.py:303
  33.1 1.1 %collective-permute-start.12 = (bf16[2,144,128]{2,1,0:T(8,128)(2,1)S(1)}, bf16[2,144,128]{2,1,0:T(8,128)(2,1)S(1)}, u32[]{:S(2)}, u32[]{:S(2)}) collective-permute-start(bf16[2,144,128]{2,1,0:T(8,128)(2,1)S(1)} %get-tuple-element.59), channel_id=1, source_target_pairs={{0,2},{1,3},{2,0},{3,1},{4,6},{5,7},{6,4},{7,5},{8,10},{9,11},{10,... | collective-permute-start | bytes 221192 | tf_op jit(solution)/shard_map/ppermute | solution.py:303
  34.2 0.0 collective-permute-done.15.rest_0_
  34.2 1.2 %collective-permute-start.13 = (bf16[2,144,128]{2,1,0:T(8,128)(2,1)S(1)}, bf16[2,144,128]{2,1,0:T(8,128)(2,1)S(1)}, u32[]{:S(2)}, u32[]{:S(2)}) collective-permute-start(bf16[2,144,128]{2,1,0:T(8,128)(2,1)S(1)} %get-tuple-element.60), channel_id=1, source_target_pairs={{0,10},{1,11},{2,8},{3,9},{4,14},{5,15},{6,12},{7,13},{8,2},{9,3},... | collective-permute-start | bytes 221192 | tf_op jit(solution)/shard_map/ppermute | solution.py:303
  35.5 0.1 collective-permute-done.16.rest_1_
  35.5 2.9 %collective-permute-start.14 = (bf16[2,144,128]{2,1,0:T(8,128)(2,1)S(1)}, bf16[2,144,128]{2,1,0:T(8,128)(2,1)S(1)}, u32[]{:S(2)}, u32[]{:S(2)}) collective-permute-start(bf16[2,144,128]{2,1,0:T(8,128)(2,1)S(1)} %get-tuple-element.61), channel_id=1, source_target_pairs={{0,8},{1,9},{2,10},{3,11},{4,12},{5,13},{6,14},{7,15},{8,0},{9,1},... | collective-permute-start | bytes 221192 | tf_op jit(solution)/shard_map/ppermute | solution.py:303
  38.5 0.0 collective-permute-done.17.rest_2_
  38.5 0.0 collective-permute-done.18.rest_3_
  38.5 0.0 copy-done.1
  38.5 1.8 %gate_first.1.rest_4_ = bf16[12,192,256]{2,1,0:T(8,128)(2,1)} custom-call(s32[1]{0:T(128)} %bitcast.row_ref, f32[424,128]{1,0:T(8,128)S(1)} %get-tuple-element.50.aux_ref, bf16[2,128,256]{2,1,0:T(8,128)(2,1)S(1)} %copy-done.1, bf16[2,144,128]{2,1,0:T(8,128)(2,1)S(1)} %collective-permute-done.15.rest_0_, ...), custom_call_target="tpu_custom_call" | custom-call | flops 150994944 | bytes 1474560 | tf_op jit(solution)/shard_map/gate_first/pallas_call | solution.py:472
  40.2 0.0 collective-permute-done.12.rest_1_
  40.2 2.9 %collective-permute-done.13.rest_2_ = bf16[2,144,128]{2,1,0:T(8,128)(2,1)S(1)} collective-permute-done((bf16[2,144,128]{2,1,0:T(8,128)(2,1)S(1)}, bf16[2,144,128]{2,1,0:T(8,128)(2,1)S(1)}, u32[]{:S(2)}, u32[]{:S(2)}) %collective-permute-start.13) | collective-permute-done | bytes 73760 | tf_op jit(solution)/shard_map/ppermute | solution.py:303
  43.1 1.1 %collective-permute-done.14.rest_3_ = bf16[2,144,128]{2,1,0:T(8,128)(2,1)S(1)} collective-permute-done((bf16[2,144,128]{2,1,0:T(8,128)(2,1)S(1)}, bf16[2,144,128]{2,1,0:T(8,128)(2,1)S(1)}, u32[]{:S(2)}, u32[]{:S(2)}) %collective-permute-start.14) | collective-permute-done | bytes 73760 | tf_op jit(solution)/shard_map/ppermute | solution.py:303
  44.2 1.7 %gate_last.1 = bf16[12,192,256]{2,1,0:T(8,128)(2,1)} custom-call(s32[1]{0:T(128)} %bitcast.row_ref, f32[424,128]{1,0:T(8,128)S(1)} %get-tuple-element.50.aux_ref, bf16[2,128,256]{2,1,0:T(8,128)(2,1)S(1)} %copy-done.1, bf16[2,144,128]{2,1,0:T(8,128)(2,1)S(1)} %get-tuple-element.58.rest_0_, ...), custom_call_target="tpu_custom_call", output_to_operand_aliasing={{}: (7, {})} | custom-call | flops 150994944 | bytes 1474560 | tf_op jit(solution)/shard_map/gate_last/pallas_call | solution.py:472
  (4 shorter events, 0.1 us)
Async XLA Ops:
  3.4 8.5 %collective-permute-start = (bf16[1,192,128]{2,1,0:T(8,128)(2,1)}, bf16[1,192,128]{2,1,0:T(8,128)(2,1)S(1)}, u32[]{:S(2)}, u32[]{:S(2)}) collective-permute-start(bf16[1,192,128]{2,1,0:T(8,128)(2,1)} %get-tuple-element.35.rest_0_), channel_id=1, source_target_pairs={{0,12},{1,5},{2,14},{3,7},{4,8},{5,1},{6,10},{7,3},{8,4},{9,13},{1... | collective-permute-start | bytes 147464 | tf_op jit(solution)/shard_map/ppermute | solution.py:303
  8.5 4.3 %collective-permute-start.4 = (bf16[1,192,128]{2,1,0:T(8,128)(2,1)}, bf16[1,192,128]{2,1,0:T(8,128)(2,1)S(1)}, u32[]{:S(2)}, u32[]{:S(2)}) collective-permute-start(bf16[1,192,128]{2,1,0:T(8,128)(2,1)} %get-tuple-element.35.rest_0_), channel_id=1, source_target_pairs={{0,4},{1,9},{2,6},{3,11},{4,0},{5,13},{6,2},{7,15},{8,12},{9,1},{1... | collective-permute-start | bytes 147464 | tf_op jit(solution)/shard_map/ppermute | solution.py:303
  8.5 5.8 %collective-permute-start.2 = (bf16[1,192,128]{2,1,0:T(8,128)(2,1)}, bf16[1,192,128]{2,1,0:T(8,128)(2,1)S(1)}, u32[]{:S(2)}, u32[]{:S(2)}) collective-permute-start(bf16[1,192,128]{2,1,0:T(8,128)(2,1)} %get-tuple-element.35.rest_0_), channel_id=1, source_target_pairs={{0,8},{1,13},{2,10},{3,15},{4,12},{5,9},{6,14},{7,11},{8,0},{9,5},... | collective-permute-start | bytes 147464 | tf_op jit(solution)/shard_map/ppermute | solution.py:303
  9.2 10.0 %collective-permute-start.7 = (bf16[1,192,128]{2,1,0:T(8,128)(2,1)}, bf16[1,192,128]{2,1,0:T(8,128)(2,1)S(1)}, u32[]{:S(2)}, u32[]{:S(2)}) collective-permute-start(bf16[1,192,128]{2,1,0:T(8,128)(2,1)} %get-tuple-element.35.rest_0_), channel_id=1, source_target_pairs={{0,1},{1,0},{2,3},{3,2},{4,5},{5,4},{6,7},{7,6},{8,9},{9,8},{10,11... | collective-permute-start | bytes 147464 | tf_op jit(solution)/shard_map/ppermute | solution.py:303
  9.2 10.1 %collective-permute-start.6 = (bf16[1,192,128]{2,1,0:T(8,128)(2,1)}, bf16[1,192,128]{2,1,0:T(8,128)(2,1)S(1)}, u32[]{:S(2)}, u32[]{:S(2)}) collective-permute-start(bf16[1,192,128]{2,1,0:T(8,128)(2,1)} %get-tuple-element.35.rest_0_), channel_id=1, source_target_pairs={{0,2},{1,3},{2,0},{3,1},{4,6},{5,7},{6,4},{7,5},{8,10},{9,11},{10,... | collective-permute-start | bytes 147464 | tf_op jit(solution)/shard_map/ppermute | solution.py:303
  10.8 1.0 %copy-start.2 = (bf16[1792,128]{1,0:T(8,128)(2,1)S(1)}, bf16[1792,128]{1,0:T(8,128)(2,1)}, u32[]{:S(2)}) copy-start(bf16[1792,128]{1,0:T(8,128)(2,1)} %get-tuple-element.36.refs_0_) | copy-start | bytes 1376260
  12.8 6.5 %collective-permute-start.5 = (bf16[1,192,128]{2,1,0:T(8,128)(2,1)S(1)}, bf16[1,192,128]{2,1,0:T(8,128)(2,1)S(1)}, u32[]{:S(2)}, u32[]{:S(2)}) collective-permute-start(bf16[1,192,128]{2,1,0:T(8,128)(2,1)S(1)} %collective-permute-done.4.refs_2_), channel_id=1, source_target_pairs={{0,2},{1,3},{2,0},{3,1},{4,6},{5,7},{6,4},{7,5},{8,10},{9,11},{10,... | collective-permute-start | bytes 147464 | tf_op jit(solution)/shard_map/ppermute | solution.py:303
  14.4 4.9 %collective-permute-start.3 = (bf16[1,192,128]{2,1,0:T(8,128)(2,1)S(1)}, bf16[1,192,128]{2,1,0:T(8,128)(2,1)S(1)}, u32[]{:S(2)}, u32[]{:S(2)}) collective-permute-start(bf16[1,192,128]{2,1,0:T(8,128)(2,1)S(1)} %collective-permute-done.2.refs_1_), channel_id=1, source_target_pairs={{0,2},{1,3},{2,0},{3,1},{4,6},{5,7},{6,4},{7,5},{8,10},{9,11},{10,... | collective-permute-start | bytes 147464 | tf_op jit(solution)/shard_map/ppermute | solution.py:303
  15.5 4.1 %collective-permute-start.1 = (bf16[1,192,128]{2,1,0:T(8,128)(2,1)S(1)}, bf16[1,192,128]{2,1,0:T(8,128)(2,1)S(1)}, u32[]{:S(2)}, u32[]{:S(2)}) collective-permute-start(bf16[1,192,128]{2,1,0:T(8,128)(2,1)S(1)} %collective-permute-done.refs_0_), channel_id=1, source_target_pairs={{0,2},{1,3},{2,0},{3,1},{4,6},{5,7},{6,4},{7,5},{8,10},{9,11},{10,... | collective-permute-start | bytes 147464 | tf_op jit(solution)/shard_map/ppermute | solution.py:303
  16.4 4.2 %copy-start = (bf16[12,192,128]{2,1,0:T(8,128)(2,1)S(1)}, bf16[12,192,128]{2,1,0:T(8,128)(2,1)}, u32[]{:S(2)}) copy-start(bf16[12,192,128]{2,1,0:T(8,128)(2,1)} %state_ref.1) | copy-start | bytes 1769476
  16.4 4.2 %copy-start.3 = (f32[424,128]{1,0:T(8,128)S(1)}, f32[424,128]{1,0:T(8,128)}, u32[]{:S(2)}) copy-start(f32[424,128]{1,0:T(8,128)} %get-tuple-element.34.aux_ref) | copy-start | bytes 651268
  16.4 4.2 %copy-start.4 = (bf16[1,192,128]{2,1,0:T(8,128)(2,1)S(1)}, bf16[1,192,128]{2,1,0:T(8,128)(2,1)}, u32[]{:S(2)}) copy-start(bf16[1,192,128]{2,1,0:T(8,128)(2,1)} %get-tuple-element.35.rest_0_) | copy-start | bytes 147460
  19.2 1.4 %collective-permute-start.8 = (bf16[3,192,128]{2,1,0:T(8,128)(2,1)S(1)}, bf16[3,192,128]{2,1,0:T(8,128)(2,1)S(1)}, u32[]{:S(2)}, u32[]{:S(2)}) collective-permute-start(bf16[3,192,128]{2,1,0:T(8,128)(2,1)S(1)} %join.2.rest_3_), channel_id=1, source_target_pairs={{0,1},{1,0},{2,3},{3,2},{4,5},{5,4},{6,7},{7,6},{8,9},{9,8},{10,11... | collective-permute-start | bytes 442376 | tf_op jit(solution)/shard_map/ppermute | solution.py:303
  19.7 1.5 %collective-permute-start.10 = (bf16[3,192,128]{2,1,0:T(8,128)(2,1)S(1)}, bf16[3,192,128]{2,1,0:T(8,128)(2,1)S(1)}, u32[]{:S(2)}, u32[]{:S(2)}) collective-permute-start(bf16[3,192,128]{2,1,0:T(8,128)(2,1)S(1)} %join.3.rest_5_), channel_id=1, source_target_pairs={{0,1},{1,0},{2,3},{3,2},{4,5},{5,4},{6,7},{7,6},{8,9},{9,8},{10,11... | collective-permute-start | bytes 442376 | tf_op jit(solution)/shard_map/ppermute | solution.py:303
  19.9 1.3 %collective-permute-start.9 = (bf16[1,192,128]{2,1,0:T(8,128)(2,1)S(1)}, bf16[1,192,128]{2,1,0:T(8,128)(2,1)S(1)}, u32[]{:S(2)}, u32[]{:S(2)}) collective-permute-start(bf16[1,192,128]{2,1,0:T(8,128)(2,1)S(1)} %collective-permute-done.6.rest_2_), channel_id=1, source_target_pairs={{0,1},{1,0},{2,3},{3,2},{4,5},{5,4},{6,7},{7,6},{8,9},{9,8},{10,11... | collective-permute-start | bytes 147464 | tf_op jit(solution)/shard_map/ppermute | solution.py:303
  21.2 17.3 %copy-start.1 = (bf16[2,128,256]{2,1,0:T(8,128)(2,1)S(1)}, bf16[2,128,256]{2,1,0:T(8,128)(2,1)}, u32[]{:S(2)}) copy-start(bf16[2,128,256]{2,1,0:T(8,128)(2,1)} %get-tuple-element.55.gates_ref) | copy-start | bytes 393220
  24.6 1.6 %collective-permute-start.11 = (bf16[8,144,128]{2,1,0:T(8,128)(2,1)S(1)}, bf16[8,144,128]{2,1,0:T(8,128)(2,1)S(1)}, u32[]{:S(2)}, u32[]{:S(2)}) collective-permute-start(bf16[8,144,128]{2,1,0:T(8,128)(2,1)S(1)} %get-tuple-element.57), channel_id=1, source_target_pairs={{0,1},{1,0},{2,3},{3,2},{4,5},{5,4},{6,7},{7,6},{8,9},{9,8},{10,11... | collective-permute-start | bytes 884744 | tf_op jit(solution)/shard_map/ppermute | solution.py:303
  26.3 8.0 %collective-permute-start.15 = (bf16[2,144,128]{2,1,0:T(8,128)(2,1)S(1)}, bf16[2,144,128]{2,1,0:T(8,128)(2,1)S(1)}, u32[]{:S(2)}, u32[]{:S(2)}) collective-permute-start(bf16[2,144,128]{2,1,0:T(8,128)(2,1)S(1)} %get-tuple-element.62), channel_id=1, source_target_pairs={{0,14},{1,7},{2,12},{3,5},{4,10},{5,3},{6,8},{7,1},{8,6},{9,15},{1... | collective-permute-start | bytes 221192 | tf_op jit(solution)/shard_map/ppermute | solution.py:303
  29.3 6.3 %collective-permute-start.16 = (bf16[2,144,128]{2,1,0:T(8,128)(2,1)S(1)}, bf16[2,144,128]{2,1,0:T(8,128)(2,1)S(1)}, u32[]{:S(2)}, u32[]{:S(2)}) collective-permute-start(bf16[2,144,128]{2,1,0:T(8,128)(2,1)S(1)} %get-tuple-element.63), channel_id=1, source_target_pairs={{0,12},{1,5},{2,14},{3,7},{4,8},{5,1},{6,10},{7,3},{8,4},{9,13},{1... | collective-permute-start | bytes 221192 | tf_op jit(solution)/shard_map/ppermute | solution.py:303
  30.7 7.7 %collective-permute-start.17 = (bf16[2,144,128]{2,1,0:T(8,128)(2,1)S(1)}, bf16[2,144,128]{2,1,0:T(8,128)(2,1)S(1)}, u32[]{:S(2)}, u32[]{:S(2)}) collective-permute-start(bf16[2,144,128]{2,1,0:T(8,128)(2,1)S(1)} %get-tuple-element.64), channel_id=1, source_target_pairs={{0,6},{1,15},{2,4},{3,13},{4,2},{5,11},{6,0},{7,9},{8,14},{9,7},{1... | collective-permute-start | bytes 221192 | tf_op jit(solution)/shard_map/ppermute | solution.py:303
  31.0 7.5 %collective-permute-start.18 = (bf16[2,144,128]{2,1,0:T(8,128)(2,1)S(1)}, bf16[2,144,128]{2,1,0:T(8,128)(2,1)S(1)}, u32[]{:S(2)}, u32[]{:S(2)}) collective-permute-start(bf16[2,144,128]{2,1,0:T(8,128)(2,1)S(1)} %get-tuple-element.65), channel_id=1, source_target_pairs={{0,4},{1,13},{2,6},{3,15},{4,0},{5,9},{6,2},{7,11},{8,12},{9,5},{1... | collective-permute-start | bytes 221192 | tf_op jit(solution)/shard_map/ppermute | solution.py:303
  33.1 7.1 %collective-permute-start.12 = (bf16[2,144,128]{2,1,0:T(8,128)(2,1)S(1)}, bf16[2,144,128]{2,1,0:T(8,128)(2,1)S(1)}, u32[]{:S(2)}, u32[]{:S(2)}) collective-permute-start(bf16[2,144,128]{2,1,0:T(8,128)(2,1)S(1)} %get-tuple-element.59), channel_id=1, source_target_pairs={{0,2},{1,3},{2,0},{3,1},{4,6},{5,7},{6,4},{7,5},{8,10},{9,11},{10,... | collective-permute-start | bytes 221192 | tf_op jit(solution)/shard_map/ppermute | solution.py:303
  34.2 8.9 %collective-permute-start.13 = (bf16[2,144,128]{2,1,0:T(8,128)(2,1)S(1)}, bf16[2,144,128]{2,1,0:T(8,128)(2,1)S(1)}, u32[]{:S(2)}, u32[]{:S(2)}) collective-permute-start(bf16[2,144,128]{2,1,0:T(8,128)(2,1)S(1)} %get-tuple-element.60), channel_id=1, source_target_pairs={{0,10},{1,11},{2,8},{3,9},{4,14},{5,15},{6,12},{7,13},{8,2},{9,3},... | collective-permute-start | bytes 221192 | tf_op jit(solution)/shard_map/ppermute | solution.py:303
  35.5 8.7 %collective-permute-start.14 = (bf16[2,144,128]{2,1,0:T(8,128)(2,1)S(1)}, bf16[2,144,128]{2,1,0:T(8,128)(2,1)S(1)}, u32[]{:S(2)}, u32[]{:S(2)}) collective-permute-start(bf16[2,144,128]{2,1,0:T(8,128)(2,1)S(1)} %get-tuple-element.61), channel_id=1, source_target_pairs={{0,8},{1,9},{2,10},{3,11},{4,12},{5,13},{6,14},{7,15},{8,0},{9,1},... | collective-permute-start | bytes 221192 | tf_op jit(solution)/shard_map/ppermute | solution.py:303
